TPU v7x, 32 devices: a whole 2x2x4 slice. The times are simulated.
32 devices in a mesh: tm: 16 (over z, y, x), space: 2 (over core).
Axes of the slice: x: 2, y: 2, z: 4, core: 2. Of those that a mesh axis runs over, the one named last changes fastest.
Arguments:
- diag_inverse: bfloat16 [32, 2048, 2048], P('tm', 'space'), may hold values from -0.5 to 1.25, as said below
- coupling: bfloat16 [32, 2048, 2048], P('tm', 'space'), may hold values from -0.078125 to 0.078125
- arrow: bfloat16 [32, 256, 2048], P('tm', None, 'space'), may hold values from -0.046875 to 0.046875
- tip_inverse: bfloat16 [256, 256], replicated, may hold values from -0.5 to 1.25, as said below
- noise: bfloat16 [32, 2048, 256], P('tm', 'space'), may hold values from -6 to 6
- noise_fixed: float32 [256, 256], P(None, 'space'), may hold values from -6 to 6
- section_lengths: int32 [16], replicated, may hold values from 1 to 2, 24 in all
Outputs:
- sample: bfloat16 [32, 2048, 256], P('tm', 'space')
- fixed_sample: float32 [256, 256], P(None, 'space')
Inputs may be any that keep to these rules, and one draw needn't show every extreme that they name: `diag_inverse`: each of its 32 blocks is lower triangular with a diagonal between 0.5 and 1.25. `tip_inverse`: lower triangular with a diagonal between 0.5 and 1.25. `section_lengths`: the lengths sum to 24.
All inputs are finite; a program needn't handle non-finite values.
Results may differ from a plain program's by a relative error of at most 0.012.
Values may be sent and summed in bfloat16 or wider, within the bound.
No kernel may reach another device: no remote copies, remote signals or barrier semaphores. Data moves between devices by JAX's collectives and lax.ppermute only.
A program may use at most 64 MiB of HBM per device.

v0:
```python
import jax
import jax.numpy as jnp
from jax import lax
from jax.sharding import PartitionSpec as P


def on_device(diag_inverse, coupling, arrow, tip_inverse, noise, noise_fixed, section_lengths):
    slot_count, local_rows, node_count = diag_inverse.shape
    columns = noise.shape[2]
    fixed_width = noise_fixed.shape[1]
    position = lax.axis_index("tm")
    space_index = lax.axis_index("space")
    own_length = lax.dynamic_index_in_dim(section_lengths, position, 0, keepdims=False)
    groups = 1
    group_cols = columns // groups
    contract_rows = (((0,), (0,)), ((), ()))
    stored = []
    earlier = jnp.zeros((local_rows, group_cols), jnp.bfloat16)
    for forward_slot_index in range(slot_count):
        couple = coupling[forward_slot_index]
        inverse = diag_inverse[forward_slot_index]
        source = noise[forward_slot_index].astype(jnp.float32)
        if forward_slot_index > 0:
            pulled = jnp.dot(
                couple,
                lax.all_gather(earlier, "space", axis=0, tiled=True),
                preferred_element_type=jnp.float32,
            )
            target = (source - pulled).astype(jnp.bfloat16)
        else:
            target = source.astype(jnp.bfloat16)
        solved = jnp.dot(
            inverse,
            lax.all_gather(target, "space", axis=0, tiled=True),
            preferred_element_type=jnp.float32,
        )
        stored.append(solved)
        earlier = solved.astype(jnp.bfloat16)
    values_store = [stored[s] for s in range(slot_count)]
    partial_value = jnp.zeros((arrow.shape[1], columns), jnp.float32)
    for slot_index in range(slot_count):
        kept = jnp.where(
            slot_index < own_length,
            values_store[slot_index].astype(jnp.bfloat16),
            jnp.zeros((local_rows, columns), jnp.bfloat16),
        )
        partial_value = partial_value + jnp.dot(
            arrow[slot_index], kept, preferred_element_type=jnp.float32
        )
    placed = lax.dynamic_update_slice(
        jnp.zeros_like(partial_value),
        jnp.where(position == 0, noise_fixed, 0.0),
        (jnp.int32(0), space_index * fixed_width),
    )
    mixed_sum = lax.psum(placed - partial_value, ("tm", "space"))
    tip_forward = jnp.dot(
        tip_inverse, mixed_sum.astype(jnp.bfloat16), preferred_element_type=jnp.float32
    )
    fixed_sample = lax.dot_general(
        tip_inverse,
        tip_forward.astype(jnp.bfloat16),
        contract_rows,
        preferred_element_type=jnp.float32,
    )
    fixed_bar = fixed_sample.astype(jnp.bfloat16)
    outputs = [None] * slot_count
    carried = jnp.zeros((local_rows, group_cols), jnp.float32)
    for slot_index in reversed(range(slot_count)):
        slot_live = slot_index < own_length
        backward_couple = coupling[slot_index]
        backward_inverse = diag_inverse[slot_index]
        spread = lax.dot_general(
            arrow[slot_index], fixed_bar, contract_rows, preferred_element_type=jnp.float32
        )
        forward_part = values_store[slot_index]
        target = (forward_part - spread - carried).astype(jnp.bfloat16)
        solved = lax.psum_scatter(
            lax.dot_general(
                backward_inverse, target, contract_rows, preferred_element_type=jnp.float32
            ).astype(jnp.bfloat16),
            "space",
            scatter_dimension=0,
            tiled=True,
        ).astype(jnp.float32)
        rounded = jnp.where(
            slot_live,
            solved.astype(jnp.bfloat16),
            jnp.zeros((local_rows, group_cols), jnp.bfloat16),
        )
        outputs[slot_index] = rounded
        if slot_index > 0:
            passed = lax.psum_scatter(
                lax.dot_general(
                    backward_couple, rounded, contract_rows, preferred_element_type=jnp.float32
                ).astype(jnp.bfloat16),
                "space",
                scatter_dimension=0,
                tiled=True,
            ).astype(jnp.float32)
            carried = jnp.where(slot_live, passed, carried)
    sample_store = jnp.stack([outputs[s] for s in range(slot_count)])
    fixed_out = lax.dynamic_slice_in_dim(fixed_sample, space_index * fixed_width, fixed_width, 1)
    return (sample_store, fixed_out)


def solution(mesh):
    return jax.shard_map(
        on_device,
        mesh=mesh,
        in_specs=(
            P("tm", "space", None),
            P("tm", "space", None),
            P("tm", None, "space"),
            P(),
            P("tm", "space", None),
            P(None, "space"),
            P(),
        ),
        out_specs=(P("tm", "space", None), P(None, "space")),
        check_vma=False,
    )
```

profile of v0, /device:TPU:0, one launch (start us, length us, event | category | flops | bytes accessed | tf_op | source)
XLA Modules:
  0.0 152.0 jit_solution(9434606551771679091)
XLA Ops:
  7.2 0.0 copy-start
  7.2 0.0 all-gather.9.cloned.1.call-start
  7.2 1.9 %slice.27 = bf16[1,1024,256]{2,1,0:T(8,128)(2,1)} slice(bf16[2,1024,256]{2,1,0:T(8,128)(2,1)} %param.11), slice={[0:1], [0:1024], [0:256]} | slice | bytes 1048576 | tf_op jit(solution)/shard_map/slice | solution.py:22
  9.1 0.0 all-gather.9.cloned.1.call-update
  9.1 0.0 copy-start.3
  9.2 0.0 all-gather.5.cloned.1.call-start
  9.2 12.7 %all-gather.9.cloned.1.call-done = bf16[1,2048,256]{2,1,0:T(8,128)(2,1)} async-done(((bf16[1,1024,256]{2,1,0:T(8,128)(2,1)}), bf16[1,2048,256]{2,1,0:T(8,128)(2,1)}) %all-gather.9.cloned.1.call-update) | async-done | bytes 1048592 | tf_op jit(solution)/shard_map/all_gather | solution.py:34
  21.9 4.9 %fusion.89 = (bf16[1024,256]{1,0:T(8,128)(2,1)}, f32[1024,256]{1,0:T(8,128)}) fusion(bf16[1,2048,256]{2,1,0:T(8,128)(2,1)} %all-gather.9.cloned.1.call-done, bf16[2,1024,2048]{2,1,0:T(8,128)(2,1)} %param.7), kind=kOutput, calls=%fused_computation.73 | convolution fusion | flops 1074003968 | bytes 6815744 | tf_op jit(solution)/shard_map/dot_general | solution.py:32
  26.8 0.0 all-gather.5.cloned.1.call-update
  26.8 0.0 copy-start.6
  26.9 0.0 copy-start.5
  26.9 0.0 all-gather.7.cloned.1.call-start
  26.9 10.3 %all-gather.5.cloned.1.call-done = bf16[2048,256]{1,0:T(8,128)(2,1)} async-done(((bf16[1024,256]{1,0:T(8,128)(2,1)}), bf16[2048,256]{1,0:T(8,128)(2,1)}) %all-gather.5.cloned.1.call-update) | async-done | bytes 1048592 | tf_op jit(solution)/shard_map/all_gather | solution.py:26
  37.2 0.0 copy-done.3
  37.2 4.5 %fusion.44 = bf16[1024,256]{1,0:T(8,128)(2,1)} fusion(bf16[2048,256]{1,0:T(8,128)(2,1)} %all-gather.5.cloned.1.call-done, bf16[2,1024,2048]{2,1,0:T(8,128)(2,1)} %param.8, bf16[2,1024,256]{2,1,0:T(8,128)(2,1)S(1)} %copy-done.3), kind=kOutput, calls=%fused_computation.30 | convolution fusion | flops 1074528256 | bytes 6291456 | tf_op jit(solution)/shard_map/dot_general | solution.py:24
  41.7 0.0 all-gather.7.cloned.1.call-update
  41.8 0.0 reduce-scatter.4.cloned.1.call-start
  41.8 0.0 copy-done.6
  41.8 0.6 dynamic_slice.7
  43.8 0.0 copy-done.5
  43.8 0.0 copy-start.4
  43.8 0.0 copy-start.1
  43.8 8.3 %all-gather.7.cloned.1.call-done = bf16[2048,256]{1,0:T(8,128)(2,1)} async-done(((bf16[1024,256]{1,0:T(8,128)(2,1)}), bf16[2048,256]{1,0:T(8,128)(2,1)}) %all-gather.7.cloned.1.call-update) | async-done | bytes 1048592 | tf_op jit(solution)/shard_map/all_gather | solution.py:34
  52.1 3.8 %fusion.2 = f32[256,1024]{1,0:T(8,128)S(1)} fusion(bf16[2048,256]{1,0:T(8,128)(2,1)} %all-gather.7.cloned.1.call-done, bf16[2,1024,2048]{2,1,0:T(8,128)(2,1)} %param.7), kind=kOutput, calls=%fused_computation.2 | convolution fusion | flops 1073741824 | bytes 6291456 | tf_op jit(solution)/shard_map/dot_general | solution.py:32
  55.9 0.0 copy-done.4
  55.9 0.3 fusion.57
  56.3 0.0 copy-done.1
  56.3 0.3 fusion.50
  56.6 43.2 %all-reduce.1 = bf16[256,256]{1,0:T(8,128)(2,1)S(1)} all-reduce(f32[256,256]{1,0:T(8,128)S(1)} %fusion.50), channel_id=1, replica_groups=mesh['tm'=16,'space'=2] {'tm','space'}, use_global_device_ids=true, to_apply=%region_0.1 | all-reduce | flops 65536 | bytes 393216 | tf_op jit(solution)/shard_map/psum | solution.py:55
  99.8 0.0 copy-done
  99.8 0.4 fusion.51
  100.2 4.9 %fusion.27 = bf16[2048,256]{1,0:T(8,128)(2,1)} fusion(bf16[2,1024,2048]{2,1,0:T(8,128)(2,1)} %param.7, f32[256,1024]{1,0:T(8,128)S(1)} %fusion.2, bf16[2,256,1024]{2,1,0:T(8,128)(2,1)S(1)} %copy-done.4, f32[256,256]{1,0:T(8,128)S(1)} %fusion.51), kind=kOutput, calls=%fused_computation.21 | convolution fusion | flops 1209073664 | bytes 7077888 | tf_op jit(solution)/shard_map/dot_general | solution.py:78
  105.1 0.0 reduce-scatter.4.cloned.1.call-update
  105.2 0.0 copy-start.7
  105.2 0.0 reduce-scatter.6.cloned.1.call-start
  105.2 7.7 %reduce-scatter.4.cloned.1.call-done = bf16[1024,256]{1,0:T(8,128)(2,1)} async-done(((bf16[2048,256]{1,0:T(8,128)(2,1)}), bf16[1024,256]{1,0:T(8,128)(2,1)}) %reduce-scatter.4.cloned.1.call-update) | async-done | bytes 524304 | tf_op jit(solution)/shard_map/reduce_scatter | solution.py:77
  112.9 4.9 %fusion.30 = bf16[2048,256]{1,0:T(8,128)(2,1)} fusion(bf16[2,1024,2048]{2,1,0:T(8,128)(2,1)} %param.8, bf16[1024,256]{1,0:T(8,128)(2,1)} %reduce-scatter.4.cloned.1.call-done, pred[]{:T(512)} %bitcast.4), kind=kOutput, calls=%fused_computation.22 | convolution fusion | flops 1074528256 | bytes 5767680 | tf_op jit(solution)/shard_map/dot_general | solution.py:93
  117.8 0.0 reduce-scatter.6.cloned.1.call-update
  117.8 0.0 reduce-scatter.8.cloned.1.call-start
  117.9 9.8 %reduce-scatter.6.cloned.1.call-done = bf16[1024,256]{1,0:T(8,128)(2,1)} async-done(((bf16[2048,256]{1,0:T(8,128)(2,1)}), bf16[1024,256]{1,0:T(8,128)(2,1)}) %reduce-scatter.6.cloned.1.call-update) | async-done | bytes 524304 | tf_op jit(solution)/shard_map/reduce_scatter | solution.py:92
  127.7 0.0 copy-done.7
  127.7 0.0 copy-start.2
  127.7 5.4 %fusion.33 = bf16[2048,256]{1,0:T(8,128)(2,1)} fusion(bf16[2,1024,2048]{2,1,0:T(8,128)(2,1)} %param.7, f32[1024,256]{1,0:T(8,128)S(1)} %copy-done.7, bf16[1024,256]{1,0:T(8,128)(2,1)} %reduce-scatter.6.cloned.1.call-done, pred[]{:T(512)} %bitcast.4, bf16[2,256,1024]{2,1,0:T(8,128)(2,1)S(1)} %copy-done.4, f32[256,256]{1,0:T(8,128)S(1)} %fusion.51), kind=kOutput, calls=%fused_computation.23 | convolution fusion | flops 1209860096 | bytes 7602688 | tf_op jit(solution)/shard_map/dot_general | solution.py:78
  133.1 0.0 reduce-scatter.8.cloned.1.call-update
  133.1 0.8 copy.11
  133.9 0.0 copy-done.2
  133.9 9.0 %reduce-scatter.8.cloned.1.call-done = bf16[1024,256]{1,0:T(8,128)(2,1)} async-done(((bf16[2048,256]{1,0:T(8,128)(2,1)}), bf16[1024,256]{1,0:T(8,128)(2,1)}) %reduce-scatter.8.cloned.1.call-update) | async-done | bytes 524304 | tf_op jit(solution)/shard_map/reduce_scatter | solution.py:77
  143.0 1.1 select_bitcast_fusion
  144.1 1.1 pad_maximum_fusion
  (4 shorter events, 0.1 us)
Async XLA Ops:
  7.2 92.7 %copy-start = (bf16[256,256]{1,0:T(8,128)(2,1)S(1)}, bf16[256,256]{1,0:T(8,128)(2,1)}, u32[]{:S(2)}) copy-start(bf16[256,256]{1,0:T(8,128)(2,1)} %param.10) | copy-start | bytes 393220
  7.2 14.7 %all-gather.9.cloned.1.call-start = ((), (), s32[]{:S(2)}) async-start(), calls=%async_computation.8 | async-start | bytes 1572864 | tf_op jit(solution)/shard_map/all_gather | solution.py:34
  9.1 28.0 %copy-start.3 = (bf16[2,1024,256]{2,1,0:T(8,128)(2,1)S(1)}, bf16[2,1024,256]{2,1,0:T(8,128)(2,1)}, u32[]{:S(2)}) copy-start(bf16[2,1024,256]{2,1,0:T(8,128)(2,1)} %param.11) | copy-start | bytes 3145732
  9.2 28.0 %all-gather.5.cloned.1.call-start = ((), (), s32[]{:S(2)}) async-start(), calls=%async_computation.3 | async-start | bytes 1572864 | tf_op jit(solution)/shard_map/all_gather | solution.py:26
  26.8 15.0 %copy-start.6 = (s32[16]{0:T(128)S(1)}, s32[16]{0:T(128)}, u32[]{:S(2)}) copy-start(s32[16]{0:T(128)} %param.13) | copy-start | bytes 196
  26.9 16.9 %copy-start.5 = (f32[256,128]{1,0:T(8,128)S(1)}, f32[256,128]{1,0:T(8,128)}, u32[]{:S(2)}) copy-start(f32[256,128]{1,0:T(8,128)} %param.12) | copy-start | bytes 393220
  26.9 25.3 %all-gather.7.cloned.1.call-start = ((), (), s32[]{:S(2)}) async-start(), calls=%async_computation.4 | async-start | bytes 1572864 | tf_op jit(solution)/shard_map/all_gather | solution.py:34
  41.8 71.1 %reduce-scatter.4.cloned.1.call-start = ((), (), s32[]{:S(2)}) async-start(), calls=%async_computation.5 | async-start | bytes 1572864 | tf_op jit(solution)/shard_map/reduce_scatter | solution.py:77
  43.8 12.2 %copy-start.4 = (bf16[2,256,1024]{2,1,0:T(8,128)(2,1)S(1)}, bf16[2,256,1024]{2,1,0:T(8,128)(2,1)}, u32[]{:S(2)}) copy-start(bf16[2,256,1024]{2,1,0:T(8,128)(2,1)} %param.9) | copy-start | bytes 3145732
  43.8 12.5 %copy-start.1 = (bf16[1024,256]{1,0:T(8,128)(2,1)S(1)}, bf16[1024,256]{1,0:T(8,128)(2,1)}, u32[]{:S(2)}) copy-start(bf16[1024,256]{1,0:T(8,128)(2,1)} %get-tuple-element.4) | copy-start | bytes 1572868
  105.2 22.5 %copy-start.7 = (f32[1024,256]{1,0:T(8,128)S(1)}, f32[1024,256]{1,0:T(8,128)}, u32[]{:S(2)}) copy-start(f32[1024,256]{1,0:T(8,128)} %get-tuple-element.5) | copy-start | bytes 3145732
  105.2 22.5 %reduce-scatter.6.cloned.1.call-start = ((), (), s32[]{:S(2)}) async-start(), calls=%async_computation.6 | async-start | bytes 1572864 | tf_op jit(solution)/shard_map/reduce_scatter | solution.py:92
  117.8 25.1 %reduce-scatter.8.cloned.1.call-start = ((), (), s32[]{:S(2)}) async-start(), calls=%async_computation.7 | async-start | bytes 1572864 | tf_op jit(solution)/shard_map/reduce_scatter | solution.py:77
  127.7 6.2 %copy-start.2 = (bf16[1024,256]{1,0:T(8,128)(2,1)S(1)}, bf16[1024,256]{1,0:T(8,128)(2,1)}, u32[]{:S(2)}) copy-start(bf16[1024,256]{1,0:T(8,128)(2,1)} %reduce-scatter.4.cloned.1.call-done) | copy-start | bytes 1572868
Sparse Core Ops, SparseCore 0:
  10.1 11.7 all-gather.8
  27.0 10.1 all-gather.4
  41.9 10.1 all-gather.6
  105.3 7.5 reduce-scatter.3
  118.0 9.6 reduce-scatter.5
  133.2 9.6 reduce-scatter.7
where the time goes:
time: 152 us
  waiting for transfers between devices  57.9 us (38%)
  blocking collectives  43.2 us (28%)
  matrix products  29.5 us (19%)
  between operations  15.6 us (10%)
  local copies, waits for them, and re-layouts  3.33 us (2%)
  other arithmetic  2.2 us (1%)
    psum x1, blocking collectives, on_device(): mixed_sum = lax.psum(placed - partial_value, ('tm', 'space'))  43.2 us
    all_gather x2, waiting for transfers between devices, on_device(): lax.all_gather(target, 'space', axis=0, tiled=True)  21 us
    reduce_scatter x2, waiting for transfers between devices, on_device(): lax.psum_scatter(lax.dot_general(backward_inverse, target, contract_rows,...  16.7 us
    dot_general x2, matrix products, on_device(): lax.dot_general(backward_inverse, target, contract_rows, preferred_elemen...  10.3 us
    all_gather x1, waiting for transfers between devices, on_device(): lax.all_gather(earlier, 'space', axis=0, tiled=True)  10.3 us
    reduce_scatter x1, waiting for transfers between devices, on_device(): lax.psum_scatter(lax.dot_general(backward_couple, rounded, contract_rows,...  9.81 us
    dot_general x2, matrix products, on_device(): jnp.dot(inverse, lax.all_gather(target, 'space', axis=0, tiled=True), pre...  8.72 us
    dot_general x1, matrix products, on_device(): lax.dot_general(backward_couple, rounded, contract_rows, preferred_elemen...  4.92 us
  transfers between devices with their start and end apart: 6, of which 6 were waited for; matrix products, arithmetic and copies ran while one was open for 1% of the time, Pallas kernels for 0%

commit v1 on v0

v1 whole, which is shorter than its diff:
```python
import jax
import jax.numpy as jnp
from jax import lax
from jax.sharding import PartitionSpec as P

ROWS = (((0,), (0,)), ((), ()))


def dot(left, right):
    return jnp.dot(left, right, preferred_element_type=jnp.float32)


def dot_rows(left, right):
    return lax.dot_general(left, right, ROWS, preferred_element_type=jnp.float32)


def make_on_device(n_tm, n_space):
    def shift_space(value, step, wrap):
        pairs = [
            (i, (i + step) % n_space)
            for i in range(n_space)
            if wrap or 0 <= i + step < n_space
        ]
        return lax.ppermute(value, "space", pairs)

    def on_device(diag_inverse, coupling, arrow, tip_inverse, noise, noise_fixed, section_lengths):
        slot_count, rows, _ = diag_inverse.shape
        fixed_rows = arrow.shape[1]
        fixed_width = noise_fixed.shape[1]
        position = lax.axis_index("tm")
        core = lax.axis_index("space")
        own_length = lax.dynamic_index_in_dim(section_lengths, position, 0, keepdims=False)
        live = [s < own_length for s in range(slot_count)]

        def gather(piece, lower):
            whole = jnp.zeros((n_space * rows, piece.shape[1]), piece.dtype)
            whole = lax.dynamic_update_slice(whole, piece, (core * rows, 0))
            for step in range(1, n_space):
                other = shift_space(piece, step, not lower)
                source = (core - step) % n_space
                if lower:
                    other = jnp.where(core >= step, other, jnp.zeros_like(other))
                whole = lax.dynamic_update_slice(whole, other, (source * rows, 0))
            return whole

        def scatter_sum(partial, axis, lower):
            def block(index):
                return lax.dynamic_slice_in_dim(partial, index * rows, rows, axis)

            total = lax.reduce_precision(block(core), 8, 7)
            for step in range(1, n_space):
                sent = block((core - step) % n_space).astype(jnp.bfloat16)
                got = shift_space(sent, -step, not lower).astype(jnp.float32)
                total = total + got
            return total

        def solve(slot, right):
            return dot(diag_inverse[slot], gather(right, True))

        response = [None] * slot_count
        pushed = None
        for slot in reversed(range(1, slot_count)):
            right = jnp.where(live[slot], arrow[slot], jnp.zeros_like(arrow[slot]))
            if pushed is not None:
                right = (right.astype(jnp.float32) - pushed).astype(jnp.bfloat16)
            response[slot] = scatter_sum(
                dot(right, diag_inverse[slot]), 1, True
            ).astype(jnp.bfloat16)
            pushed = scatter_sum(dot(response[slot], coupling[slot]), 1, False)

        first = solve(0, noise[0])
        bars = [first.astype(jnp.bfloat16)]
        arrow_part = dot(arrow[0], bars[0])
        values = [first]
        for slot in range(1, slot_count):
            pulled = dot(coupling[slot], gather(bars[slot - 1], False))
            target = (noise[slot].astype(jnp.float32) - pulled).astype(jnp.bfloat16)
            if slot == 1:
                arrow_part = arrow_part + dot(response[1], target)
            else:
                arrow_part = arrow_part + dot(response[slot], noise[slot])
            values.append(solve(slot, target))
            bars.append(values[slot].astype(jnp.bfloat16))

        def own_columns(index):
            return lax.dynamic_slice_in_dim(arrow_part, index * fixed_width, fixed_width, 1)

        total = own_columns(core)
        for step in range(1, n_space):
            sent = own_columns((core - step) % n_space).astype(jnp.bfloat16)
            total = total + shift_space(sent, -step, True).astype(jnp.float32)
        bit = 1
        while bit < n_tm:
            rounded = lax.reduce_precision(total, 8, 7)
            got = lax.ppermute(
                rounded.astype(jnp.bfloat16), "tm", [(i, i ^ bit) for i in range(n_tm)]
            )
            total = rounded + got.astype(jnp.float32)
            bit *= 2
        mixed = (noise_fixed - total).astype(jnp.bfloat16)
        tip_forward = dot(tip_inverse, mixed)
        fixed_out = dot_rows(tip_inverse, tip_forward.astype(jnp.bfloat16))
        fixed_own = fixed_out.astype(jnp.bfloat16)
        fixed_bar = jnp.zeros((fixed_rows, n_space * fixed_width), jnp.bfloat16)
        fixed_bar = lax.dynamic_update_slice(fixed_bar, fixed_own, (0, core * fixed_width))
        for step in range(1, n_space):
            fixed_bar = lax.dynamic_update_slice(
                fixed_bar,
                shift_space(fixed_own, step, True),
                (0, ((core - step) % n_space) * fixed_width),
            )

        base = [None] * slot_count
        carried = None
        for slot in reversed(range(slot_count)):
            target = values[slot]
            if carried is not None:
                target = target - carried
            solved = scatter_sum(
                dot_rows(diag_inverse[slot], target.astype(jnp.bfloat16)), 0, True
            )
            base[slot] = jnp.where(live[slot], solved, 0.0)
            if slot > 0:
                carried = scatter_sum(
                    dot_rows(coupling[slot], base[slot].astype(jnp.bfloat16)), 0, False
                )
        right = arrow[0]
        if pushed is not None:
            right = (right.astype(jnp.float32) - pushed).astype(jnp.bfloat16)
        response[0] = scatter_sum(dot(right, diag_inverse[0]), 1, True).astype(jnp.bfloat16)
        outputs = [
            (base[s] - dot_rows(response[s], fixed_bar)).astype(jnp.bfloat16)
            for s in range(slot_count)
        ]
        return (jnp.stack(outputs), fixed_out)

    return on_device


def solution(mesh):
    shape = dict(mesh.shape)
    return jax.shard_map(
        make_on_device(shape["tm"], shape["space"]),
        mesh=mesh,
        in_specs=(
            P("tm", "space", None),
            P("tm", "space", None),
            P("tm", None, "space"),
            P(),
            P("tm", "space", None),
            P(None, "space"),
            P(),
        ),
        out_specs=(P("tm", "space", None), P(None, "space")),
        check_vma=False,
    )
```

time: 152 us -> 77.5 us (0.51)
  waiting for transfers between devices: 57.9 us -> 1.2 us
  blocking collectives: 43.2 us -> 0 us
  starting transfers between devices: 0.25 us -> 24.1 us
  between operations: 15.6 us -> 2.53 us
  local copies, waits for them, and re-layouts: 3.33 us -> 13.6 us
  matrix products: 29.5 us -> 33.2 us
    psum x1 -> x0, blocking collectives: 43.2 us -> none  [on_device(): mixed_sum = lax.psum(placed - partial_value, ('tm', 'space'))]
    all_gather x3 -> x0, waiting for transfers between devices: 31.3 us -> none  [the longest x2 21 us: on_device(): lax.all_gather(target, 'space', axis=0, tiled=True)]
    reduce_scatter x3 -> x0, waiting for transfers between devices: 26.5 us -> none  [the longest x2 16.7 us: on_device(): lax.psum_scatter(lax.dot_general(backward_inverse, target, contract_rows,...]
    ppermute x0 -> x15, starting transfers between devices: none -> 24.1 us  [the longest x11 15.8 us: shift_space(): return lax.ppermute(value, 'space', pairs)]
    unnamed x17 -> x37, local copies, waits for them, and re-layouts: 0.8 us -> 5.64 us
    convert_element_type x0 -> x7, local copies, waits for them, and re-layouts: none -> 3.73 us  [the longest x6 3.71 us: scatter_sum(): sent = block((core - step) % n_space).astype(jnp.bfloat16)]
    dot_general x9 -> x13, matrix products: 29.5 us -> 33.2 us  [the longest x6 16.6 us: dot_rows(): lax.dot_general(left, right, ROWS, preferred_element_type=jnp.float32)]
    another operation x3 -> x1, other arithmetic: 2.18 us -> 0.1 us  [on_device(): return (jnp.stack(outputs), fixed_out)]
  transfers between devices with their start and end apart: 6 -> 15, of which waited for: 6 -> 2; matrix products, arithmetic and copies ran while one was open for 1% -> 52% of each run, Pallas kernels for 0% -> 0%
where the time goes in v1:
time: 77.5 us; the launch traced here: 77 us
  matrix products  33.2 us (43%)
  starting transfers between devices  24.1 us (31%)
  local copies, waits for them, and re-layouts  13.6 us (18%)
  between operations  2.53 us (3%)
  other arithmetic  2.43 us (3%)
  waiting for transfers between devices  1.2 us (2%)
    dot_general x6, matrix products, dot_rows(): lax.dot_general(left, right, ROWS, preferred_element_type=jnp.float32)  16.6 us
    dot_general x7, matrix products, dot(): return jnp.dot(left, right, preferred_element_type=jnp.float32)  16.6 us
    ppermute x11, starting transfers between devices, shift_space(): return lax.ppermute(value, 'space', pairs)  15.8 us
    ppermute x4, starting transfers between devices, on_device(): lax.ppermute(rounded.astype(jnp.bfloat16), 'tm', [(i, i ^ bit) for i in r...  8.26 us
    unnamed x37, local copies, waits for them, and re-layouts  5.64 us
    convert_element_type x6, local copies, waits for them, and re-layouts, scatter_sum(): sent = block((core - step) % n_space).astype(jnp.bfloat16)  3.71 us
  transfers between devices with their start and end apart: 15, of which 2 were waited for; matrix products, arithmetic and copies ran while one was open for 52% of the time, Pallas kernels for 0%

profile of v1, /device:TPU:0, one launch (start us, length us, event | category | flops | bytes accessed | tf_op | source)
XLA Modules:
  0.0 77.0 jit_solution(14758620996479663468)
XLA Ops:
  0.6 0.0 copy-start
  0.6 1.3 %fusion.81 = (bf16[1,1024,256]{2,1,0:T(8,128)(2,1)S(1)}, bf16[1,1024,256]{2,1,0:T(8,128)(2,1)S(1)}) fusion(bf16[2,1024,256]{2,1,0:T(8,128)(2,1)} %param.11), kind=kLoop, calls=%fused_computation.99 | loop fusion | bytes 2097152 | tf_op jit(solution)/shard_map/slice | solution.py:77
  2.0 0.2 copy.20
  2.2 3.2 %collective-permute-start = (bf16[1024,256]{0,1:T(8,128)(2,1)S(1)}, bf16[1024,256]{0,1:T(8,128)(2,1)}, u32[]{:S(2)}, u32[]{:S(2)}) collective-permute-start(bf16[1024,256]{0,1:T(8,128)(2,1)S(1)} %bitcast.116), channel_id=1, source_target_pairs={{0,1},{2,3},{4,5},{6,7},{8,9},{10,11},{12,13},{14,15},{16,17},{18,... | collective-permute-start | bytes 1572872 | tf_op jit(solution)/shard_map/ppermute | solution.py:24
  5.3 1.3 %dynamic_slice.46 = s32[1]{0:T(128)} dynamic-slice(s32[16]{0:T(128)} %param.13, s32[]{:T(128)S(6)} %select_n.98), dynamic_slice_sizes={1} | dynamic-slice | bytes 12 | tf_op jit(solution)/shard_map/jit(dynamic_index_in_dim)/dynamic_slice | solution.py:32
  7.3 0.0 copy-start.9
  7.3 3.6 %fusion = f32[256,2048]{1,0:T(8,128)S(1)} fusion(bf16[2,1024,2048]{2,1,0:T(8,128)(2,1)} %param.7, bf16[2,256,1024]{2,1,0:T(8,128)(2,1)} %param.9, pred[]{:T(512)} %bitcast.4), kind=kOutput, calls=%fused_computation | convolution fusion | flops 1074003968 | bytes 6816256 | tf_op jit(solution)/shard_map/dot_general | solution.py:10
  11.0 0.9 %dynamic-slice_convert_fusion.2 = bf16[256,1024]{1,0:T(8,128)(2,1)} fusion(f32[256,2048]{1,0:T(8,128)S(1)} %fusion, s32[]{:T(128)S(6)} %select_n.104), kind=kLoop, calls=%fused_computation.54 | loop fusion | bytes 1048580 | tf_op jit(solution)/shard_map/convert_element_type | solution.py:52
  11.9 1.3 %collective-permute-start.6 = (bf16[256,1024]{1,0:T(8,128)(2,1)}, bf16[256,1024]{1,0:T(8,128)(2,1)}, u32[]{:S(2)}, u32[]{:S(2)}) collective-permute-start(bf16[256,1024]{1,0:T(8,128)(2,1)} %dynamic-slice_convert_fusion.2), channel_id=1, source_target_pairs={{1,0},{3,2},{5,4},{7,6},{9,8},{11,10},{13,12},{15,14},{17,16},{19,... | collective-permute-start | bytes 1572872 | tf_op jit(solution)/shard_map/ppermute | solution.py:24
  13.2 0.8 copy.12
  14.0 1.0 %copy.21 = bf16[1,1024,256]{1,2,0:T(8,128)(2,1)} copy(bf16[1,1024,256]{2,1,0:T(8,128)(2,1)S(1)} %get-tuple-element.10) | data formatting | bytes 1048576
  15.0 0.1 broadcast.9.clone.1
  15.1 0.1 constant_dynamic-update-slice_fusion.5
  15.1 0.1 select_dynamic-update-slice_fusion.1
  15.3 0.1 broadcast.9.clone
  15.4 0.0 copy-start.7
  15.4 0.0 slice-start.3
  15.4 4.7 %constant_dynamic-update-slice_fusion.4 = (bf16[2048,256]{0,1:T(8,128)(2,1)S(1)}, bf16[1024,256]{0,1:T(8,128)(2,1)S(1)}, f32[1024,256]{0,1:T(8,128)}) fusion(bf16[2048,256]{0,1:T(8,128)(2,1)S(1)} %broadcast.9.clone, s32[]{:T(128)S(6)} %select_n.100, bf16[2048,256]{0,1:T(8,128)(2,1)S(1)} %select_dynamic-update-slice_fusion.1, bf16[2,1024,2048]{2,1,0:T(8,128)(2,1)} %param.7), kind=kOutput, calls=%fused_computation.94 | convolution fusion | flops 1074003968 | bytes 7340036 | tf_op jit(solution)/shard_map/dot_general | solution.py:10
  20.1 3.0 %collective-permute-start.1 = (bf16[1024,256]{0,1:T(8,128)(2,1)S(1)}, bf16[1024,256]{0,1:T(8,128)(2,1)S(1)}, u32[]{:S(2)}, u32[]{:S(2)}) collective-permute-start(bf16[1024,256]{0,1:T(8,128)(2,1)S(1)} %get-tuple-element.9), channel_id=1, source_target_pairs={{0,1},{1,0},{2,3},{3,2},{4,5},{5,4},{6,7},{7,6},{8,9},{9,8},{10,11... | collective-permute-start | bytes 1572872 | tf_op jit(solution)/shard_map/ppermute | solution.py:24
  23.1 0.3 convolution_bitcast_fusion
  23.5 1.2 %add_convert_fusion.1 = bf16[256,1024]{1,0:T(8,128)(2,1)S(1)} fusion(bf16[256,1024]{1,0:T(8,128)(2,1)} %collective-permute-done.6, f32[256,2048]{1,0:T(8,128)S(1)} %fusion, s32[]{:T(128)S(6)} %select_n.100), kind=kLoop, calls=%fused_computation.53 | loop fusion | flops 1048576 | bytes 2097156 | tf_op jit(solution)/shard_map/convert_element_type | solution.py:68
  24.7 1.2 %fusion.6 = f32[256,2048]{1,0:T(8,128)S(1)} fusion(bf16[256,1024]{1,0:T(8,128)(2,1)S(1)} %add_convert_fusion.1, bf16[2,1024,2048]{2,1,0:T(8,128)(2,1)S(1)} %bitcast.118), kind=kOutput, calls=%fused_computation.6 | convolution fusion | flops 1073741824 | bytes 6815744 | tf_op jit(solution)/shard_map/dot_general | solution.py:10
  26.0 0.1 constant_dynamic-update-slice_fusion.3
  26.0 1.2 %broadcast.9 = bf16[2048,256]{0,1:T(8,128)(2,1)} broadcast(bf16[]{:T(256)} %constant.59.clone.1), dimensions={} | broadcast | bytes 1048578 | tf_op jit(solution)/shard_map/broadcast.3
  27.3 2.1 %constant_dynamic-update-slice_fusion.2 = (bf16[2048,256]{0,1:T(8,128)(2,1)}, bf16[1024,256]{0,1:T(8,128)(2,1)S(1)}) fusion(bf16[2048,256]{0,1:T(8,128)(2,1)} %broadcast.9, s32[]{:T(128)S(6)} %select_n.100, bf16[2048,256]{0,1:T(8,128)(2,1)S(1)} %constant_dynamic-update-slice_fusion.3, bf16[2,1024,2048]{2,1,0:T(8,128)(2,1)S(1)} %bitcast.118, ...), kind=kOutput, calls=%fused_computation.92 | convolution fusion | flops 1074528256 | bytes 6815748 | tf_op jit(solution)/shard_map/dot_general | solution.py:10
  29.4 1.9 %collective-permute-start.2 = (bf16[1024,256]{0,1:T(8,128)(2,1)S(1)}, bf16[1024,256]{0,1:T(8,128)(2,1)S(1)}, u32[]{:S(2)}, u32[]{:S(2)}) collective-permute-start(bf16[1024,256]{0,1:T(8,128)(2,1)S(1)} %get-tuple-element.15), channel_id=1, source_target_pairs={{0,1},{2,3},{4,5},{6,7},{8,9},{10,11},{12,13},{14,15},{16,17},{18,... | collective-permute-start | bytes 1572872 | tf_op jit(solution)/shard_map/ppermute | solution.py:24
  31.3 0.3 convolution_add_fusion
  31.7 0.1 collective-permute-start.9
  31.8 0.9 %dynamic-slice_convert_fusion.1 = bf16[256,1024]{1,0:T(8,128)(2,1)} fusion(f32[256,2048]{1,0:T(8,128)S(1)} %fusion.6, s32[]{:T(128)S(6)} %select_n.104), kind=kLoop, calls=%fused_computation.52 | loop fusion | bytes 1048580 | tf_op jit(solution)/shard_map/convert_element_type | solution.py:52
  32.7 0.5 collective-permute-start.7
  33.2 2.4 %collective-permute-start.10 = (bf16[256,128]{0,1:T(8,128)(2,1)S(1)}, bf16[256,128]{0,1:T(8,128)(2,1)S(1)}, u32[]{:S(2)}, u32[]{:S(2)}) collective-permute-start(bf16[256,128]{0,1:T(8,128)(2,1)S(1)} %fusion.73), channel_id=1, source_target_pairs={{0,2},{2,0},{4,6},{6,4},{8,10},{10,8},{12,14},{14,12},{16,18},{18,... | collective-permute-start | bytes 196616 | tf_op jit(solution)/shard_map/ppermute | solution.py:95
  35.6 0.0 collective-permute-done.2
  35.6 0.9 %select_dynamic-update-slice_fusion = bf16[2048,256]{0,1:T(8,128)(2,1)} fusion(bf16[2048,256]{0,1:T(8,128)(2,1)} %get-tuple-element.14, s32[]{:T(128)S(6)} %select_n.104, bf16[1024,256]{0,1:T(8,128)(2,1)S(1)} %collective-permute-done.2, pred[]{:T(512)S(6)} %ge.4), kind=kLoop, calls=%fused_computation.70 | loop fusion | flops 262144 | bytes 1048581 | tf_op jit(solution)/shard_map/dynamic_update_slice | solution.py:43
  36.5 6.1 %fusion.2 = f32[256,2048]{1,0:T(8,128)S(1)} fusion(bf16[2,1024,2048]{2,1,0:T(8,128)(2,1)} %param.7, bf16[2048,256]{0,1:T(8,128)(2,1)} %select_dynamic-update-slice_fusion), kind=kOutput, calls=%fused_computation.2 | convolution fusion | flops 2147745792 | bytes 11534336 | tf_op jit(solution)/shard_map/dot_general | solution.py:14
  42.6 0.1 fusion.54
  42.7 1.3 %collective-permute-start.3 = (bf16[1024,256]{0,1:T(8,128)(2,1)S(1)}, bf16[1024,256]{0,1:T(8,128)(2,1)S(1)}, u32[]{:S(2)}, u32[]{:S(2)}) collective-permute-start(bf16[1024,256]{0,1:T(8,128)(2,1)S(1)} %fusion.54), channel_id=1, source_target_pairs={{1,0},{3,2},{5,4},{7,6},{9,8},{11,10},{13,12},{15,14},{17,16},{19,... | collective-permute-start | bytes 1572872 | tf_op jit(solution)/shard_map/ppermute | solution.py:24
  44.0 0.0 collective-permute-done.7
  44.0 0.0 slice-start
  44.0 4.2 %fusion.12 = f32[256,2048]{1,0:T(8,128)S(1)} fusion(bf16[2,1024,2048]{2,1,0:T(8,128)(2,1)} %param.7, bf16[256,1024]{1,0:T(8,128)(2,1)} %collective-permute-done.7, f32[256,2048]{1,0:T(8,128)} %copy-done.10, s32[]{:T(128)S(6)} %select_n.100, bf16[2,256,1024]{2,1,0:T(8,128)(2,1)} %param.9), kind=kOutput, calls=%fused_computation.12 | convolution fusion | flops 1075314688 | bytes 8388612 | tf_op jit(solution)/shard_map/dot_general | solution.py:10
  48.3 0.0 slice-start.1
  48.4 0.0 copy-start.3
  48.4 1.6 %collective-permute-start.11 = (bf16[256,128]{0,1:T(8,128)(2,1)S(1)}, bf16[256,128]{0,1:T(8,128)(2,1)S(1)}, u32[]{:S(2)}, u32[]{:S(2)}) collective-permute-start(bf16[256,128]{0,1:T(8,128)(2,1)S(1)} %fusion.71), channel_id=1, source_target_pairs={{0,4},{2,6},{4,0},{6,2},{8,12},{10,14},{12,8},{14,10},{16,20},{18,... | collective-permute-start | bytes 196616 | tf_op jit(solution)/shard_map/ppermute | solution.py:95
  50.0 0.0 collective-permute-done.3
  50.0 3.9 %fusion.8 = f32[256,2048]{1,0:T(8,128)S(1)} fusion(bf16[2,1024,2048]{2,1,0:T(8,128)(2,1)} %param.8, bf16[1024,256]{0,1:T(8,128)(2,1)S(1)} %collective-permute-done.3, f32[256,2048]{1,0:T(8,128)S(1)} %fusion.2, s32[]{:T(128)S(6)} %select_n.100, pred[]{:T(512)} %bitcast.4), kind=kOutput, calls=%fused_computation.8 | convolution fusion | flops 1075052544 | bytes 7864836 | tf_op jit(solution)/shard_map/dot_general | solution.py:14
  53.9 0.1 fusion.55
  53.9 0.8 %collective-permute-start.4 = (bf16[1024,256]{0,1:T(8,128)(2,1)S(1)}, bf16[1024,256]{0,1:T(8,128)(2,1)S(1)}, u32[]{:S(2)}, u32[]{:S(2)}) collective-permute-start(bf16[1024,256]{0,1:T(8,128)(2,1)S(1)} %fusion.55), channel_id=1, source_target_pairs={{0,1},{1,0},{2,3},{3,2},{4,5},{5,4},{6,7},{7,6},{8,9},{9,8},{10,11... | collective-permute-start | bytes 1572872 | tf_op jit(solution)/shard_map/ppermute | solution.py:24
  54.7 0.1 fusion.80
  54.8 1.6 %collective-permute-start.12 = (bf16[256,128]{0,1:T(8,128)(2,1)S(1)}, bf16[256,128]{0,1:T(8,128)(2,1)S(1)}, u32[]{:S(2)}, u32[]{:S(2)}) collective-permute-start(bf16[256,128]{0,1:T(8,128)(2,1)S(1)} %get-tuple-element.6), channel_id=1, source_target_pairs={{0,8},{2,10},{4,12},{6,14},{8,0},{10,2},{12,4},{14,6},{16,24},{18,... | collective-permute-start | bytes 196616 | tf_op jit(solution)/shard_map/ppermute | solution.py:95
  56.4 0.9 %dynamic-slice_convert_fusion = bf16[256,1024]{1,0:T(8,128)(2,1)} fusion(f32[256,2048]{1,0:T(8,128)S(1)} %fusion.12, s32[]{:T(128)S(6)} %select_n.104), kind=kLoop, calls=%fused_computation.50 | loop fusion | bytes 1048580 | tf_op jit(solution)/shard_map/convert_element_type | solution.py:52
  57.3 1.5 %collective-permute-start.8 = (bf16[256,1024]{1,0:T(8,128)(2,1)}, bf16[256,1024]{1,0:T(8,128)(2,1)}, u32[]{:S(2)}, u32[]{:S(2)}) collective-permute-start(bf16[256,1024]{1,0:T(8,128)(2,1)} %dynamic-slice_convert_fusion), channel_id=1, source_target_pairs={{1,0},{3,2},{5,4},{7,6},{9,8},{11,10},{13,12},{15,14},{17,16},{19,... | collective-permute-start | bytes 1572872 | tf_op jit(solution)/shard_map/ppermute | solution.py:24
  58.8 0.3 collective-permute-done.12
  59.1 2.6 %collective-permute-start.13 = (bf16[256,128]{0,1:T(8,128)(2,1)S(1)}, bf16[256,128]{0,1:T(8,128)(2,1)S(1)}, u32[]{:S(2)}, u32[]{:S(2)}) collective-permute-start(bf16[256,128]{0,1:T(8,128)(2,1)S(1)} %fusion.72), channel_id=1, source_target_pairs={{0,16},{2,18},{4,20},{6,22},{8,24},{10,26},{12,28},{14,30},{16,0},... | collective-permute-start | bytes 196616 | tf_op jit(solution)/shard_map/ppermute | solution.py:95
  61.8 1.3 %fusion.14 = f32[256,2048]{1,0:T(8,128)S(1)} fusion(bf16[2,1024,2048]{2,1,0:T(8,128)(2,1)S(1)} %bitcast.115, f32[1024,256]{0,1:T(8,128)S(1)} %copy-done.3, bf16[1024,256]{0,1:T(8,128)(2,1)S(1)} %collective-permute-done.4, f32[256,2048]{1,0:T(8,128)S(1)} %fusion.8, s32[]{:T(128)S(6)} %select_n.100), kind=kOutput, calls=%fused_computation.14 | convolution fusion | flops 1075052544 | bytes 8912900 | tf_op jit(solution)/shard_map/dot_general | solution.py:14
  63.1 0.9 %fusion.56 = bf16[1024,256]{0,1:T(8,128)(2,1)} fusion(f32[256,2048]{1,0:T(8,128)S(1)} %fusion.14, s32[]{:T(128)S(6)} %select_n.104), kind=kLoop, calls=%fused_computation.61 | loop fusion | bytes 1048580 | tf_op jit(solution)/shard_map/convert_element_type | solution.py:52
  64.0 1.3 %collective-permute-start.5 = (bf16[1024,256]{0,1:T(8,128)(2,1)}, bf16[1024,256]{0,1:T(8,128)(2,1)}, u32[]{:S(2)}, u32[]{:S(2)}) collective-permute-start(bf16[1024,256]{0,1:T(8,128)(2,1)} %fusion.56), channel_id=1, source_target_pairs={{1,0},{3,2},{5,4},{7,6},{9,8},{11,10},{13,12},{15,14},{17,16},{19,... | collective-permute-start | bytes 1572872 | tf_op jit(solution)/shard_map/ppermute | solution.py:24
  65.3 0.8 %collective-permute-done.13 = bf16[256,128]{0,1:T(8,128)(2,1)S(1)} collective-permute-done((bf16[256,128]{0,1:T(8,128)(2,1)S(1)}, bf16[256,128]{0,1:T(8,128)(2,1)S(1)}, u32[]{:S(2)}, u32[]{:S(2)}) %collective-permute-start.13) | collective-permute-done | bytes 65568 | tf_op jit(solution)/shard_map/ppermute | solution.py:95
  66.1 0.6 copy-done.11
  66.8 2.0 %constant_dynamic-update-slice_fusion.1 = (bf16[256,256]{0,1:T(8,128)(2,1)S(1)}, bf16[256,128]{0,1:T(8,128)(2,1)}, f32[256,128]{0,1:T(8,128)}) fusion(bf16[256,256]{0,1:T(8,128)(2,1)S(1)} %broadcast_in_dim.13, s32[]{:T(128)S(6)} %select_n.112, bf16[256,256]{1,0:T(8,128)(2,1)S(1)} %copy-done, f32[256,128]{0,1:T(8,128)} %copy.12, ...), kind=kOutput, calls=%fused_computation.87 | convolution fusion | flops 33849344 | bytes 917508 | tf_op jit(solution)/shard_map/dot_general | solution.py:14
  68.7 1.1 %collective-permute-start.14 = (bf16[256,128]{0,1:T(8,128)(2,1)}, bf16[256,128]{0,1:T(8,128)(2,1)S(1)}, u32[]{:S(2)}, u32[]{:S(2)}) collective-permute-start(bf16[256,128]{0,1:T(8,128)(2,1)} %get-tuple-element.5), channel_id=1, source_target_pairs={{0,1},{1,0},{2,3},{3,2},{4,5},{5,4},{6,7},{7,6},{8,9},{9,8},{10,11... | collective-permute-start | bytes 196616 | tf_op jit(solution)/shard_map/ppermute | solution.py:24
  70.5 1.7 %copy.16 = f32[256,128]{1,0:T(8,128)} copy(f32[256,128]{0,1:T(8,128)} %get-tuple-element.13) | data formatting | bytes 262144
  72.2 1.5 %fusion.45 = bf16[1,1024,256]{1,2,0:T(8,128)(2,1)S(1)} fusion(bf16[256,256]{0,1:T(8,128)(2,1)S(1)} %constant_dynamic-update-slice_fusion, bf16[256,1024]{1,0:T(8,128)(2,1)S(1)} %add_convert_fusion.1, bf16[1024,256]{0,1:T(8,128)(2,1)S(1)} %copy-done.5, f32[256,2048]{1,0:T(8,128)} %copy-done.2, s32[]{:T(128)S(6)} %select_n.100, pred[]{:T(512)} %bitcast.4), kind=kOutput, calls=%fused_computation.34 | convolution fusion | flops 135790592 | bytes 2752517 | tf_op jit(solution)/shard_map/dot_general | solution.py:14
  73.8 1.9 %fusion.58 = bf16[1,1024,256]{1,2,0:T(8,128)(2,1)S(1)} fusion(bf16[256,256]{0,1:T(8,128)(2,1)S(1)} %constant_dynamic-update-slice_fusion, bf16[256,1024]{1,0:T(8,128)(2,1)} %collective-permute-done.8, f32[256,2048]{1,0:T(8,128)} %copy-done.1, s32[]{:T(128)S(6)} %select_n.100, bf16[1024,256]{0,1:T(8,128)(2,1)} %collective-permute-done.5, ...), kind=kOutput, calls=%fused_computation.63 | convolution fusion | flops 136839168 | bytes 3802624 | tf_op jit(solution)/shard_map/dot_general | solution.py:14
  75.6 0.1 pad_maximum_fusion
  75.7 1.3 %copy.15 = bf16[2,1024,256]{2,1,0:T(8,128)(2,1)} copy(bf16[2,1024,256]{1,2,0:T(8,128)(2,1)S(1)} %pad_maximum_fusion) | data formatting | bytes 2097152
  (42 shorter events, 0.2 us)
Async XLA Ops:
  0.6 66.1 %copy-start = (bf16[256,256]{1,0:T(8,128)(2,1)S(1)}, bf16[256,256]{1,0:T(8,128)(2,1)}, u32[]{:S(2)}) copy-start(bf16[256,256]{1,0:T(8,128)(2,1)} %param.10) | copy-start | bytes 393220
  2.2 13.0 %collective-permute-start = (bf16[1024,256]{0,1:T(8,128)(2,1)S(1)}, bf16[1024,256]{0,1:T(8,128)(2,1)}, u32[]{:S(2)}, u32[]{:S(2)}) collective-permute-start(bf16[1024,256]{0,1:T(8,128)(2,1)S(1)} %bitcast.116), channel_id=1, source_target_pairs={{0,1},{2,3},{4,5},{6,7},{8,9},{10,11},{12,13},{14,15},{16,17},{18,... | collective-permute-start | bytes 1572872 | tf_op jit(solution)/shard_map/ppermute | solution.py:24
  7.3 5.9 %copy-start.9 = (f32[256,128]{1,0:T(8,128)S(1)}, f32[256,128]{1,0:T(8,128)}, u32[]{:S(2)}) copy-start(f32[256,128]{1,0:T(8,128)} %param.12) | copy-start | bytes 393220
  11.9 11.6 %collective-permute-start.6 = (bf16[256,1024]{1,0:T(8,128)(2,1)}, bf16[256,1024]{1,0:T(8,128)(2,1)}, u32[]{:S(2)}, u32[]{:S(2)}) collective-permute-start(bf16[256,1024]{1,0:T(8,128)(2,1)} %dynamic-slice_convert_fusion.2), channel_id=1, source_target_pairs={{1,0},{3,2},{5,4},{7,6},{9,8},{11,10},{13,12},{15,14},{17,16},{19,... | collective-permute-start | bytes 1572872 | tf_op jit(solution)/shard_map/ppermute | solution.py:24
  15.0 9.7 %slice-start.2 = ((s8[8388608]{0:T(1024)(128)(4,1)}), s8[4194304]{0:T(1024)(128)(4,1)S(1)}, s32[]{:S(2)}) async-start(s8[8388608]{0:T(1024)(128)(4,1)} %bitcast.117), calls=%async_computation.2 | async-start | bytes 8388608
  15.4 7.7 %copy-start.7 = (bf16[2,256,1024]{2,1,0:T(8,128)(2,1)S(1)}, bf16[2,256,1024]{2,1,0:T(8,128)(2,1)}, u32[]{:S(2)}) copy-start(bf16[2,256,1024]{2,1,0:T(8,128)(2,1)} %param.9) | copy-start | bytes 3145732
  15.4 9.3 %slice-start.3 = ((s8[8388608]{0:T(1024)(128)(4,1)}), s8[4194304]{0:T(1024)(128)(4,1)S(1)}, s32[]{:S(2)}) async-start(s8[8388608]{0:T(1024)(128)(4,1)} %bitcast.117), calls=%async_computation.3 | async-start | bytes 8388608
  20.1 5.9 %collective-permute-start.1 = (bf16[1024,256]{0,1:T(8,128)(2,1)S(1)}, bf16[1024,256]{0,1:T(8,128)(2,1)S(1)}, u32[]{:S(2)}, u32[]{:S(2)}) collective-permute-start(bf16[1024,256]{0,1:T(8,128)(2,1)S(1)} %get-tuple-element.9), channel_id=1, source_target_pairs={{0,1},{1,0},{2,3},{3,2},{4,5},{5,4},{6,7},{7,6},{8,9},{9,8},{10,11... | collective-permute-start | bytes 1572872 | tf_op jit(solution)/shard_map/ppermute | solution.py:24
  24.7 2.6 %copy-start.6 = (bf16[1,1024,256]{1,2,0:T(8,128)(2,1)S(1)}, bf16[1,1024,256]{1,2,0:T(8,128)(2,1)}, u32[]{:S(2)}) copy-start(bf16[1,1024,256]{1,2,0:T(8,128)(2,1)} %copy.21) | copy-start | bytes 1572868
  26.0 5.8 %copy-start.10 = (f32[256,2048]{1,0:T(8,128)}, f32[256,2048]{1,0:T(8,128)S(1)}, u32[]{:S(2)}) copy-start(f32[256,2048]{1,0:T(8,128)S(1)} %fusion.6) | copy-start | bytes 6291460
  29.4 6.2 %collective-permute-start.2 = (bf16[1024,256]{0,1:T(8,128)(2,1)S(1)}, bf16[1024,256]{0,1:T(8,128)(2,1)S(1)}, u32[]{:S(2)}, u32[]{:S(2)}) collective-permute-start(bf16[1024,256]{0,1:T(8,128)(2,1)S(1)} %get-tuple-element.15), channel_id=1, source_target_pairs={{0,1},{2,3},{4,5},{6,7},{8,9},{10,11},{12,13},{14,15},{16,17},{18,... | collective-permute-start | bytes 1572872 | tf_op jit(solution)/shard_map/ppermute | solution.py:24
  31.7 1.5 %collective-permute-start.9 = (bf16[256,128]{0,1:T(8,128)(2,1)S(1)}, bf16[256,128]{0,1:T(8,128)(2,1)S(1)}, u32[]{:S(2)}, u32[]{:S(2)}) collective-permute-start(bf16[256,128]{0,1:T(8,128)(2,1)S(1)} %dynamic-slice_convert_fusion.6), channel_id=1, source_target_pairs={{0,1},{1,0},{2,3},{3,2},{4,5},{5,4},{6,7},{7,6},{8,9},{9,8},{10,11... | collective-permute-start | bytes 196616 | tf_op jit(solution)/shard_map/ppermute | solution.py:24
  32.7 11.3 %collective-permute-start.7 = (bf16[256,1024]{1,0:T(8,128)(2,1)}, bf16[256,1024]{1,0:T(8,128)(2,1)}, u32[]{:S(2)}, u32[]{:S(2)}) collective-permute-start(bf16[256,1024]{1,0:T(8,128)(2,1)} %dynamic-slice_convert_fusion.1), channel_id=1, source_target_pairs={{0,1},{1,0},{2,3},{3,2},{4,5},{5,4},{6,7},{7,6},{8,9},{9,8},{10,11... | collective-permute-start | bytes 1572872 | tf_op jit(solution)/shard_map/ppermute | solution.py:24
  33.2 15.1 %collective-permute-start.10 = (bf16[256,128]{0,1:T(8,128)(2,1)S(1)}, bf16[256,128]{0,1:T(8,128)(2,1)S(1)}, u32[]{:S(2)}, u32[]{:S(2)}) collective-permute-start(bf16[256,128]{0,1:T(8,128)(2,1)S(1)} %fusion.73), channel_id=1, source_target_pairs={{0,2},{2,0},{4,6},{6,4},{8,10},{10,8},{12,14},{14,12},{16,18},{18,... | collective-permute-start | bytes 196616 | tf_op jit(solution)/shard_map/ppermute | solution.py:95
  42.6 7.3 %copy-start.2 = (f32[256,2048]{1,0:T(8,128)}, f32[256,2048]{1,0:T(8,128)S(1)}, u32[]{:S(2)}) copy-start(f32[256,2048]{1,0:T(8,128)S(1)} %fusion.2) | copy-start | bytes 6291460
  42.7 7.2 %collective-permute-start.3 = (bf16[1024,256]{0,1:T(8,128)(2,1)S(1)}, bf16[1024,256]{0,1:T(8,128)(2,1)S(1)}, u32[]{:S(2)}, u32[]{:S(2)}) collective-permute-start(bf16[1024,256]{0,1:T(8,128)(2,1)S(1)} %fusion.54), channel_id=1, source_target_pairs={{1,0},{3,2},{5,4},{7,6},{9,8},{11,10},{13,12},{15,14},{17,16},{19,... | collective-permute-start | bytes 1572872 | tf_op jit(solution)/shard_map/ppermute | solution.py:24
  44.0 17.8 %slice-start = ((s8[8388608]{0:T(1024)(128)(4,1)}), s8[4194304]{0:T(1024)(128)(4,1)S(1)}, s32[]{:S(2)}) async-start(s8[8388608]{0:T(1024)(128)(4,1)} %bitcast.114), calls=%async_computation | async-start | bytes 8388608
  48.3 8.2 %copy-start.1 = (f32[256,2048]{1,0:T(8,128)}, f32[256,2048]{1,0:T(8,128)S(1)}, u32[]{:S(2)}) copy-start(f32[256,2048]{1,0:T(8,128)S(1)} %fusion.12) | copy-start | bytes 6291460
  48.3 13.5 %slice-start.1 = ((s8[8388608]{0:T(1024)(128)(4,1)}), s8[4194304]{0:T(1024)(128)(4,1)S(1)}, s32[]{:S(2)}) async-start(s8[8388608]{0:T(1024)(128)(4,1)} %bitcast.114), calls=%async_computation.1 | async-start | bytes 8388608
  48.4 13.5 %copy-start.3 = (f32[1024,256]{0,1:T(8,128)S(1)}, f32[1024,256]{0,1:T(8,128)}, u32[]{:S(2)}) copy-start(f32[1024,256]{0,1:T(8,128)} %get-tuple-element.12) | copy-start | bytes 3145732
  48.4 6.4 %collective-permute-start.11 = (bf16[256,128]{0,1:T(8,128)(2,1)S(1)}, bf16[256,128]{0,1:T(8,128)(2,1)S(1)}, u32[]{:S(2)}, u32[]{:S(2)}) collective-permute-start(bf16[256,128]{0,1:T(8,128)(2,1)S(1)} %fusion.71), channel_id=1, source_target_pairs={{0,4},{2,6},{4,0},{6,2},{8,12},{10,14},{12,8},{14,10},{16,20},{18,... | collective-permute-start | bytes 196616 | tf_op jit(solution)/shard_map/ppermute | solution.py:95
  50.0 3.9 %copy-start.4 = (bf16[1024,256]{0,1:T(8,128)(2,1)}, bf16[1024,256]{0,1:T(8,128)(2,1)S(1)}, u32[]{:S(2)}) copy-start(bf16[1024,256]{0,1:T(8,128)(2,1)S(1)} %collective-permute-done.3) | copy-start | bytes 1572868
  53.9 7.9 %collective-permute-start.4 = (bf16[1024,256]{0,1:T(8,128)(2,1)S(1)}, bf16[1024,256]{0,1:T(8,128)(2,1)S(1)}, u32[]{:S(2)}, u32[]{:S(2)}) collective-permute-start(bf16[1024,256]{0,1:T(8,128)(2,1)S(1)} %fusion.55), channel_id=1, source_target_pairs={{0,1},{1,0},{2,3},{3,2},{4,5},{5,4},{6,7},{7,6},{8,9},{9,8},{10,11... | collective-permute-start | bytes 1572872 | tf_op jit(solution)/shard_map/ppermute | solution.py:24
  54.8 4.3 %collective-permute-start.12 = (bf16[256,128]{0,1:T(8,128)(2,1)S(1)}, bf16[256,128]{0,1:T(8,128)(2,1)S(1)}, u32[]{:S(2)}, u32[]{:S(2)}) collective-permute-start(bf16[256,128]{0,1:T(8,128)(2,1)S(1)} %get-tuple-element.6), channel_id=1, source_target_pairs={{0,8},{2,10},{4,12},{6,14},{8,0},{10,2},{12,4},{14,6},{16,24},{18,... | collective-permute-start | bytes 196616 | tf_op jit(solution)/shard_map/ppermute | solution.py:95
  57.3 16.4 %collective-permute-start.8 = (bf16[256,1024]{1,0:T(8,128)(2,1)}, bf16[256,1024]{1,0:T(8,128)(2,1)}, u32[]{:S(2)}, u32[]{:S(2)}) collective-permute-start(bf16[256,1024]{1,0:T(8,128)(2,1)} %dynamic-slice_convert_fusion), channel_id=1, source_target_pairs={{1,0},{3,2},{5,4},{7,6},{9,8},{11,10},{13,12},{15,14},{17,16},{19,... | collective-permute-start | bytes 1572872 | tf_op jit(solution)/shard_map/ppermute | solution.py:24
  59.1 2.7 %copy-start.8 = (bf16[256,128]{0,1:T(8,128)(2,1)}, bf16[256,128]{0,1:T(8,128)(2,1)S(1)}, u32[]{:S(2)}) copy-start(bf16[256,128]{0,1:T(8,128)(2,1)S(1)} %collective-permute-done.12) | copy-start | bytes 196612
  59.1 7.0 %collective-permute-start.13 = (bf16[256,128]{0,1:T(8,128)(2,1)S(1)}, bf16[256,128]{0,1:T(8,128)(2,1)S(1)}, u32[]{:S(2)}, u32[]{:S(2)}) collective-permute-start(bf16[256,128]{0,1:T(8,128)(2,1)S(1)} %fusion.72), channel_id=1, source_target_pairs={{0,16},{2,18},{4,20},{6,22},{8,24},{10,26},{12,28},{14,30},{16,0},... | collective-permute-start | bytes 196616 | tf_op jit(solution)/shard_map/ppermute | solution.py:95
  61.8 10.4 %copy-start.5 = (bf16[1024,256]{0,1:T(8,128)(2,1)S(1)}, bf16[1024,256]{0,1:T(8,128)(2,1)}, u32[]{:S(2)}) copy-start(bf16[1024,256]{0,1:T(8,128)(2,1)} %copy-done.4) | copy-start | bytes 1572868
  64.0 9.7 %collective-permute-start.5 = (bf16[1024,256]{0,1:T(8,128)(2,1)}, bf16[1024,256]{0,1:T(8,128)(2,1)}, u32[]{:S(2)}, u32[]{:S(2)}) collective-permute-start(bf16[1024,256]{0,1:T(8,128)(2,1)} %fusion.56), channel_id=1, source_target_pairs={{1,0},{3,2},{5,4},{7,6},{9,8},{11,10},{13,12},{15,14},{17,16},{19,... | collective-permute-start | bytes 1572872 | tf_op jit(solution)/shard_map/ppermute | solution.py:24
  66.1 0.6 copy-start.11
  68.7 3.4 %collective-permute-start.14 = (bf16[256,128]{0,1:T(8,128)(2,1)}, bf16[256,128]{0,1:T(8,128)(2,1)S(1)}, u32[]{:S(2)}, u32[]{:S(2)}) collective-permute-start(bf16[256,128]{0,1:T(8,128)(2,1)} %get-tuple-element.5), channel_id=1, source_target_pairs={{0,1},{1,0},{2,3},{3,2},{4,5},{5,4},{6,7},{7,6},{8,9},{9,8},{10,11... | collective-permute-start | bytes 196616 | tf_op jit(solution)/shard_map/ppermute | solution.py:24

commit v2 on v0

v2 whole, which is shorter than its diff:
```python
import jax
import jax.numpy as jnp
from jax import lax
from jax.experimental import pallas as pl
from jax.experimental.pallas import tpu as pltpu
from jax.sharding import PartitionSpec as P

BF = jnp.bfloat16
F32 = jnp.float32
MIB = 1 << 20


def dot(left, right):
    return jnp.dot(left, right, preferred_element_type=F32)


def dot_last(left, right):
    return lax.dot_general(left, right, (((1,), (1,)), ((), ())), preferred_element_type=F32)


def rounded(value):
    return value.astype(BF).astype(F32)


def total_of(own_ref, got_refs):
    total = rounded(own_ref[...])
    for got in got_refs:
        total = total + got[...].astype(F32)
    return total


def shape_of(shape, dtype):
    return jax.ShapeDtypeStruct(shape, dtype)


def build(n_tm, n_space, rows, columns, fixed_rows):
    nodes = n_space * rows
    tile = 256 if rows % 256 == 0 else rows
    tiles = rows // tile
    width = columns // n_space
    peers = range(1, n_space)

    def at_core():
        return lax.axis_index("space")

    def block(step, offset=0, size=rows):
        owner = lax.rem(at_core() - step + n_space, n_space)
        return pl.ds(pl.multiple_of(owner * rows + offset, tile), size)

    def call(body, outs, args, flops, moved, places=None, scratch=()):
        places = places or {}
        specs = [pl.BlockSpec(memory_space=places.get(i, pltpu.VMEM)) for i in range(len(args))]
        args = [
            pltpu.with_memory_space_constraint(a, pltpu.HBM)
            if places.get(i) is pltpu.HBM
            else a
            for i, a in enumerate(args)
        ]
        return pl.pallas_call(
            body,
            in_specs=specs,
            out_specs=[pl.BlockSpec(memory_space=pltpu.VMEM)] * len(outs),
            out_shape=outs,
            scratch_shapes=list(scratch),
            cost_estimate=pl.CostEstimate(flops=flops, bytes_accessed=moved, transcendentals=0),
            compiler_params=pltpu.CompilerParams(vmem_limit_bytes=16 * MIB),
        )(*args)

    def lower_rows(left, factor, own_ref, other_ref, wait=None):
        for j in range(tiles):
            at = j * tile
            if wait:
                wait(0, j)
            own_ref[:, at : at + tile] = dot(
                left[:, at:], factor[at:, block(0, at, tile)]
            )
        for step in peers:

            @pl.when(at_core() >= step)
            def _():
                for j in range(tiles):
                    at = j * tile
                    if wait:
                        wait(step, j)
                    other_ref[step - 1, :, at : at + tile] = dot(
                        left, factor[:, block(step, at, tile)]
                    ).astype(BF)

            @pl.when(at_core() < step)
            def _():
                other_ref[step - 1] = jnp.zeros_like(other_ref[step - 1])

    def full_rows(left, factor, own_ref, other_ref, wait=None):
        for step in (*peers, 0):
            for j in range(tiles):
                at = j * tile
                if wait:
                    wait(step, j)
                product = dot(left, factor[:, block(step, at, tile)])
                if step:
                    other_ref[step - 1, :, at : at + tile] = product.astype(BF)
                else:
                    own_ref[:, at : at + tile] = product

    def lower_own(factor, right, out_ref, wait=None):
        for i in range(tiles):
            at = i * tile
            if wait:
                wait(0, i)
            out_ref[at : at + tile] = dot(
                factor[at : at + tile, block(0, 0, at + tile)], right[: at + tile]
            )

    def start_kernel(diag, arrow, noise, lengths, d0, d1, own, other, first, e1, n0, sem1, sem0, sems):
        copies1, copies0 = {}, {}
        arrow_copy = pltpu.make_async_copy(arrow.at[1], e1, sems.at[0])
        noise_copy = pltpu.make_async_copy(noise.at[0], n0, sems.at[1])
        arrow_copy.start()
        for j in range(tiles):
            at = j * tile
            part = (pl.ds(at, rows - at), block(0, at, tile))
            copies1[0, j] = pltpu.make_async_copy(diag.at[(1, *part)], d1.at[part], sem1.at[0, j])
            copies1[0, j].start()
            part = (pl.ds(at, tile), block(0, 0, at + tile))
            copies0[0, j] = pltpu.make_async_copy(diag.at[(0, *part)], d0.at[part], sem0.at[0, j])
        for step in peers:
            for j in range(tiles):
                at = j * tile
                part = (pl.ds(0, rows), block(step, at, tile))
                copies1[step, j] = pltpu.make_async_copy(
                    diag.at[(1, *part)], d1.at[part], sem1.at[step, j]
                )
                part = (pl.ds(at, tile), block(step))
                copies0[step, j] = pltpu.make_async_copy(
                    diag.at[(0, *part)], d0.at[part], sem0.at[step, j]
                )

            @pl.when(at_core() >= step)
            def _():
                for j in range(tiles):
                    copies1[step, j].start()

        noise_copy.start()
        for j in range(tiles):
            copies0[0, j].start()
        for step in peers:

            @pl.when(at_core() >= step)
            def _():
                for j in range(tiles):
                    copies0[step, j].start()

        arrow_copy.wait()
        live = lengths[lax.axis_index("tm")] > 1
        left = jnp.where(live, e1[...], jnp.zeros_like(e1[...]))
        lower_rows(left, d1, own, other, lambda step, j: copies1[step, j].wait())
        noise_copy.wait()
        lower_own(d0, n0, first, lambda step, j: copies0[step, j].wait())
        for step in peers:

            @pl.when(at_core() >= step)
            def _():
                for j in range(tiles):
                    copies0[step, j].wait()

    def lower_rest(factor, first, got, at):
        out = first[at : at + tile]
        for step in peers:
            out = out + dot(factor[at : at + tile, block(step)], got[step - 1][...])
        return out

    def first_value_kernel(factor, first, *refs):
        got, (value, bar) = refs[: n_space - 1], refs[n_space - 1 :]
        value[...] = first[...]
        for step in peers:

            @pl.when(at_core() >= step)
            def _():
                for i in range(tiles):
                    at = i * tile
                    value[at : at + tile] = value[at : at + tile] + dot(
                        factor[at : at + tile, block(step)], got[step - 1][...]
                    )

        bar[...] = value[...].astype(BF)

    def response_kernel(coupling, value, own, *refs):
        got = refs[: n_space - 1]
        k1, response, pushed_own, pushed_other, value_rows, sem = refs[n_space - 1 :]
        copies = {}
        for step in (*peers, 0):
            for j in range(tiles):
                part = (pl.ds(0, rows), block(step, j * tile, tile))
                copies[step, j] = pltpu.make_async_copy(
                    coupling.at[(1, *part)], k1.at[part], sem.at[step, j]
                )
                copies[step, j].start()
        response[...] = total_of(own, got).astype(BF)
        full_rows(
            response[...], k1, pushed_own, pushed_other, lambda step, j: copies[step, j].wait()
        )
        value_rows[...] = value[...].T

    def target_kernel(k1, bar, noise, arrow, response, *refs):
        got, (target, part) = refs[: n_space - 1], refs[n_space - 1 :]
        pieces = [bar, *got]
        for i in range(tiles):
            at = i * tile
            pulled = jnp.zeros((tile, columns), F32)
            for step, piece in enumerate(pieces):
                pulled = pulled + dot(k1[at : at + tile, block(step)], piece[...])
            source = noise[1, at : at + tile].astype(F32)
            target[at : at + tile] = (source - pulled).astype(BF)
        total = dot(arrow[0], bar[...]) + dot(response[...], target[...])
        part[...] = total.T

    def first_response_kernel(d0, d1, arrow, target, pushed_own, *refs):
        got, (own, other, first) = refs[: n_space - 1], refs[n_space - 1 :]
        left = (arrow[0].astype(F32) - total_of(pushed_own, got)).astype(BF)
        lower_rows(left, d0, own, other)
        lower_own(d1, target, first)

    def last_solve_kernel(d1, first, *refs):
        got, (own, other, value) = refs[: n_space - 1], refs[n_space - 1 :]
        value[...] = first[...]
        for step in peers:

            @pl.when(at_core() >= step)
            def _():
                for i in range(tiles):
                    at = i * tile
                    value[at : at + tile] = value[at : at + tile] + dot(
                        d1[at : at + tile, block(step)], got[step - 1][...]
                    )

        lower_rows(value[...].T.astype(BF), d1, own, other)

    def pass_kernel(k1, lengths, solved, *refs):
        got, (base, own, other) = refs[: n_space - 1], refs[n_space - 1 :]
        live = lengths[lax.axis_index("tm")] > 1
        value = jnp.where(live, total_of(solved, got), 0.0)
        base[...] = value
        full_rows(value.astype(BF), k1, own, other)

    def first_solve_kernel(d0, value_rows, passed, *refs):
        got, (own, other) = refs[: n_space - 1], refs[n_space - 1 :]
        left = (value_rows[...] - total_of(passed, got)).astype(BF)
        lower_rows(left, d0, own, other)

    def tip_kernel(noise_fixed, tip, total, got, out, fixed):
        whole = total[...] + got[...].astype(F32)
        mixed = (noise_fixed[...].T - whole).astype(BF)
        forward = dot_last(mixed, tip[...])
        sample = dot(forward.astype(BF), tip[...])
        fixed[...] = sample.astype(BF)
        out[...] = sample.T

    def final_kernel(response, base, solved, pushed, fixed, *refs):
        got_solved, refs = refs[: n_space - 1], refs[n_space - 1 :]
        got_pushed, refs = refs[: n_space - 1], refs[n_space - 1 :]
        got_fixed, (out, whole) = refs[: n_space - 1], refs[n_space - 1 :]
        for step, piece in enumerate([fixed, *got_fixed]):
            owner = lax.rem(at_core() - step + n_space, n_space)
            whole[pl.ds(pl.multiple_of(owner * width, width), width)] = piece[...]
        out[1] = (base[...] - dot(whole[...], response[...])).T.astype(BF)
        left = total_of(pushed, got_pushed).astype(BF)
        out[0] = (total_of(solved, got_solved) - dot(whole[...], left)).T.astype(BF)

    def swap(value, step):
        pairs = [(i, (i - step) % n_space) for i in range(n_space)]
        return lax.ppermute(value, "space", pairs)

    def send_up(value):
        return [swap(value, -step) for step in peers]

    def send_down(values):
        return [swap(values[step - 1], step) for step in peers]

    wide = 2 * rows * nodes * columns
    factor_bytes = 2 * rows * nodes
    node_f32, node_bf = shape_of((rows, columns), F32), shape_of((rows, columns), BF)
    flat_f32 = shape_of((columns, rows), F32)
    flat_others = shape_of((n_space - 1, columns, rows), BF)
    fixed_f32 = shape_of((fixed_rows, rows), F32)
    fixed_bf = shape_of((fixed_rows, rows), BF)
    fixed_others = shape_of((n_space - 1, fixed_rows, rows), BF)
    in_vmem = pltpu.VMEM((rows, nodes), BF)
    dma = pltpu.SemaphoreType.DMA

    def on_device(diag_inverse, coupling, arrow, tip_inverse, noise, noise_fixed, section_lengths):
        core = at_core()
        got_noise = send_up(noise[0])
        d0, d1, own, other, first = call(
            start_kernel,
            [in_vmem, in_vmem, fixed_f32, fixed_others, node_f32],
            [diag_inverse, arrow, noise, section_lengths],
            wide,
            2 * factor_bytes,
            {0: pltpu.HBM, 1: pltpu.HBM, 2: pltpu.HBM, 3: pltpu.SMEM},
            [
                pltpu.VMEM((fixed_rows, rows), BF),
                pltpu.VMEM((rows, columns), BF),
                dma((n_space, tiles)),
                dma((n_space, tiles)),
                dma((2,)),
            ],
        )
        got_response = send_down(other)
        value, bar = call(
            first_value_kernel, [node_f32, node_bf], [d0, first, *got_noise], wide // 2, factor_bytes
        )
        got_bar = send_up(bar)
        k1, response, pushed_own, pushed_other, value_rows = call(
            response_kernel,
            [in_vmem, fixed_bf, fixed_f32, fixed_others, flat_f32],
            [coupling, value, own, *got_response],
            wide,
            factor_bytes,
            {0: pltpu.HBM},
            [dma((n_space, tiles))],
        )
        target, part = call(
            target_kernel,
            [node_bf, shape_of((columns, fixed_rows), F32)],
            [k1, bar, noise, arrow, response, *got_bar],
            wide,
            factor_bytes,
        )
        got_target = send_up(target)
        got_pushed = send_down(pushed_other)

        def own_part(step):
            return lax.dynamic_slice_in_dim(part, ((core - step) % n_space) * width, width, 0)

        total = own_part(0)
        for step in peers:
            total = total + swap(own_part(step).astype(BF), step).astype(F32)
        got = jnp.zeros_like(total, BF)
        bit = 1
        while bit < n_tm:
            total = lax.reduce_precision(total + got.astype(F32), 8, 7)
            got = lax.ppermute(total.astype(BF), "tm", [(i, i ^ bit) for i in range(n_tm)])
            bit *= 2

        first_own, first_other, first = call(
            first_response_kernel,
            [fixed_f32, fixed_others, node_f32],
            [d0, d1, arrow, target, pushed_own, *got_pushed],
            wide,
            factor_bytes,
        )
        got_first = send_down(first_other)
        solved, other, _ = call(
            last_solve_kernel,
            [flat_f32, flat_others, node_f32],
            [d1, first, *got_target],
            wide * 3 // 2,
            factor_bytes,
        )
        got_solved = send_down(other)
        base, passed, other = call(
            pass_kernel,
            [flat_f32, flat_f32, flat_others],
            [k1, section_lengths, solved, *got_solved],
            wide,
            factor_bytes,
            {1: pltpu.SMEM},
        )
        got_passed = send_down(other)
        solved, other = call(
            first_solve_kernel,
            [flat_f32, flat_others],
            [d0, value_rows, passed, *got_passed],
            wide,
            factor_bytes,
        )
        got_solved = send_down(other)
        fixed_out, fixed = call(
            tip_kernel,
            [shape_of((fixed_rows, width), F32), shape_of((width, fixed_rows), BF)],
            [noise_fixed, tip_inverse, total, got],
            4 * fixed_rows * fixed_rows * width,
            8 * fixed_rows * fixed_rows,
        )
        (sample,) = call(
            final_kernel,
            [shape_of((2, rows, columns), BF)],
            [response, base, solved, first_own, fixed, *got_solved, *got_first, *send_up(fixed)],
            4 * rows * fixed_rows * columns,
            factor_bytes,
            scratch=[pltpu.VMEM((columns, fixed_rows), BF)],
        )
        return (sample, fixed_out)

    return on_device


def solution(mesh):
    sizes = dict(mesh.shape)

    def program(diag_inverse, coupling, arrow, tip_inverse, noise, noise_fixed, section_lengths):
        device = build(
            sizes["tm"],
            sizes["space"],
            diag_inverse.shape[1] // sizes["space"],
            noise.shape[2],
            arrow.shape[1],
        )
        return jax.shard_map(
            device,
            mesh=mesh,
            in_specs=(
                P("tm", "space", None),
                P("tm", "space", None),
                P("tm", None, "space"),
                P(),
                P("tm", "space", None),
                P(None, "space"),
                P(),
            ),
            out_specs=(P("tm", "space", None), P(None, "space")),
            check_vma=False,
        )(diag_inverse, coupling, arrow, tip_inverse, noise, noise_fixed, section_lengths)

    return program
```

time: 152 us -> 63.6 us (0.42)
  waiting for transfers between devices: 57.9 us -> 13.2 us
  blocking collectives: 43.2 us -> 0 us
  matrix products: 29.5 us -> 0 us
  Pallas kernels: 0 us -> 20.2 us
  starting transfers between devices: 0.25 us -> 15.3 us
  between operations: 15.6 us -> 0.79 us
  local copies, waits for them, and re-layouts: 3.33 us -> 13.6 us
  other arithmetic: 2.2 us -> 0.16 us
    psum x1 -> x0, blocking collectives: 43.2 us -> none  [on_device(): mixed_sum = lax.psum(placed - partial_value, ('tm', 'space'))]
    all_gather x3 -> x0, waiting for transfers between devices: 31.3 us -> none  [the longest x2 21 us: on_device(): lax.all_gather(target, 'space', axis=0, tiled=True)]
    dot_general x9 -> x0, matrix products: 29.5 us -> none  [the longest x2 10.3 us: on_device(): lax.dot_general(backward_inverse, target, contract_rows, preferred_elemen...]
    reduce_scatter x3 -> x0, waiting for transfers between devices: 26.5 us -> none  [the longest x2 16.7 us: on_device(): lax.psum_scatter(lax.dot_general(backward_inverse, target, contract_rows,...]
    pallas_call x0 -> x10, Pallas kernels: none -> 20.2 us  [call(): pl.pallas_call(body, in_specs=specs, out_specs=[pl.BlockSpec(memory_space...]
    ppermute x0 -> x15, starting transfers between devices: none -> 15.3 us  [the longest x4 9.27 us: on_device(): lax.ppermute(total.astype(BF), 'tm', [(i, i ^ bit) for i in range(n_tm)])]
    ppermute x0 -> x15, waiting for transfers between devices: none -> 13.2 us  [the longest x4 9.01 us: on_device(): lax.ppermute(total.astype(BF), 'tm', [(i, i ^ bit) for i in range(n_tm)])]
    unnamed x17 -> x34, local copies, waits for them, and re-layouts: 0.8 us -> 12.5 us
  transfers between devices with their start and end apart: 6 -> 15, of which waited for: 6 -> 7; matrix products, arithmetic and copies ran while one was open for 1% -> 0% of each run, Pallas kernels for 0% -> 26%
where the time goes in v2:
time: 63.6 us; the launch traced here: 63.3 us
  Pallas kernels  20.2 us (32%)
  starting transfers between devices  15.3 us (24%)
  local copies, waits for them, and re-layouts  13.6 us (21%)
  waiting for transfers between devices  13.2 us (21%)
  between operations  0.79 us (1%)
    pallas_call x10, Pallas kernels, call(): pl.pallas_call(body, in_specs=specs, out_specs=[pl.BlockSpec(memory_space...  20.2 us
    unnamed x34, local copies, waits for them, and re-layouts  12.5 us
    ppermute x4, starting transfers between devices, on_device(): lax.ppermute(total.astype(BF), 'tm', [(i, i ^ bit) for i in range(n_tm)])  9.27 us
    ppermute x4, waiting for transfers between devices, on_device(): lax.ppermute(total.astype(BF), 'tm', [(i, i ^ bit) for i in range(n_tm)])  9.01 us
    ppermute x11, starting transfers between devices, swap(): return lax.ppermute(value, 'space', pairs)  6.06 us
    ppermute x11, waiting for transfers between devices, swap(): return lax.ppermute(value, 'space', pairs)  4.15 us
  transfers between devices with their start and end apart: 15, of which 7 were waited for; matrix products, arithmetic and copies ran while one was open for 0% of the time, Pallas kernels for 26%

profile of v2, /device:TPU:0, one launch (start us, length us, event | category | flops | bytes accessed | tf_op | source)
XLA Modules:
  0.0 63.3 jit_solution(16200701445821166792)
XLA Ops:
  0.6 1.1 %slice_bitcast_fusion = bf16[1024,256]{1,0:T(8,128)(2,1)S(1)} fusion(bf16[2,1024,256]{2,1,0:T(8,128)(2,1)} %noise.3), kind=kLoop, calls=%fused_computation | loop fusion | bytes 1048576 | tf_op jit(solution)/shard_map/squeeze | solution.py:292
  1.7 0.5 collective-permute-start
  2.2 0.7 %copy-done.14 = s32[16]{0:T(128)S(1)} copy-done((s32[16]{0:T(128)S(1)}, s32[16]{0:T(128)}, u32[]{:S(2)}) %copy-start.14) | copy-done | bytes 88
  2.9 4.6 %shard_map.86 = (bf16[1024,2048]{1,0:T(8,128)(2,1)S(1)}, bf16[1024,2048]{1,0:T(8,128)(2,1)S(1)}, f32[256,1024]{1,0:T(8,128)S(1)}, bf16[1,256,1024]{2,1,0:T(8,128)(2,1)S(1)}, f32[1024,256]{1,0:T(8,128)S(1)}) custom-call(bf16[2,1024,2048]{2,1,0:T(8,128)(2,1)} %diag.1, bf16[2,256,1024]{2,1,0:T(8,128)(2,1)} %arrow.5, bf16[2,1024,256]{2,1,0:T(8,128)(2,1)} %noise.3, ...), custom_call_target="tpu_custom_call" | custom-call | flops 1073741824 | bytes 8388608 | tf_op jit(solution)/shard_map/pallas_call | solution.py:59
  7.5 0.0 copy-start
  7.5 1.8 %collective-permute-start.1 = (bf16[256,1024]{1,0:T(8,128)(2,1)S(1)}, bf16[256,1024]{1,0:T(8,128)(2,1)S(1)}, u32[]{:S(2)}, u32[]{:S(2)}) collective-permute-start(bf16[256,1024]{1,0:T(8,128)(2,1)S(1)} %bitcast.11), channel_id=1, source_target_pairs={{0,1},{1,0},{2,3},{3,2},{4,5},{5,4},{6,7},{7,6},{8,9},{9,8},{10,11... | collective-permute-start | bytes 1572872 | tf_op jit(solution)/shard_map/ppermute | solution.py:271
  9.3 0.0 collective-permute-done.refs_0_
  9.3 0.1 shard_map.87
  9.4 0.8 %collective-permute-start.2 = (bf16[1024,256]{1,0:T(8,128)(2,1)S(1)}, bf16[1024,256]{1,0:T(8,128)(2,1)S(1)}, u32[]{:S(2)}, u32[]{:S(2)}) collective-permute-start(bf16[1024,256]{1,0:T(8,128)(2,1)S(1)} %get-tuple-element.36.bar), channel_id=1, source_target_pairs={{0,1},{1,0},{2,3},{3,2},{4,5},{5,4},{6,7},{7,6},{8,9},{9,8},{10,11... | collective-permute-start | bytes 1572872 | tf_op jit(solution)/shard_map/ppermute | solution.py:271
  10.2 0.6 collective-permute-done.1.refs_0_
  10.8 4.7 %shard_map.88 = (bf16[1024,2048]{1,0:T(8,128)(2,1)S(1)}, bf16[256,1024]{1,0:T(8,128)(2,1)S(1)}, f32[256,1024]{1,0:T(8,128)S(1)}, bf16[1,256,1024]{2,1,0:T(8,128)(2,1)S(1)}, f32[256,1024]{1,0:T(8,128)S(1)}) custom-call(bf16[2,1024,2048]{2,1,0:T(8,128)(2,1)} %coupling.1, f32[1024,256]{1,0:T(8,128)S(1)} %get-tuple-element.30.value, ...), custom_call_target="tpu_custom_call" | custom-call | flops 1073741824 | bytes 4194304 | tf_op jit(solution)/shard_map/pallas_call | solution.py:59
  15.5 0.4 collective-permute-start.3
  15.9 0.0 collective-permute-done.2.refs_0_
  15.9 0.0 copy-done.4
  15.9 0.0 copy-done.5
  15.9 2.0 %shard_map.89 = (bf16[1024,256]{1,0:T(8,128)(2,1)S(1)}, f32[256,256]{1,0:T(8,128)S(1)}) custom-call(bf16[1024,2048]{1,0:T(8,128)(2,1)S(1)} %get-tuple-element.34.k1, bf16[1024,256]{1,0:T(8,128)(2,1)S(1)} %get-tuple-element.36.bar, bf16[2,1024,256]{2,1,0:T(8,128)(2,1)S(1)} %copy-done.5, bf16[2,256,1024]{2,1,0:T(8,128)(2,1)S(1)} %copy-done.4, ...), custom_call_target="tpu_custom_call" | custom-call | flops 1073741824 | bytes 4194304 | tf_op jit(solution)/shard_map/pallas_call | solution.py:59
  18.0 0.0 copy-start.2
  18.0 2.0 %copy-done.2 = bf16[1024,2048]{1,0:T(8,128)(2,1)} copy-done((bf16[1024,2048]{1,0:T(8,128)(2,1)}, bf16[1024,2048]{1,0:T(8,128)(2,1)S(1)}, u32[]{:S(2)}) %copy-start.2) | copy-done | bytes 4194328
  20.0 0.1 collective-permute-start.4
  20.2 0.0 collective-permute-done.3.refs_0_
  20.2 0.0 copy-done
  20.2 1.1 %shard_map.90 = (f32[256,1024]{1,0:T(8,128)S(1)}, bf16[1,256,1024]{2,1,0:T(8,128)(2,1)S(1)}, f32[1024,256]{1,0:T(8,128)S(1)}) custom-call(bf16[1024,2048]{1,0:T(8,128)(2,1)S(1)} %get-tuple-element.28.factor.d0, bf16[1024,2048]{1,0:T(8,128)(2,1)S(1)} %get-tuple-element.35.d1, bf16[2,256,1024]{2,1,0:T(8,128)(2,1)S(1)} %copy-done.4, ...), custom_call_target="tpu_custom_call" | custom-call | flops 1073741824 | bytes 4194304 | tf_op jit(solution)/shard_map/pallas_call | solution.py:59
  21.3 0.0 copy-start.16
  21.3 0.0 copy-start.15
  21.3 0.6 collective-permute-done.4.refs_0_
  21.9 2.0 %shard_map.91 = (f32[256,1024]{1,0:T(8,128)S(1)}, bf16[1,256,1024]{2,1,0:T(8,128)(2,1)}, f32[1024,256]{1,0:T(8,128)}) custom-call(bf16[1024,2048]{1,0:T(8,128)(2,1)S(1)} %get-tuple-element.35.d1, f32[1024,256]{1,0:T(8,128)S(1)} %get-tuple-element.40.first, bf16[1024,256]{1,0:T(8,128)(2,1)S(1)} %collective-permute-done.4.refs_0_), custom_call_target="tpu_custom_call" | custom-call | flops 1610612736 | bytes 4194304 | tf_op jit(solution)/shard_map/pallas_call | solution.py:59
  23.9 1.0 %copy-done.10 = f32[256,1024]{1,0:T(8,128)} copy-done((f32[256,1024]{1,0:T(8,128)}, f32[256,1024]{1,0:T(8,128)S(1)}, u32[]{:S(2)}) %copy-start.10) | copy-done | bytes 1048600
  24.9 0.0 copy-done.16
  24.9 1.9 %collective-permute-start.5 = (bf16[256,1024]{1,0:T(8,128)(2,1)}, bf16[256,1024]{1,0:T(8,128)(2,1)S(1)}, u32[]{:S(2)}, u32[]{:S(2)}) collective-permute-start(bf16[256,1024]{1,0:T(8,128)(2,1)} %bitcast.3), channel_id=1, source_target_pairs={{0,1},{1,0},{2,3},{3,2},{4,5},{5,4},{6,7},{7,6},{8,9},{9,8},{10,11... | collective-permute-start | bytes 1572872 | tf_op jit(solution)/shard_map/ppermute | solution.py:271
  26.8 0.1 collective-permute-start.7
  26.9 1.7 %collective-permute-done.5.refs_0_ = bf16[256,1024]{1,0:T(8,128)(2,1)S(1)} collective-permute-done((bf16[256,1024]{1,0:T(8,128)(2,1)}, bf16[256,1024]{1,0:T(8,128)(2,1)S(1)}, u32[]{:S(2)}, u32[]{:S(2)}) %collective-permute-start.5) | collective-permute-done | bytes 524320 | tf_op jit(solution)/shard_map/ppermute | solution.py:271
  28.5 0.0 copy-done.15
  28.5 2.2 %copy-done.3 = bf16[1024,2048]{1,0:T(8,128)(2,1)S(1)} copy-done((bf16[1024,2048]{1,0:T(8,128)(2,1)S(1)}, bf16[1024,2048]{1,0:T(8,128)(2,1)}, u32[]{:S(2)}) %copy-start.3) | copy-done | bytes 4194328
  30.7 1.2 %copy-done.11 = f32[256,1024]{1,0:T(8,128)S(1)} copy-done((f32[256,1024]{1,0:T(8,128)S(1)}, f32[256,1024]{1,0:T(8,128)}, u32[]{:S(2)}) %copy-start.11) | copy-done | bytes 1048600
  31.9 2.4 %shard_map.92 = (f32[256,1024]{1,0:T(8,128)S(1)}, f32[256,1024]{1,0:T(8,128)S(1)}, bf16[1,256,1024]{2,1,0:T(8,128)(2,1)}) custom-call(bf16[1024,2048]{1,0:T(8,128)(2,1)S(1)} %copy-done.3, s32[16]{0:T(128)S(1)} %copy-done.15, f32[256,1024]{1,0:T(8,128)S(1)} %copy-done.11, bf16[256,1024]{1,0:T(8,128)(2,1)S(1)} %collective-permute-done.5.refs_0_), custom_call_target="tpu_custom_call" | custom-call | flops 1073741824 | bytes 4194304 | tf_op jit(solution)/shard_map/pallas_call | solution.py:59
  34.4 1.0 %copy-done.6 = f32[256,1024]{1,0:T(8,128)} copy-done((f32[256,1024]{1,0:T(8,128)}, f32[256,1024]{1,0:T(8,128)S(1)}, u32[]{:S(2)}) %copy-start.6) | copy-done | bytes 1048600
  35.3 1.0 %copy-done.8 = f32[256,1024]{1,0:T(8,128)} copy-done((f32[256,1024]{1,0:T(8,128)}, f32[256,1024]{1,0:T(8,128)S(1)}, u32[]{:S(2)}) %copy-start.8) | copy-done | bytes 1048600
  36.3 0.4 collective-permute-start.6
  36.7 0.0 collective-permute-done.7
  36.7 3.0 %collective-permute-start.8 = (bf16[128,256]{1,0:T(8,128)(2,1)S(1)}, bf16[128,256]{1,0:T(8,128)(2,1)S(1)}, u32[]{:S(2)}, u32[]{:S(2)}) collective-permute-start(bf16[128,256]{1,0:T(8,128)(2,1)S(1)} %fusion.2), channel_id=1, source_target_pairs={{0,2},{2,0},{4,6},{6,4},{8,10},{10,8},{12,14},{14,12},{16,18},{18,... | collective-permute-start | bytes 196616 | tf_op jit(solution)/shard_map/ppermute | solution.py:342
  39.8 0.0 collective-permute-start.13
  39.8 2.4 %collective-permute-done.8 = bf16[128,256]{1,0:T(8,128)(2,1)S(1)} collective-permute-done((bf16[128,256]{1,0:T(8,128)(2,1)S(1)}, bf16[128,256]{1,0:T(8,128)(2,1)S(1)}, u32[]{:S(2)}, u32[]{:S(2)}) %collective-permute-start.8) | collective-permute-done | bytes 65568 | tf_op jit(solution)/shard_map/ppermute | solution.py:342
  42.2 2.0 %collective-permute-start.9 = (bf16[128,256]{1,0:T(8,128)(2,1)S(1)}, bf16[128,256]{1,0:T(8,128)(2,1)S(1)}, u32[]{:S(2)}, u32[]{:S(2)}) collective-permute-start(bf16[128,256]{1,0:T(8,128)(2,1)S(1)} %fusion), channel_id=1, source_target_pairs={{0,4},{2,6},{4,0},{6,2},{8,12},{10,14},{12,8},{14,10},{16,20},{18,... | collective-permute-start | bytes 196616 | tf_op jit(solution)/shard_map/ppermute | solution.py:342
  44.1 0.0 collective-permute-done.6.refs_0_
  44.1 2.2 %copy-done.1 = bf16[1024,2048]{1,0:T(8,128)(2,1)S(1)} copy-done((bf16[1024,2048]{1,0:T(8,128)(2,1)S(1)}, bf16[1024,2048]{1,0:T(8,128)(2,1)}, u32[]{:S(2)}) %copy-start.1) | copy-done | bytes 4194328
  46.3 1.2 %copy-done.9 = f32[256,1024]{1,0:T(8,128)S(1)} copy-done((f32[256,1024]{1,0:T(8,128)S(1)}, f32[256,1024]{1,0:T(8,128)}, u32[]{:S(2)}) %copy-start.9) | copy-done | bytes 1048600
  47.6 0.6 shard_map.93
  48.2 0.1 collective-permute-start.12
  48.3 0.0 collective-permute-done.9
  48.3 0.1 fusion.1
  48.3 1.6 %collective-permute-start.10 = (bf16[128,256]{1,0:T(8,128)(2,1)S(1)}, bf16[128,256]{1,0:T(8,128)(2,1)S(1)}, u32[]{:S(2)}, u32[]{:S(2)}) collective-permute-start(bf16[128,256]{1,0:T(8,128)(2,1)S(1)} %fusion.1), channel_id=1, source_target_pairs={{0,8},{2,10},{4,12},{6,14},{8,0},{10,2},{12,4},{14,6},{16,24},{18,... | collective-permute-start | bytes 196616 | tf_op jit(solution)/shard_map/ppermute | solution.py:342
  50.0 2.9 %collective-permute-done.10 = bf16[128,256]{1,0:T(8,128)(2,1)S(1)} collective-permute-done((bf16[128,256]{1,0:T(8,128)(2,1)S(1)}, bf16[128,256]{1,0:T(8,128)(2,1)S(1)}, u32[]{:S(2)}, u32[]{:S(2)}) %collective-permute-start.10) | collective-permute-done | bytes 65568 | tf_op jit(solution)/shard_map/ppermute | solution.py:342
  52.9 0.1 fusion.3
  52.9 2.7 %collective-permute-start.11 = (bf16[128,256]{1,0:T(8,128)(2,1)S(1)}, bf16[128,256]{1,0:T(8,128)(2,1)S(1)}, u32[]{:S(2)}, u32[]{:S(2)}) collective-permute-start(bf16[128,256]{1,0:T(8,128)(2,1)S(1)} %get-tuple-element.54), channel_id=1, source_target_pairs={{0,16},{2,18},{4,20},{6,22},{8,24},{10,26},{12,28},{14,30},{16,0},... | collective-permute-start | bytes 196616 | tf_op jit(solution)/shard_map/ppermute | solution.py:342
  55.6 3.7 %collective-permute-done.11.got = bf16[128,256]{1,0:T(8,128)(2,1)S(1)} collective-permute-done((bf16[128,256]{1,0:T(8,128)(2,1)S(1)}, bf16[128,256]{1,0:T(8,128)(2,1)S(1)}, u32[]{:S(2)}, u32[]{:S(2)}) %collective-permute-start.11) | collective-permute-done | bytes 65568 | tf_op jit(solution)/shard_map/ppermute | solution.py:342
  59.3 0.0 copy-done.12
  59.3 0.0 copy-done.13
  59.3 1.1 %shard_map.94 = (f32[256,128]{1,0:T(8,128)}, bf16[128,256]{1,0:T(8,128)(2,1)S(1)}) custom-call(f32[256,128]{1,0:T(8,128)S(1)} %copy-done.12, bf16[256,256]{1,0:T(8,128)(2,1)S(1)} %copy-done.13, f32[128,256]{1,0:T(8,128)S(1)} %get-tuple-element.55.total, bf16[128,256]{1,0:T(8,128)(2,1)S(1)} %collective-permute-done.11.got), custom_call_target="tpu_custom_call" | custom-call | flops 33554432 | bytes 524288 | tf_op jit(solution)/shard_map/pallas_call | solution.py:59
  60.4 0.0 collective-permute-start.14
  60.4 1.3 %collective-permute-done.14.refs_2_ = bf16[128,256]{1,0:T(8,128)(2,1)S(1)} collective-permute-done((bf16[128,256]{1,0:T(8,128)(2,1)S(1)}, bf16[128,256]{1,0:T(8,128)(2,1)S(1)}, u32[]{:S(2)}, u32[]{:S(2)}) %collective-permute-start.14) | collective-permute-done | bytes 65568 | tf_op jit(solution)/shard_map/ppermute | solution.py:271
  61.7 0.0 collective-permute-done.13.refs_1_
  61.7 0.0 collective-permute-done.12.refs_0_
  61.7 0.0 copy-done.7
  61.7 1.6 %shard_map.95 = bf16[2,1024,256]{2,1,0:T(8,128)(2,1)} custom-call(bf16[256,1024]{1,0:T(8,128)(2,1)S(1)} %get-tuple-element.33.response, f32[256,1024]{1,0:T(8,128)S(1)} %copy-done.7, f32[256,1024]{1,0:T(8,128)S(1)} %get-tuple-element.47.solved, f32[256,1024]{1,0:T(8,128)S(1)} %get-tuple-element.48.pushed, bf16[128,256]{1,0:T(8,128)(2,1)S(1)} %get-tuple-element.50.fixed, ...), custom_call_target="tpu_custom_call" | custom-call | flops 268435456 | bytes 4194304 | tf_op jit(solution)/shard_map/pallas_call | solution.py:59
  (16 shorter events, 0.1 us)
Async XLA Ops:
  1.7 7.6 %collective-permute-start = (bf16[1024,256]{1,0:T(8,128)(2,1)S(1)}, bf16[1024,256]{1,0:T(8,128)(2,1)S(1)}, u32[]{:S(2)}, u32[]{:S(2)}) collective-permute-start(bf16[1024,256]{1,0:T(8,128)(2,1)S(1)} %slice_bitcast_fusion), channel_id=1, source_target_pairs={{0,1},{1,0},{2,3},{3,2},{4,5},{5,4},{6,7},{7,6},{8,9},{9,8},{10,11... | collective-permute-start | bytes 1572872 | tf_op jit(solution)/shard_map/ppermute | solution.py:271
  2.2 0.7 %copy-start.14 = (s32[16]{0:T(128)S(1)}, s32[16]{0:T(128)}, u32[]{:S(2)}) copy-start(s32[16]{0:T(128)} %lengths.3) | copy-start | bytes 196
  7.5 12.7 %copy-start = (bf16[1024,2048]{1,0:T(8,128)(2,1)}, bf16[1024,2048]{1,0:T(8,128)(2,1)S(1)}, u32[]{:S(2)}) copy-start(bf16[1024,2048]{1,0:T(8,128)(2,1)S(1)} %get-tuple-element.28.factor.d0) | copy-start | bytes 12582916
  7.5 3.3 %collective-permute-start.1 = (bf16[256,1024]{1,0:T(8,128)(2,1)S(1)}, bf16[256,1024]{1,0:T(8,128)(2,1)S(1)}, u32[]{:S(2)}, u32[]{:S(2)}) collective-permute-start(bf16[256,1024]{1,0:T(8,128)(2,1)S(1)} %bitcast.11), channel_id=1, source_target_pairs={{0,1},{1,0},{2,3},{3,2},{4,5},{5,4},{6,7},{7,6},{8,9},{9,8},{10,11... | collective-permute-start | bytes 1572872 | tf_op jit(solution)/shard_map/ppermute | solution.py:271
  9.4 6.5 %collective-permute-start.2 = (bf16[1024,256]{1,0:T(8,128)(2,1)S(1)}, bf16[1024,256]{1,0:T(8,128)(2,1)S(1)}, u32[]{:S(2)}, u32[]{:S(2)}) collective-permute-start(bf16[1024,256]{1,0:T(8,128)(2,1)S(1)} %get-tuple-element.36.bar), channel_id=1, source_target_pairs={{0,1},{1,0},{2,3},{3,2},{4,5},{5,4},{6,7},{7,6},{8,9},{9,8},{10,11... | collective-permute-start | bytes 1572872 | tf_op jit(solution)/shard_map/ppermute | solution.py:271
  10.8 5.1 %copy-start.4 = (bf16[2,256,1024]{2,1,0:T(8,128)(2,1)S(1)}, bf16[2,256,1024]{2,1,0:T(8,128)(2,1)}, u32[]{:S(2)}) copy-start(bf16[2,256,1024]{2,1,0:T(8,128)(2,1)} %arrow.5) | copy-start | bytes 3145732
  10.8 5.1 %copy-start.5 = (bf16[2,1024,256]{2,1,0:T(8,128)(2,1)S(1)}, bf16[2,1024,256]{2,1,0:T(8,128)(2,1)}, u32[]{:S(2)}) copy-start(bf16[2,1024,256]{2,1,0:T(8,128)(2,1)} %noise.3) | copy-start | bytes 3145732
  15.5 4.7 %collective-permute-start.3 = (bf16[256,1024]{1,0:T(8,128)(2,1)S(1)}, bf16[256,1024]{1,0:T(8,128)(2,1)S(1)}, u32[]{:S(2)}, u32[]{:S(2)}) collective-permute-start(bf16[256,1024]{1,0:T(8,128)(2,1)S(1)} %bitcast.10), channel_id=1, source_target_pairs={{0,1},{1,0},{2,3},{3,2},{4,5},{5,4},{6,7},{7,6},{8,9},{9,8},{10,11... | collective-permute-start | bytes 1572872 | tf_op jit(solution)/shard_map/ppermute | solution.py:271
  18.0 2.0 %copy-start.2 = (bf16[1024,2048]{1,0:T(8,128)(2,1)}, bf16[1024,2048]{1,0:T(8,128)(2,1)S(1)}, u32[]{:S(2)}) copy-start(bf16[1024,2048]{1,0:T(8,128)(2,1)S(1)} %get-tuple-element.34.k1) | copy-start | bytes 12582916
  20.0 1.9 %collective-permute-start.4 = (bf16[1024,256]{1,0:T(8,128)(2,1)S(1)}, bf16[1024,256]{1,0:T(8,128)(2,1)S(1)}, u32[]{:S(2)}, u32[]{:S(2)}) collective-permute-start(bf16[1024,256]{1,0:T(8,128)(2,1)S(1)} %get-tuple-element.37.target), channel_id=1, source_target_pairs={{0,1},{1,0},{2,3},{3,2},{4,5},{5,4},{6,7},{7,6},{8,9},{9,8},{10,11... | collective-permute-start | bytes 1572872 | tf_op jit(solution)/shard_map/ppermute | solution.py:271
  21.3 3.6 %copy-start.16 = (bf16[1,256,1024]{2,1,0:T(8,128)(2,1)}, bf16[1,256,1024]{2,1,0:T(8,128)(2,1)S(1)}, u32[]{:S(2)}) copy-start(bf16[1,256,1024]{2,1,0:T(8,128)(2,1)S(1)} %get-tuple-element.52) | copy-start | bytes 1572868
  21.3 7.2 %copy-start.15 = (s32[16]{0:T(128)S(1)}, s32[16]{0:T(128)}, u32[]{:S(2)}) copy-start(s32[16]{0:T(128)} %lengths.3) | copy-start | bytes 196
  23.9 1.0 %copy-start.10 = (f32[256,1024]{1,0:T(8,128)}, f32[256,1024]{1,0:T(8,128)S(1)}, u32[]{:S(2)}) copy-start(f32[256,1024]{1,0:T(8,128)S(1)} %get-tuple-element.41.solved) | copy-start | bytes 3145732
  24.9 3.6 %collective-permute-start.5 = (bf16[256,1024]{1,0:T(8,128)(2,1)}, bf16[256,1024]{1,0:T(8,128)(2,1)S(1)}, u32[]{:S(2)}, u32[]{:S(2)}) collective-permute-start(bf16[256,1024]{1,0:T(8,128)(2,1)} %bitcast.3), channel_id=1, source_target_pairs={{0,1},{1,0},{2,3},{3,2},{4,5},{5,4},{6,7},{7,6},{8,9},{9,8},{10,11... | collective-permute-start | bytes 1572872 | tf_op jit(solution)/shard_map/ppermute | solution.py:271
  26.8 9.9 %collective-permute-start.7 = (bf16[128,256]{1,0:T(8,128)(2,1)S(1)}, bf16[128,256]{1,0:T(8,128)(2,1)S(1)}, u32[]{:S(2)}, u32[]{:S(2)}) collective-permute-start(bf16[128,256]{1,0:T(8,128)(2,1)S(1)} %dynamic-slice_convert_fusion), channel_id=1, source_target_pairs={{0,1},{1,0},{2,3},{3,2},{4,5},{5,4},{6,7},{7,6},{8,9},{9,8},{10,11... | collective-permute-start | bytes 196616 | tf_op jit(solution)/shard_map/ppermute | solution.py:271
  28.5 2.2 %copy-start.3 = (bf16[1024,2048]{1,0:T(8,128)(2,1)S(1)}, bf16[1024,2048]{1,0:T(8,128)(2,1)}, u32[]{:S(2)}) copy-start(bf16[1024,2048]{1,0:T(8,128)(2,1)} %copy-done.2) | copy-start | bytes 12582916
  30.7 1.2 %copy-start.11 = (f32[256,1024]{1,0:T(8,128)S(1)}, f32[256,1024]{1,0:T(8,128)}, u32[]{:S(2)}) copy-start(f32[256,1024]{1,0:T(8,128)} %copy-done.10) | copy-start | bytes 3145732
  34.4 1.0 %copy-start.6 = (f32[256,1024]{1,0:T(8,128)}, f32[256,1024]{1,0:T(8,128)S(1)}, u32[]{:S(2)}) copy-start(f32[256,1024]{1,0:T(8,128)S(1)} %get-tuple-element.43.base) | copy-start | bytes 3145732
  35.3 1.0 %copy-start.8 = (f32[256,1024]{1,0:T(8,128)}, f32[256,1024]{1,0:T(8,128)S(1)}, u32[]{:S(2)}) copy-start(f32[256,1024]{1,0:T(8,128)S(1)} %get-tuple-element.45.passed) | copy-start | bytes 3145732
  36.3 7.8 %collective-permute-start.6 = (bf16[256,1024]{1,0:T(8,128)(2,1)}, bf16[256,1024]{1,0:T(8,128)(2,1)S(1)}, u32[]{:S(2)}, u32[]{:S(2)}) collective-permute-start(bf16[256,1024]{1,0:T(8,128)(2,1)} %bitcast.4), channel_id=1, source_target_pairs={{0,1},{1,0},{2,3},{3,2},{4,5},{5,4},{6,7},{7,6},{8,9},{9,8},{10,11... | collective-permute-start | bytes 1572872 | tf_op jit(solution)/shard_map/ppermute | solution.py:271
  36.7 22.6 %copy-start.12 = (f32[256,128]{1,0:T(8,128)S(1)}, f32[256,128]{1,0:T(8,128)}, u32[]{:S(2)}) copy-start(f32[256,128]{1,0:T(8,128)} %noise_fixed.1) | copy-start | bytes 393220
  36.7 22.6 %copy-start.13 = (bf16[256,256]{1,0:T(8,128)(2,1)S(1)}, bf16[256,256]{1,0:T(8,128)(2,1)}, u32[]{:S(2)}) copy-start(bf16[256,256]{1,0:T(8,128)(2,1)} %tip.1) | copy-start | bytes 393220
  36.7 5.4 %collective-permute-start.8 = (bf16[128,256]{1,0:T(8,128)(2,1)S(1)}, bf16[128,256]{1,0:T(8,128)(2,1)S(1)}, u32[]{:S(2)}, u32[]{:S(2)}) collective-permute-start(bf16[128,256]{1,0:T(8,128)(2,1)S(1)} %fusion.2), channel_id=1, source_target_pairs={{0,2},{2,0},{4,6},{6,4},{8,10},{10,8},{12,14},{14,12},{16,18},{18,... | collective-permute-start | bytes 196616 | tf_op jit(solution)/shard_map/ppermute | solution.py:342
  39.8 21.9 %collective-permute-start.13 = (bf16[256,1024]{1,0:T(8,128)(2,1)}, bf16[256,1024]{1,0:T(8,128)(2,1)S(1)}, u32[]{:S(2)}, u32[]{:S(2)}) collective-permute-start(bf16[256,1024]{1,0:T(8,128)(2,1)} %bitcast.8), channel_id=1, source_target_pairs={{0,1},{1,0},{2,3},{3,2},{4,5},{5,4},{6,7},{7,6},{8,9},{9,8},{10,11... | collective-permute-start | bytes 1572872 | tf_op jit(solution)/shard_map/ppermute | solution.py:271
  42.2 6.1 %collective-permute-start.9 = (bf16[128,256]{1,0:T(8,128)(2,1)S(1)}, bf16[128,256]{1,0:T(8,128)(2,1)S(1)}, u32[]{:S(2)}, u32[]{:S(2)}) collective-permute-start(bf16[128,256]{1,0:T(8,128)(2,1)S(1)} %fusion), channel_id=1, source_target_pairs={{0,4},{2,6},{4,0},{6,2},{8,12},{10,14},{12,8},{14,10},{16,20},{18,... | collective-permute-start | bytes 196616 | tf_op jit(solution)/shard_map/ppermute | solution.py:342
  44.1 2.2 %copy-start.1 = (bf16[1024,2048]{1,0:T(8,128)(2,1)S(1)}, bf16[1024,2048]{1,0:T(8,128)(2,1)}, u32[]{:S(2)}) copy-start(bf16[1024,2048]{1,0:T(8,128)(2,1)} %copy-done) | copy-start | bytes 12582916
  46.3 1.2 %copy-start.9 = (f32[256,1024]{1,0:T(8,128)S(1)}, f32[256,1024]{1,0:T(8,128)}, u32[]{:S(2)}) copy-start(f32[256,1024]{1,0:T(8,128)} %copy-done.8) | copy-start | bytes 3145732
  47.6 14.1 %copy-start.7 = (f32[256,1024]{1,0:T(8,128)S(1)}, f32[256,1024]{1,0:T(8,128)}, u32[]{:S(2)}) copy-start(f32[256,1024]{1,0:T(8,128)} %copy-done.6) | copy-start | bytes 3145732
  48.2 13.5 %collective-permute-start.12 = (bf16[256,1024]{1,0:T(8,128)(2,1)S(1)}, bf16[256,1024]{1,0:T(8,128)(2,1)S(1)}, u32[]{:S(2)}, u32[]{:S(2)}) collective-permute-start(bf16[256,1024]{1,0:T(8,128)(2,1)S(1)} %bitcast.9), channel_id=1, source_target_pairs={{0,1},{1,0},{2,3},{3,2},{4,5},{5,4},{6,7},{7,6},{8,9},{9,8},{10,11... | collective-permute-start | bytes 1572872 | tf_op jit(solution)/shard_map/ppermute | solution.py:271
  48.3 4.5 %collective-permute-start.10 = (bf16[128,256]{1,0:T(8,128)(2,1)S(1)}, bf16[128,256]{1,0:T(8,128)(2,1)S(1)}, u32[]{:S(2)}, u32[]{:S(2)}) collective-permute-start(bf16[128,256]{1,0:T(8,128)(2,1)S(1)} %fusion.1), channel_id=1, source_target_pairs={{0,8},{2,10},{4,12},{6,14},{8,0},{10,2},{12,4},{14,6},{16,24},{18,... | collective-permute-start | bytes 196616 | tf_op jit(solution)/shard_map/ppermute | solution.py:342
  52.9 6.4 %collective-permute-start.11 = (bf16[128,256]{1,0:T(8,128)(2,1)S(1)}, bf16[128,256]{1,0:T(8,128)(2,1)S(1)}, u32[]{:S(2)}, u32[]{:S(2)}) collective-permute-start(bf16[128,256]{1,0:T(8,128)(2,1)S(1)} %get-tuple-element.54), channel_id=1, source_target_pairs={{0,16},{2,18},{4,20},{6,22},{8,24},{10,26},{12,28},{14,30},{16,0},... | collective-permute-start | bytes 196616 | tf_op jit(solution)/shard_map/ppermute | solution.py:342
  60.4 1.3 %collective-permute-start.14 = (bf16[128,256]{1,0:T(8,128)(2,1)S(1)}, bf16[128,256]{1,0:T(8,128)(2,1)S(1)}, u32[]{:S(2)}, u32[]{:S(2)}) collective-permute-start(bf16[128,256]{1,0:T(8,128)(2,1)S(1)} %get-tuple-element.50.fixed), channel_id=1, source_target_pairs={{0,1},{1,0},{2,3},{3,2},{4,5},{5,4},{6,7},{7,6},{8,9},{9,8},{10,11... | collective-permute-start | bytes 196616 | tf_op jit(solution)/shard_map/ppermute | solution.py:271

commit v3 on v2

v3 whole, which is shorter than its diff:
```python
import jax
import jax.numpy as jnp
from jax import lax
from jax.experimental import pallas as pl
from jax.experimental.pallas import tpu as pltpu
from jax.sharding import PartitionSpec as P

BF = jnp.bfloat16
F32 = jnp.float32
MIB = 1 << 20


def dot(left, right):
    return jnp.dot(left, right, preferred_element_type=F32)


def dot_last(left, right):
    return lax.dot_general(left, right, (((1,), (1,)), ((), ())), preferred_element_type=F32)


def rounded(value):
    return value.astype(BF).astype(F32)


def total_of(own_ref, got_refs):
    total = rounded(own_ref[...])
    for got in got_refs:
        total = total + got[...].astype(F32)
    return total


def shape_of(shape, dtype):
    return jax.ShapeDtypeStruct(shape, dtype)


def build(n_tm, n_space, rows, columns, fixed_rows):
    nodes = n_space * rows
    tile = 256 if rows % 256 == 0 else rows
    tiles = rows // tile
    width = columns // n_space
    peers = range(1, n_space)

    def at_core():
        return lax.axis_index("space")

    def block(step, offset=0, size=rows):
        owner = lax.rem(at_core() - step + n_space, n_space)
        return pl.ds(pl.multiple_of(owner * rows + offset, tile), size)

    def part_rows(step):
        owner = lax.rem(at_core() - step + n_space, n_space)
        return pl.ds(pl.multiple_of(owner * width, width), width)

    def call(body, outs, args, flops, moved, places=None, scratch=()):
        places = places or {}
        specs = [pl.BlockSpec(memory_space=places.get(i, pltpu.VMEM)) for i in range(len(args))]
        args = [
            pltpu.with_memory_space_constraint(a, pltpu.HBM)
            if places.get(i) is pltpu.HBM
            else a
            for i, a in enumerate(args)
        ]
        return pl.pallas_call(
            body,
            in_specs=specs,
            out_specs=[pl.BlockSpec(memory_space=pltpu.VMEM)] * len(outs),
            out_shape=outs,
            scratch_shapes=list(scratch),
            cost_estimate=pl.CostEstimate(flops=flops, bytes_accessed=moved, transcendentals=0),
            compiler_params=pltpu.CompilerParams(vmem_limit_bytes=16 * MIB),
        )(*args)

    def lower_rows(left, factor, own_ref, other_ref):
        for step in peers:

            @pl.when(at_core() >= step)
            def _():
                other_ref[step - 1] = dot(left[...], factor[:, block(step)]).astype(BF)

            @pl.when(at_core() < step)
            def _():
                other_ref[step - 1] = jnp.zeros_like(other_ref[step - 1])

        for j in range(tiles):
            at = j * tile
            own_ref[:, at : at + tile] = dot(left[:, at:], factor[at:, block(0, at, tile)])

    def full_rows(left, factor, own_ref, other_ref):
        for step in peers:
            other_ref[step - 1] = dot(left[...], factor[:, block(step)]).astype(BF)
        own_ref[...] = dot(left[...], factor[:, block(0)])

    def lower_own(factor, right, out_ref, wait=None):
        for i in range(tiles):
            at = i * tile
            if wait:
                wait(i)
            out_ref[at : at + tile] = dot(
                factor[at : at + tile, block(0, 0, at + tile)], right[: at + tile]
            )

    def lower_rest(factor, got, value):
        for step in peers:

            @pl.when(at_core() >= step)
            def _():
                value[...] = value[...] + dot(factor[:, block(step)], got[step - 1][...])

    def start_kernel(
        diag, coupling, arrow, noise, lengths,
        d0, d1, k1, own, other, first, mask,
        e1, n0, live_scratch, sem1, sem0, semk, sems,
    ):
        arrow_copy = pltpu.make_async_copy(arrow.at[1], e1, sems.at[0])
        noise_copy = pltpu.make_async_copy(noise.at[0], n0, sems.at[1])
        live_copy = pltpu.make_async_copy(lengths, live_scratch, sems.at[2])

        def lower_copies(slot, target, sem):
            copies = {}
            for step in range(n_space):
                for i in range(tiles):
                    at = i * tile
                    size = rows if step else at + tile
                    part = (pl.ds(at, tile), block(step, 0, size))
                    copies[step, i] = pltpu.make_async_copy(
                        diag.at[(slot, *part)], target.at[part], sem.at[step, i]
                    )
            return copies

        def each(copies, act):
            for i in range(tiles):
                act(copies[0, i])
            for step in peers:

                @pl.when(at_core() >= step)
                def _():
                    for i in range(tiles):
                        act(copies[step, i])

        copies1 = lower_copies(1, d1, sem1)
        copies0 = lower_copies(0, d0, sem0)
        copiesk = []
        for i in range(tiles):
            part = pl.ds(i * tile, tile)
            copiesk.append(pltpu.make_async_copy(coupling.at[1, part], k1.at[part], semk.at[i]))
        live_copy.start()
        arrow_copy.start()
        each(copies1, lambda copy: copy.start())
        noise_copy.start()
        each(copies0, lambda copy: copy.start())
        for copy in copiesk:
            copy.start()
        live_copy.wait()
        arrow_copy.wait()
        live = live_scratch[lax.axis_index("tm")] > 1
        mask[...] = jnp.where(live, jnp.ones_like(mask[...]), jnp.zeros_like(mask[...]))
        e1[...] = jnp.where(live, e1[...], jnp.zeros_like(e1[...]))
        each(copies1, lambda copy: copy.wait())
        lower_rows(e1, d1, own, other)
        noise_copy.wait()
        lower_own(d0, n0, first, lambda i: copies0[0, i].wait())
        for step in peers:

            @pl.when(at_core() >= step)
            def _():
                for i in range(tiles):
                    copies0[step, i].wait()

        for copy in copiesk:
            copy.wait()

    def first_value_kernel(d0, value, *refs):
        got, (out, bar) = refs[: n_space - 1], refs[n_space - 1 :]
        out[...] = value[...]
        lower_rest(d0, [piece.at[0] for piece in got], out)
        bar[...] = out[...].astype(BF)

    def response_kernel(k1, value, own, *refs):
        got = refs[: n_space - 1]
        response, pushed_own, pushed_other, value_rows = refs[n_space - 1 :]
        response[...] = total_of(own, got).astype(BF)
        full_rows(response, k1, pushed_own, pushed_other)
        value_rows[...] = value[...].T

    def target_kernel(k1, bar, noise, arrow, response, *refs):
        got, (target, part_own, part_other, whole) = refs[: n_space - 1], refs[n_space - 1 :]
        pieces = [bar, *got]
        for i in range(tiles):
            at = i * tile
            pulled = jnp.zeros((tile, columns), F32)
            for step, piece in enumerate(pieces):
                pulled = pulled + dot(k1[at : at + tile, block(step)], piece[...])
            source = noise[1, at : at + tile].astype(F32)
            target[at : at + tile] = (source - pulled).astype(BF)
        whole[...] = (dot(arrow[0], bar[...]) + dot(response[...], target[...])).T
        part_own[...] = whole[part_rows(0)]
        for step in peers:
            part_other[step - 1] = whole[part_rows(step)].astype(BF)

    def first_response_kernel(d0, d1, arrow, target, pushed_own, part, *refs):
        got, refs = refs[: n_space - 1], refs[n_space - 1 :]
        got_parts, (own, other, first, sent) = refs[: n_space - 1], refs[n_space - 1 :]
        total = part[...]
        for piece in got_parts:
            total = total + piece[...].astype(F32)
        sent[...] = total.astype(BF)
        left = (arrow[0].astype(F32) - total_of(pushed_own, got)).astype(BF)
        lower_rows(left, d0, own, other)
        lower_own(d1, target, first)

    def fold_kernel(sent, got, out):
        out[...] = (sent[...].astype(F32) + got[...].astype(F32)).astype(BF)

    def last_solve_kernel(d1, first, *refs):
        got, (own, other, value) = refs[: n_space - 1], refs[n_space - 1 :]
        value[...] = first[...]
        lower_rest(d1, got, value)
        lower_rows(value[...].T.astype(BF), d1, own, other)

    def pass_kernel(k1, mask, solved, *refs):
        got, (base, own, other) = refs[: n_space - 1], refs[n_space - 1 :]
        value = jnp.where(mask[:1, :1] > 0, total_of(solved, got), 0.0)
        base[...] = value
        full_rows(value.astype(BF), k1, own, other)

    def first_solve_kernel(d0, value_rows, passed, *refs):
        got, (own, other) = refs[: n_space - 1], refs[n_space - 1 :]
        left = (value_rows[...] - total_of(passed, got)).astype(BF)
        lower_rows(left, d0, own, other)

    def tip_kernel(noise_fixed, tip, sent, *refs):
        got, (out, fixed) = refs[:-2], refs[-2:]
        whole = sent[...].astype(F32)
        for piece in got:
            whole = whole + piece[...].astype(F32)
        mixed = (noise_fixed[...].T - whole).astype(BF)
        forward = dot_last(mixed, tip[...])
        sample = dot(forward.astype(BF), tip[...])
        fixed[...] = sample.astype(BF)
        out[...] = sample.T

    def final_kernel(response, base, solved, pushed, fixed, *refs):
        got_solved, refs = refs[: n_space - 1], refs[n_space - 1 :]
        got_pushed, refs = refs[: n_space - 1], refs[n_space - 1 :]
        got_fixed, (out, whole) = refs[: n_space - 1], refs[n_space - 1 :]
        for step, piece in enumerate([fixed, *got_fixed]):
            whole[part_rows(step)] = piece[...]
        out[1] = (base[...] - dot(whole[...], response[...])).T.astype(BF)
        left = total_of(pushed, got_pushed).astype(BF)
        out[0] = (total_of(solved, got_solved) - dot(whole[...], left)).T.astype(BF)

    def swap(value, step):
        pairs = [(i, (i - step) % n_space) for i in range(n_space)]
        return lax.ppermute(value, "space", pairs)

    def send_up(value):
        return [swap(value, -step) for step in peers]

    def send_down(values):
        return [swap(values[step - 1], step) for step in peers]

    bits = [1 << i for i in range(n_tm.bit_length() - 1)]
    assert n_tm == 1 << len(bits)

    def swap_bit(value, bit):
        return lax.ppermute(value, "tm", [(i, i ^ bit) for i in range(n_tm)])

    wide = 2 * rows * nodes * columns
    factor_bytes = 2 * rows * nodes
    node_f32, node_bf = shape_of((rows, columns), F32), shape_of((rows, columns), BF)
    flat_f32 = shape_of((columns, rows), F32)
    flat_others = shape_of((n_space - 1, columns, rows), BF)
    fixed_f32 = shape_of((fixed_rows, rows), F32)
    fixed_bf = shape_of((fixed_rows, rows), BF)
    fixed_others = shape_of((n_space - 1, fixed_rows, rows), BF)
    part_bf = shape_of((width, fixed_rows), BF)
    in_vmem = pltpu.VMEM((rows, nodes), BF)
    dma = pltpu.SemaphoreType.DMA

    def fold(sent, got):
        return call(fold_kernel, [part_bf], [sent, got], width * fixed_rows, 6 * width * fixed_rows)[0]

    class Sum:
        def __init__(self, sent):
            self.left = list(bits)
            self.send(sent)

        def send(self, sent):
            self.sent, self.got = sent, None
            if self.left:
                self.got = swap_bit(sent, self.left.pop(0))

        def fold(self):
            if self.left:
                self.send(fold(self.sent, self.got))

        def fold_into(self, body, outs, args, *rest):
            if not self.left:
                return call(body, outs, args, *rest)
            count = len(args)

            def both(*refs):
                ins, (sent, got) = refs[:count], refs[count : count + 2]
                outs_refs, folded = refs[count + 2 : -1], refs[-1]
                fold_kernel(sent, got, folded)
                body(*ins, *outs_refs)

            *results, sent = call(both, [*outs, part_bf], [*args, self.sent, self.got], *rest)
            self.send(sent)
            return results

    def on_device(diag_inverse, coupling, arrow, tip_inverse, noise, noise_fixed, section_lengths):
        got_noise = send_up(noise)
        d0, d1, k1, own, other, value, mask = call(
            start_kernel,
            [in_vmem, in_vmem, in_vmem, fixed_f32, fixed_others, node_f32, shape_of((8, 128), F32)],
            [diag_inverse, coupling, arrow, noise, section_lengths],
            wide,
            3 * factor_bytes,
            {i: pltpu.HBM for i in range(5)},
            [
                pltpu.VMEM((fixed_rows, rows), BF),
                pltpu.VMEM((rows, columns), BF),
                pltpu.SMEM(section_lengths.shape, jnp.int32),
                dma((n_space, tiles)),
                dma((n_space, tiles)),
                dma((tiles,)),
                dma((3,)),
            ],
        )
        got_response = send_down(other)
        value, bar = call(
            first_value_kernel, [node_f32, node_bf], [d0, value, *got_noise], wide // 2, factor_bytes
        )
        got_bar = send_up(bar)
        response, pushed_own, pushed_other, value_rows = call(
            response_kernel,
            [fixed_bf, fixed_f32, fixed_others, flat_f32],
            [k1, value, own, *got_response],
            wide,
            factor_bytes,
        )
        got_pushed = send_down(pushed_other)
        target, part_own, part_other = call(
            target_kernel,
            [node_bf, shape_of((width, fixed_rows), F32), shape_of((n_space - 1, width, fixed_rows), BF)],
            [k1, bar, noise, arrow, response, *got_bar],
            wide,
            factor_bytes,
            scratch=[pltpu.VMEM((columns, fixed_rows), F32)],
        )
        got_target = send_up(target)
        got_parts = send_down(part_other)
        first_own, first_other, value, sent = call(
            first_response_kernel,
            [fixed_f32, fixed_others, node_f32, part_bf],
            [d0, d1, arrow, target, pushed_own, part_own, *got_pushed, *got_parts],
            wide,
            factor_bytes,
        )
        summed = Sum(sent)
        got_first = send_down(first_other)
        solved, other, _ = summed.fold_into(
            last_solve_kernel,
            [flat_f32, flat_others, node_f32],
            [d1, value, *got_target],
            wide * 3 // 2,
            factor_bytes,
        )
        got_solved = send_down(other)
        summed.fold()
        base, passed, other = summed.fold_into(
            pass_kernel,
            [flat_f32, flat_f32, flat_others],
            [k1, mask, solved, *got_solved],
            wide,
            factor_bytes,
        )
        got_passed = send_down(other)
        while summed.left:
            summed.fold()
        last = [summed.sent, summed.got] if bits else [summed.sent]
        fixed_out, fixed = call(
            tip_kernel,
            [shape_of((fixed_rows, width), F32), part_bf],
            [noise_fixed, tip_inverse, *last],
            4 * fixed_rows * fixed_rows * width,
            8 * fixed_rows * fixed_rows,
        )
        solved, other = call(
            first_solve_kernel,
            [flat_f32, flat_others],
            [d0, value_rows, passed, *got_passed],
            wide,
            factor_bytes,
        )
        got_solved = send_down(other)
        (sample,) = call(
            final_kernel,
            [shape_of((2, rows, columns), BF)],
            [response, base, solved, first_own, fixed, *got_solved, *got_first, *send_up(fixed)],
            4 * rows * fixed_rows * columns,
            factor_bytes,
            scratch=[pltpu.VMEM((columns, fixed_rows), BF)],
        )
        return (sample, fixed_out)

    return on_device


def solution(mesh):
    sizes = dict(mesh.shape)

    def program(diag_inverse, coupling, arrow, tip_inverse, noise, noise_fixed, section_lengths):
        device = build(
            sizes["tm"],
            sizes["space"],
            diag_inverse.shape[1] // sizes["space"],
            noise.shape[2],
            arrow.shape[1],
        )
        return jax.shard_map(
            device,
            mesh=mesh,
            in_specs=(
                P("tm", "space", None),
                P("tm", "space", None),
                P("tm", None, "space"),
                P(),
                P("tm", "space", None),
                P(None, "space"),
                P(),
            ),
            out_specs=(P("tm", "space", None), P(None, "space")),
            check_vma=False,
        )(diag_inverse, coupling, arrow, tip_inverse, noise, noise_fixed, section_lengths)

    return program
```

time: 63.6 us -> 50.2 us (0.79)
  local copies, waits for them, and re-layouts: 13.6 us -> 0.03 us
  Pallas kernels: 20.2 us -> 15.9 us
  waiting for transfers between devices: 13.2 us -> 16 us
  starting transfers between devices: 15.3 us -> 17.3 us
    unnamed x34 -> x8, local copies, waits for them, and re-layouts: 12.5 us -> 0.03 us
    pallas_call x10 -> x11, Pallas kernels: 20.2 us -> 15.9 us  [call(): pl.pallas_call(body, in_specs=specs, out_specs=[pl.BlockSpec(memory_space...]
    ppermute x4, waiting for transfers between devices: 9.01 us -> 11.3 us  [swap_bit(): return lax.ppermute(value, 'tm', [(i, i ^ bit) for i in range(n_tm)])]
    ppermute x11, starting transfers between devices: 6.06 us -> 7.45 us  [swap(): return lax.ppermute(value, 'space', pairs)]
    squeeze x1 -> x0, local copies, waits for them, and re-layouts: 1.08 us -> none  [on_device(): got_noise = send_up(noise[0])]
  transfers between devices with their start and end apart: 15 -> 15, of which waited for: 7 -> 8; matrix products, arithmetic and copies ran while one was open for 0% -> 0% of each run, Pallas kernels for 26% -> 23%
where the time goes in v3:
time: 50.2 us; the launch traced here: 50 us
  starting transfers between devices  17.3 us (34%)
  waiting for transfers between devices  16 us (32%)
  Pallas kernels  15.9 us (32%)
  between operations  0.74 us (1%)
    pallas_call x11, Pallas kernels, call(): pl.pallas_call(body, in_specs=specs, out_specs=[pl.BlockSpec(memory_space...  15.9 us
    ppermute x4, waiting for transfers between devices, swap_bit(): return lax.ppermute(value, 'tm', [(i, i ^ bit) for i in range(n_tm)])  11.3 us
    ppermute x4, starting transfers between devices, swap_bit(): return lax.ppermute(value, 'tm', [(i, i ^ bit) for i in range(n_tm)])  9.87 us
    ppermute x11, starting transfers between devices, swap(): return lax.ppermute(value, 'space', pairs)  7.45 us
    ppermute x11, waiting for transfers between devices, swap(): return lax.ppermute(value, 'space', pairs)  4.73 us
  transfers between devices with their start and end apart: 15, of which 8 were waited for; matrix products, arithmetic and copies ran while one was open for 0% of the time, Pallas kernels for 23%

profile of v3, /device:TPU:0, one launch (start us, length us, event | category | flops | bytes accessed | tf_op | source)
XLA Modules:
  0.0 50.0 jit_solution(9006110421050351436)
XLA Ops:
  0.6 0.5 %collective-permute-start = (bf16[2,1024,256]{2,1,0:T(8,128)(2,1)}, bf16[2,1024,256]{2,1,0:T(8,128)(2,1)S(1)}, u32[]{:S(2)}, u32[]{:S(2)}) collective-permute-start(bf16[2,1024,256]{2,1,0:T(8,128)(2,1)} %noise.3), channel_id=1, source_target_pairs={{0,1},{1,0},{2,3},{3,2},{4,5},{5,4},{6,7},{7,6},{8,9},{9,8},{10,11... | collective-permute-start | bytes 3145736 | tf_op jit(solution)/shard_map/ppermute | solution.py:254
  1.1 4.6 %shard_map.86 = (bf16[1024,2048]{1,0:T(8,128)(2,1)S(1)}, bf16[1024,2048]{1,0:T(8,128)(2,1)S(1)}, bf16[1024,2048]{1,0:T(8,128)(2,1)S(1)}, f32[256,1024]{1,0:T(8,1...) custom-call(bf16[2,1024,2048]{2,1,0:T(8,128)(2,1)} %diag.1, ...), custom_call_target="tpu_custom_call" | custom-call | flops 1073741824 | bytes 12582912 | tf_op jit(solution)/shard_map/pallas_call | solution.py:63
  5.8 2.1 %collective-permute-start.1 = (bf16[256,1024]{1,0:T(8,128)(2,1)S(1)}, bf16[256,1024]{1,0:T(8,128)(2,1)S(1)}, u32[]{:S(2)}, u32[]{:S(2)}) collective-permute-start(bf16[256,1024]{1,0:T(8,128)(2,1)S(1)} %bitcast.11), channel_id=1, source_target_pairs={{0,1},{1,0},{2,3},{3,2},{4,5},{5,4},{6,7},{7,6},{8,9},{9,8},{10,11... | collective-permute-start | bytes 1572872 | tf_op jit(solution)/shard_map/ppermute | solution.py:254
  7.9 0.0 collective-permute-done.refs_0_
  7.9 0.1 shard_map.87
  8.0 0.0 copy-start
  8.0 0.0 copy-start.1
  8.0 0.8 %collective-permute-start.2 = (bf16[1024,256]{1,0:T(8,128)(2,1)S(1)}, bf16[1024,256]{1,0:T(8,128)(2,1)S(1)}, u32[]{:S(2)}, u32[]{:S(2)}) collective-permute-start(bf16[1024,256]{1,0:T(8,128)(2,1)S(1)} %get-tuple-element.42.bar), channel_id=1, source_target_pairs={{0,1},{1,0},{2,3},{3,2},{4,5},{5,4},{6,7},{7,6},{8,9},{9,8},{10,11... | collective-permute-start | bytes 1572872 | tf_op jit(solution)/shard_map/ppermute | solution.py:254
  8.9 0.6 %collective-permute-done.1.refs_0_ = bf16[256,1024]{1,0:T(8,128)(2,1)S(1)} collective-permute-done((bf16[256,1024]{1,0:T(8,128)(2,1)S(1)}, bf16[256,1024]{1,0:T(8,128)(2,1)S(1)}, u32[]{:S(2)}, u32[]{:S(2)}) %collective-permute-start.1) | collective-permute-done | bytes 524320 | tf_op jit(solution)/shard_map/ppermute | solution.py:254
  9.4 1.3 %shard_map.88 = (bf16[256,1024]{1,0:T(8,128)(2,1)S(1)}, f32[256,1024]{1,0:T(8,128)S(1)}, bf16[1,256,1024]{2,1,0:T(8,128)(2,1)S(1)}, f32[256,1024]{1,0:T(8,128)S(1)}) custom-call(bf16[1024,2048]{1,0:T(8,128)(2,1)S(1)} %get-tuple-element.33.k1.refs_0_, f32[1024,256]{1,0:T(8,128)S(1)} %get-tuple-element.36.value, f32[256,1024]{1,0:T(8,128)S(1)} %get-tuple-element.37.own, ...), custom_call_target="tpu_custom_call" | custom-call | flops 1073741824 | bytes 4194304 | tf_op jit(solution)/shard_map/pallas_call | solution.py:63
  10.7 0.4 collective-permute-start.3
  11.2 0.0 collective-permute-done.2.refs_0_
  11.2 0.0 copy-done
  11.2 0.0 copy-done.1
  11.2 2.1 %shard_map.89 = (bf16[1024,256]{1,0:T(8,128)(2,1)S(1)}, f32[128,256]{1,0:T(8,128)S(1)}, bf16[1,128,256]{2,1,0:T(8,128)(2,1)S(1)}) custom-call(bf16[1024,2048]{1,0:T(8,128)(2,1)S(1)} %get-tuple-element.33.k1.refs_0_, bf16[1024,256]{1,0:T(8,128)(2,1)S(1)} %get-tuple-element.42.bar, bf16[2,1024,256]{2,1,0:T(8,128)(2,1)S(1)} %copy-done.1, ...), custom_call_target="tpu_custom_call" | custom-call | flops 1073741824 | bytes 4194304 | tf_op jit(solution)/shard_map/pallas_call | solution.py:63
  13.3 0.2 collective-permute-start.5
  13.5 0.4 collective-permute-start.4
  13.9 0.0 collective-permute-done.3.refs_0_
  13.9 1.5 %collective-permute-done.4.refs_1_ = bf16[128,256]{1,0:T(8,128)(2,1)S(1)} collective-permute-done((bf16[128,256]{1,0:T(8,128)(2,1)S(1)}, bf16[128,256]{1,0:T(8,128)(2,1)S(1)}, u32[]{:S(2)}, u32[]{:S(2)}) %collective-permute-start.4) | collective-permute-done | bytes 65568 | tf_op jit(solution)/shard_map/ppermute | solution.py:254
  15.4 1.3 %shard_map.90 = (f32[256,1024]{1,0:T(8,128)S(1)}, bf16[1,256,1024]{2,1,0:T(8,128)(2,1)S(1)}, f32[1024,256]{1,0:T(8,128)S(1)}, bf16[128,256]{1,0:T(8,128)(2,1)S(1)}) custom-call(bf16[1024,2048]{1,0:T(8,128)(2,1)S(1)} %get-tuple-element.34.d0, bf16[1024,2048]{1,0:T(8,128)(2,1)S(1)} %get-tuple-element.41.d1.refs_0_, bf16[2,256,1024]{2,1,0:T(8,128)(2,1)S(1)} %copy-done, ...), custom_call_target="tpu_custom_call" | custom-call | flops 1073741824 | bytes 4194304 | tf_op jit(solution)/shard_map/pallas_call | solution.py:63
  16.7 3.0 %collective-permute-start.6 = (bf16[128,256]{1,0:T(8,128)(2,1)S(1)}, bf16[128,256]{1,0:T(8,128)(2,1)S(1)}, u32[]{:S(2)}, u32[]{:S(2)}) collective-permute-start(bf16[128,256]{1,0:T(8,128)(2,1)S(1)} %get-tuple-element.49.refs_3_), channel_id=1, source_target_pairs={{0,2},{2,0},{4,6},{6,4},{8,10},{10,8},{12,14},{14,12},{16,18},{18,... | collective-permute-start | bytes 196616 | tf_op jit(solution)/shard_map/ppermute | solution.py:266
  19.7 2.8 %collective-permute-done.6.refs_4_ = bf16[128,256]{1,0:T(8,128)(2,1)S(1)} collective-permute-done((bf16[128,256]{1,0:T(8,128)(2,1)S(1)}, bf16[128,256]{1,0:T(8,128)(2,1)S(1)}, u32[]{:S(2)}, u32[]{:S(2)}) %collective-permute-start.6) | collective-permute-done | bytes 65568 | tf_op jit(solution)/shard_map/ppermute | solution.py:266
  22.5 0.0 collective-permute-done.5.refs_2_
  22.5 1.6 %shard_map.91 = (f32[256,1024]{1,0:T(8,128)S(1)}, bf16[1,256,1024]{2,1,0:T(8,128)(2,1)S(1)}, f32[1024,256]{1,0:T(8,128)}, bf16[128,256]{1,0:T(8,128)(2,1)S(1)}) custom-call(bf16[1024,2048]{1,0:T(8,128)(2,1)S(1)} %get-tuple-element.41.d1.refs_0_, f32[1024,256]{1,0:T(8,128)S(1)} %get-tuple-element.48.refs_1_, ...), custom_call_target="tpu_custom_call" | custom-call | flops 1610612736 | bytes 4194304 | tf_op jit(solution)/shard_map/pallas_call | solution.py:63
  24.1 1.5 %collective-permute-start.7 = (bf16[256,1024]{1,0:T(8,128)(2,1)S(1)}, bf16[256,1024]{1,0:T(8,128)(2,1)S(1)}, u32[]{:S(2)}, u32[]{:S(2)}) collective-permute-start(bf16[256,1024]{1,0:T(8,128)(2,1)S(1)} %bitcast.9), channel_id=1, source_target_pairs={{0,1},{1,0},{2,3},{3,2},{4,5},{5,4},{6,7},{7,6},{8,9},{9,8},{10,11... | collective-permute-start | bytes 1572872 | tf_op jit(solution)/shard_map/ppermute | solution.py:254
  25.6 1.9 %collective-permute-start.8 = (bf16[128,256]{1,0:T(8,128)(2,1)S(1)}, bf16[128,256]{1,0:T(8,128)(2,1)S(1)}, u32[]{:S(2)}, u32[]{:S(2)}) collective-permute-start(bf16[128,256]{1,0:T(8,128)(2,1)S(1)} %get-tuple-element.52.sent), channel_id=1, source_target_pairs={{0,4},{2,6},{4,0},{6,2},{8,12},{10,14},{12,8},{14,10},{16,20},{18,... | collective-permute-start | bytes 196616 | tf_op jit(solution)/shard_map/ppermute | solution.py:266
  27.5 2.4 %collective-permute-done.8.got = bf16[128,256]{1,0:T(8,128)(2,1)S(1)} collective-permute-done((bf16[128,256]{1,0:T(8,128)(2,1)S(1)}, bf16[128,256]{1,0:T(8,128)(2,1)S(1)}, u32[]{:S(2)}, u32[]{:S(2)}) %collective-permute-start.8) | collective-permute-done | bytes 65568 | tf_op jit(solution)/shard_map/ppermute | solution.py:266
  29.9 2.0 %collective-permute-start.9 = (bf16[128,256]{1,0:T(8,128)(2,1)S(1)}, bf16[128,256]{1,0:T(8,128)(2,1)S(1)}, u32[]{:S(2)}, u32[]{:S(2)}) collective-permute-start(bf16[128,256]{1,0:T(8,128)(2,1)S(1)} %shard_map.92.refs_4_), channel_id=1, source_target_pairs={{0,8},{2,10},{4,12},{6,14},{8,0},{10,2},{12,4},{14,6},{16,24},{18,... | collective-permute-start | bytes 196616 | tf_op jit(solution)/shard_map/ppermute | solution.py:266
  31.9 2.3 %collective-permute-done.9.refs_5_ = bf16[128,256]{1,0:T(8,128)(2,1)S(1)} collective-permute-done((bf16[128,256]{1,0:T(8,128)(2,1)S(1)}, bf16[128,256]{1,0:T(8,128)(2,1)S(1)}, u32[]{:S(2)}, u32[]{:S(2)}) %collective-permute-start.9) | collective-permute-done | bytes 65568 | tf_op jit(solution)/shard_map/ppermute | solution.py:266
  34.3 0.0 collective-permute-done.7.refs_3_
  34.3 1.3 %shard_map.93 = (f32[256,1024]{1,0:T(8,128)S(1)}, f32[256,1024]{1,0:T(8,128)S(1)}, bf16[1,256,1024]{2,1,0:T(8,128)(2,1)S(1)}, bf16[128,256]{1,0:T(8,128)(2,1)S(1)}) custom-call(bf16[1024,2048]{1,0:T(8,128)(2,1)S(1)} %get-tuple-element.33.k1.refs_0_, f32[8,128]{1,0:T(8,128)S(1)} %get-tuple-element.40.refs_1_, f32[256,1024]{1,0:T(8,128)S(1)} %get-tuple-element.50.refs_2_, ...), custom_call_target="tpu_custom_call" | custom-call | flops 1073741824 | bytes 4194304 | tf_op jit(solution)/shard_map/pallas_call | solution.py:63
  35.6 0.0 copy-start.2
  35.6 0.0 copy-start.3
  35.6 0.1 collective-permute-start.10
  35.7 0.5 collective-permute-start.13
  36.2 1.4 %collective-permute-done.10.refs_0_ = bf16[256,1024]{1,0:T(8,128)(2,1)S(1)} collective-permute-done((bf16[256,1024]{1,0:T(8,128)(2,1)S(1)}, bf16[256,1024]{1,0:T(8,128)(2,1)S(1)}, u32[]{:S(2)}, u32[]{:S(2)}) %collective-permute-start.10) | collective-permute-done | bytes 524320 | tf_op jit(solution)/shard_map/ppermute | solution.py:254
  37.6 0.9 %shard_map.94 = (f32[256,1024]{1,0:T(8,128)S(1)}, bf16[1,256,1024]{2,1,0:T(8,128)(2,1)S(1)}) custom-call(bf16[1024,2048]{1,0:T(8,128)(2,1)S(1)} %get-tuple-element.34.d0, f32[256,1024]{1,0:T(8,128)S(1)} %get-tuple-element.54.value_rows, f32[256,1024]{1,0:T(8,128)S(1)} %get-tuple-element.55.passed, bf16[256,1024]{1,0:T(8,128)(2,1)S(1)} %collective-permute-done.10.refs_0_), custom_call_target="tpu_custom_call" | custom-call | flops 1073741824 | bytes 4194304 | tf_op jit(solution)/shard_map/pallas_call | solution.py:63
  38.5 0.9 %collective-permute-start.12 = (bf16[256,1024]{1,0:T(8,128)(2,1)S(1)}, bf16[256,1024]{1,0:T(8,128)(2,1)S(1)}, u32[]{:S(2)}, u32[]{:S(2)}) collective-permute-start(bf16[256,1024]{1,0:T(8,128)(2,1)S(1)} %bitcast.8), channel_id=1, source_target_pairs={{0,1},{1,0},{2,3},{3,2},{4,5},{5,4},{6,7},{7,6},{8,9},{9,8},{10,11... | collective-permute-start | bytes 1572872 | tf_op jit(solution)/shard_map/ppermute | solution.py:254
  39.4 3.0 %collective-permute-start.11 = (bf16[128,256]{1,0:T(8,128)(2,1)S(1)}, bf16[128,256]{1,0:T(8,128)(2,1)S(1)}, u32[]{:S(2)}, u32[]{:S(2)}) collective-permute-start(bf16[128,256]{1,0:T(8,128)(2,1)S(1)} %get-tuple-element.59.sent), channel_id=1, source_target_pairs={{0,16},{2,18},{4,20},{6,22},{8,24},{10,26},{12,28},{14,30},{16,0},... | collective-permute-start | bytes 196616 | tf_op jit(solution)/shard_map/ppermute | solution.py:266
  42.3 3.7 %collective-permute-done.11.refs_0_ = bf16[128,256]{1,0:T(8,128)(2,1)S(1)} collective-permute-done((bf16[128,256]{1,0:T(8,128)(2,1)S(1)}, bf16[128,256]{1,0:T(8,128)(2,1)S(1)}, u32[]{:S(2)}, u32[]{:S(2)}) %collective-permute-start.11) | collective-permute-done | bytes 65568 | tf_op jit(solution)/shard_map/ppermute | solution.py:266
  46.1 0.0 copy-done.2
  46.1 0.0 copy-done.3
  46.1 1.1 %shard_map.95 = (f32[256,128]{1,0:T(8,128)}, bf16[128,256]{1,0:T(8,128)(2,1)S(1)}) custom-call(f32[256,128]{1,0:T(8,128)S(1)} %copy-done.2, bf16[256,256]{1,0:T(8,128)(2,1)S(1)} %copy-done.3, bf16[128,256]{1,0:T(8,128)(2,1)S(1)} %get-tuple-element.59.sent, bf16[128,256]{1,0:T(8,128)(2,1)S(1)} %collective-permute-done.11.refs_0_), custom_call_target="tpu_custom_call" | custom-call | flops 33554432 | bytes 524288 | tf_op jit(solution)/shard_map/pallas_call | solution.py:63
  47.1 0.0 collective-permute-start.14
  47.1 0.0 collective-permute-done.13.refs_1_
  47.1 1.2 %collective-permute-done.14.refs_2_ = bf16[128,256]{1,0:T(8,128)(2,1)S(1)} collective-permute-done((bf16[128,256]{1,0:T(8,128)(2,1)S(1)}, bf16[128,256]{1,0:T(8,128)(2,1)S(1)}, u32[]{:S(2)}, u32[]{:S(2)}) %collective-permute-start.14) | collective-permute-done | bytes 65568 | tf_op jit(solution)/shard_map/ppermute | solution.py:254
  48.4 0.0 collective-permute-done.12.refs_0_
  48.4 1.6 %shard_map.96 = bf16[2,1024,256]{2,1,0:T(8,128)(2,1)} custom-call(bf16[256,1024]{1,0:T(8,128)(2,1)S(1)} %get-tuple-element.39.response, f32[256,1024]{1,0:T(8,128)S(1)} %get-tuple-element.53.base, f32[256,1024]{1,0:T(8,128)S(1)} %get-tuple-element.57.solved, f32[256,1024]{1,0:T(8,128)S(1)} %get-tuple-element.58.pushed, ...), custom_call_target="tpu_custom_call" | custom-call | flops 268435456 | bytes 4194304 | tf_op jit(solution)/shard_map/pallas_call | solution.py:63
  (1 shorter events, 0.0 us)
Async XLA Ops:
  0.6 7.3 %collective-permute-start = (bf16[2,1024,256]{2,1,0:T(8,128)(2,1)}, bf16[2,1024,256]{2,1,0:T(8,128)(2,1)S(1)}, u32[]{:S(2)}, u32[]{:S(2)}) collective-permute-start(bf16[2,1024,256]{2,1,0:T(8,128)(2,1)} %noise.3), channel_id=1, source_target_pairs={{0,1},{1,0},{2,3},{3,2},{4,5},{5,4},{6,7},{7,6},{8,9},{9,8},{10,11... | collective-permute-start | bytes 3145736 | tf_op jit(solution)/shard_map/ppermute | solution.py:254
  5.8 3.7 %collective-permute-start.1 = (bf16[256,1024]{1,0:T(8,128)(2,1)S(1)}, bf16[256,1024]{1,0:T(8,128)(2,1)S(1)}, u32[]{:S(2)}, u32[]{:S(2)}) collective-permute-start(bf16[256,1024]{1,0:T(8,128)(2,1)S(1)} %bitcast.11), channel_id=1, source_target_pairs={{0,1},{1,0},{2,3},{3,2},{4,5},{5,4},{6,7},{7,6},{8,9},{9,8},{10,11... | collective-permute-start | bytes 1572872 | tf_op jit(solution)/shard_map/ppermute | solution.py:254
  8.0 3.2 %copy-start = (bf16[2,256,1024]{2,1,0:T(8,128)(2,1)S(1)}, bf16[2,256,1024]{2,1,0:T(8,128)(2,1)}, u32[]{:S(2)}) copy-start(bf16[2,256,1024]{2,1,0:T(8,128)(2,1)} %arrow.5) | copy-start | bytes 3145732
  8.0 3.2 %copy-start.1 = (bf16[2,1024,256]{2,1,0:T(8,128)(2,1)S(1)}, bf16[2,1024,256]{2,1,0:T(8,128)(2,1)}, u32[]{:S(2)}) copy-start(bf16[2,1024,256]{2,1,0:T(8,128)(2,1)} %noise.3) | copy-start | bytes 3145732
  8.0 3.2 %collective-permute-start.2 = (bf16[1024,256]{1,0:T(8,128)(2,1)S(1)}, bf16[1024,256]{1,0:T(8,128)(2,1)S(1)}, u32[]{:S(2)}, u32[]{:S(2)}) collective-permute-start(bf16[1024,256]{1,0:T(8,128)(2,1)S(1)} %get-tuple-element.42.bar), channel_id=1, source_target_pairs={{0,1},{1,0},{2,3},{3,2},{4,5},{5,4},{6,7},{7,6},{8,9},{9,8},{10,11... | collective-permute-start | bytes 1572872 | tf_op jit(solution)/shard_map/ppermute | solution.py:254
  10.7 3.2 %collective-permute-start.3 = (bf16[256,1024]{1,0:T(8,128)(2,1)S(1)}, bf16[256,1024]{1,0:T(8,128)(2,1)S(1)}, u32[]{:S(2)}, u32[]{:S(2)}) collective-permute-start(bf16[256,1024]{1,0:T(8,128)(2,1)S(1)} %bitcast.10), channel_id=1, source_target_pairs={{0,1},{1,0},{2,3},{3,2},{4,5},{5,4},{6,7},{7,6},{8,9},{9,8},{10,11... | collective-permute-start | bytes 1572872 | tf_op jit(solution)/shard_map/ppermute | solution.py:254
  13.3 9.2 %collective-permute-start.5 = (bf16[1024,256]{1,0:T(8,128)(2,1)S(1)}, bf16[1024,256]{1,0:T(8,128)(2,1)S(1)}, u32[]{:S(2)}, u32[]{:S(2)}) collective-permute-start(bf16[1024,256]{1,0:T(8,128)(2,1)S(1)} %get-tuple-element.43.target), channel_id=1, source_target_pairs={{0,1},{1,0},{2,3},{3,2},{4,5},{5,4},{6,7},{7,6},{8,9},{9,8},{10,11... | collective-permute-start | bytes 1572872 | tf_op jit(solution)/shard_map/ppermute | solution.py:254
  13.5 1.9 %collective-permute-start.4 = (bf16[128,256]{1,0:T(8,128)(2,1)S(1)}, bf16[128,256]{1,0:T(8,128)(2,1)S(1)}, u32[]{:S(2)}, u32[]{:S(2)}) collective-permute-start(bf16[128,256]{1,0:T(8,128)(2,1)S(1)} %bitcast.13), channel_id=1, source_target_pairs={{0,1},{1,0},{2,3},{3,2},{4,5},{5,4},{6,7},{7,6},{8,9},{9,8},{10,11... | collective-permute-start | bytes 196616 | tf_op jit(solution)/shard_map/ppermute | solution.py:254
  16.7 5.8 %collective-permute-start.6 = (bf16[128,256]{1,0:T(8,128)(2,1)S(1)}, bf16[128,256]{1,0:T(8,128)(2,1)S(1)}, u32[]{:S(2)}, u32[]{:S(2)}) collective-permute-start(bf16[128,256]{1,0:T(8,128)(2,1)S(1)} %get-tuple-element.49.refs_3_), channel_id=1, source_target_pairs={{0,2},{2,0},{4,6},{6,4},{8,10},{10,8},{12,14},{14,12},{16,18},{18,... | collective-permute-start | bytes 196616 | tf_op jit(solution)/shard_map/ppermute | solution.py:266
  24.1 10.1 %collective-permute-start.7 = (bf16[256,1024]{1,0:T(8,128)(2,1)S(1)}, bf16[256,1024]{1,0:T(8,128)(2,1)S(1)}, u32[]{:S(2)}, u32[]{:S(2)}) collective-permute-start(bf16[256,1024]{1,0:T(8,128)(2,1)S(1)} %bitcast.9), channel_id=1, source_target_pairs={{0,1},{1,0},{2,3},{3,2},{4,5},{5,4},{6,7},{7,6},{8,9},{9,8},{10,11... | collective-permute-start | bytes 1572872 | tf_op jit(solution)/shard_map/ppermute | solution.py:254
  25.6 4.3 %collective-permute-start.8 = (bf16[128,256]{1,0:T(8,128)(2,1)S(1)}, bf16[128,256]{1,0:T(8,128)(2,1)S(1)}, u32[]{:S(2)}, u32[]{:S(2)}) collective-permute-start(bf16[128,256]{1,0:T(8,128)(2,1)S(1)} %get-tuple-element.52.sent), channel_id=1, source_target_pairs={{0,4},{2,6},{4,0},{6,2},{8,12},{10,14},{12,8},{14,10},{16,20},{18,... | collective-permute-start | bytes 196616 | tf_op jit(solution)/shard_map/ppermute | solution.py:266
  29.9 4.3 %collective-permute-start.9 = (bf16[128,256]{1,0:T(8,128)(2,1)S(1)}, bf16[128,256]{1,0:T(8,128)(2,1)S(1)}, u32[]{:S(2)}, u32[]{:S(2)}) collective-permute-start(bf16[128,256]{1,0:T(8,128)(2,1)S(1)} %shard_map.92.refs_4_), channel_id=1, source_target_pairs={{0,8},{2,10},{4,12},{6,14},{8,0},{10,2},{12,4},{14,6},{16,24},{18,... | collective-permute-start | bytes 196616 | tf_op jit(solution)/shard_map/ppermute | solution.py:266
  35.6 10.5 %copy-start.2 = (f32[256,128]{1,0:T(8,128)S(1)}, f32[256,128]{1,0:T(8,128)}, u32[]{:S(2)}) copy-start(f32[256,128]{1,0:T(8,128)} %noise_fixed.1) | copy-start | bytes 393220
  35.6 10.5 %copy-start.3 = (bf16[256,256]{1,0:T(8,128)(2,1)S(1)}, bf16[256,256]{1,0:T(8,128)(2,1)}, u32[]{:S(2)}) copy-start(bf16[256,256]{1,0:T(8,128)(2,1)} %tip.1) | copy-start | bytes 393220
  35.6 2.0 %collective-permute-start.10 = (bf16[256,1024]{1,0:T(8,128)(2,1)S(1)}, bf16[256,1024]{1,0:T(8,128)(2,1)S(1)}, u32[]{:S(2)}, u32[]{:S(2)}) collective-permute-start(bf16[256,1024]{1,0:T(8,128)(2,1)S(1)} %bitcast.12), channel_id=1, source_target_pairs={{0,1},{1,0},{2,3},{3,2},{4,5},{5,4},{6,7},{7,6},{8,9},{9,8},{10,11... | collective-permute-start | bytes 1572872 | tf_op jit(solution)/shard_map/ppermute | solution.py:254
  35.7 11.4 %collective-permute-start.13 = (bf16[256,1024]{1,0:T(8,128)(2,1)S(1)}, bf16[256,1024]{1,0:T(8,128)(2,1)S(1)}, u32[]{:S(2)}, u32[]{:S(2)}) collective-permute-start(bf16[256,1024]{1,0:T(8,128)(2,1)S(1)} %bitcast.7), channel_id=1, source_target_pairs={{0,1},{1,0},{2,3},{3,2},{4,5},{5,4},{6,7},{7,6},{8,9},{9,8},{10,11... | collective-permute-start | bytes 1572872 | tf_op jit(solution)/shard_map/ppermute | solution.py:254
  38.5 9.9 %collective-permute-start.12 = (bf16[256,1024]{1,0:T(8,128)(2,1)S(1)}, bf16[256,1024]{1,0:T(8,128)(2,1)S(1)}, u32[]{:S(2)}, u32[]{:S(2)}) collective-permute-start(bf16[256,1024]{1,0:T(8,128)(2,1)S(1)} %bitcast.8), channel_id=1, source_target_pairs={{0,1},{1,0},{2,3},{3,2},{4,5},{5,4},{6,7},{7,6},{8,9},{9,8},{10,11... | collective-permute-start | bytes 1572872 | tf_op jit(solution)/shard_map/ppermute | solution.py:254
  39.4 6.7 %collective-permute-start.11 = (bf16[128,256]{1,0:T(8,128)(2,1)S(1)}, bf16[128,256]{1,0:T(8,128)(2,1)S(1)}, u32[]{:S(2)}, u32[]{:S(2)}) collective-permute-start(bf16[128,256]{1,0:T(8,128)(2,1)S(1)} %get-tuple-element.59.sent), channel_id=1, source_target_pairs={{0,16},{2,18},{4,20},{6,22},{8,24},{10,26},{12,28},{14,30},{16,0},... | collective-permute-start | bytes 196616 | tf_op jit(solution)/shard_map/ppermute | solution.py:266
  47.1 1.3 %collective-permute-start.14 = (bf16[128,256]{1,0:T(8,128)(2,1)S(1)}, bf16[128,256]{1,0:T(8,128)(2,1)S(1)}, u32[]{:S(2)}, u32[]{:S(2)}) collective-permute-start(bf16[128,256]{1,0:T(8,128)(2,1)S(1)} %get-tuple-element.60.fixed), channel_id=1, source_target_pairs={{0,1},{1,0},{2,3},{3,2},{4,5},{5,4},{6,7},{7,6},{8,9},{9,8},{10,11... | collective-permute-start | bytes 196616 | tf_op jit(solution)/shard_map/ppermute | solution.py:254

commit v4 on v3

v4 whole, which is shorter than its diff:
```python
import jax
import jax.numpy as jnp
from jax import lax
from jax.experimental import pallas as pl
from jax.experimental.pallas import tpu as pltpu
from jax.sharding import PartitionSpec as P

BF = jnp.bfloat16
F32 = jnp.float32
MIB = 1 << 20


def dot(left, right):
    return jnp.dot(left, right, preferred_element_type=F32)


def dot_last(left, right):
    return lax.dot_general(left, right, (((1,), (1,)), ((), ())), preferred_element_type=F32)


def rounded(value):
    return value.astype(BF).astype(F32)


def total_of(own_ref, got_refs):
    total = rounded(own_ref[...])
    for got in got_refs:
        total = total + got[...].astype(F32)
    return total


def shape_of(shape, dtype):
    return jax.ShapeDtypeStruct(shape, dtype)


def build(n_tm, n_space, rows, columns, fixed_rows):
    nodes = n_space * rows
    tile = 256 if rows % 256 == 0 else rows
    tiles = rows // tile
    half = rows // 2
    width = columns // n_space
    peers = range(1, n_space)

    def at_core():
        return lax.axis_index("space")

    def block(step, offset=0, size=rows):
        owner = lax.rem(at_core() - step + n_space, n_space)
        return pl.ds(pl.multiple_of(owner * rows + offset, tile), size)

    def part_rows(step):
        owner = lax.rem(at_core() - step + n_space, n_space)
        return pl.ds(pl.multiple_of(owner * width, width), width)

    def call(body, outs, args, flops, moved, places=None, scratch=(), after=None):
        places = dict(places or {})
        args = list(args)
        count = len(args)
        if after is not None:
            args.append(after)
            places[count] = pl.ANY

        def run(*refs):
            body(*refs[:count], *refs[len(args) :])

        specs = [pl.BlockSpec(memory_space=places.get(i, pltpu.VMEM)) for i in range(len(args))]
        args = [
            pltpu.with_memory_space_constraint(a, pltpu.HBM)
            if places.get(i) is pltpu.HBM
            else a
            for i, a in enumerate(args)
        ]
        return pl.pallas_call(
            run,
            in_specs=specs,
            out_specs=[
                pl.BlockSpec(memory_space=places.get(("out", i), pltpu.VMEM))
                for i in range(len(outs))
            ],
            out_shape=outs,
            scratch_shapes=list(scratch),
            cost_estimate=pl.CostEstimate(flops=flops, bytes_accessed=moved, transcendentals=0),
            compiler_params=pltpu.CompilerParams(vmem_limit_bytes=16 * MIB),
        )(*args)

    def lower_rows(left, factor, own_ref, other_ref):
        for step in peers:

            @pl.when(at_core() >= step)
            def _():
                other_ref[step - 1] = dot(left[...], factor[:, block(step)]).astype(BF)

            @pl.when(at_core() < step)
            def _():
                other_ref[step - 1] = jnp.zeros_like(other_ref[step - 1])

        for j in range(tiles):
            at = j * tile
            own_ref[:, at : at + tile] = dot(left[:, at:], factor[at:, block(0, at, tile)])

    def full_rows(left, low, high, own_ref, other_ref):
        for step in (*peers, 0):
            product = dot(left[:, :half], low[:, block(step)])
            product = product + dot(left[:, half:], high[:, block(step)])
            if step:
                other_ref[step - 1] = product.astype(BF)
            else:
                own_ref[...] = product

    def lower_own(factor, right, out_ref, wait=None):
        for i in range(tiles):
            at = i * tile
            if wait:
                wait(i)
            out_ref[at : at + tile] = dot(
                factor[at : at + tile, block(0, 0, at + tile)], right[: at + tile]
            )

    def lower_rest(factor, got, value):
        for step in peers:

            @pl.when(at_core() >= step)
            def _():
                value[...] = value[...] + dot(factor[:, block(step)], got[step - 1][...])

    def start_kernel(
        diag, arrow, noise, lengths,
        d0, d1, own, other, first, mask,
        e1, n0, live_scratch, sem1, sem0, sems,
    ):
        arrow_copy = pltpu.make_async_copy(arrow.at[1], e1, sems.at[0])
        noise_copy = pltpu.make_async_copy(noise.at[0], n0, sems.at[1])
        live_copy = pltpu.make_async_copy(lengths, live_scratch, sems.at[2])

        def lower_copies(slot, target, sem):
            copies = {}
            for step in range(n_space):
                for i in range(tiles):
                    at = i * tile
                    size = rows if step else at + tile
                    part = (pl.ds(at, tile), block(step, 0, size))
                    copies[step, i] = pltpu.make_async_copy(
                        diag.at[(slot, *part)], target.at[part], sem.at[step, i]
                    )
            return copies

        def each(copies, act):
            for i in range(tiles):
                act(copies[0, i])
            for step in peers:

                @pl.when(at_core() >= step)
                def _():
                    for i in range(tiles):
                        act(copies[step, i])

        copies1 = lower_copies(1, d1, sem1)
        copies0 = lower_copies(0, d0, sem0)
        live_copy.start()
        arrow_copy.start()
        each(copies1, lambda copy: copy.start())
        noise_copy.start()
        each(copies0, lambda copy: copy.start())
        live_copy.wait()
        arrow_copy.wait()
        live = live_scratch[lax.axis_index("tm")] > 1
        mask[...] = jnp.where(live, jnp.ones_like(mask[...]), jnp.zeros_like(mask[...]))
        e1[...] = jnp.where(live, e1[...], jnp.zeros_like(e1[...]))
        each(copies1, lambda copy: copy.wait())
        lower_rows(e1, d1, own, other)
        noise_copy.wait()
        lower_own(d0, n0, first, lambda i: copies0[0, i].wait())
        for step in peers:

            @pl.when(at_core() >= step)
            def _():
                for i in range(tiles):
                    copies0[step, i].wait()

    def first_value_kernel(d0, value, *refs):
        got, (out, bar) = refs[: n_space - 1], refs[n_space - 1 :]
        out[...] = value[...]
        lower_rest(d0, [piece.at[0] for piece in got], out)
        bar[...] = out[...].astype(BF)

    def load_kernel(coupling, value, low, value_rows, sems):
        copies = []
        for i in range(2):
            size = half // 2
            copies.append(
                pltpu.make_async_copy(
                    coupling.at[1, pl.ds(i * size, size)], low.at[pl.ds(i * size, size)], sems.at[i]
                )
            )
            copies[i].start()
        value_rows[...] = value[...].T
        for copy in copies:
            copy.wait()

    def target_kernel(low, coupling, bar, noise, arrow, own, *refs):
        got, refs = refs[: n_space - 1], refs[n_space - 1 :]
        got_own, refs = refs[: n_space - 1], refs[n_space - 1 :]
        high, target, part_own, part_other, response, whole, sems = refs
        size = half // 2
        copies = []
        for i in range(2):
            copies.append(
                pltpu.make_async_copy(
                    coupling.at[1, pl.ds(half + i * size, size)],
                    high.at[pl.ds(i * size, size)],
                    sems.at[i],
                )
            )
            copies[i].start()
        response[...] = total_of(own, got_own).astype(BF)
        whole[...] = dot(arrow[0], bar[...])
        pieces = [bar, *got]
        for i in range(4):
            if i >= 2:
                copies[i - 2].wait()
            factor = low if i < 2 else high
            inner = (i % 2) * size
            pulled = dot(factor[inner : inner + size, block(0)], bar[...])
            for step in peers:
                pulled = pulled + dot(
                    factor[inner : inner + size, block(step)], pieces[step][...]
                )
            at = i * size
            source = noise[1, at : at + size].astype(F32)
            target[at : at + size] = (source - pulled).astype(BF)
        whole[...] = (whole[...] + dot(response[...], target[...])).T
        part_own[...] = whole[part_rows(0)]
        for step in peers:
            part_other[step - 1] = whole[part_rows(step)].astype(BF)

    def core_sum_kernel(part, *refs):
        got, out = refs[:-1], refs[-1]
        total = part[...]
        for piece in got:
            total = total + piece[...].astype(F32)
        out[...] = total.astype(BF)

    def fold_kernel(sent, got, out):
        out[...] = (sent[...].astype(F32) + got[...].astype(F32)).astype(BF)

    def last_solve_kernel(d1, target, *refs):
        got, (own, other, value) = refs[: n_space - 1], refs[n_space - 1 :]
        lower_own(d1, target, value)
        lower_rest(d1, got, value)
        lower_rows(value[...].T.astype(BF), d1, own, other)

    def response_kernel(low, high, response, own, other):
        full_rows(response, low, high, own, other)

    def pass_kernel(low, high, mask, solved, *refs):
        got, (base, own, other) = refs[: n_space - 1], refs[n_space - 1 :]
        value = jnp.where(mask[:1, :1] > 0, total_of(solved, got), 0.0)
        base[...] = value
        full_rows(value.astype(BF), low, high, own, other)

    def first_response_kernel(d0, arrow, pushed, *refs):
        got, (own, other) = refs[: n_space - 1], refs[n_space - 1 :]
        left = (arrow[0].astype(F32) - total_of(pushed, got)).astype(BF)
        lower_rows(left, d0, own, other)

    def first_solve_kernel(d0, value_rows, passed, *refs):
        got, (own, other) = refs[: n_space - 1], refs[n_space - 1 :]
        left = (value_rows[...] - total_of(passed, got)).astype(BF)
        lower_rows(left, d0, own, other)

    def turn_kernel(base, response, first, noise_fixed, *refs):
        got, (last_base, last_resp, first_resp, noise_rows) = refs[: n_space - 1], refs[n_space - 1 :]
        noise_rows[...] = noise_fixed[...].T
        last_base[...] = base[...].T
        last_resp[...] = response[...].astype(F32).T.astype(BF)
        first_resp[...] = total_of(first, got).T.astype(BF)

    def turn_first_kernel(solved, *refs):
        got, out = refs[:-1], refs[-1]
        out[...] = total_of(solved, got).T

    def mixed_kernel(noise_rows, *refs):
        terms, out = refs[:-1], refs[-1]
        total = terms[0][...].astype(F32)
        for piece in terms[1:]:
            total = total + piece[...].astype(F32)
        out[...] = (noise_rows[...] - total).astype(BF)

    def final_kernel(tip, bases, responses, mixed, *refs):
        got, (out, fixed_out, whole, fixed, result, sems) = refs[: n_space - 1], refs[n_space - 1 :]
        for step, piece in enumerate([mixed, *got]):
            whole[part_rows(step)] = piece[...]
        forward = dot_last(whole[...], tip[...])
        fixed[...] = dot(forward.astype(BF), tip[...])
        bar = fixed[...].astype(BF)
        copies = []
        for slot in range(2):
            for i in range(tiles):
                at = i * tile
                part = (slot, pl.ds(at, tile))
                update = dot_last(responses[slot][at : at + tile], bar)
                result[part] = (bases[slot][at : at + tile] - update).astype(BF)
                copies.append(
                    pltpu.make_async_copy(result.at[part], out.at[part], sems.at[slot, i])
                )
                copies[-1].start()
        fixed_out[...] = fixed[part_rows(0)].T
        for copy in copies:
            copy.wait()

    def swap(value, step):
        pairs = [(i, (i - step) % n_space) for i in range(n_space)]
        return lax.ppermute(value, "space", pairs)

    def send_up(value):
        return [swap(value, -step) for step in peers]

    def send_down(values):
        return [swap(values[step - 1], step) for step in peers]

    bits = [1 << i for i in range(n_tm.bit_length() - 1)]
    assert n_tm == 1 << len(bits)

    wide = 2 * rows * nodes * columns
    factor_bytes = 2 * rows * nodes
    node_f32, node_bf = shape_of((rows, columns), F32), shape_of((rows, columns), BF)
    flat_f32 = shape_of((columns, rows), F32)
    flat_others = shape_of((n_space - 1, columns, rows), BF)
    fixed_f32 = shape_of((fixed_rows, rows), F32)
    fixed_bf = shape_of((fixed_rows, rows), BF)
    fixed_others = shape_of((n_space - 1, fixed_rows, rows), BF)
    part_bf = shape_of((width, fixed_rows), BF)
    by_node = shape_of((rows, fixed_rows), BF)
    in_vmem, half_vmem = pltpu.VMEM((rows, nodes), BF), pltpu.VMEM((half, nodes), BF)
    dma = pltpu.SemaphoreType.DMA

    def fold(sent, got, after):
        size = width * fixed_rows
        return call(fold_kernel, [part_bf], [sent, got], size, 6 * size, after=after)[0]

    def swap_bit(value, bit):
        return lax.ppermute(value, "tm", [(i, i ^ bit) for i in range(n_tm)])

    def on_device(diag_inverse, coupling, arrow, tip_inverse, noise, noise_fixed, section_lengths):
        got_noise = send_up(noise)
        d0, d1, own, other, value, mask = call(
            start_kernel,
            [in_vmem, in_vmem, fixed_f32, fixed_others, node_f32, shape_of((8, 128), F32)],
            [diag_inverse, arrow, noise, section_lengths],
            wide,
            2 * factor_bytes,
            {i: pltpu.HBM for i in range(4)},
            [
                pltpu.VMEM((fixed_rows, rows), BF),
                pltpu.VMEM((rows, columns), BF),
                pltpu.SMEM(section_lengths.shape, jnp.int32),
                dma((n_space, tiles)),
                dma((n_space, tiles)),
                dma((3,)),
            ],
        )
        got_response = send_down(other)
        value, bar = call(
            first_value_kernel, [node_f32, node_bf], [d0, value, *got_noise], wide // 2, factor_bytes
        )
        got_bar = send_up(bar)
        low, value_rows = call(
            load_kernel,
            [half_vmem, flat_f32],
            [coupling, value],
            wide // 8,
            factor_bytes,
            {0: pltpu.HBM},
            [dma((2,))],
        )
        high, target, part_own, part_other, response = call(
            target_kernel,
            [
                half_vmem,
                node_bf,
                shape_of((width, fixed_rows), F32),
                shape_of((n_space - 1, width, fixed_rows), BF),
                fixed_bf,
            ],
            [low, coupling, bar, noise, arrow, own, *got_bar, *got_response],
            wide,
            factor_bytes,
            {1: pltpu.HBM},
            [pltpu.VMEM((columns, fixed_rows), F32), dma((2,))],
        )
        got_parts = send_down(part_other)
        got_target = send_up(target)
        (sent,) = call(
            core_sum_kernel, [part_bf], [part_own, *got_parts], width * fixed_rows, 8 * width * fixed_rows
        )
        left = list(bits)
        got = [swap_bit(sent, left.pop(0))] if left else []

        def advance(after):
            nonlocal sent, got
            if left:
                sent = fold(sent, *got, after)
                got = [swap_bit(sent, left.pop(0))]

        solved, other = call(
            last_solve_kernel,
            [flat_f32, flat_others],
            [d1, target, *got_target],
            wide * 3 // 2,
            factor_bytes,
            scratch=[pltpu.VMEM((rows, columns), F32)],
            after=sent,
        )
        got_solved = send_down(other)
        advance(solved)
        pushed, other = call(
            response_kernel, [fixed_f32, fixed_others], [low, high, response], wide, factor_bytes, after=sent
        )
        got_pushed = send_down(other)
        base, passed, other = call(
            pass_kernel,
            [flat_f32, flat_f32, flat_others],
            [low, high, mask, solved, *got_solved],
            wide,
            factor_bytes,
            after=pushed,
        )
        got_passed = send_down(other)
        advance(base)
        first, other = call(
            first_response_kernel,
            [fixed_f32, fixed_others],
            [d0, arrow, pushed, *got_pushed],
            wide,
            factor_bytes,
            after=sent,
        )
        got_first = send_down(other)
        solved, other = call(
            first_solve_kernel,
            [flat_f32, flat_others],
            [d0, value_rows, passed, *got_passed],
            wide,
            factor_bytes,
            after=first,
        )
        got_solved = send_down(other)
        advance(solved)
        last_base, last_resp, first_resp, noise_rows = call(
            turn_kernel,
            [node_f32, by_node, by_node, shape_of((width, fixed_rows), F32)],
            [base, response, first, noise_fixed, *got_first],
            wide // 2,
            factor_bytes,
            after=sent,
        )
        (first_base,) = call(
            turn_first_kernel, [node_f32], [solved, *got_solved], wide // 4, factor_bytes // 2, after=noise_rows
        )
        while left:
            advance(None)
        (mixed,) = call(
            mixed_kernel,
            [part_bf],
            [noise_rows, sent, *got],
            width * fixed_rows,
            8 * width * fixed_rows,
            after=first_base,
        )
        sample, fixed_out = call(
            lambda tip, a, b, c, d, *refs: final_kernel(tip, (a, b), (c, d), *refs),
            [shape_of((2, rows, columns), BF), shape_of((fixed_rows, width), F32)],
            [tip_inverse, first_base, last_base, first_resp, last_resp, mixed, *send_up(mixed)],
            4 * rows * fixed_rows * columns,
            factor_bytes,
            {("out", 0): pl.ANY},
            [
                pltpu.VMEM((columns, fixed_rows), BF),
                pltpu.VMEM((columns, fixed_rows), F32),
                pltpu.VMEM((2, rows, columns), BF),
                dma((2, tiles)),
            ],
        )
        return (sample, fixed_out)

    return on_device


def solution(mesh):
    sizes = dict(mesh.shape)

    def program(diag_inverse, coupling, arrow, tip_inverse, noise, noise_fixed, section_lengths):
        device = build(
            sizes["tm"],
            sizes["space"],
            diag_inverse.shape[1] // sizes["space"],
            noise.shape[2],
            arrow.shape[1],
        )
        return jax.shard_map(
            device,
            mesh=mesh,
            in_specs=(
                P("tm", "space", None),
                P("tm", "space", None),
                P("tm", None, "space"),
                P(),
                P("tm", "space", None),
                P(None, "space"),
                P(),
            ),
            out_specs=(P("tm", "space", None), P(None, "space")),
            check_vma=False,
        )(diag_inverse, coupling, arrow, tip_inverse, noise, noise_fixed, section_lengths)

    return program
```

time: 50.2 us -> 47.5 us (0.946)
  waiting for transfers between devices: 16 us -> 11 us
  Pallas kernels: 15.9 us -> 17.6 us
    ppermute x4, waiting for transfers between devices: 11.3 us -> 8.21 us  [swap_bit(): return lax.ppermute(value, 'tm', [(i, i ^ bit) for i in range(n_tm)])]
    ppermute x11, waiting for transfers between devices: 4.73 us -> 2.76 us  [swap(): return lax.ppermute(value, 'space', pairs)]
    pallas_call x11 -> x17, Pallas kernels: 15.9 us -> 17.6 us  [call(): pl.pallas_call(run, in_specs=specs, out_specs=[pl.BlockSpec(memory_space=...]
  transfers between devices with their start and end apart: 15 -> 15, of which waited for: 8 -> 6; matrix products, arithmetic and copies ran while one was open for 0% -> 0% of each run, Pallas kernels for 23% -> 23%
where the time goes in v4:
time: 47.5 us; the launch traced here: 47.3 us
  Pallas kernels  17.6 us (37%)
  starting transfers between devices  17.5 us (37%)
  waiting for transfers between devices  11 us (23%)
  between operations  0.8 us (2%)
    pallas_call x17, Pallas kernels, call(): pl.pallas_call(run, in_specs=specs, out_specs=[pl.BlockSpec(memory_space=...  17.6 us
    ppermute x4, starting transfers between devices, swap_bit(): return lax.ppermute(value, 'tm', [(i, i ^ bit) for i in range(n_tm)])  9.89 us
    ppermute x4, waiting for transfers between devices, swap_bit(): return lax.ppermute(value, 'tm', [(i, i ^ bit) for i in range(n_tm)])  8.21 us
    ppermute x11, starting transfers between devices, swap(): return lax.ppermute(value, 'space', pairs)  7.58 us
    ppermute x11, waiting for transfers between devices, swap(): return lax.ppermute(value, 'space', pairs)  2.76 us
  transfers between devices with their start and end apart: 15, of which 6 were waited for; matrix products, arithmetic and copies ran while one was open for 0% of the time, Pallas kernels for 23%

profile of v4, /device:TPU:0, one launch (start us, length us, event | category | flops | bytes accessed | tf_op | source)
XLA Modules:
  0.0 47.3 jit_solution(456292943668788120)
XLA Ops:
  0.6 0.5 %collective-permute-start = (bf16[2,1024,256]{2,1,0:T(8,128)(2,1)}, bf16[2,1024,256]{2,1,0:T(8,128)(2,1)S(1)}, u32[]{:S(2)}, u32[]{:S(2)}) collective-permute-start(bf16[2,1024,256]{2,1,0:T(8,128)(2,1)} %refs_3_.4), channel_id=1, source_target_pairs={{0,1},{1,0},{2,3},{3,2},{4,5},{5,4},{6,7},{7,6},{8,9},{9,8},{10,11... | collective-permute-start | bytes 3145736 | tf_op jit(solution)/shard_map/ppermute | solution.py:313
  1.1 3.7 %shard_map.86 = (bf16[1024,2048]{1,0:T(8,128)(2,1)S(1)}, bf16[1024,2048]{1,0:T(8,128)(2,1)S(1)}, f32[256,1024]{1,0:T(8,128)S(1)}, bf16[1,256,1024]{2,1,0:T(8,128...) custom-call(bf16[2,1024,2048]{2,1,0:T(8,128)(2,1)} %refs_0_.3, bf16[2,256,1024]{2,1,0:T(8,128)(2,1)} %refs_1_.5, ...), custom_call_target="tpu_custom_call" | custom-call | flops 1073741824 | bytes 8388608 | tf_op jit(solution)/shard_map/pallas_call | solution.py:73
  4.9 2.1 %collective-permute-start.2 = (bf16[256,1024]{1,0:T(8,128)(2,1)S(1)}, bf16[256,1024]{1,0:T(8,128)(2,1)S(1)}, u32[]{:S(2)}, u32[]{:S(2)}) collective-permute-start(bf16[256,1024]{1,0:T(8,128)(2,1)S(1)} %bitcast.12), channel_id=1, source_target_pairs={{0,1},{1,0},{2,3},{3,2},{4,5},{5,4},{6,7},{7,6},{8,9},{9,8},{10,11... | collective-permute-start | bytes 1572872 | tf_op jit(solution)/shard_map/ppermute | solution.py:313
  7.0 0.0 collective-permute-done.refs_2_
  7.0 0.1 shard_map.87
  7.1 0.8 %collective-permute-start.1 = (bf16[1024,256]{1,0:T(8,128)(2,1)S(1)}, bf16[1024,256]{1,0:T(8,128)(2,1)S(1)}, u32[]{:S(2)}, u32[]{:S(2)}) collective-permute-start(bf16[1024,256]{1,0:T(8,128)(2,1)S(1)} %get-tuple-element.37.refs_2_), channel_id=1, source_target_pairs={{0,1},{1,0},{2,3},{3,2},{4,5},{5,4},{6,7},{7,6},{8,9},{9,8},{10,11... | collective-permute-start | bytes 1572872 | tf_op jit(solution)/shard_map/ppermute | solution.py:313
  7.9 0.0 copy-start
  7.9 0.0 copy-start.1
  7.9 1.7 %shard_map.88 = (bf16[512,2048]{1,0:T(8,128)(2,1)S(1)}, f32[256,1024]{1,0:T(8,128)S(1)}) custom-call(bf16[2,1024,2048]{2,1,0:T(8,128)(2,1)} %refs_1_.4, f32[1024,256]{1,0:T(8,128)S(1)} %get-tuple-element.34.refs_1_), custom_call_target="tpu_custom_call" | custom-call | flops 134217728 | bytes 4194304 | tf_op jit(solution)/shard_map/pallas_call | solution.py:73
  9.6 0.0 collective-permute-done.2.refs_7_
  9.6 0.0 collective-permute-done.1.refs_6_
  9.6 0.1 copy-done
  9.8 0.3 copy-done.1
  10.1 3.0 %shard_map.89 = (bf16[512,2048]{1,0:T(8,128)(2,1)S(1)}, bf16[1024,256]{1,0:T(8,128)(2,1)S(1)}, f32[128,256]{1,0:T(8,128)S(1)}, bf16[1,128,256]{2,1,0:T(8,128)(2,1)S(1)}, bf16[256,1024]{1,0:T(8,128)(2,1)S(1)}) custom-call(bf16[512,2048]{1,0:T(8,128)(2,1)S(1)} %get-tuple-element.36.refs_0_, bf16[2,1024,2048]{2,1,0:T(8,128)(2,1)} %refs_1_.4, ...), custom_call_target="tpu_custom_call" | custom-call | flops 1073741824 | bytes 4194304 | tf_op jit(solution)/shard_map/pallas_call | solution.py:73
  13.1 0.1 collective-permute-start.3
  13.2 0.5 %collective-permute-start.4 = (bf16[128,256]{1,0:T(8,128)(2,1)S(1)}, bf16[128,256]{1,0:T(8,128)(2,1)S(1)}, u32[]{:S(2)}, u32[]{:S(2)}) collective-permute-start(bf16[128,256]{1,0:T(8,128)(2,1)S(1)} %bitcast.13), channel_id=1, source_target_pairs={{0,1},{1,0},{2,3},{3,2},{4,5},{5,4},{6,7},{7,6},{8,9},{9,8},{10,11... | collective-permute-start | bytes 196616 | tf_op jit(solution)/shard_map/ppermute | solution.py:313
  13.7 1.5 %collective-permute-done.4.refs_1_ = bf16[128,256]{1,0:T(8,128)(2,1)S(1)} collective-permute-done((bf16[128,256]{1,0:T(8,128)(2,1)S(1)}, bf16[128,256]{1,0:T(8,128)(2,1)S(1)}, u32[]{:S(2)}, u32[]{:S(2)}) %collective-permute-start.4) | collective-permute-done | bytes 65568 | tf_op jit(solution)/shard_map/ppermute | solution.py:313
  15.2 0.0 collective-permute-done.3.refs_2_
  15.2 1.3 %shard_map.91 = (f32[256,1024]{1,0:T(8,128)S(1)}, bf16[1,256,1024]{2,1,0:T(8,128)(2,1)S(1)}) custom-call(bf16[1024,2048]{1,0:T(8,128)(2,1)S(1)} %get-tuple-element.42.refs_0_, bf16[1024,256]{1,0:T(8,128)(2,1)S(1)} %get-tuple-element.43.refs_1_, bf16[1024,256]{1,0:T(8,128)(2,1)S(1)} %collective-permute-done.3.refs_2_, ...), custom_call_target="tpu_custom_call" | custom-call | flops 1610612736 | bytes 4194304 | tf_op jit(solution)/shard_map/pallas_call | solution.py:73
  16.5 1.6 %collective-permute-start.5 = (bf16[256,1024]{1,0:T(8,128)(2,1)S(1)}, bf16[256,1024]{1,0:T(8,128)(2,1)S(1)}, u32[]{:S(2)}, u32[]{:S(2)}) collective-permute-start(bf16[256,1024]{1,0:T(8,128)(2,1)S(1)} %bitcast.11), channel_id=1, source_target_pairs={{0,1},{1,0},{2,3},{3,2},{4,5},{5,4},{6,7},{7,6},{8,9},{9,8},{10,11... | collective-permute-start | bytes 1572872 | tf_op jit(solution)/shard_map/ppermute | solution.py:313
  18.1 2.9 %collective-permute-start.6 = (bf16[128,256]{1,0:T(8,128)(2,1)S(1)}, bf16[128,256]{1,0:T(8,128)(2,1)S(1)}, u32[]{:S(2)}, u32[]{:S(2)}) collective-permute-start(bf16[128,256]{1,0:T(8,128)(2,1)S(1)} %shard_map.90.refs_3_.refs_0_), channel_id=1, source_target_pairs={{0,2},{2,0},{4,6},{6,4},{8,10},{10,8},{12,14},{14,12},{16,18},{18,... | collective-permute-start | bytes 196616 | tf_op jit(solution)/shard_map/ppermute | solution.py:342
  21.0 2.3 %collective-permute-done.6.refs_1_ = bf16[128,256]{1,0:T(8,128)(2,1)S(1)} collective-permute-done((bf16[128,256]{1,0:T(8,128)(2,1)S(1)}, bf16[128,256]{1,0:T(8,128)(2,1)S(1)}, u32[]{:S(2)}, u32[]{:S(2)}) %collective-permute-start.6) | collective-permute-done | bytes 65568 | tf_op jit(solution)/shard_map/ppermute | solution.py:342
  23.4 1.3 %shard_map.93 = (f32[256,1024]{1,0:T(8,128)S(1)}, bf16[1,256,1024]{2,1,0:T(8,128)(2,1)S(1)}) custom-call(bf16[512,2048]{1,0:T(8,128)(2,1)S(1)} %get-tuple-element.36.refs_0_, bf16[512,2048]{1,0:T(8,128)(2,1)S(1)} %get-tuple-element.40.refs_1_, bf16[256,1024]{1,0:T(8,128)(2,1)S(1)} %get-tuple-element.48.refs_2_.refs_1_, ...), custom_call_target="tpu_custom_call" | custom-call | flops 1073741824 | bytes 4194304 | tf_op jit(solution)/shard_map/pallas_call | solution.py:73
  24.6 0.1 collective-permute-start.8
  24.7 0.0 collective-permute-done.5.refs_4_
  24.7 1.3 %shard_map.94 = (f32[256,1024]{1,0:T(8,128)S(1)}, f32[256,1024]{1,0:T(8,128)S(1)}, bf16[1,256,1024]{2,1,0:T(8,128)(2,1)S(1)}) custom-call(bf16[512,2048]{1,0:T(8,128)(2,1)S(1)} %get-tuple-element.36.refs_0_, bf16[512,2048]{1,0:T(8,128)(2,1)S(1)} %get-tuple-element.40.refs_1_, f32[8,128]{1,0:T(8,128)S(1)} %get-tuple-element.41.refs_2_, ...), custom_call_target="tpu_custom_call" | custom-call | flops 1073741824 | bytes 4194304 | tf_op jit(solution)/shard_map/pallas_call | solution.py:73
  26.1 0.6 %collective-permute-start.7 = (bf16[256,1024]{1,0:T(8,128)(2,1)S(1)}, bf16[256,1024]{1,0:T(8,128)(2,1)S(1)}, u32[]{:S(2)}, u32[]{:S(2)}) collective-permute-start(bf16[256,1024]{1,0:T(8,128)(2,1)S(1)} %bitcast.9), channel_id=1, source_target_pairs={{0,1},{1,0},{2,3},{3,2},{4,5},{5,4},{6,7},{7,6},{8,9},{9,8},{10,11... | collective-permute-start | bytes 1572872 | tf_op jit(solution)/shard_map/ppermute | solution.py:313
  26.6 2.0 %collective-permute-start.9 = (bf16[128,256]{1,0:T(8,128)(2,1)S(1)}, bf16[128,256]{1,0:T(8,128)(2,1)S(1)}, u32[]{:S(2)}, u32[]{:S(2)}) collective-permute-start(bf16[128,256]{1,0:T(8,128)(2,1)S(1)} %shard_map.92.refs_3_.refs_0_), channel_id=1, source_target_pairs={{0,4},{2,6},{4,0},{6,2},{8,12},{10,14},{12,8},{14,10},{16,20},{18,... | collective-permute-start | bytes 196616 | tf_op jit(solution)/shard_map/ppermute | solution.py:342
  28.6 2.3 %collective-permute-done.9.refs_1_ = bf16[128,256]{1,0:T(8,128)(2,1)S(1)} collective-permute-done((bf16[128,256]{1,0:T(8,128)(2,1)S(1)}, bf16[128,256]{1,0:T(8,128)(2,1)S(1)}, u32[]{:S(2)}, u32[]{:S(2)}) %collective-permute-start.9) | collective-permute-done | bytes 65568 | tf_op jit(solution)/shard_map/ppermute | solution.py:342
  30.9 0.0 collective-permute-done.8.refs_3_
  30.9 0.9 %shard_map.96 = (f32[256,1024]{1,0:T(8,128)S(1)}, bf16[1,256,1024]{2,1,0:T(8,128)(2,1)S(1)}) custom-call(bf16[1024,2048]{1,0:T(8,128)(2,1)S(1)} %get-tuple-element.32.refs_0_, bf16[2,256,1024]{2,1,0:T(8,128)(2,1)S(1)} %copy-done, f32[256,1024]{1,0:T(8,128)S(1)} %get-tuple-element.49.refs_5_.refs_2_, bf16[256,1024]{1,0:T(8,128)(2,1)S(1)} %collective-permute-done.8.refs_3_, ...), custom_call_target="tpu_custom_call" | custom-call | flops 1073741824 | bytes 4194304 | tf_op jit(solution)/shard_map/pallas_call | solution.py:73
  31.9 0.2 collective-permute-start.11
  32.1 0.0 collective-permute-done.7.refs_3_
  32.1 0.0 copy-start.2
  32.1 0.9 %shard_map.97 = (f32[256,1024]{1,0:T(8,128)S(1)}, bf16[1,256,1024]{2,1,0:T(8,128)(2,1)S(1)}) custom-call(bf16[1024,2048]{1,0:T(8,128)(2,1)S(1)} %get-tuple-element.32.refs_0_, f32[256,1024]{1,0:T(8,128)S(1)} %get-tuple-element.35.refs_1_, f32[256,1024]{1,0:T(8,128)S(1)} %get-tuple-element.50.refs_2_, bf16[256,1024]{1,0:T(8,128)(2,1)S(1)} %collective-permute-done.7.refs_3_, ...), custom_call_target="tpu_custom_call" | custom-call | flops 1073741824 | bytes 4194304 | tf_op jit(solution)/shard_map/pallas_call | solution.py:73
  33.0 1.1 %collective-permute-start.10 = (bf16[256,1024]{1,0:T(8,128)(2,1)S(1)}, bf16[256,1024]{1,0:T(8,128)(2,1)S(1)}, u32[]{:S(2)}, u32[]{:S(2)}) collective-permute-start(bf16[256,1024]{1,0:T(8,128)(2,1)S(1)} %bitcast.8), channel_id=1, source_target_pairs={{0,1},{1,0},{2,3},{3,2},{4,5},{5,4},{6,7},{7,6},{8,9},{9,8},{10,11... | collective-permute-start | bytes 1572872 | tf_op jit(solution)/shard_map/ppermute | solution.py:313
  34.1 2.0 %collective-permute-start.12 = (bf16[128,256]{1,0:T(8,128)(2,1)S(1)}, bf16[128,256]{1,0:T(8,128)(2,1)S(1)}, u32[]{:S(2)}, u32[]{:S(2)}) collective-permute-start(bf16[128,256]{1,0:T(8,128)(2,1)S(1)} %shard_map.95.refs_4_.refs_0_), channel_id=1, source_target_pairs={{0,8},{2,10},{4,12},{6,14},{8,0},{10,2},{12,4},{14,6},{16,24},{18,... | collective-permute-start | bytes 196616 | tf_op jit(solution)/shard_map/ppermute | solution.py:342
  36.1 2.3 %collective-permute-done.12.refs_1_ = bf16[128,256]{1,0:T(8,128)(2,1)S(1)} collective-permute-done((bf16[128,256]{1,0:T(8,128)(2,1)S(1)}, bf16[128,256]{1,0:T(8,128)(2,1)S(1)}, u32[]{:S(2)}, u32[]{:S(2)}) %collective-permute-start.12) | collective-permute-done | bytes 65568 | tf_op jit(solution)/shard_map/ppermute | solution.py:342
  38.4 0.0 copy-start.3
  38.4 3.0 %collective-permute-start.13 = (bf16[128,256]{1,0:T(8,128)(2,1)S(1)}, bf16[128,256]{1,0:T(8,128)(2,1)S(1)}, u32[]{:S(2)}, u32[]{:S(2)}) collective-permute-start(bf16[128,256]{1,0:T(8,128)(2,1)S(1)} %shard_map.98.refs_5_.refs_1_), channel_id=1, source_target_pairs={{0,16},{2,18},{4,20},{6,22},{8,24},{10,26},{12,28},{14,30},{16,0},... | collective-permute-start | bytes 196616 | tf_op jit(solution)/shard_map/ppermute | solution.py:342
  41.5 0.0 collective-permute-done.11.refs_4_
  41.5 0.0 copy-done.2
  41.5 0.7 %shard_map.99 = (f32[1024,256]{1,0:T(8,128)S(1)}, bf16[1024,256]{1,0:T(8,128)(2,1)S(1)}, bf16[1024,256]{1,0:T(8,128)(2,1)S(1)}, f32[128,256]{1,0:T(8,128)S(1)}) custom-call(f32[256,1024]{1,0:T(8,128)S(1)} %get-tuple-element.53.refs_2_.refs_0_, bf16[256,1024]{1,0:T(8,128)(2,1)S(1)} %get-tuple-element.48.refs_2_.refs_1_, ...), custom_call_target="tpu_custom_call" | custom-call | flops 536870912 | bytes 4194304 | tf_op jit(solution)/shard_map/pallas_call | solution.py:73
  42.1 0.0 collective-permute-done.10.refs_1_
  42.2 0.3 shard_map.100.refs_3_.refs_1_
  42.5 1.2 %collective-permute-done.13.refs_2_ = bf16[128,256]{1,0:T(8,128)(2,1)S(1)} collective-permute-done((bf16[128,256]{1,0:T(8,128)(2,1)S(1)}, bf16[128,256]{1,0:T(8,128)(2,1)S(1)}, u32[]{:S(2)}, u32[]{:S(2)}) %collective-permute-start.13) | collective-permute-done | bytes 65568 | tf_op jit(solution)/shard_map/ppermute | solution.py:342
  43.7 0.1 collective-permute-start.14
  43.8 1.2 %collective-permute-done.14.refs_6_ = bf16[128,256]{1,0:T(8,128)(2,1)S(1)} collective-permute-done((bf16[128,256]{1,0:T(8,128)(2,1)S(1)}, bf16[128,256]{1,0:T(8,128)(2,1)S(1)}, u32[]{:S(2)}, u32[]{:S(2)}) %collective-permute-start.14) | collective-permute-done | bytes 65568 | tf_op jit(solution)/shard_map/ppermute | solution.py:313
  45.0 0.0 copy-done.3
  45.1 2.2 %shard_map.102 = (bf16[2,1024,256]{2,1,0:T(8,128)(2,1)}, f32[256,128]{1,0:T(8,128)}) custom-call(bf16[256,256]{1,0:T(8,128)(2,1)S(1)} %copy-done.3, f32[1024,256]{1,0:T(8,128)S(1)} %shard_map.100.refs_3_.refs_1_, f32[1024,256]{1,0:T(8,128)S(1)} %get-tuple-element.59.refs_2_, bf16[1024,256]{1,0:T(8,128)(2,1)S(1)} %get-tuple-element.60.refs_3_, ...), custom_call_target="tpu_custom_call" | custom-call | flops 268435456 | bytes 4194304 | tf_op jit(solution)/shard_map/pallas_call | solution.py:73
  (5 shorter events, 0.1 us)
Async XLA Ops:
  0.6 6.3 %collective-permute-start = (bf16[2,1024,256]{2,1,0:T(8,128)(2,1)}, bf16[2,1024,256]{2,1,0:T(8,128)(2,1)S(1)}, u32[]{:S(2)}, u32[]{:S(2)}) collective-permute-start(bf16[2,1024,256]{2,1,0:T(8,128)(2,1)} %refs_3_.4), channel_id=1, source_target_pairs={{0,1},{1,0},{2,3},{3,2},{4,5},{5,4},{6,7},{7,6},{8,9},{9,8},{10,11... | collective-permute-start | bytes 3145736 | tf_op jit(solution)/shard_map/ppermute | solution.py:313
  4.9 4.7 %collective-permute-start.2 = (bf16[256,1024]{1,0:T(8,128)(2,1)S(1)}, bf16[256,1024]{1,0:T(8,128)(2,1)S(1)}, u32[]{:S(2)}, u32[]{:S(2)}) collective-permute-start(bf16[256,1024]{1,0:T(8,128)(2,1)S(1)} %bitcast.12), channel_id=1, source_target_pairs={{0,1},{1,0},{2,3},{3,2},{4,5},{5,4},{6,7},{7,6},{8,9},{9,8},{10,11... | collective-permute-start | bytes 1572872 | tf_op jit(solution)/shard_map/ppermute | solution.py:313
  7.1 2.5 %collective-permute-start.1 = (bf16[1024,256]{1,0:T(8,128)(2,1)S(1)}, bf16[1024,256]{1,0:T(8,128)(2,1)S(1)}, u32[]{:S(2)}, u32[]{:S(2)}) collective-permute-start(bf16[1024,256]{1,0:T(8,128)(2,1)S(1)} %get-tuple-element.37.refs_2_), channel_id=1, source_target_pairs={{0,1},{1,0},{2,3},{3,2},{4,5},{5,4},{6,7},{7,6},{8,9},{9,8},{10,11... | collective-permute-start | bytes 1572872 | tf_op jit(solution)/shard_map/ppermute | solution.py:313
  7.9 1.9 %copy-start = (bf16[2,256,1024]{2,1,0:T(8,128)(2,1)S(1)}, bf16[2,256,1024]{2,1,0:T(8,128)(2,1)}, u32[]{:S(2)}) copy-start(bf16[2,256,1024]{2,1,0:T(8,128)(2,1)} %refs_1_.5) | copy-start | bytes 3145732
  7.9 2.2 %copy-start.1 = (bf16[2,1024,256]{2,1,0:T(8,128)(2,1)S(1)}, bf16[2,1024,256]{2,1,0:T(8,128)(2,1)}, u32[]{:S(2)}) copy-start(bf16[2,1024,256]{2,1,0:T(8,128)(2,1)} %refs_3_.4) | copy-start | bytes 3145732
  13.1 2.1 %collective-permute-start.3 = (bf16[1024,256]{1,0:T(8,128)(2,1)S(1)}, bf16[1024,256]{1,0:T(8,128)(2,1)S(1)}, u32[]{:S(2)}, u32[]{:S(2)}) collective-permute-start(bf16[1024,256]{1,0:T(8,128)(2,1)S(1)} %get-tuple-element.43.refs_1_), channel_id=1, source_target_pairs={{0,1},{1,0},{2,3},{3,2},{4,5},{5,4},{6,7},{7,6},{8,9},{9,8},{10,11... | collective-permute-start | bytes 1572872 | tf_op jit(solution)/shard_map/ppermute | solution.py:313
  13.2 2.0 %collective-permute-start.4 = (bf16[128,256]{1,0:T(8,128)(2,1)S(1)}, bf16[128,256]{1,0:T(8,128)(2,1)S(1)}, u32[]{:S(2)}, u32[]{:S(2)}) collective-permute-start(bf16[128,256]{1,0:T(8,128)(2,1)S(1)} %bitcast.13), channel_id=1, source_target_pairs={{0,1},{1,0},{2,3},{3,2},{4,5},{5,4},{6,7},{7,6},{8,9},{9,8},{10,11... | collective-permute-start | bytes 196616 | tf_op jit(solution)/shard_map/ppermute | solution.py:313
  16.5 8.2 %collective-permute-start.5 = (bf16[256,1024]{1,0:T(8,128)(2,1)S(1)}, bf16[256,1024]{1,0:T(8,128)(2,1)S(1)}, u32[]{:S(2)}, u32[]{:S(2)}) collective-permute-start(bf16[256,1024]{1,0:T(8,128)(2,1)S(1)} %bitcast.11), channel_id=1, source_target_pairs={{0,1},{1,0},{2,3},{3,2},{4,5},{5,4},{6,7},{7,6},{8,9},{9,8},{10,11... | collective-permute-start | bytes 1572872 | tf_op jit(solution)/shard_map/ppermute | solution.py:313
  18.1 5.3 %collective-permute-start.6 = (bf16[128,256]{1,0:T(8,128)(2,1)S(1)}, bf16[128,256]{1,0:T(8,128)(2,1)S(1)}, u32[]{:S(2)}, u32[]{:S(2)}) collective-permute-start(bf16[128,256]{1,0:T(8,128)(2,1)S(1)} %shard_map.90.refs_3_.refs_0_), channel_id=1, source_target_pairs={{0,2},{2,0},{4,6},{6,4},{8,10},{10,8},{12,14},{14,12},{16,18},{18,... | collective-permute-start | bytes 196616 | tf_op jit(solution)/shard_map/ppermute | solution.py:342
  24.6 6.3 %collective-permute-start.8 = (bf16[256,1024]{1,0:T(8,128)(2,1)S(1)}, bf16[256,1024]{1,0:T(8,128)(2,1)S(1)}, u32[]{:S(2)}, u32[]{:S(2)}) collective-permute-start(bf16[256,1024]{1,0:T(8,128)(2,1)S(1)} %bitcast.10), channel_id=1, source_target_pairs={{0,1},{1,0},{2,3},{3,2},{4,5},{5,4},{6,7},{7,6},{8,9},{9,8},{10,11... | collective-permute-start | bytes 1572872 | tf_op jit(solution)/shard_map/ppermute | solution.py:313
  26.1 6.1 %collective-permute-start.7 = (bf16[256,1024]{1,0:T(8,128)(2,1)S(1)}, bf16[256,1024]{1,0:T(8,128)(2,1)S(1)}, u32[]{:S(2)}, u32[]{:S(2)}) collective-permute-start(bf16[256,1024]{1,0:T(8,128)(2,1)S(1)} %bitcast.9), channel_id=1, source_target_pairs={{0,1},{1,0},{2,3},{3,2},{4,5},{5,4},{6,7},{7,6},{8,9},{9,8},{10,11... | collective-permute-start | bytes 1572872 | tf_op jit(solution)/shard_map/ppermute | solution.py:313
  26.6 4.3 %collective-permute-start.9 = (bf16[128,256]{1,0:T(8,128)(2,1)S(1)}, bf16[128,256]{1,0:T(8,128)(2,1)S(1)}, u32[]{:S(2)}, u32[]{:S(2)}) collective-permute-start(bf16[128,256]{1,0:T(8,128)(2,1)S(1)} %shard_map.92.refs_3_.refs_0_), channel_id=1, source_target_pairs={{0,4},{2,6},{4,0},{6,2},{8,12},{10,14},{12,8},{14,10},{16,20},{18,... | collective-permute-start | bytes 196616 | tf_op jit(solution)/shard_map/ppermute | solution.py:342
  31.9 9.6 %collective-permute-start.11 = (bf16[256,1024]{1,0:T(8,128)(2,1)S(1)}, bf16[256,1024]{1,0:T(8,128)(2,1)S(1)}, u32[]{:S(2)}, u32[]{:S(2)}) collective-permute-start(bf16[256,1024]{1,0:T(8,128)(2,1)S(1)} %bitcast.7), channel_id=1, source_target_pairs={{0,1},{1,0},{2,3},{3,2},{4,5},{5,4},{6,7},{7,6},{8,9},{9,8},{10,11... | collective-permute-start | bytes 1572872 | tf_op jit(solution)/shard_map/ppermute | solution.py:313
  32.1 9.3 %copy-start.2 = (f32[256,128]{1,0:T(8,128)S(1)}, f32[256,128]{1,0:T(8,128)}, u32[]{:S(2)}) copy-start(f32[256,128]{1,0:T(8,128)} %refs_3_.5) | copy-start | bytes 393220
  33.0 9.1 %collective-permute-start.10 = (bf16[256,1024]{1,0:T(8,128)(2,1)S(1)}, bf16[256,1024]{1,0:T(8,128)(2,1)S(1)}, u32[]{:S(2)}, u32[]{:S(2)}) collective-permute-start(bf16[256,1024]{1,0:T(8,128)(2,1)S(1)} %bitcast.8), channel_id=1, source_target_pairs={{0,1},{1,0},{2,3},{3,2},{4,5},{5,4},{6,7},{7,6},{8,9},{9,8},{10,11... | collective-permute-start | bytes 1572872 | tf_op jit(solution)/shard_map/ppermute | solution.py:313
  34.1 4.3 %collective-permute-start.12 = (bf16[128,256]{1,0:T(8,128)(2,1)S(1)}, bf16[128,256]{1,0:T(8,128)(2,1)S(1)}, u32[]{:S(2)}, u32[]{:S(2)}) collective-permute-start(bf16[128,256]{1,0:T(8,128)(2,1)S(1)} %shard_map.95.refs_4_.refs_0_), channel_id=1, source_target_pairs={{0,8},{2,10},{4,12},{6,14},{8,0},{10,2},{12,4},{14,6},{16,24},{18,... | collective-permute-start | bytes 196616 | tf_op jit(solution)/shard_map/ppermute | solution.py:342
  38.4 6.6 %copy-start.3 = (bf16[256,256]{1,0:T(8,128)(2,1)S(1)}, bf16[256,256]{1,0:T(8,128)(2,1)}, u32[]{:S(2)}) copy-start(bf16[256,256]{1,0:T(8,128)(2,1)} %refs_0_.5) | copy-start | bytes 393220
  38.4 5.3 %collective-permute-start.13 = (bf16[128,256]{1,0:T(8,128)(2,1)S(1)}, bf16[128,256]{1,0:T(8,128)(2,1)S(1)}, u32[]{:S(2)}, u32[]{:S(2)}) collective-permute-start(bf16[128,256]{1,0:T(8,128)(2,1)S(1)} %shard_map.98.refs_5_.refs_1_), channel_id=1, source_target_pairs={{0,16},{2,18},{4,20},{6,22},{8,24},{10,26},{12,28},{14,30},{16,0},... | collective-permute-start | bytes 196616 | tf_op jit(solution)/shard_map/ppermute | solution.py:342
  43.7 1.3 %collective-permute-start.14 = (bf16[128,256]{1,0:T(8,128)(2,1)S(1)}, bf16[128,256]{1,0:T(8,128)(2,1)S(1)}, u32[]{:S(2)}, u32[]{:S(2)}) collective-permute-start(bf16[128,256]{1,0:T(8,128)(2,1)S(1)} %shard_map.101.refs_5_), channel_id=1, source_target_pairs={{0,1},{1,0},{2,3},{3,2},{4,5},{5,4},{6,7},{7,6},{8,9},{9,8},{10,11... | collective-permute-start | bytes 196616 | tf_op jit(solution)/shard_map/ppermute | solution.py:313

commit v5 on v4

--- a/solution.py
+++ b/solution.py
@@ -37,7 +37,7 @@
     nodes = n_space * rows
     tile = 256 if rows % 256 == 0 else rows
     tiles = rows // tile
-    half = rows // 2
+    quarter = rows // 4
     width = columns // n_space
     peers = range(1, n_space)
 
@@ -52,7 +52,7 @@
         owner = lax.rem(at_core() - step + n_space, n_space)
         return pl.ds(pl.multiple_of(owner * width, width), width)
 
-    def call(body, outs, args, flops, moved, places=None, scratch=(), after=None):
+    def call(body, outs, args, flops, moved, places=None, scratch=(), after=None, aliases=None):
         places = dict(places or {})
         args = list(args)
         count = len(args)
@@ -79,7 +79,10 @@
             ],
             out_shape=outs,
             scratch_shapes=list(scratch),
-            cost_estimate=pl.CostEstimate(flops=flops, bytes_accessed=moved, transcendentals=0),
+            input_output_aliases=aliases or {},
+            cost_estimate=pl.CostEstimate(
+                flops=8 * flops, bytes_accessed=8 * moved, transcendentals=0
+            ),
             compiler_params=pltpu.CompilerParams(vmem_limit_bytes=16 * MIB),
         )(*args)
 
@@ -98,10 +101,11 @@
             at = j * tile
             own_ref[:, at : at + tile] = dot(left[:, at:], factor[at:, block(0, at, tile)])
 
-    def full_rows(left, low, high, own_ref, other_ref):
+    def full_rows(left, factor, tail, own_ref, other_ref):
+        at = rows - quarter
         for step in (*peers, 0):
-            product = dot(left[:, :half], low[:, block(step)])
-            product = product + dot(left[:, half:], high[:, block(step)])
+            product = dot(left[:, :at], factor[:at, block(step)])
+            product = product + dot(left[:, at:], tail[:, block(step)])
             if step:
                 other_ref[step - 1] = product.astype(BF)
             else:
@@ -144,29 +148,29 @@
                     )
             return copies
 
-        def each(copies, act):
-            for i in range(tiles):
-                act(copies[0, i])
+        def each(copies, i, act):
+            act(copies[0, i])
             for step in peers:
 
                 @pl.when(at_core() >= step)
                 def _():
-                    for i in range(tiles):
-                        act(copies[step, i])
+                    act(copies[step, i])
 
         copies1 = lower_copies(1, d1, sem1)
         copies0 = lower_copies(0, d0, sem0)
         live_copy.start()
         arrow_copy.start()
-        each(copies1, lambda copy: copy.start())
+        for i in range(tiles):
+            each(copies1, i, lambda copy: copy.start())
         noise_copy.start()
-        each(copies0, lambda copy: copy.start())
         live_copy.wait()
         arrow_copy.wait()
         live = live_scratch[lax.axis_index("tm")] > 1
         mask[...] = jnp.where(live, jnp.ones_like(mask[...]), jnp.zeros_like(mask[...]))
         e1[...] = jnp.where(live, e1[...], jnp.zeros_like(e1[...]))
-        each(copies1, lambda copy: copy.wait())
+        for i in range(tiles):
+            each(copies1, i, lambda copy: copy.wait())
+            each(copies0, i, lambda copy: copy.start())
         lower_rows(e1, d1, own, other)
         noise_copy.wait()
         lower_own(d0, n0, first, lambda i: copies0[0, i].wait())
@@ -177,58 +181,56 @@
                 for i in range(tiles):
                     copies0[step, i].wait()
 
-    def first_value_kernel(d0, value, *refs):
-        got, (out, bar) = refs[: n_space - 1], refs[n_space - 1 :]
+    def k1_copies(coupling, k1, quarters, sems):
+        copies = {}
+        for i, q in enumerate(quarters):
+            part = pl.ds(q * quarter, quarter)
+            target = k1.at[part] if k1.shape[0] == rows else k1
+            copies[q] = pltpu.make_async_copy(coupling.at[1, part], target, sems.at[i])
+        return copies
+
+    def first_value_kernel(d0, value, coupling, *refs):
+        got, (out, bar, k1, sems) = refs[: n_space - 1], refs[n_space - 1 :]
+        copies = k1_copies(coupling, k1, [0], sems)
+        copies[0].start()
         out[...] = value[...]
         lower_rest(d0, [piece.at[0] for piece in got], out)
         bar[...] = out[...].astype(BF)
-
-    def load_kernel(coupling, value, low, value_rows, sems):
-        copies = []
-        for i in range(2):
-            size = half // 2
-            copies.append(
-                pltpu.make_async_copy(
-                    coupling.at[1, pl.ds(i * size, size)], low.at[pl.ds(i * size, size)], sems.at[i]
-                )
-            )
-            copies[i].start()
+        copies[0].wait()
+
+    def load_kernel(coupling, value, _, value_rows, k1, sems):
+        copies = k1_copies(coupling, k1, [1, 2], sems)
+        for copy in copies.values():
+            copy.start()
         value_rows[...] = value[...].T
-        for copy in copies:
+        for copy in copies.values():
             copy.wait()
 
-    def target_kernel(low, coupling, bar, noise, arrow, own, *refs):
+    def target_kernel(k1, coupling, bar, noise, arrow, own, *refs):
         got, refs = refs[: n_space - 1], refs[n_space - 1 :]
         got_own, refs = refs[: n_space - 1], refs[n_space - 1 :]
-        high, target, part_own, part_other, response, whole, sems = refs
-        size = half // 2
-        copies = []
-        for i in range(2):
-            copies.append(
-                pltpu.make_async_copy(
-                    coupling.at[1, pl.ds(half + i * size, size)],
-                    high.at[pl.ds(i * size, size)],
-                    sems.at[i],
-                )
-            )
-            copies[i].start()
+        tail, target, part_own, part_other, response, e0, n1, whole, sems = refs
+        noise_copy = pltpu.make_async_copy(noise.at[1], n1, sems.at[1])
+        arrow_copy = pltpu.make_async_copy(arrow.at[0], e0, sems.at[2])
+        copies = k1_copies(coupling, tail, [3], sems)
+        noise_copy.start()
+        copies[3].start()
+        arrow_copy.start()
         response[...] = total_of(own, got_own).astype(BF)
-        whole[...] = dot(arrow[0], bar[...])
-        pieces = [bar, *got]
         for i in range(4):
-            if i >= 2:
-                copies[i - 2].wait()
-            factor = low if i < 2 else high
-            inner = (i % 2) * size
-            pulled = dot(factor[inner : inner + size, block(0)], bar[...])
+            at = i * quarter
+            if i in copies:
+                copies[i].wait()
+            factor = tail if i == 3 else k1.at[at : at + quarter]
+            pulled = dot(factor[:, block(0)], bar[...])
             for step in peers:
-                pulled = pulled + dot(
-                    factor[inner : inner + size, block(step)], pieces[step][...]
-                )
-            at = i * size
-            source = noise[1, at : at + size].astype(F32)
-            target[at : at + size] = (source - pulled).astype(BF)
-        whole[...] = (whole[...] + dot(response[...], target[...])).T
+                pulled = pulled + dot(factor[:, block(step)], got[step - 1][...])
+            if i == 0:
+                noise_copy.wait()
+            source = n1[at : at + quarter].astype(F32)
+            target[at : at + quarter] = (source - pulled).astype(BF)
+        arrow_copy.wait()
+        whole[...] = (dot(e0[...], bar[...]) + dot(response[...], target[...])).T
         part_own[...] = whole[part_rows(0)]
         for step in peers:
             part_other[step - 1] = whole[part_rows(step)].astype(BF)
@@ -249,18 +251,18 @@
         lower_rest(d1, got, value)
         lower_rows(value[...].T.astype(BF), d1, own, other)
 
-    def response_kernel(low, high, response, own, other):
-        full_rows(response, low, high, own, other)
-
-    def pass_kernel(low, high, mask, solved, *refs):
+    def response_kernel(k1, tail, response, own, other):
+        full_rows(response, k1, tail, own, other)
+
+    def pass_kernel(k1, tail, mask, solved, *refs):
         got, (base, own, other) = refs[: n_space - 1], refs[n_space - 1 :]
         value = jnp.where(mask[:1, :1] > 0, total_of(solved, got), 0.0)
         base[...] = value
-        full_rows(value.astype(BF), low, high, own, other)
-
-    def first_response_kernel(d0, arrow, pushed, *refs):
+        full_rows(value.astype(BF), k1, tail, own, other)
+
+    def first_response_kernel(d0, e0, pushed, *refs):
         got, (own, other) = refs[: n_space - 1], refs[n_space - 1 :]
-        left = (arrow[0].astype(F32) - total_of(pushed, got)).astype(BF)
+        left = (e0[...].astype(F32) - total_of(pushed, got)).astype(BF)
         lower_rows(left, d0, own, other)
 
     def first_solve_kernel(d0, value_rows, passed, *refs):
@@ -268,12 +270,18 @@
         left = (value_rows[...] - total_of(passed, got)).astype(BF)
         lower_rows(left, d0, own, other)
 
-    def turn_kernel(base, response, first, noise_fixed, *refs):
+    def turn_kernel(base, response, first, noise_fixed, tip, *refs):
         got, (last_base, last_resp, first_resp, noise_rows) = refs[: n_space - 1], refs[n_space - 1 :]
         noise_rows[...] = noise_fixed[...].T
         last_base[...] = base[...].T
-        last_resp[...] = response[...].astype(F32).T.astype(BF)
-        first_resp[...] = total_of(first, got).T.astype(BF)
+        upper = tip[...].astype(F32).T.astype(BF)
+
+        def through_tip(right):
+            inner = dot(tip[...], right).astype(BF)
+            return dot(upper, inner).T.astype(BF)
+
+        last_resp[...] = through_tip(response[...])
+        first_resp[...] = through_tip(total_of(first, got).astype(BF))
 
     def turn_first_kernel(solved, *refs):
         got, out = refs[:-1], refs[-1]
@@ -287,24 +295,22 @@
         out[...] = (noise_rows[...] - total).astype(BF)
 
     def final_kernel(tip, bases, responses, mixed, *refs):
-        got, (out, fixed_out, whole, fixed, result, sems) = refs[: n_space - 1], refs[n_space - 1 :]
+        got, (out, fixed_out, whole, result, sems) = refs[: n_space - 1], refs[n_space - 1 :]
         for step, piece in enumerate([mixed, *got]):
             whole[part_rows(step)] = piece[...]
-        forward = dot_last(whole[...], tip[...])
-        fixed[...] = dot(forward.astype(BF), tip[...])
-        bar = fixed[...].astype(BF)
         copies = []
         for slot in range(2):
             for i in range(tiles):
                 at = i * tile
                 part = (slot, pl.ds(at, tile))
-                update = dot_last(responses[slot][at : at + tile], bar)
+                update = dot_last(responses[slot][at : at + tile], whole[...])
                 result[part] = (bases[slot][at : at + tile] - update).astype(BF)
                 copies.append(
                     pltpu.make_async_copy(result.at[part], out.at[part], sems.at[slot, i])
                 )
                 copies[-1].start()
-        fixed_out[...] = fixed[part_rows(0)].T
+        forward = dot_last(mixed[...], tip[...])
+        fixed_out[...] = dot(forward.astype(BF), tip[...]).T
         for copy in copies:
             copy.wait()
 
@@ -331,7 +337,7 @@
     fixed_others = shape_of((n_space - 1, fixed_rows, rows), BF)
     part_bf = shape_of((width, fixed_rows), BF)
     by_node = shape_of((rows, fixed_rows), BF)
-    in_vmem, half_vmem = pltpu.VMEM((rows, nodes), BF), pltpu.VMEM((half, nodes), BF)
+    in_vmem = pltpu.VMEM((rows, nodes), BF)
     dma = pltpu.SemaphoreType.DMA
 
     def fold(sent, got, after):
@@ -360,33 +366,45 @@
             ],
         )
         got_response = send_down(other)
-        value, bar = call(
-            first_value_kernel, [node_f32, node_bf], [d0, value, *got_noise], wide // 2, factor_bytes
+        value, bar, k1 = call(
+            first_value_kernel,
+            [node_f32, node_bf, in_vmem],
+            [d0, value, coupling, *got_noise],
+            wide // 2,
+            factor_bytes,
+            {2: pltpu.HBM},
+            [dma((1,))],
         )
         got_bar = send_up(bar)
-        low, value_rows = call(
+        value_rows, k1 = call(
             load_kernel,
-            [half_vmem, flat_f32],
-            [coupling, value],
+            [flat_f32, in_vmem],
+            [coupling, value, k1],
             wide // 8,
             factor_bytes,
-            {0: pltpu.HBM},
+            {0: pltpu.HBM, 2: pl.ANY, ("out", 1): pl.ANY},
             [dma((2,))],
-        )
-        high, target, part_own, part_other, response = call(
+            aliases={2: 1},
+        )
+        tail, target, part_own, part_other, response, e0 = call(
             target_kernel,
             [
-                half_vmem,
+                pltpu.VMEM((quarter, nodes), BF),
                 node_bf,
                 shape_of((width, fixed_rows), F32),
                 shape_of((n_space - 1, width, fixed_rows), BF),
                 fixed_bf,
+                fixed_bf,
             ],
-            [low, coupling, bar, noise, arrow, own, *got_bar, *got_response],
+            [k1, coupling, bar, noise, arrow, own, *got_bar, *got_response],
             wide,
             factor_bytes,
-            {1: pltpu.HBM},
-            [pltpu.VMEM((columns, fixed_rows), F32), dma((2,))],
+            {1: pltpu.HBM, 3: pltpu.HBM, 4: pltpu.HBM},
+            [
+                pltpu.VMEM((rows, columns), BF),
+                pltpu.VMEM((columns, fixed_rows), F32),
+                dma((3,)),
+            ],
         )
         got_parts = send_down(part_other)
         got_target = send_up(target)
@@ -414,13 +432,13 @@
         got_solved = send_down(other)
         advance(solved)
         pushed, other = call(
-            response_kernel, [fixed_f32, fixed_others], [low, high, response], wide, factor_bytes, after=sent
+            response_kernel, [fixed_f32, fixed_others], [k1, tail, response], wide, factor_bytes, after=sent
         )
         got_pushed = send_down(other)
         base, passed, other = call(
             pass_kernel,
             [flat_f32, flat_f32, flat_others],
-            [low, high, mask, solved, *got_solved],
+            [k1, tail, mask, solved, *got_solved],
             wide,
             factor_bytes,
             after=pushed,
@@ -430,7 +448,7 @@
         first, other = call(
             first_response_kernel,
             [fixed_f32, fixed_others],
-            [d0, arrow, pushed, *got_pushed],
+            [d0, e0, pushed, *got_pushed],
             wide,
             factor_bytes,
             after=sent,
@@ -449,7 +467,7 @@
         last_base, last_resp, first_resp, noise_rows = call(
             turn_kernel,
             [node_f32, by_node, by_node, shape_of((width, fixed_rows), F32)],
-            [base, response, first, noise_fixed, *got_first],
+            [base, response, first, noise_fixed, tip_inverse, *got_first],
             wide // 2,
             factor_bytes,
             after=sent,
@@ -476,7 +494,6 @@
             {("out", 0): pl.ANY},
             [
                 pltpu.VMEM((columns, fixed_rows), BF),
-                pltpu.VMEM((columns, fixed_rows), F32),
                 pltpu.VMEM((2, rows, columns), BF),
                 dma((2, tiles)),
             ],

time: 47.5 us -> 42.8 us (0.901)
  starting transfers between devices: 17.5 us -> 14.5 us
  waiting for transfers between devices: 11 us -> 8.1 us
  Pallas kernels: 17.6 us -> 19 us
    ppermute x4, waiting for transfers between devices: 8.21 us -> 4.97 us  [swap_bit(): return lax.ppermute(value, 'tm', [(i, i ^ bit) for i in range(n_tm)])]
    ppermute x11, starting transfers between devices: 7.58 us -> 5.35 us  [swap(): return lax.ppermute(value, 'space', pairs)]
    pallas_call x17, Pallas kernels: 17.6 us -> 19 us  [call(): pl.pallas_call(run, in_specs=specs, out_specs=[pl.BlockSpec(memory_space=...]
    ppermute x4, starting transfers between devices: 9.89 us -> 9.13 us  [swap_bit(): return lax.ppermute(value, 'tm', [(i, i ^ bit) for i in range(n_tm)])]
  transfers between devices with their start and end apart: 15 -> 15, of which waited for: 6 -> 7; matrix products, arithmetic and copies ran while one was open for 0% -> 0% of each run, Pallas kernels for 23% -> 32%
where the time goes in v5:
time: 42.8 us; the launch traced here: 42.5 us
  Pallas kernels  19 us (44%)
  starting transfers between devices  14.5 us (34%)
  waiting for transfers between devices  8.1 us (19%)
  between operations  0.93 us (2%)
    pallas_call x17, Pallas kernels, call(): pl.pallas_call(run, in_specs=specs, out_specs=[pl.BlockSpec(memory_space=...  19 us
    ppermute x4, starting transfers between devices, swap_bit(): return lax.ppermute(value, 'tm', [(i, i ^ bit) for i in range(n_tm)])  9.13 us
    ppermute x11, starting transfers between devices, swap(): return lax.ppermute(value, 'space', pairs)  5.35 us
    ppermute x4, waiting for transfers between devices, swap_bit(): return lax.ppermute(value, 'tm', [(i, i ^ bit) for i in range(n_tm)])  4.97 us
    ppermute x11, waiting for transfers between devices, swap(): return lax.ppermute(value, 'space', pairs)  3.13 us
  transfers between devices with their start and end apart: 15, of which 7 were waited for; matrix products, arithmetic and copies ran while one was open for 0% of the time, Pallas kernels for 32%

profile of v5, /device:TPU:0, one launch (start us, length us, event | category | flops | bytes accessed | tf_op | source)
XLA Modules:
  0.0 42.5 jit_solution(1038592748715103546)
XLA Ops:
  0.6 0.5 %collective-permute-start = (bf16[2,1024,256]{2,1,0:T(8,128)(2,1)}, bf16[2,1024,256]{2,1,0:T(8,128)(2,1)S(1)}, u32[]{:S(2)}, u32[]{:S(2)}) collective-permute-start(bf16[2,1024,256]{2,1,0:T(8,128)(2,1)} %refs_3_.4), channel_id=1, source_target_pairs={{0,1},{1,0},{2,3},{3,2},{4,5},{5,4},{6,7},{7,6},{8,9},{9,8},{10,11... | collective-permute-start | bytes 3145736 | tf_op jit(solution)/shard_map/ppermute | solution.py:319
  1.1 3.5 %shard_map.86 = (bf16[1024,2048]{1,0:T(8,128)(2,1)S(1)}, bf16[1024,2048]{1,0:T(8,128)(2,1)S(1)}, f32[256,1024]{1,0:T(8,128)S(1)}, bf16[1,256,1024]{2,1,0:T(8,128...) custom-call(bf16[2,1024,2048]{2,1,0:T(8,128)(2,1)} %refs_0_.3, bf16[2,256,1024]{2,1,0:T(8,128)(2,1)} %refs_4_.2, ...), custom_call_target="tpu_custom_call" | custom-call | flops 8589934592 | bytes 67108864 | tf_op jit(solution)/shard_map/pallas_call | solution.py:73
  4.7 1.4 %collective-permute-start.2 = (bf16[256,1024]{1,0:T(8,128)(2,1)S(1)}, bf16[256,1024]{1,0:T(8,128)(2,1)S(1)}, u32[]{:S(2)}, u32[]{:S(2)}) collective-permute-start(bf16[256,1024]{1,0:T(8,128)(2,1)S(1)} %bitcast.11), channel_id=1, source_target_pairs={{0,1},{1,0},{2,3},{3,2},{4,5},{5,4},{6,7},{7,6},{8,9},{9,8},{10,11... | collective-permute-start | bytes 1572872 | tf_op jit(solution)/shard_map/ppermute | solution.py:319
  6.1 0.0 collective-permute-done.refs_3_
  6.1 1.2 %shard_map.87 = (f32[1024,256]{1,0:T(8,128)S(1)}, bf16[1024,256]{1,0:T(8,128)(2,1)S(1)}, bf16[1024,2048]{1,0:T(8,128)(2,1)S(1)}) custom-call(bf16[1024,2048]{1,0:T(8,128)(2,1)S(1)} %get-tuple-element.34.refs_0_, f32[1024,256]{1,0:T(8,128)S(1)} %get-tuple-element.35.refs_1_, bf16[2,1024,2048]{2,1,0:T(8,128)(2,1)} %refs_1_.3, ...), custom_call_target="tpu_custom_call" | custom-call | flops 4294967296 | bytes 33554432 | tf_op jit(solution)/shard_map/pallas_call | solution.py:73
  7.3 0.1 collective-permute-start.1
  7.4 1.6 %shard_map.88 = (f32[256,1024]{1,0:T(8,128)S(1)}, bf16[1024,2048]{1,0:T(8,128)(2,1)S(1)}) custom-call(bf16[2,1024,2048]{2,1,0:T(8,128)(2,1)} %refs_1_.3, f32[1024,256]{1,0:T(8,128)S(1)} %get-tuple-element.36.refs_1_, bf16[1024,2048]{1,0:T(8,128)(2,1)S(1)} %get-tuple-element.37.refs_2_), custom_call_target="tpu_custom_call", output_to_operand_aliasing={{1}: (2, {})} | custom-call | flops 1073741824 | bytes 33554432 | tf_op jit(solution)/shard_map/pallas_call | solution.py:73
  9.0 0.0 collective-permute-done.2.refs_7_
  9.0 0.3 collective-permute-done.1.refs_6_
  9.3 3.3 %shard_map.89 = (bf16[256,2048]{1,0:T(8,128)(2,1)S(1)}, bf16[1024,256]{1,0:T(8,128)(2,1)S(1)}, f32[128,256]{1,0:T(8,128)S(1)}, bf16[1,128,256]{2,1,0:T(8,128)(2,...) custom-call(bf16[1024,2048]{1,0:T(8,128)(2,1)S(1)} %get-tuple-element.39.refs_0_, ...), custom_call_target="tpu_custom_call" | custom-call | flops 8589934592 | bytes 33554432 | tf_op jit(solution)/shard_map/pallas_call | solution.py:73
  12.7 0.3 collective-permute-start.3
  12.9 0.3 collective-permute-start.4
  13.2 1.5 %collective-permute-done.4.refs_1_ = bf16[128,256]{1,0:T(8,128)(2,1)S(1)} collective-permute-done((bf16[128,256]{1,0:T(8,128)(2,1)S(1)}, bf16[128,256]{1,0:T(8,128)(2,1)S(1)}, u32[]{:S(2)}, u32[]{:S(2)}) %collective-permute-start.4) | collective-permute-done | bytes 65568 | tf_op jit(solution)/shard_map/ppermute | solution.py:319
  14.7 3.0 %collective-permute-start.6 = (bf16[128,256]{1,0:T(8,128)(2,1)S(1)}, bf16[128,256]{1,0:T(8,128)(2,1)S(1)}, u32[]{:S(2)}, u32[]{:S(2)}) collective-permute-start(bf16[128,256]{1,0:T(8,128)(2,1)S(1)} %shard_map.90.refs_3_.refs_0_), channel_id=1, source_target_pairs={{0,2},{2,0},{4,6},{6,4},{8,10},{10,8},{12,14},{14,12},{16,18},{18,... | collective-permute-start | bytes 196616 | tf_op jit(solution)/shard_map/ppermute | solution.py:348
  17.7 0.0 collective-permute-done.3.refs_2_
  17.7 1.3 %shard_map.91 = (f32[256,1024]{1,0:T(8,128)S(1)}, bf16[1,256,1024]{2,1,0:T(8,128)(2,1)S(1)}) custom-call(bf16[1024,2048]{1,0:T(8,128)(2,1)S(1)} %get-tuple-element.45.refs_0_, bf16[1024,256]{1,0:T(8,128)(2,1)S(1)} %get-tuple-element.46.refs_1_, bf16[1024,256]{1,0:T(8,128)(2,1)S(1)} %collective-permute-done.3.refs_2_, ...), custom_call_target="tpu_custom_call" | custom-call | flops 12884901888 | bytes 33554432 | tf_op jit(solution)/shard_map/pallas_call | solution.py:73
  19.0 1.2 %collective-permute-done.6.refs_1_ = bf16[128,256]{1,0:T(8,128)(2,1)S(1)} collective-permute-done((bf16[128,256]{1,0:T(8,128)(2,1)S(1)}, bf16[128,256]{1,0:T(8,128)(2,1)S(1)}, u32[]{:S(2)}, u32[]{:S(2)}) %collective-permute-start.6) | collective-permute-done | bytes 65568 | tf_op jit(solution)/shard_map/ppermute | solution.py:348
  20.2 1.9 %collective-permute-start.9 = (bf16[128,256]{1,0:T(8,128)(2,1)S(1)}, bf16[128,256]{1,0:T(8,128)(2,1)S(1)}, u32[]{:S(2)}, u32[]{:S(2)}) collective-permute-start(bf16[128,256]{1,0:T(8,128)(2,1)S(1)} %shard_map.92.refs_3_.refs_0_), channel_id=1, source_target_pairs={{0,4},{2,6},{4,0},{6,2},{8,12},{10,14},{12,8},{14,10},{16,20},{18,... | collective-permute-start | bytes 196616 | tf_op jit(solution)/shard_map/ppermute | solution.py:348
  22.1 0.0 collective-permute-start.5
  22.1 1.3 %shard_map.93 = (f32[256,1024]{1,0:T(8,128)S(1)}, bf16[1,256,1024]{2,1,0:T(8,128)(2,1)S(1)}) custom-call(bf16[1024,2048]{1,0:T(8,128)(2,1)S(1)} %get-tuple-element.39.refs_0_, bf16[256,2048]{1,0:T(8,128)(2,1)S(1)} %get-tuple-element.43.refs_1_, bf16[256,1024]{1,0:T(8,128)(2,1)S(1)} %get-tuple-element.51.refs_2_.refs_1_, ...), custom_call_target="tpu_custom_call" | custom-call | flops 8589934592 | bytes 33554432 | tf_op jit(solution)/shard_map/pallas_call | solution.py:73
  23.4 0.6 %collective-permute-start.8 = (bf16[256,1024]{1,0:T(8,128)(2,1)S(1)}, bf16[256,1024]{1,0:T(8,128)(2,1)S(1)}, u32[]{:S(2)}, u32[]{:S(2)}) collective-permute-start(bf16[256,1024]{1,0:T(8,128)(2,1)S(1)} %bitcast.10), channel_id=1, source_target_pairs={{0,1},{1,0},{2,3},{3,2},{4,5},{5,4},{6,7},{7,6},{8,9},{9,8},{10,11... | collective-permute-start | bytes 1572872 | tf_op jit(solution)/shard_map/ppermute | solution.py:319
  24.0 0.1 collective-permute-done.5.refs_4_
  24.0 1.3 %shard_map.94 = (f32[256,1024]{1,0:T(8,128)S(1)}, f32[256,1024]{1,0:T(8,128)S(1)}, bf16[1,256,1024]{2,1,0:T(8,128)(2,1)S(1)}) custom-call(bf16[1024,2048]{1,0:T(8,128)(2,1)S(1)} %get-tuple-element.39.refs_0_, bf16[256,2048]{1,0:T(8,128)(2,1)S(1)} %get-tuple-element.43.refs_1_, f32[8,128]{1,0:T(8,128)S(1)} %get-tuple-element.44.refs_2_, ...), custom_call_target="tpu_custom_call" | custom-call | flops 8589934592 | bytes 33554432 | tf_op jit(solution)/shard_map/pallas_call | solution.py:73
  25.4 0.2 collective-permute-start.7
  25.6 0.0 collective-permute-done.9.refs_1_
  25.6 0.0 collective-permute-done.8.refs_3_
  25.6 0.9 %shard_map.96 = (f32[256,1024]{1,0:T(8,128)S(1)}, bf16[1,256,1024]{2,1,0:T(8,128)(2,1)S(1)}) custom-call(bf16[1024,2048]{1,0:T(8,128)(2,1)S(1)} %get-tuple-element.34.refs_0_, bf16[256,1024]{1,0:T(8,128)(2,1)S(1)} %get-tuple-element.55.refs_1_, f32[256,1024]{1,0:T(8,128)S(1)} %get-tuple-element.52.refs_5_.refs_2_, ...), custom_call_target="tpu_custom_call" | custom-call | flops 8589934592 | bytes 33554432 | tf_op jit(solution)/shard_map/pallas_call | solution.py:73
  26.5 1.1 %collective-permute-start.11 = (bf16[256,1024]{1,0:T(8,128)(2,1)S(1)}, bf16[256,1024]{1,0:T(8,128)(2,1)S(1)}, u32[]{:S(2)}, u32[]{:S(2)}) collective-permute-start(bf16[256,1024]{1,0:T(8,128)(2,1)S(1)} %bitcast.7), channel_id=1, source_target_pairs={{0,1},{1,0},{2,3},{3,2},{4,5},{5,4},{6,7},{7,6},{8,9},{9,8},{10,11... | collective-permute-start | bytes 1572872 | tf_op jit(solution)/shard_map/ppermute | solution.py:319
  27.7 0.0 collective-permute-done.7.refs_3_
  27.7 0.0 copy-start
  27.7 0.0 copy-start.1
  27.7 1.1 %shard_map.97 = (f32[256,1024]{1,0:T(8,128)S(1)}, bf16[1,256,1024]{2,1,0:T(8,128)(2,1)S(1)}) custom-call(bf16[1024,2048]{1,0:T(8,128)(2,1)S(1)} %get-tuple-element.34.refs_0_, f32[256,1024]{1,0:T(8,128)S(1)} %get-tuple-element.38.refs_1_, f32[256,1024]{1,0:T(8,128)S(1)} %get-tuple-element.53.refs_2_, bf16[256,1024]{1,0:T(8,128)(2,1)S(1)} %collective-permute-done.7.refs_3_, ...), custom_call_target="tpu_custom_call" | custom-call | flops 8589934592 | bytes 33554432 | tf_op jit(solution)/shard_map/pallas_call | solution.py:73
  28.8 0.8 %collective-permute-start.10 = (bf16[256,1024]{1,0:T(8,128)(2,1)S(1)}, bf16[256,1024]{1,0:T(8,128)(2,1)S(1)}, u32[]{:S(2)}, u32[]{:S(2)}) collective-permute-start(bf16[256,1024]{1,0:T(8,128)(2,1)S(1)} %bitcast.8), channel_id=1, source_target_pairs={{0,1},{1,0},{2,3},{3,2},{4,5},{5,4},{6,7},{7,6},{8,9},{9,8},{10,11... | collective-permute-start | bytes 1572872 | tf_op jit(solution)/shard_map/ppermute | solution.py:319
  29.5 1.6 %collective-permute-start.12 = (bf16[128,256]{1,0:T(8,128)(2,1)S(1)}, bf16[128,256]{1,0:T(8,128)(2,1)S(1)}, u32[]{:S(2)}, u32[]{:S(2)}) collective-permute-start(bf16[128,256]{1,0:T(8,128)(2,1)S(1)} %shard_map.95.refs_4_.refs_0_), channel_id=1, source_target_pairs={{0,8},{2,10},{4,12},{6,14},{8,0},{10,2},{12,4},{14,6},{16,24},{18,... | collective-permute-start | bytes 196616 | tf_op jit(solution)/shard_map/ppermute | solution.py:348
  31.1 2.7 %collective-permute-done.12.refs_1_ = bf16[128,256]{1,0:T(8,128)(2,1)S(1)} collective-permute-done((bf16[128,256]{1,0:T(8,128)(2,1)S(1)}, bf16[128,256]{1,0:T(8,128)(2,1)S(1)}, u32[]{:S(2)}, u32[]{:S(2)}) %collective-permute-start.12) | collective-permute-done | bytes 65568 | tf_op jit(solution)/shard_map/ppermute | solution.py:348
  33.8 2.7 %collective-permute-start.13 = (bf16[128,256]{1,0:T(8,128)(2,1)S(1)}, bf16[128,256]{1,0:T(8,128)(2,1)S(1)}, u32[]{:S(2)}, u32[]{:S(2)}) collective-permute-start(bf16[128,256]{1,0:T(8,128)(2,1)S(1)} %shard_map.98.refs_6_.refs_1_), channel_id=1, source_target_pairs={{0,16},{2,18},{4,20},{6,22},{8,24},{10,26},{12,28},{14,30},{16,0},... | collective-permute-start | bytes 196616 | tf_op jit(solution)/shard_map/ppermute | solution.py:348
  36.5 0.0 collective-permute-done.11.refs_5_
  36.5 0.0 copy-done
  36.5 0.0 copy-done.1
  36.5 1.1 %shard_map.99 = (f32[1024,256]{1,0:T(8,128)S(1)}, bf16[1024,256]{1,0:T(8,128)(2,1)S(1)}, bf16[1024,256]{1,0:T(8,128)(2,1)S(1)}, f32[128,256]{1,0:T(8,128)S(1)}) custom-call(f32[256,1024]{1,0:T(8,128)S(1)} %get-tuple-element.57.refs_2_.refs_0_, bf16[256,1024]{1,0:T(8,128)(2,1)S(1)} %get-tuple-element.51.refs_2_.refs_1_, ...), custom_call_target="tpu_custom_call" | custom-call | flops 4294967296 | bytes 33554432 | tf_op jit(solution)/shard_map/pallas_call | solution.py:73
  37.6 0.0 collective-permute-done.10.refs_1_
  37.6 0.3 shard_map.100.refs_3_.refs_1_
  38.0 1.1 %collective-permute-done.13.refs_2_ = bf16[128,256]{1,0:T(8,128)(2,1)S(1)} collective-permute-done((bf16[128,256]{1,0:T(8,128)(2,1)S(1)}, bf16[128,256]{1,0:T(8,128)(2,1)S(1)}, u32[]{:S(2)}, u32[]{:S(2)}) %collective-permute-start.13) | collective-permute-done | bytes 65568 | tf_op jit(solution)/shard_map/ppermute | solution.py:348
  39.1 0.1 collective-permute-start.14
  39.2 1.2 %collective-permute-done.14.refs_6_ = bf16[128,256]{1,0:T(8,128)(2,1)S(1)} collective-permute-done((bf16[128,256]{1,0:T(8,128)(2,1)S(1)}, bf16[128,256]{1,0:T(8,128)(2,1)S(1)}, u32[]{:S(2)}, u32[]{:S(2)}) %collective-permute-start.14) | collective-permute-done | bytes 65568 | tf_op jit(solution)/shard_map/ppermute | solution.py:319
  40.4 2.0 %shard_map.102 = (bf16[2,1024,256]{2,1,0:T(8,128)(2,1)}, f32[256,128]{1,0:T(8,128)}) custom-call(bf16[256,256]{1,0:T(8,128)(2,1)S(1)} %copy-done.1, f32[1024,256]{1,0:T(8,128)S(1)} %shard_map.100.refs_3_.refs_1_, f32[1024,256]{1,0:T(8,128)S(1)} %get-tuple-element.63.refs_2_, bf16[1024,256]{1,0:T(8,128)(2,1)S(1)} %get-tuple-element.64.refs_3_, ...), custom_call_target="tpu_custom_call" | custom-call | flops 2147483648 | bytes 33554432 | tf_op jit(solution)/shard_map/pallas_call | solution.py:73
  (5 shorter events, 0.1 us)
Async XLA Ops:
  0.6 5.5 %collective-permute-start = (bf16[2,1024,256]{2,1,0:T(8,128)(2,1)}, bf16[2,1024,256]{2,1,0:T(8,128)(2,1)S(1)}, u32[]{:S(2)}, u32[]{:S(2)}) collective-permute-start(bf16[2,1024,256]{2,1,0:T(8,128)(2,1)} %refs_3_.4), channel_id=1, source_target_pairs={{0,1},{1,0},{2,3},{3,2},{4,5},{5,4},{6,7},{7,6},{8,9},{9,8},{10,11... | collective-permute-start | bytes 3145736 | tf_op jit(solution)/shard_map/ppermute | solution.py:319
  4.7 4.3 %collective-permute-start.2 = (bf16[256,1024]{1,0:T(8,128)(2,1)S(1)}, bf16[256,1024]{1,0:T(8,128)(2,1)S(1)}, u32[]{:S(2)}, u32[]{:S(2)}) collective-permute-start(bf16[256,1024]{1,0:T(8,128)(2,1)S(1)} %bitcast.11), channel_id=1, source_target_pairs={{0,1},{1,0},{2,3},{3,2},{4,5},{5,4},{6,7},{7,6},{8,9},{9,8},{10,11... | collective-permute-start | bytes 1572872 | tf_op jit(solution)/shard_map/ppermute | solution.py:319
  7.3 2.0 %collective-permute-start.1 = (bf16[1024,256]{1,0:T(8,128)(2,1)S(1)}, bf16[1024,256]{1,0:T(8,128)(2,1)S(1)}, u32[]{:S(2)}, u32[]{:S(2)}) collective-permute-start(bf16[1024,256]{1,0:T(8,128)(2,1)S(1)} %get-tuple-element.40.refs_2_), channel_id=1, source_target_pairs={{0,1},{1,0},{2,3},{3,2},{4,5},{5,4},{6,7},{7,6},{8,9},{9,8},{10,11... | collective-permute-start | bytes 1572872 | tf_op jit(solution)/shard_map/ppermute | solution.py:319
  12.7 5.1 %collective-permute-start.3 = (bf16[1024,256]{1,0:T(8,128)(2,1)S(1)}, bf16[1024,256]{1,0:T(8,128)(2,1)S(1)}, u32[]{:S(2)}, u32[]{:S(2)}) collective-permute-start(bf16[1024,256]{1,0:T(8,128)(2,1)S(1)} %get-tuple-element.46.refs_1_), channel_id=1, source_target_pairs={{0,1},{1,0},{2,3},{3,2},{4,5},{5,4},{6,7},{7,6},{8,9},{9,8},{10,11... | collective-permute-start | bytes 1572872 | tf_op jit(solution)/shard_map/ppermute | solution.py:319
  12.9 1.8 %collective-permute-start.4 = (bf16[128,256]{1,0:T(8,128)(2,1)S(1)}, bf16[128,256]{1,0:T(8,128)(2,1)S(1)}, u32[]{:S(2)}, u32[]{:S(2)}) collective-permute-start(bf16[128,256]{1,0:T(8,128)(2,1)S(1)} %bitcast.13), channel_id=1, source_target_pairs={{0,1},{1,0},{2,3},{3,2},{4,5},{5,4},{6,7},{7,6},{8,9},{9,8},{10,11... | collective-permute-start | bytes 196616 | tf_op jit(solution)/shard_map/ppermute | solution.py:319
  14.7 5.5 %collective-permute-start.6 = (bf16[128,256]{1,0:T(8,128)(2,1)S(1)}, bf16[128,256]{1,0:T(8,128)(2,1)S(1)}, u32[]{:S(2)}, u32[]{:S(2)}) collective-permute-start(bf16[128,256]{1,0:T(8,128)(2,1)S(1)} %shard_map.90.refs_3_.refs_0_), channel_id=1, source_target_pairs={{0,2},{2,0},{4,6},{6,4},{8,10},{10,8},{12,14},{14,12},{16,18},{18,... | collective-permute-start | bytes 196616 | tf_op jit(solution)/shard_map/ppermute | solution.py:348
  20.2 5.4 %collective-permute-start.9 = (bf16[128,256]{1,0:T(8,128)(2,1)S(1)}, bf16[128,256]{1,0:T(8,128)(2,1)S(1)}, u32[]{:S(2)}, u32[]{:S(2)}) collective-permute-start(bf16[128,256]{1,0:T(8,128)(2,1)S(1)} %shard_map.92.refs_3_.refs_0_), channel_id=1, source_target_pairs={{0,4},{2,6},{4,0},{6,2},{8,12},{10,14},{12,8},{14,10},{16,20},{18,... | collective-permute-start | bytes 196616 | tf_op jit(solution)/shard_map/ppermute | solution.py:348
  22.1 1.9 %collective-permute-start.5 = (bf16[256,1024]{1,0:T(8,128)(2,1)S(1)}, bf16[256,1024]{1,0:T(8,128)(2,1)S(1)}, u32[]{:S(2)}, u32[]{:S(2)}) collective-permute-start(bf16[256,1024]{1,0:T(8,128)(2,1)S(1)} %bitcast.12), channel_id=1, source_target_pairs={{0,1},{1,0},{2,3},{3,2},{4,5},{5,4},{6,7},{7,6},{8,9},{9,8},{10,11... | collective-permute-start | bytes 1572872 | tf_op jit(solution)/shard_map/ppermute | solution.py:319
  23.4 2.2 %collective-permute-start.8 = (bf16[256,1024]{1,0:T(8,128)(2,1)S(1)}, bf16[256,1024]{1,0:T(8,128)(2,1)S(1)}, u32[]{:S(2)}, u32[]{:S(2)}) collective-permute-start(bf16[256,1024]{1,0:T(8,128)(2,1)S(1)} %bitcast.10), channel_id=1, source_target_pairs={{0,1},{1,0},{2,3},{3,2},{4,5},{5,4},{6,7},{7,6},{8,9},{9,8},{10,11... | collective-permute-start | bytes 1572872 | tf_op jit(solution)/shard_map/ppermute | solution.py:319
  25.4 2.3 %collective-permute-start.7 = (bf16[256,1024]{1,0:T(8,128)(2,1)S(1)}, bf16[256,1024]{1,0:T(8,128)(2,1)S(1)}, u32[]{:S(2)}, u32[]{:S(2)}) collective-permute-start(bf16[256,1024]{1,0:T(8,128)(2,1)S(1)} %bitcast.9), channel_id=1, source_target_pairs={{0,1},{1,0},{2,3},{3,2},{4,5},{5,4},{6,7},{7,6},{8,9},{9,8},{10,11... | collective-permute-start | bytes 1572872 | tf_op jit(solution)/shard_map/ppermute | solution.py:319
  26.5 9.9 %collective-permute-start.11 = (bf16[256,1024]{1,0:T(8,128)(2,1)S(1)}, bf16[256,1024]{1,0:T(8,128)(2,1)S(1)}, u32[]{:S(2)}, u32[]{:S(2)}) collective-permute-start(bf16[256,1024]{1,0:T(8,128)(2,1)S(1)} %bitcast.7), channel_id=1, source_target_pairs={{0,1},{1,0},{2,3},{3,2},{4,5},{5,4},{6,7},{7,6},{8,9},{9,8},{10,11... | collective-permute-start | bytes 1572872 | tf_op jit(solution)/shard_map/ppermute | solution.py:319
  27.7 8.8 %copy-start = (f32[256,128]{1,0:T(8,128)S(1)}, f32[256,128]{1,0:T(8,128)}, u32[]{:S(2)}) copy-start(f32[256,128]{1,0:T(8,128)} %refs_3_.5) | copy-start | bytes 393220
  27.7 8.8 %copy-start.1 = (bf16[256,256]{1,0:T(8,128)(2,1)S(1)}, bf16[256,256]{1,0:T(8,128)(2,1)}, u32[]{:S(2)}) copy-start(bf16[256,256]{1,0:T(8,128)(2,1)} %refs_0_.5) | copy-start | bytes 393220
  28.8 8.9 %collective-permute-start.10 = (bf16[256,1024]{1,0:T(8,128)(2,1)S(1)}, bf16[256,1024]{1,0:T(8,128)(2,1)S(1)}, u32[]{:S(2)}, u32[]{:S(2)}) collective-permute-start(bf16[256,1024]{1,0:T(8,128)(2,1)S(1)} %bitcast.8), channel_id=1, source_target_pairs={{0,1},{1,0},{2,3},{3,2},{4,5},{5,4},{6,7},{7,6},{8,9},{9,8},{10,11... | collective-permute-start | bytes 1572872 | tf_op jit(solution)/shard_map/ppermute | solution.py:319
  29.5 4.3 %collective-permute-start.12 = (bf16[128,256]{1,0:T(8,128)(2,1)S(1)}, bf16[128,256]{1,0:T(8,128)(2,1)S(1)}, u32[]{:S(2)}, u32[]{:S(2)}) collective-permute-start(bf16[128,256]{1,0:T(8,128)(2,1)S(1)} %shard_map.95.refs_4_.refs_0_), channel_id=1, source_target_pairs={{0,8},{2,10},{4,12},{6,14},{8,0},{10,2},{12,4},{14,6},{16,24},{18,... | collective-permute-start | bytes 196616 | tf_op jit(solution)/shard_map/ppermute | solution.py:348
  33.8 5.2 %collective-permute-start.13 = (bf16[128,256]{1,0:T(8,128)(2,1)S(1)}, bf16[128,256]{1,0:T(8,128)(2,1)S(1)}, u32[]{:S(2)}, u32[]{:S(2)}) collective-permute-start(bf16[128,256]{1,0:T(8,128)(2,1)S(1)} %shard_map.98.refs_6_.refs_1_), channel_id=1, source_target_pairs={{0,16},{2,18},{4,20},{6,22},{8,24},{10,26},{12,28},{14,30},{16,0},... | collective-permute-start | bytes 196616 | tf_op jit(solution)/shard_map/ppermute | solution.py:348
  39.1 1.3 %collective-permute-start.14 = (bf16[128,256]{1,0:T(8,128)(2,1)S(1)}, bf16[128,256]{1,0:T(8,128)(2,1)S(1)}, u32[]{:S(2)}, u32[]{:S(2)}) collective-permute-start(bf16[128,256]{1,0:T(8,128)(2,1)S(1)} %shard_map.101.refs_5_), channel_id=1, source_target_pairs={{0,1},{1,0},{2,3},{3,2},{4,5},{5,4},{6,7},{7,6},{8,9},{9,8},{10,11... | collective-permute-start | bytes 196616 | tf_op jit(solution)/shard_map/ppermute | solution.py:319

commit v6 on v5

--- a/solution.py
+++ b/solution.py
@@ -81,7 +81,7 @@
             scratch_shapes=list(scratch),
             input_output_aliases=aliases or {},
             cost_estimate=pl.CostEstimate(
-                flops=8 * flops, bytes_accessed=8 * moved, transcendentals=0
+                flops=16 * flops, bytes_accessed=16 * moved, transcendentals=0
             ),
             compiler_params=pltpu.CompilerParams(vmem_limit_bytes=16 * MIB),
         )(*args)
@@ -161,7 +161,7 @@
         live_copy.start()
         arrow_copy.start()
         for i in range(tiles):
-            each(copies1, i, lambda copy: copy.start())
+            each(copies1, i, lambda copy: copy.start(priority=i % 2))
         noise_copy.start()
         live_copy.wait()
         arrow_copy.wait()
@@ -170,7 +170,7 @@
         e1[...] = jnp.where(live, e1[...], jnp.zeros_like(e1[...]))
         for i in range(tiles):
             each(copies1, i, lambda copy: copy.wait())
-            each(copies0, i, lambda copy: copy.start())
+            each(copies0, i, lambda copy: copy.start(priority=i % 2))
         lower_rows(e1, d1, own, other)
         noise_copy.wait()
         lower_own(d0, n0, first, lambda i: copies0[0, i].wait())
@@ -200,8 +200,8 @@
 
     def load_kernel(coupling, value, _, value_rows, k1, sems):
         copies = k1_copies(coupling, k1, [1, 2], sems)
-        for copy in copies.values():
-            copy.start()
+        for q, copy in copies.items():
+            copy.start(priority=q % 2)
         value_rows[...] = value[...].T
         for copy in copies.values():
             copy.wait()
@@ -214,29 +214,31 @@
         arrow_copy = pltpu.make_async_copy(arrow.at[0], e0, sems.at[2])
         copies = k1_copies(coupling, tail, [3], sems)
         noise_copy.start()
-        copies[3].start()
+        copies[3].start(priority=1)
         arrow_copy.start()
-        response[...] = total_of(own, got_own).astype(BF)
-        for i in range(4):
-            at = i * quarter
-            if i in copies:
-                copies[i].wait()
-            factor = tail if i == 3 else k1.at[at : at + quarter]
+        at = rows - quarter
+
+        def pull(factor, part, before):
             pulled = dot(factor[:, block(0)], bar[...])
             for step in peers:
                 pulled = pulled + dot(factor[:, block(step)], got[step - 1][...])
-            if i == 0:
-                noise_copy.wait()
-            source = n1[at : at + quarter].astype(F32)
-            target[at : at + quarter] = (source - pulled).astype(BF)
-        arrow_copy.wait()
+            before.wait()
+            target[part] = (n1[part].astype(F32) - pulled).astype(BF)
+
+        response[...] = total_of(own, got_own).astype(BF)
+        pull(k1.at[:at], pl.ds(0, at), noise_copy)
+        copies[3].wait()
+        pull(tail, pl.ds(at, quarter), arrow_copy)
         whole[...] = (dot(e0[...], bar[...]) + dot(response[...], target[...])).T
         part_own[...] = whole[part_rows(0)]
         for step in peers:
             part_other[step - 1] = whole[part_rows(step)].astype(BF)
 
-    def core_sum_kernel(part, *refs):
-        got, out = refs[:-1], refs[-1]
+    def last_own_kernel(d1, target, value):
+        lower_own(d1, target, value)
+
+    def core_sum_kernel(part, _, *refs):
+        got, (out, _) = refs[:-2], refs[-2:]
         total = part[...]
         for piece in got:
             total = total + piece[...].astype(F32)
@@ -245,9 +247,9 @@
     def fold_kernel(sent, got, out):
         out[...] = (sent[...].astype(F32) + got[...].astype(F32)).astype(BF)
 
-    def last_solve_kernel(d1, target, *refs):
+    def last_solve_kernel(d1, first, *refs):
         got, (own, other, value) = refs[: n_space - 1], refs[n_space - 1 :]
-        lower_own(d1, target, value)
+        value[...] = first[...]
         lower_rest(d1, got, value)
         lower_rows(value[...].T.astype(BF), d1, own, other)
 
@@ -294,8 +296,8 @@
             total = total + piece[...].astype(F32)
         out[...] = (noise_rows[...] - total).astype(BF)
 
-    def final_kernel(tip, bases, responses, mixed, *refs):
-        got, (out, fixed_out, whole, result, sems) = refs[: n_space - 1], refs[n_space - 1 :]
+    def final_kernel(bases, responses, mixed, *refs):
+        got, (out, whole, result, sems) = refs[: n_space - 1], refs[n_space - 1 :]
         for step, piece in enumerate([mixed, *got]):
             whole[part_rows(step)] = piece[...]
         copies = []
@@ -309,10 +311,12 @@
                     pltpu.make_async_copy(result.at[part], out.at[part], sems.at[slot, i])
                 )
                 copies[-1].start()
-        forward = dot_last(mixed[...], tip[...])
-        fixed_out[...] = dot(forward.astype(BF), tip[...]).T
         for copy in copies:
             copy.wait()
+
+    def fixed_kernel(tip, mixed, out):
+        forward = dot_last(mixed[...], tip[...])
+        out[...] = dot(forward.astype(BF), tip[...]).T
 
     def swap(value, step):
         pairs = [(i, (i - step) % n_space) for i in range(n_space)]
@@ -407,10 +411,18 @@
             ],
         )
         got_parts = send_down(part_other)
+        (value,) = call(last_own_kernel, [node_f32], [d1, target], wide // 3, factor_bytes // 4)
+        sent, target = call(
+            core_sum_kernel,
+            [part_bf, node_bf],
+            [part_own, target, *got_parts],
+            width * fixed_rows,
+            8 * width * fixed_rows,
+            {1: pl.ANY, ("out", 1): pl.ANY},
+            aliases={1: 1},
+            after=value,
+        )
         got_target = send_up(target)
-        (sent,) = call(
-            core_sum_kernel, [part_bf], [part_own, *got_parts], width * fixed_rows, 8 * width * fixed_rows
-        )
         left = list(bits)
         got = [swap_bit(sent, left.pop(0))] if left else []
 
@@ -423,7 +435,7 @@
         solved, other = call(
             last_solve_kernel,
             [flat_f32, flat_others],
-            [d1, target, *got_target],
+            [d1, value, *got_target],
             wide * 3 // 2,
             factor_bytes,
             scratch=[pltpu.VMEM((rows, columns), F32)],
@@ -445,6 +457,16 @@
         )
         got_passed = send_down(other)
         advance(base)
+        solved, other = call(
+            first_solve_kernel,
+            [flat_f32, flat_others],
+            [d0, value_rows, passed, *got_passed],
+            wide,
+            factor_bytes,
+            after=sent,
+        )
+        got_solved = send_down(other)
+        advance(solved)
         first, other = call(
             first_response_kernel,
             [fixed_f32, fixed_others],
@@ -454,26 +476,16 @@
             after=sent,
         )
         got_first = send_down(other)
-        solved, other = call(
-            first_solve_kernel,
-            [flat_f32, flat_others],
-            [d0, value_rows, passed, *got_passed],
-            wide,
-            factor_bytes,
-            after=first,
-        )
-        got_solved = send_down(other)
-        advance(solved)
         last_base, last_resp, first_resp, noise_rows = call(
             turn_kernel,
             [node_f32, by_node, by_node, shape_of((width, fixed_rows), F32)],
             [base, response, first, noise_fixed, tip_inverse, *got_first],
-            wide // 2,
-            factor_bytes,
-            after=sent,
+            wide,
+            factor_bytes,
+            after=first,
         )
         (first_base,) = call(
-            turn_first_kernel, [node_f32], [solved, *got_solved], wide // 4, factor_bytes // 2, after=noise_rows
+            turn_first_kernel, [node_f32], [solved, *got_solved], wide, factor_bytes, after=noise_rows
         )
         while left:
             advance(None)
@@ -485,10 +497,18 @@
             8 * width * fixed_rows,
             after=first_base,
         )
-        sample, fixed_out = call(
-            lambda tip, a, b, c, d, *refs: final_kernel(tip, (a, b), (c, d), *refs),
-            [shape_of((2, rows, columns), BF), shape_of((fixed_rows, width), F32)],
-            [tip_inverse, first_base, last_base, first_resp, last_resp, mixed, *send_up(mixed)],
+        got_mixed = send_up(mixed)
+        (fixed_out,) = call(
+            fixed_kernel,
+            [shape_of((fixed_rows, width), F32)],
+            [tip_inverse, mixed],
+            wide,
+            factor_bytes,
+        )
+        (sample,) = call(
+            lambda a, b, c, d, *refs: final_kernel((a, b), (c, d), *refs),
+            [shape_of((2, rows, columns), BF)],
+            [first_base, last_base, first_resp, last_resp, mixed, *got_mixed],
             4 * rows * fixed_rows * columns,
             factor_bytes,
             {("out", 0): pl.ANY},
@@ -497,6 +517,7 @@
                 pltpu.VMEM((2, rows, columns), BF),
                 dma((2, tiles)),
             ],
+            after=fixed_out,
         )
         return (sample, fixed_out)
 

time: 42.8 us -> 44 us (1.028)
  local copies, waits for them, and re-layouts: 0.01 us -> 0.92 us
  Pallas kernels: 19 us -> 19.7 us
  waiting for transfers between devices: 8.1 us -> 7.54 us
    ppermute x11, waiting for transfers between devices: 3.13 us -> 1.66 us  [swap(): return lax.ppermute(value, 'space', pairs)]
    ppermute x4, waiting for transfers between devices: 4.97 us -> 5.88 us  [swap_bit(): return lax.ppermute(value, 'tm', [(i, i ^ bit) for i in range(n_tm)])]
    unnamed x4 -> x6, local copies, waits for them, and re-layouts: 0.01 us -> 0.92 us
    ppermute x4, starting transfers between devices: 9.13 us -> 9.86 us  [swap_bit(): return lax.ppermute(value, 'tm', [(i, i ^ bit) for i in range(n_tm)])]
    pallas_call x17 -> x19, Pallas kernels: 19 us -> 19.7 us  [call(): pl.pallas_call(run, in_specs=specs, out_specs=[pl.BlockSpec(memory_space=...]
    ppermute x11, starting transfers between devices: 5.35 us -> 4.76 us  [swap(): return lax.ppermute(value, 'space', pairs)]
  transfers between devices with their start and end apart: 15 -> 15, of which waited for: 7 -> 8; matrix products, arithmetic and copies ran while one was open for 0% -> 0% of each run, Pallas kernels for 32% -> 29%
where the time goes in v6:
time: 44 us; the launch traced here: 43.7 us
  Pallas kernels  19.7 us (45%)
  starting transfers between devices  14.6 us (33%)
  waiting for transfers between devices  7.54 us (17%)
  between operations  0.95 us (2%)
  local copies, waits for them, and re-layouts  0.92 us (2%)
    pallas_call x19, Pallas kernels, call(): pl.pallas_call(run, in_specs=specs, out_specs=[pl.BlockSpec(memory_space=...  19.7 us
    ppermute x4, starting transfers between devices, swap_bit(): return lax.ppermute(value, 'tm', [(i, i ^ bit) for i in range(n_tm)])  9.86 us
    ppermute x4, waiting for transfers between devices, swap_bit(): return lax.ppermute(value, 'tm', [(i, i ^ bit) for i in range(n_tm)])  5.88 us
    ppermute x11, starting transfers between devices, swap(): return lax.ppermute(value, 'space', pairs)  4.76 us
    ppermute x11, waiting for transfers between devices, swap(): return lax.ppermute(value, 'space', pairs)  1.66 us
    unnamed x6, local copies, waits for them, and re-layouts  0.92 us
  transfers between devices with their start and end apart: 15, of which 8 were waited for; matrix products, arithmetic and copies ran while one was open for 0% of the time, Pallas kernels for 29%

profile of v6, /device:TPU:0, one launch (start us, length us, event | category | flops | bytes accessed | tf_op | source)
XLA Modules:
  0.0 43.7 jit_solution(1766441783307845764)
XLA Ops:
  0.6 0.5 %collective-permute-start = (bf16[2,1024,256]{2,1,0:T(8,128)(2,1)}, bf16[2,1024,256]{2,1,0:T(8,128)(2,1)S(1)}, u32[]{:S(2)}, u32[]{:S(2)}) collective-permute-start(bf16[2,1024,256]{2,1,0:T(8,128)(2,1)} %refs_3_.4), channel_id=1, source_target_pairs={{0,1},{1,0},{2,3},{3,2},{4,5},{5,4},{6,7},{7,6},{8,9},{9,8},{10,11... | collective-permute-start | bytes 3145736 | tf_op jit(solution)/shard_map/ppermute | solution.py:323
  1.1 3.8 %shard_map.86 = (bf16[1024,2048]{1,0:T(8,128)(2,1)S(1)}, bf16[1024,2048]{1,0:T(8,128)(2,1)S(1)}, f32[256,1024]{1,0:T(8,128)S(1)}, bf16[1,256,1024]{2,1,0:T(8,128...) custom-call(bf16[2,1024,2048]{2,1,0:T(8,128)(2,1)} %refs_0_.3, bf16[2,256,1024]{2,1,0:T(8,128)(2,1)} %refs_4_.2, ...), custom_call_target="tpu_custom_call" | custom-call | flops 17179869184 | bytes 134217728 | tf_op jit(solution)/shard_map/pallas_call | solution.py:73
  4.9 1.3 %collective-permute-start.2 = (bf16[256,1024]{1,0:T(8,128)(2,1)S(1)}, bf16[256,1024]{1,0:T(8,128)(2,1)S(1)}, u32[]{:S(2)}, u32[]{:S(2)}) collective-permute-start(bf16[256,1024]{1,0:T(8,128)(2,1)S(1)} %bitcast.10), channel_id=1, source_target_pairs={{0,1},{1,0},{2,3},{3,2},{4,5},{5,4},{6,7},{7,6},{8,9},{9,8},{10,11... | collective-permute-start | bytes 1572872 | tf_op jit(solution)/shard_map/ppermute | solution.py:323
  6.3 0.0 collective-permute-done.refs_3_
  6.3 1.2 %shard_map.87 = (f32[1024,256]{1,0:T(8,128)S(1)}, bf16[1024,256]{1,0:T(8,128)(2,1)S(1)}, bf16[1024,2048]{1,0:T(8,128)(2,1)S(1)}) custom-call(bf16[1024,2048]{1,0:T(8,128)(2,1)S(1)} %get-tuple-element.36.refs_0_, f32[1024,256]{1,0:T(8,128)S(1)} %get-tuple-element.37.refs_1_, bf16[2,1024,2048]{2,1,0:T(8,128)(2,1)} %refs_1_.3, ...), custom_call_target="tpu_custom_call" | custom-call | flops 8589934592 | bytes 67108864 | tf_op jit(solution)/shard_map/pallas_call | solution.py:73
  7.5 0.1 collective-permute-start.1
  7.6 1.6 %shard_map.88 = (f32[256,1024]{1,0:T(8,128)S(1)}, bf16[1024,2048]{1,0:T(8,128)(2,1)S(1)}) custom-call(bf16[2,1024,2048]{2,1,0:T(8,128)(2,1)} %refs_1_.3, f32[1024,256]{1,0:T(8,128)S(1)} %get-tuple-element.38.refs_1_, bf16[1024,2048]{1,0:T(8,128)(2,1)S(1)} %get-tuple-element.39.refs_2_), custom_call_target="tpu_custom_call", output_to_operand_aliasing={{1}: (2, {})} | custom-call | flops 2147483648 | bytes 67108864 | tf_op jit(solution)/shard_map/pallas_call | solution.py:73
  9.2 0.0 collective-permute-done.2.refs_7_
  9.2 0.3 collective-permute-done.1.refs_6_
  9.5 3.3 %shard_map.89 = (bf16[256,2048]{1,0:T(8,128)(2,1)S(1)}, bf16[1024,256]{1,0:T(8,128)(2,1)S(1)}, f32[128,256]{1,0:T(8,128)S(1)}, bf16[1,128,256]{2,1,0:T(8,128)(2,...) custom-call(bf16[1024,2048]{1,0:T(8,128)(2,1)S(1)} %get-tuple-element.41.refs_0_, ...), custom_call_target="tpu_custom_call" | custom-call | flops 17179869184 | bytes 67108864 | tf_op jit(solution)/shard_map/pallas_call | solution.py:73
  12.8 0.3 collective-permute-start.3
  13.0 0.5 %shard_map.90.refs_3_.refs_1_ = f32[1024,256]{1,0:T(8,128)S(1)} custom-call(bf16[1024,2048]{1,0:T(8,128)(2,1)S(1)} %get-tuple-element.47.refs_0_, bf16[1024,256]{1,0:T(8,128)(2,1)S(1)} %get-tuple-element.48.refs_1_), custom_call_target="tpu_custom_call" | custom-call | flops 5726623232 | bytes 16777216 | tf_op jit(solution)/shard_map/pallas_call | solution.py:73
  13.6 0.5 %collective-permute-done.3.refs_2_ = bf16[128,256]{1,0:T(8,128)(2,1)S(1)} collective-permute-done((bf16[128,256]{1,0:T(8,128)(2,1)S(1)}, bf16[128,256]{1,0:T(8,128)(2,1)S(1)}, u32[]{:S(2)}, u32[]{:S(2)}) %collective-permute-start.3) | collective-permute-done | bytes 65568 | tf_op jit(solution)/shard_map/ppermute | solution.py:323
  14.1 0.3 collective-permute-start.4
  14.4 2.9 %collective-permute-start.6 = (bf16[128,256]{1,0:T(8,128)(2,1)S(1)}, bf16[128,256]{1,0:T(8,128)(2,1)S(1)}, u32[]{:S(2)}, u32[]{:S(2)}) collective-permute-start(bf16[128,256]{1,0:T(8,128)(2,1)S(1)} %get-tuple-element.52.refs_3_.refs_0_), channel_id=1, source_target_pairs={{0,2},{2,0},{4,6},{6,4},{8,10},{10,8},{12,14},{14,12},{16,18},{18,... | collective-permute-start | bytes 196616 | tf_op jit(solution)/shard_map/ppermute | solution.py:352
  17.3 0.0 collective-permute-done.4.refs_2_
  17.3 0.8 %shard_map.92 = (f32[256,1024]{1,0:T(8,128)S(1)}, bf16[1,256,1024]{2,1,0:T(8,128)(2,1)S(1)}) custom-call(bf16[1024,2048]{1,0:T(8,128)(2,1)S(1)} %get-tuple-element.47.refs_0_, f32[1024,256]{1,0:T(8,128)S(1)} %shard_map.90.refs_3_.refs_1_, bf16[1024,256]{1,0:T(8,128)(2,1)S(1)} %collective-permute-done.4.refs_2_, ...), custom_call_target="tpu_custom_call" | custom-call | flops 25769803776 | bytes 67108864 | tf_op jit(solution)/shard_map/pallas_call | solution.py:73
  18.2 1.5 %collective-permute-start.5 = (bf16[256,1024]{1,0:T(8,128)(2,1)S(1)}, bf16[256,1024]{1,0:T(8,128)(2,1)S(1)}, u32[]{:S(2)}, u32[]{:S(2)}) collective-permute-start(bf16[256,1024]{1,0:T(8,128)(2,1)S(1)} %bitcast.12), channel_id=1, source_target_pairs={{0,1},{1,0},{2,3},{3,2},{4,5},{5,4},{6,7},{7,6},{8,9},{9,8},{10,11... | collective-permute-start | bytes 1572872 | tf_op jit(solution)/shard_map/ppermute | solution.py:323
  19.7 0.2 collective-permute-done.6.refs_1_
  19.9 1.3 %shard_map.94 = (f32[256,1024]{1,0:T(8,128)S(1)}, bf16[1,256,1024]{2,1,0:T(8,128)(2,1)S(1)}) custom-call(bf16[1024,2048]{1,0:T(8,128)(2,1)S(1)} %get-tuple-element.41.refs_0_, bf16[256,2048]{1,0:T(8,128)(2,1)S(1)} %get-tuple-element.45.refs_1_, bf16[256,1024]{1,0:T(8,128)(2,1)S(1)} %get-tuple-element.55.refs_2_.refs_1_, ...), custom_call_target="tpu_custom_call" | custom-call | flops 17179869184 | bytes 67108864 | tf_op jit(solution)/shard_map/pallas_call | solution.py:73
  21.2 0.0 collective-permute-done.5.refs_4_
  21.2 1.3 %shard_map.95 = (f32[256,1024]{1,0:T(8,128)S(1)}, f32[256,1024]{1,0:T(8,128)S(1)}, bf16[1,256,1024]{2,1,0:T(8,128)(2,1)S(1)}) custom-call(bf16[1024,2048]{1,0:T(8,128)(2,1)S(1)} %get-tuple-element.41.refs_0_, bf16[256,2048]{1,0:T(8,128)(2,1)S(1)} %get-tuple-element.45.refs_1_, f32[8,128]{1,0:T(8,128)S(1)} %get-tuple-element.46.refs_2_, ...), custom_call_target="tpu_custom_call" | custom-call | flops 17179869184 | bytes 67108864 | tf_op jit(solution)/shard_map/pallas_call | solution.py:73
  22.5 0.4 %collective-permute-start.7 = (bf16[256,1024]{1,0:T(8,128)(2,1)S(1)}, bf16[256,1024]{1,0:T(8,128)(2,1)S(1)}, u32[]{:S(2)}, u32[]{:S(2)}) collective-permute-start(bf16[256,1024]{1,0:T(8,128)(2,1)S(1)} %bitcast.9), channel_id=1, source_target_pairs={{0,1},{1,0},{2,3},{3,2},{4,5},{5,4},{6,7},{7,6},{8,9},{9,8},{10,11... | collective-permute-start | bytes 1572872 | tf_op jit(solution)/shard_map/ppermute | solution.py:323
  23.0 1.9 %collective-permute-start.8 = (bf16[128,256]{1,0:T(8,128)(2,1)S(1)}, bf16[128,256]{1,0:T(8,128)(2,1)S(1)}, u32[]{:S(2)}, u32[]{:S(2)}) collective-permute-start(bf16[128,256]{1,0:T(8,128)(2,1)S(1)} %shard_map.93.refs_3_.refs_0_), channel_id=1, source_target_pairs={{0,4},{2,6},{4,0},{6,2},{8,12},{10,14},{12,8},{14,10},{16,20},{18,... | collective-permute-start | bytes 196616 | tf_op jit(solution)/shard_map/ppermute | solution.py:352
  24.9 0.0 collective-permute-start.10
  24.9 2.4 %collective-permute-done.8.refs_1_ = bf16[128,256]{1,0:T(8,128)(2,1)S(1)} collective-permute-done((bf16[128,256]{1,0:T(8,128)(2,1)S(1)}, bf16[128,256]{1,0:T(8,128)(2,1)S(1)}, u32[]{:S(2)}, u32[]{:S(2)}) %collective-permute-start.8) | collective-permute-done | bytes 65568 | tf_op jit(solution)/shard_map/ppermute | solution.py:352
  27.3 2.0 %collective-permute-start.11 = (bf16[128,256]{1,0:T(8,128)(2,1)S(1)}, bf16[128,256]{1,0:T(8,128)(2,1)S(1)}, u32[]{:S(2)}, u32[]{:S(2)}) collective-permute-start(bf16[128,256]{1,0:T(8,128)(2,1)S(1)} %shard_map.96.refs_4_.refs_0_), channel_id=1, source_target_pairs={{0,8},{2,10},{4,12},{6,14},{8,0},{10,2},{12,4},{14,6},{16,24},{18,... | collective-permute-start | bytes 196616 | tf_op jit(solution)/shard_map/ppermute | solution.py:352
  29.3 0.0 collective-permute-done.7.refs_3_
  29.3 0.9 %shard_map.97 = (f32[256,1024]{1,0:T(8,128)S(1)}, bf16[1,256,1024]{2,1,0:T(8,128)(2,1)S(1)}) custom-call(bf16[1024,2048]{1,0:T(8,128)(2,1)S(1)} %get-tuple-element.36.refs_0_, f32[256,1024]{1,0:T(8,128)S(1)} %get-tuple-element.40.refs_1_, f32[256,1024]{1,0:T(8,128)S(1)} %get-tuple-element.57.refs_2_, bf16[256,1024]{1,0:T(8,128)(2,1)S(1)} %collective-permute-done.7.refs_3_, ...), custom_call_target="tpu_custom_call" | custom-call | flops 17179869184 | bytes 67108864 | tf_op jit(solution)/shard_map/pallas_call | solution.py:73
  30.2 1.4 %collective-permute-done.11.refs_1_ = bf16[128,256]{1,0:T(8,128)(2,1)S(1)} collective-permute-done((bf16[128,256]{1,0:T(8,128)(2,1)S(1)}, bf16[128,256]{1,0:T(8,128)(2,1)S(1)}, u32[]{:S(2)}, u32[]{:S(2)}) %collective-permute-start.11) | collective-permute-done | bytes 65568 | tf_op jit(solution)/shard_map/ppermute | solution.py:352
  31.6 0.0 collective-permute-done.10.refs_3_
  31.6 0.0 copy-start
  31.7 0.0 copy-start.1
  31.7 1.1 %shard_map.99 = (f32[256,1024]{1,0:T(8,128)S(1)}, bf16[1,256,1024]{2,1,0:T(8,128)(2,1)S(1)}) custom-call(bf16[1024,2048]{1,0:T(8,128)(2,1)S(1)} %get-tuple-element.36.refs_0_, bf16[256,1024]{1,0:T(8,128)(2,1)S(1)} %get-tuple-element.62.refs_1_, f32[256,1024]{1,0:T(8,128)S(1)} %get-tuple-element.56.refs_5_.refs_2_, ...), custom_call_target="tpu_custom_call" | custom-call | flops 17179869184 | bytes 67108864 | tf_op jit(solution)/shard_map/pallas_call | solution.py:73
  32.8 0.1 collective-permute-start.12
  32.9 3.0 %collective-permute-start.13 = (bf16[128,256]{1,0:T(8,128)(2,1)S(1)}, bf16[128,256]{1,0:T(8,128)(2,1)S(1)}, u32[]{:S(2)}, u32[]{:S(2)}) collective-permute-start(bf16[128,256]{1,0:T(8,128)(2,1)S(1)} %shard_map.98.refs_4_.refs_1_), channel_id=1, source_target_pairs={{0,16},{2,18},{4,20},{6,22},{8,24},{10,26},{12,28},{14,30},{16,0},... | collective-permute-start | bytes 196616 | tf_op jit(solution)/shard_map/ppermute | solution.py:352
  35.9 0.2 collective-permute-start.9
  36.0 0.0 collective-permute-done.12.refs_5_
  36.1 0.0 copy-done
  36.1 0.0 copy-done.1
  36.1 1.1 %shard_map.100 = (f32[1024,256]{1,0:T(8,128)S(1)}, bf16[1024,256]{1,0:T(8,128)(2,1)S(1)}, bf16[1024,256]{1,0:T(8,128)(2,1)S(1)}, f32[128,256]{1,0:T(8,128)S(1)}) custom-call(f32[256,1024]{1,0:T(8,128)S(1)} %get-tuple-element.59.refs_2_.refs_0_, bf16[256,1024]{1,0:T(8,128)(2,1)S(1)} %get-tuple-element.55.refs_2_.refs_1_, ...), custom_call_target="tpu_custom_call" | custom-call | flops 17179869184 | bytes 67108864 | tf_op jit(solution)/shard_map/pallas_call | solution.py:73
  37.2 0.6 %collective-permute-done.9.refs_1_ = bf16[256,1024]{1,0:T(8,128)(2,1)S(1)} collective-permute-done((bf16[256,1024]{1,0:T(8,128)(2,1)S(1)}, bf16[256,1024]{1,0:T(8,128)(2,1)S(1)}, u32[]{:S(2)}, u32[]{:S(2)}) %collective-permute-start.9) | collective-permute-done | bytes 524320 | tf_op jit(solution)/shard_map/ppermute | solution.py:323
  37.8 0.3 shard_map.101.refs_3_.refs_0_
  38.1 1.8 %collective-permute-done.13.refs_2_ = bf16[128,256]{1,0:T(8,128)(2,1)S(1)} collective-permute-done((bf16[128,256]{1,0:T(8,128)(2,1)S(1)}, bf16[128,256]{1,0:T(8,128)(2,1)S(1)}, u32[]{:S(2)}, u32[]{:S(2)}) %collective-permute-start.13) | collective-permute-done | bytes 65568 | tf_op jit(solution)/shard_map/ppermute | solution.py:352
  40.0 0.1 collective-permute-start.14
  40.1 1.1 %shard_map.103.refs_6_ = f32[256,128]{1,0:T(8,128)} custom-call(bf16[256,256]{1,0:T(8,128)(2,1)S(1)} %copy-done.1, bf16[128,256]{1,0:T(8,128)(2,1)S(1)} %shard_map.102.refs_1_.refs_4_), custom_call_target="tpu_custom_call" | custom-call | flops 17179869184 | bytes 67108864 | tf_op jit(solution)/shard_map/pallas_call | solution.py:73
  41.1 0.2 collective-permute-done.14.refs_5_
  41.3 0.0 copy-start.2
  41.3 0.9 %copy-done.2 = f32[256,128]{1,0:T(8,128)S(1)} copy-done((f32[256,128]{1,0:T(8,128)S(1)}, f32[256,128]{1,0:T(8,128)}, u32[]{:S(2)}) %copy-start.2) | copy-done | bytes 131096
  42.2 1.3 %shard_map.104 = bf16[2,1024,256]{2,1,0:T(8,128)(2,1)} custom-call(f32[1024,256]{1,0:T(8,128)S(1)} %shard_map.101.refs_3_.refs_0_, f32[1024,256]{1,0:T(8,128)S(1)} %get-tuple-element.67.refs_1_, bf16[1024,256]{1,0:T(8,128)(2,1)S(1)} %get-tuple-element.68.refs_2_, bf16[1024,256]{1,0:T(8,128)(2,1)S(1)} %get-tuple-element.69.refs_3_, ...), custom_call_target="tpu_custom_call" | custom-call | flops 4294967296 | bytes 67108864 | tf_op jit(solution)/shard_map/pallas_call | solution.py:73
  (5 shorter events, 0.1 us)
Async XLA Ops:
  0.6 5.6 %collective-permute-start = (bf16[2,1024,256]{2,1,0:T(8,128)(2,1)}, bf16[2,1024,256]{2,1,0:T(8,128)(2,1)S(1)}, u32[]{:S(2)}, u32[]{:S(2)}) collective-permute-start(bf16[2,1024,256]{2,1,0:T(8,128)(2,1)} %refs_3_.4), channel_id=1, source_target_pairs={{0,1},{1,0},{2,3},{3,2},{4,5},{5,4},{6,7},{7,6},{8,9},{9,8},{10,11... | collective-permute-start | bytes 3145736 | tf_op jit(solution)/shard_map/ppermute | solution.py:323
  4.9 4.3 %collective-permute-start.2 = (bf16[256,1024]{1,0:T(8,128)(2,1)S(1)}, bf16[256,1024]{1,0:T(8,128)(2,1)S(1)}, u32[]{:S(2)}, u32[]{:S(2)}) collective-permute-start(bf16[256,1024]{1,0:T(8,128)(2,1)S(1)} %bitcast.10), channel_id=1, source_target_pairs={{0,1},{1,0},{2,3},{3,2},{4,5},{5,4},{6,7},{7,6},{8,9},{9,8},{10,11... | collective-permute-start | bytes 1572872 | tf_op jit(solution)/shard_map/ppermute | solution.py:323
  7.5 2.0 %collective-permute-start.1 = (bf16[1024,256]{1,0:T(8,128)(2,1)S(1)}, bf16[1024,256]{1,0:T(8,128)(2,1)S(1)}, u32[]{:S(2)}, u32[]{:S(2)}) collective-permute-start(bf16[1024,256]{1,0:T(8,128)(2,1)S(1)} %get-tuple-element.42.refs_2_), channel_id=1, source_target_pairs={{0,1},{1,0},{2,3},{3,2},{4,5},{5,4},{6,7},{7,6},{8,9},{9,8},{10,11... | collective-permute-start | bytes 1572872 | tf_op jit(solution)/shard_map/ppermute | solution.py:323
  12.8 1.3 %collective-permute-start.3 = (bf16[128,256]{1,0:T(8,128)(2,1)S(1)}, bf16[128,256]{1,0:T(8,128)(2,1)S(1)}, u32[]{:S(2)}, u32[]{:S(2)}) collective-permute-start(bf16[128,256]{1,0:T(8,128)(2,1)S(1)} %bitcast.13), channel_id=1, source_target_pairs={{0,1},{1,0},{2,3},{3,2},{4,5},{5,4},{6,7},{7,6},{8,9},{9,8},{10,11... | collective-permute-start | bytes 196616 | tf_op jit(solution)/shard_map/ppermute | solution.py:323
  14.1 3.2 %collective-permute-start.4 = (bf16[1024,256]{1,0:T(8,128)(2,1)S(1)}, bf16[1024,256]{1,0:T(8,128)(2,1)S(1)}, u32[]{:S(2)}, u32[]{:S(2)}) collective-permute-start(bf16[1024,256]{1,0:T(8,128)(2,1)S(1)} %get-tuple-element.51), channel_id=1, source_target_pairs={{0,1},{1,0},{2,3},{3,2},{4,5},{5,4},{6,7},{7,6},{8,9},{9,8},{10,11... | collective-permute-start | bytes 1572872 | tf_op jit(solution)/shard_map/ppermute | solution.py:323
  14.4 5.5 %collective-permute-start.6 = (bf16[128,256]{1,0:T(8,128)(2,1)S(1)}, bf16[128,256]{1,0:T(8,128)(2,1)S(1)}, u32[]{:S(2)}, u32[]{:S(2)}) collective-permute-start(bf16[128,256]{1,0:T(8,128)(2,1)S(1)} %get-tuple-element.52.refs_3_.refs_0_), channel_id=1, source_target_pairs={{0,2},{2,0},{4,6},{6,4},{8,10},{10,8},{12,14},{14,12},{16,18},{18,... | collective-permute-start | bytes 196616 | tf_op jit(solution)/shard_map/ppermute | solution.py:352
  18.2 3.0 %collective-permute-start.5 = (bf16[256,1024]{1,0:T(8,128)(2,1)S(1)}, bf16[256,1024]{1,0:T(8,128)(2,1)S(1)}, u32[]{:S(2)}, u32[]{:S(2)}) collective-permute-start(bf16[256,1024]{1,0:T(8,128)(2,1)S(1)} %bitcast.12), channel_id=1, source_target_pairs={{0,1},{1,0},{2,3},{3,2},{4,5},{5,4},{6,7},{7,6},{8,9},{9,8},{10,11... | collective-permute-start | bytes 1572872 | tf_op jit(solution)/shard_map/ppermute | solution.py:323
  22.5 6.8 %collective-permute-start.7 = (bf16[256,1024]{1,0:T(8,128)(2,1)S(1)}, bf16[256,1024]{1,0:T(8,128)(2,1)S(1)}, u32[]{:S(2)}, u32[]{:S(2)}) collective-permute-start(bf16[256,1024]{1,0:T(8,128)(2,1)S(1)} %bitcast.9), channel_id=1, source_target_pairs={{0,1},{1,0},{2,3},{3,2},{4,5},{5,4},{6,7},{7,6},{8,9},{9,8},{10,11... | collective-permute-start | bytes 1572872 | tf_op jit(solution)/shard_map/ppermute | solution.py:323
  23.0 4.3 %collective-permute-start.8 = (bf16[128,256]{1,0:T(8,128)(2,1)S(1)}, bf16[128,256]{1,0:T(8,128)(2,1)S(1)}, u32[]{:S(2)}, u32[]{:S(2)}) collective-permute-start(bf16[128,256]{1,0:T(8,128)(2,1)S(1)} %shard_map.93.refs_3_.refs_0_), channel_id=1, source_target_pairs={{0,4},{2,6},{4,0},{6,2},{8,12},{10,14},{12,8},{14,10},{16,20},{18,... | collective-permute-start | bytes 196616 | tf_op jit(solution)/shard_map/ppermute | solution.py:352
  24.9 6.8 %collective-permute-start.10 = (bf16[256,1024]{1,0:T(8,128)(2,1)S(1)}, bf16[256,1024]{1,0:T(8,128)(2,1)S(1)}, u32[]{:S(2)}, u32[]{:S(2)}) collective-permute-start(bf16[256,1024]{1,0:T(8,128)(2,1)S(1)} %bitcast.7), channel_id=1, source_target_pairs={{0,1},{1,0},{2,3},{3,2},{4,5},{5,4},{6,7},{7,6},{8,9},{9,8},{10,11... | collective-permute-start | bytes 1572872 | tf_op jit(solution)/shard_map/ppermute | solution.py:323
  27.3 4.3 %collective-permute-start.11 = (bf16[128,256]{1,0:T(8,128)(2,1)S(1)}, bf16[128,256]{1,0:T(8,128)(2,1)S(1)}, u32[]{:S(2)}, u32[]{:S(2)}) collective-permute-start(bf16[128,256]{1,0:T(8,128)(2,1)S(1)} %shard_map.96.refs_4_.refs_0_), channel_id=1, source_target_pairs={{0,8},{2,10},{4,12},{6,14},{8,0},{10,2},{12,4},{14,6},{16,24},{18,... | collective-permute-start | bytes 196616 | tf_op jit(solution)/shard_map/ppermute | solution.py:352
  31.6 4.4 %copy-start = (f32[256,128]{1,0:T(8,128)S(1)}, f32[256,128]{1,0:T(8,128)}, u32[]{:S(2)}) copy-start(f32[256,128]{1,0:T(8,128)} %refs_3_.5) | copy-start | bytes 393220
  31.7 4.4 %copy-start.1 = (bf16[256,256]{1,0:T(8,128)(2,1)S(1)}, bf16[256,256]{1,0:T(8,128)(2,1)}, u32[]{:S(2)}) copy-start(bf16[256,256]{1,0:T(8,128)(2,1)} %refs_0_.5) | copy-start | bytes 393220
  32.8 3.3 %collective-permute-start.12 = (bf16[256,1024]{1,0:T(8,128)(2,1)S(1)}, bf16[256,1024]{1,0:T(8,128)(2,1)S(1)}, u32[]{:S(2)}, u32[]{:S(2)}) collective-permute-start(bf16[256,1024]{1,0:T(8,128)(2,1)S(1)} %bitcast.11), channel_id=1, source_target_pairs={{0,1},{1,0},{2,3},{3,2},{4,5},{5,4},{6,7},{7,6},{8,9},{9,8},{10,11... | collective-permute-start | bytes 1572872 | tf_op jit(solution)/shard_map/ppermute | solution.py:323
  32.9 7.1 %collective-permute-start.13 = (bf16[128,256]{1,0:T(8,128)(2,1)S(1)}, bf16[128,256]{1,0:T(8,128)(2,1)S(1)}, u32[]{:S(2)}, u32[]{:S(2)}) collective-permute-start(bf16[128,256]{1,0:T(8,128)(2,1)S(1)} %shard_map.98.refs_4_.refs_1_), channel_id=1, source_target_pairs={{0,16},{2,18},{4,20},{6,22},{8,24},{10,26},{12,28},{14,30},{16,0},... | collective-permute-start | bytes 196616 | tf_op jit(solution)/shard_map/ppermute | solution.py:352
  35.9 1.9 %collective-permute-start.9 = (bf16[256,1024]{1,0:T(8,128)(2,1)S(1)}, bf16[256,1024]{1,0:T(8,128)(2,1)S(1)}, u32[]{:S(2)}, u32[]{:S(2)}) collective-permute-start(bf16[256,1024]{1,0:T(8,128)(2,1)S(1)} %bitcast.8), channel_id=1, source_target_pairs={{0,1},{1,0},{2,3},{3,2},{4,5},{5,4},{6,7},{7,6},{8,9},{9,8},{10,11... | collective-permute-start | bytes 1572872 | tf_op jit(solution)/shard_map/ppermute | solution.py:323
  40.0 1.3 %collective-permute-start.14 = (bf16[128,256]{1,0:T(8,128)(2,1)S(1)}, bf16[128,256]{1,0:T(8,128)(2,1)S(1)}, u32[]{:S(2)}, u32[]{:S(2)}) collective-permute-start(bf16[128,256]{1,0:T(8,128)(2,1)S(1)} %shard_map.102.refs_1_.refs_4_), channel_id=1, source_target_pairs={{0,1},{1,0},{2,3},{3,2},{4,5},{5,4},{6,7},{7,6},{8,9},{9,8},{10,11... | collective-permute-start | bytes 196616 | tf_op jit(solution)/shard_map/ppermute | solution.py:323
  41.3 0.9 %copy-start.2 = (f32[256,128]{1,0:T(8,128)S(1)}, f32[256,128]{1,0:T(8,128)}, u32[]{:S(2)}) copy-start(f32[256,128]{1,0:T(8,128)} %shard_map.103.refs_6_) | copy-start | bytes 393220

commit v7 on v6

--- a/solution.py
+++ b/solution.py
@@ -37,7 +37,8 @@
     nodes = n_space * rows
     tile = 256 if rows % 256 == 0 else rows
     tiles = rows // tile
-    quarter = rows // 4
+    eighth = rows // 8
+    head = rows - eighth
     width = columns // n_space
     peers = range(1, n_space)
 
@@ -52,13 +53,13 @@
         owner = lax.rem(at_core() - step + n_space, n_space)
         return pl.ds(pl.multiple_of(owner * width, width), width)
 
-    def call(body, outs, args, flops, moved, places=None, scratch=(), after=None, aliases=None):
+    def call(body, outs, args, cover, places=None, scratch=(), after=None, aliases=None, after_place=pl.ANY):
         places = dict(places or {})
         args = list(args)
         count = len(args)
         if after is not None:
             args.append(after)
-            places[count] = pl.ANY
+            places[count] = after_place
 
         def run(*refs):
             body(*refs[:count], *refs[len(args) :])
@@ -81,7 +82,7 @@
             scratch_shapes=list(scratch),
             input_output_aliases=aliases or {},
             cost_estimate=pl.CostEstimate(
-                flops=16 * flops, bytes_accessed=16 * moved, transcendentals=0
+                flops=int(cover * 1e9), bytes_accessed=0, transcendentals=0
             ),
             compiler_params=pltpu.CompilerParams(vmem_limit_bytes=16 * MIB),
         )(*args)
@@ -102,10 +103,9 @@
             own_ref[:, at : at + tile] = dot(left[:, at:], factor[at:, block(0, at, tile)])
 
     def full_rows(left, factor, tail, own_ref, other_ref):
-        at = rows - quarter
         for step in (*peers, 0):
-            product = dot(left[:, :at], factor[:at, block(step)])
-            product = product + dot(left[:, at:], tail[:, block(step)])
+            product = dot(left[:, :head], factor[:head, block(step)])
+            product = product + dot(left[:, head:], tail[:, block(step)])
             if step:
                 other_ref[step - 1] = product.astype(BF)
             else:
@@ -129,8 +129,8 @@
 
     def start_kernel(
         diag, arrow, noise, lengths,
-        d0, d1, own, other, first, mask,
-        e1, n0, live_scratch, sem1, sem0, sems,
+        d0, d1, own, other, n0, mask,
+        e1, live_scratch, sem1, sem0, sems,
     ):
         arrow_copy = pltpu.make_async_copy(arrow.at[1], e1, sems.at[0])
         noise_copy = pltpu.make_async_copy(noise.at[0], n0, sems.at[1])
@@ -162,7 +162,6 @@
         arrow_copy.start()
         for i in range(tiles):
             each(copies1, i, lambda copy: copy.start(priority=i % 2))
-        noise_copy.start()
         live_copy.wait()
         arrow_copy.wait()
         live = live_scratch[lax.axis_index("tm")] > 1
@@ -171,39 +170,34 @@
         for i in range(tiles):
             each(copies1, i, lambda copy: copy.wait())
             each(copies0, i, lambda copy: copy.start(priority=i % 2))
+        noise_copy.start()
         lower_rows(e1, d1, own, other)
+        for i in range(tiles):
+            each(copies0, i, lambda copy: copy.wait())
         noise_copy.wait()
-        lower_own(d0, n0, first, lambda i: copies0[0, i].wait())
-        for step in peers:
-
-            @pl.when(at_core() >= step)
-            def _():
-                for i in range(tiles):
-                    copies0[step, i].wait()
-
-    def k1_copies(coupling, k1, quarters, sems):
-        copies = {}
-        for i, q in enumerate(quarters):
-            part = pl.ds(q * quarter, quarter)
+
+    def k1_copies(coupling, k1, first, count, sems):
+        copies = []
+        for i in range(count):
+            part = pl.ds((first + i) * eighth, eighth)
             target = k1.at[part] if k1.shape[0] == rows else k1
-            copies[q] = pltpu.make_async_copy(coupling.at[1, part], target, sems.at[i])
+            copies.append(pltpu.make_async_copy(coupling.at[1, part], target, sems.at[i]))
+            copies[-1].start(priority=i % 2)
         return copies
 
-    def first_value_kernel(d0, value, coupling, *refs):
+    def first_value_kernel(d0, n0, coupling, *refs):
         got, (out, bar, k1, sems) = refs[: n_space - 1], refs[n_space - 1 :]
-        copies = k1_copies(coupling, k1, [0], sems)
-        copies[0].start()
-        out[...] = value[...]
+        copies = k1_copies(coupling, k1, 0, 3, sems)
+        lower_own(d0, n0, out)
         lower_rest(d0, [piece.at[0] for piece in got], out)
         bar[...] = out[...].astype(BF)
-        copies[0].wait()
+        for copy in copies:
+            copy.wait()
 
     def load_kernel(coupling, value, _, value_rows, k1, sems):
-        copies = k1_copies(coupling, k1, [1, 2], sems)
-        for q, copy in copies.items():
-            copy.start(priority=q % 2)
+        copies = k1_copies(coupling, k1, 3, 4, sems)
         value_rows[...] = value[...].T
-        for copy in copies.values():
+        for copy in copies:
             copy.wait()
 
     def target_kernel(k1, coupling, bar, noise, arrow, own, *refs):
@@ -212,11 +206,9 @@
         tail, target, part_own, part_other, response, e0, n1, whole, sems = refs
         noise_copy = pltpu.make_async_copy(noise.at[1], n1, sems.at[1])
         arrow_copy = pltpu.make_async_copy(arrow.at[0], e0, sems.at[2])
-        copies = k1_copies(coupling, tail, [3], sems)
         noise_copy.start()
-        copies[3].start(priority=1)
+        (tail_copy,) = k1_copies(coupling, tail, 7, 1, sems)
         arrow_copy.start()
-        at = rows - quarter
 
         def pull(factor, part, before):
             pulled = dot(factor[:, block(0)], bar[...])
@@ -226,9 +218,9 @@
             target[part] = (n1[part].astype(F32) - pulled).astype(BF)
 
         response[...] = total_of(own, got_own).astype(BF)
-        pull(k1.at[:at], pl.ds(0, at), noise_copy)
-        copies[3].wait()
-        pull(tail, pl.ds(at, quarter), arrow_copy)
+        pull(k1.at[:head], pl.ds(0, head), noise_copy)
+        tail_copy.wait()
+        pull(tail, pl.ds(head, eighth), arrow_copy)
         whole[...] = (dot(e0[...], bar[...]) + dot(response[...], target[...])).T
         part_own[...] = whole[part_rows(0)]
         for step in peers:
@@ -272,18 +264,18 @@
         left = (value_rows[...] - total_of(passed, got)).astype(BF)
         lower_rows(left, d0, own, other)
 
-    def turn_kernel(base, response, first, noise_fixed, tip, *refs):
-        got, (last_base, last_resp, first_resp, noise_rows) = refs[: n_space - 1], refs[n_space - 1 :]
+    def through_tip(tip, right):
+        inner = dot(tip, right).astype(BF)
+        return dot(tip.astype(F32).T.astype(BF), inner).T.astype(BF)
+
+    def turn_last_kernel(base, response, noise_fixed, tip, last_base, last_resp, noise_rows):
         noise_rows[...] = noise_fixed[...].T
         last_base[...] = base[...].T
-        upper = tip[...].astype(F32).T.astype(BF)
-
-        def through_tip(right):
-            inner = dot(tip[...], right).astype(BF)
-            return dot(upper, inner).T.astype(BF)
-
-        last_resp[...] = through_tip(response[...])
-        first_resp[...] = through_tip(total_of(first, got).astype(BF))
+        last_resp[...] = through_tip(tip[...], response[...])
+
+    def turn_response_kernel(first, tip, *refs):
+        got, out = refs[:-1], refs[-1]
+        out[...] = through_tip(tip[...], total_of(first, got).astype(BF))
 
     def turn_first_kernel(solved, *refs):
         got, out = refs[:-1], refs[-1]
@@ -328,11 +320,17 @@
     def send_down(values):
         return [swap(values[step - 1], step) for step in peers]
 
-    bits = [1 << i for i in range(n_tm.bit_length() - 1)]
-    assert n_tm == 1 << len(bits)
-
-    wide = 2 * rows * nodes * columns
-    factor_bytes = 2 * rows * nodes
+    steps = n_tm.bit_length() - 1
+    assert n_tm == 1 << steps
+
+    def swap_step(value, step):
+        pairs = []
+        for i in range(n_tm):
+            for core in range(n_space):
+                bit = 1 << (step + core * steps // n_space) % steps
+                pairs.append((i * n_space + core, (i ^ bit) * n_space + core))
+        return lax.ppermute(value, ("tm", "space"), pairs)
+
     node_f32, node_bf = shape_of((rows, columns), F32), shape_of((rows, columns), BF)
     flat_f32 = shape_of((columns, rows), F32)
     flat_others = shape_of((n_space - 1, columns, rows), BF)
@@ -348,21 +346,16 @@
         size = width * fixed_rows
         return call(fold_kernel, [part_bf], [sent, got], size, 6 * size, after=after)[0]
 
-    def swap_bit(value, bit):
-        return lax.ppermute(value, "tm", [(i, i ^ bit) for i in range(n_tm)])
-
     def on_device(diag_inverse, coupling, arrow, tip_inverse, noise, noise_fixed, section_lengths):
         got_noise = send_up(noise)
-        d0, d1, own, other, value, mask = call(
+        d0, d1, own, other, n0, mask = call(
             start_kernel,
-            [in_vmem, in_vmem, fixed_f32, fixed_others, node_f32, shape_of((8, 128), F32)],
+            [in_vmem, in_vmem, fixed_f32, fixed_others, node_bf, shape_of((8, 128), F32)],
             [diag_inverse, arrow, noise, section_lengths],
-            wide,
-            2 * factor_bytes,
+            8,
             {i: pltpu.HBM for i in range(4)},
             [
                 pltpu.VMEM((fixed_rows, rows), BF),
-                pltpu.VMEM((rows, columns), BF),
                 pltpu.SMEM(section_lengths.shape, jnp.int32),
                 dma((n_space, tiles)),
                 dma((n_space, tiles)),
@@ -373,27 +366,25 @@
         value, bar, k1 = call(
             first_value_kernel,
             [node_f32, node_bf, in_vmem],
-            [d0, value, coupling, *got_noise],
-            wide // 2,
-            factor_bytes,
+            [d0, n0, coupling, *got_noise],
+            8,
             {2: pltpu.HBM},
-            [dma((1,))],
+            [dma((3,))],
         )
         got_bar = send_up(bar)
         value_rows, k1 = call(
             load_kernel,
             [flat_f32, in_vmem],
             [coupling, value, k1],
-            wide // 8,
-            factor_bytes,
+            8,
             {0: pltpu.HBM, 2: pl.ANY, ("out", 1): pl.ANY},
-            [dma((2,))],
+            [dma((4,))],
             aliases={2: 1},
         )
         tail, target, part_own, part_other, response, e0 = call(
             target_kernel,
             [
-                pltpu.VMEM((quarter, nodes), BF),
+                pltpu.VMEM((eighth, nodes), BF),
                 node_bf,
                 shape_of((width, fixed_rows), F32),
                 shape_of((n_space - 1, width, fixed_rows), BF),
@@ -401,8 +392,7 @@
                 fixed_bf,
             ],
             [k1, coupling, bar, noise, arrow, own, *got_bar, *got_response],
-            wide,
-            factor_bytes,
+            8,
             {1: pltpu.HBM, 3: pltpu.HBM, 4: pltpu.HBM},
             [
                 pltpu.VMEM((rows, columns), BF),
@@ -411,59 +401,66 @@
             ],
         )
         got_parts = send_down(part_other)
-        (value,) = call(last_own_kernel, [node_f32], [d1, target], wide // 3, factor_bytes // 4)
+        (value,) = call(last_own_kernel, [node_f32], [d1, target], 8)
         sent, target = call(
             core_sum_kernel,
             [part_bf, node_bf],
             [part_own, target, *got_parts],
-            width * fixed_rows,
-            8 * width * fixed_rows,
+            0.2,
             {1: pl.ANY, ("out", 1): pl.ANY},
             aliases={1: 1},
             after=value,
         )
         got_target = send_up(target)
-        left = list(bits)
-        got = [swap_bit(sent, left.pop(0))] if left else []
-
-        def advance(after):
-            nonlocal sent, got
-            if left:
-                sent = fold(sent, *got, after)
-                got = [swap_bit(sent, left.pop(0))]
-
+        step = 0
+        got = []
+
+        def advance(after=None):
+            nonlocal sent, got, step
+            if step == steps:
+                return
+            if step:
+                (sent,) = call(fold_kernel, [part_bf], [sent, *got], 0.2, after=after)
+            got = [swap_step(sent, step)]
+            step += 1
+
+        advance()
         solved, other = call(
             last_solve_kernel,
             [flat_f32, flat_others],
             [d1, value, *got_target],
-            wide * 3 // 2,
-            factor_bytes,
+            8,
             scratch=[pltpu.VMEM((rows, columns), F32)],
             after=sent,
         )
         got_solved = send_down(other)
         advance(solved)
         pushed, other = call(
-            response_kernel, [fixed_f32, fixed_others], [k1, tail, response], wide, factor_bytes, after=sent
+            response_kernel, [fixed_f32, fixed_others], [k1, tail, response], 8, after=sent
         )
         got_pushed = send_down(other)
         base, passed, other = call(
             pass_kernel,
             [flat_f32, flat_f32, flat_others],
             [k1, tail, mask, solved, *got_solved],
-            wide,
-            factor_bytes,
+            8,
             after=pushed,
         )
         got_passed = send_down(other)
         advance(base)
+        last_base, last_resp, noise_rows = call(
+            turn_last_kernel,
+            [node_f32, by_node, shape_of((width, fixed_rows), F32)],
+            [base, response, noise_fixed, tip_inverse],
+            8,
+            after=sent,
+        )
         solved, other = call(
             first_solve_kernel,
             [flat_f32, flat_others],
             [d0, value_rows, passed, *got_passed],
-            wide,
-            factor_bytes,
-            after=sent,
+            8,
+            after=noise_rows,
         )
         got_solved = send_down(other)
         advance(solved)
@@ -471,46 +468,26 @@
             first_response_kernel,
             [fixed_f32, fixed_others],
             [d0, e0, pushed, *got_pushed],
-            wide,
-            factor_bytes,
+            8,
             after=sent,
         )
         got_first = send_down(other)
-        last_base, last_resp, first_resp, noise_rows = call(
-            turn_kernel,
-            [node_f32, by_node, by_node, shape_of((width, fixed_rows), F32)],
-            [base, response, first, noise_fixed, tip_inverse, *got_first],
-            wide,
-            factor_bytes,
-            after=first,
-        )
-        (first_base,) = call(
-            turn_first_kernel, [node_f32], [solved, *got_solved], wide, factor_bytes, after=noise_rows
-        )
-        while left:
-            advance(None)
-        (mixed,) = call(
-            mixed_kernel,
-            [part_bf],
-            [noise_rows, sent, *got],
-            width * fixed_rows,
-            8 * width * fixed_rows,
-            after=first_base,
-        )
+        (first_base,) = call(turn_first_kernel, [node_f32], [solved, *got_solved], 8, after=first)
+        (first_resp,) = call(
+            turn_response_kernel, [by_node], [first, tip_inverse, *got_first], 8, after=first_base
+        )
+        while step < steps:
+            advance()
+        (mixed,) = call(mixed_kernel, [part_bf], [noise_rows, sent, *got], 0.2, after=first_resp)
         got_mixed = send_up(mixed)
         (fixed_out,) = call(
-            fixed_kernel,
-            [shape_of((fixed_rows, width), F32)],
-            [tip_inverse, mixed],
-            wide,
-            factor_bytes,
+            fixed_kernel, [shape_of((fixed_rows, width), F32)], [tip_inverse, mixed], 8
         )
         (sample,) = call(
             lambda a, b, c, d, *refs: final_kernel((a, b), (c, d), *refs),
             [shape_of((2, rows, columns), BF)],
             [first_base, last_base, first_resp, last_resp, mixed, *got_mixed],
-            4 * rows * fixed_rows * columns,
-            factor_bytes,
+            8,
             {("out", 0): pl.ANY},
             [
                 pltpu.VMEM((columns, fixed_rows), BF),
@@ -518,6 +495,7 @@
                 dma((2, tiles)),
             ],
             after=fixed_out,
+            after_place=pltpu.HBM,
         )
         return (sample, fixed_out)
 

time: 44 us -> 40.1 us (0.911)
  waiting for transfers between devices: 7.54 us -> 4.51 us
  local copies, waits for them, and re-layouts: 0.92 us -> 0.01 us
  Pallas kernels: 19.7 us -> 20.5 us
  starting transfers between devices: 14.6 us -> 13.9 us
    ppermute x4, waiting for transfers between devices: 5.88 us -> 1.41 us  [swap_step(): return lax.ppermute(value, ('tm', 'space'), pairs)]
    ppermute x11, waiting for transfers between devices: 1.66 us -> 3.1 us  [swap(): return lax.ppermute(value, 'space', pairs)]
    unnamed x6 -> x4, local copies, waits for them, and re-layouts: 0.92 us -> 0.01 us
    pallas_call x19 -> x20, Pallas kernels: 19.7 us -> 20.5 us  [call(): pl.pallas_call(run, in_specs=specs, out_specs=[pl.BlockSpec(memory_space=...]
    ppermute x4, starting transfers between devices: 9.86 us -> 9.16 us  [swap_step(): return lax.ppermute(value, ('tm', 'space'), pairs)]
  transfers between devices with their start and end apart: 15 -> 15, of which waited for: 8 -> 5; matrix products, arithmetic and copies ran while one was open for 0% -> 0% of each run, Pallas kernels for 29% -> 38%
where the time goes in v7:
time: 40.1 us; the launch traced here: 39.9 us
  Pallas kernels  20.5 us (51%)
  starting transfers between devices  13.9 us (35%)
  waiting for transfers between devices  4.51 us (11%)
  between operations  0.99 us (2%)
    pallas_call x20, Pallas kernels, call(): pl.pallas_call(run, in_specs=specs, out_specs=[pl.BlockSpec(memory_space=...  20.5 us
    ppermute x4, starting transfers between devices, swap_step(): return lax.ppermute(value, ('tm', 'space'), pairs)  9.16 us
    ppermute x11, starting transfers between devices, swap(): return lax.ppermute(value, 'space', pairs)  4.73 us
    ppermute x11, waiting for transfers between devices, swap(): return lax.ppermute(value, 'space', pairs)  3.1 us
    ppermute x4, waiting for transfers between devices, swap_step(): return lax.ppermute(value, ('tm', 'space'), pairs)  1.41 us
  transfers between devices with their start and end apart: 15, of which 5 were waited for; matrix products, arithmetic and copies ran while one was open for 0% of the time, Pallas kernels for 38%

profile of v7, /device:TPU:0, one launch (start us, length us, event | category | flops | bytes accessed | tf_op | source)
XLA Modules:
  0.0 39.9 jit_solution(17940877427313844422)
XLA Ops:
  0.6 0.5 %collective-permute-start = (bf16[2,1024,256]{2,1,0:T(8,128)(2,1)}, bf16[2,1024,256]{2,1,0:T(8,128)(2,1)S(1)}, u32[]{:S(2)}, u32[]{:S(2)}) collective-permute-start(bf16[2,1024,256]{2,1,0:T(8,128)(2,1)} %refs_3_.4), channel_id=1, source_target_pairs={{0,1},{1,0},{2,3},{3,2},{4,5},{5,4},{6,7},{7,6},{8,9},{9,8},{10,11... | collective-permute-start | bytes 3145736 | tf_op jit(solution)/shard_map/ppermute | solution.py:315
  1.1 2.8 %shard_map.86 = (bf16[1024,2048]{1,0:T(8,128)(2,1)S(1)}, bf16[1024,2048]{1,0:T(8,128)(2,1)S(1)}, f32[256,1024]{1,0:T(8,128)S(1)}, bf16[1,256,1024]{2,1,0:T(8,128...) custom-call(bf16[2,1024,2048]{2,1,0:T(8,128)(2,1)} %refs_0_.3, bf16[2,256,1024]{2,1,0:T(8,128)(2,1)} %refs_4_.1, ...), custom_call_target="tpu_custom_call" | custom-call | flops 8000000000 | tf_op jit(solution)/shard_map/pallas_call | solution.py:74
  4.0 1.1 %collective-permute-start.2 = (bf16[256,1024]{1,0:T(8,128)(2,1)S(1)}, bf16[256,1024]{1,0:T(8,128)(2,1)S(1)}, u32[]{:S(2)}, u32[]{:S(2)}) collective-permute-start(bf16[256,1024]{1,0:T(8,128)(2,1)S(1)} %bitcast.9), channel_id=1, source_target_pairs={{0,1},{1,0},{2,3},{3,2},{4,5},{5,4},{6,7},{7,6},{8,9},{9,8},{10,11... | collective-permute-start | bytes 1572872 | tf_op jit(solution)/shard_map/ppermute | solution.py:315
  5.1 0.0 collective-permute-done.refs_3_
  5.1 1.7 %shard_map.87 = (f32[1024,256]{1,0:T(8,128)S(1)}, bf16[1024,256]{1,0:T(8,128)(2,1)S(1)}, bf16[1024,2048]{1,0:T(8,128)(2,1)S(1)}) custom-call(bf16[1024,2048]{1,0:T(8,128)(2,1)S(1)} %get-tuple-element.35.refs_0_, bf16[1024,256]{1,0:T(8,128)(2,1)S(1)} %get-tuple-element.36.refs_1_, bf16[2,1024,2048]{2,1,0:T(8,128)(2,1)} %refs_1_.4, ...), custom_call_target="tpu_custom_call" | custom-call | flops 8000000000 | tf_op jit(solution)/shard_map/pallas_call | solution.py:74
  6.8 0.1 collective-permute-start.1
  6.9 1.6 %shard_map.88 = (f32[256,1024]{1,0:T(8,128)S(1)}, bf16[1024,2048]{1,0:T(8,128)(2,1)S(1)}) custom-call(bf16[2,1024,2048]{2,1,0:T(8,128)(2,1)} %refs_1_.4, f32[1024,256]{1,0:T(8,128)S(1)} %get-tuple-element.37.refs_1_, bf16[1024,2048]{1,0:T(8,128)(2,1)S(1)} %get-tuple-element.38.refs_2_), custom_call_target="tpu_custom_call", output_to_operand_aliasing={{1}: (2, {})} | custom-call | flops 8000000000 | tf_op jit(solution)/shard_map/pallas_call | solution.py:74
  8.4 0.0 collective-permute-done.2.refs_7_
  8.4 0.3 collective-permute-done.1.refs_6_
  8.7 3.8 %shard_map.89 = (bf16[128,2048]{1,0:T(8,128)(2,1)S(1)}, bf16[1024,256]{1,0:T(8,128)(2,1)S(1)}, f32[128,256]{1,0:T(8,128)S(1)}, bf16[1,128,256]{2,1,0:T(8,128)(2,...) custom-call(bf16[1024,2048]{1,0:T(8,128)(2,1)S(1)} %get-tuple-element.40.refs_0_, ...), custom_call_target="tpu_custom_call" | custom-call | flops 8000000000 | tf_op jit(solution)/shard_map/pallas_call | solution.py:74
  12.6 0.3 collective-permute-start.3
  12.8 0.5 %shard_map.90.refs_3_.refs_1_ = f32[1024,256]{1,0:T(8,128)S(1)} custom-call(bf16[1024,2048]{1,0:T(8,128)(2,1)S(1)} %get-tuple-element.46.refs_0_, bf16[1024,256]{1,0:T(8,128)(2,1)S(1)} %get-tuple-element.47.refs_1_), custom_call_target="tpu_custom_call" | custom-call | flops 8000000000 | tf_op jit(solution)/shard_map/pallas_call | solution.py:74
  13.3 0.6 %collective-permute-done.3.refs_2_ = bf16[128,256]{1,0:T(8,128)(2,1)S(1)} collective-permute-done((bf16[128,256]{1,0:T(8,128)(2,1)S(1)}, bf16[128,256]{1,0:T(8,128)(2,1)S(1)}, u32[]{:S(2)}, u32[]{:S(2)}) %collective-permute-start.3) | collective-permute-done | bytes 65568 | tf_op jit(solution)/shard_map/ppermute | solution.py:315
  13.9 0.3 collective-permute-start.4
  14.2 2.9 %collective-permute-start.6 = (bf16[128,256]{1,0:T(8,128)(2,1)S(1)}, bf16[128,256]{1,0:T(8,128)(2,1)S(1)}, u32[]{:S(2)}, u32[]{:S(2)}) collective-permute-start(bf16[128,256]{1,0:T(8,128)(2,1)S(1)} %get-tuple-element.51.refs_3_.refs_0_), channel_id=1, source_target_pairs={{0,2},{1,9},{2,0},{3,11},{4,6},{5,13},{6,4},{7,15},{8,10},{9,1},{1... | collective-permute-start | bytes 196616 | tf_op jit(solution)/shard_map/ppermute | solution.py:332
  17.1 0.0 collective-permute-done.4.refs_2_
  17.1 0.8 %shard_map.92 = (f32[256,1024]{1,0:T(8,128)S(1)}, bf16[1,256,1024]{2,1,0:T(8,128)(2,1)S(1)}) custom-call(bf16[1024,2048]{1,0:T(8,128)(2,1)S(1)} %get-tuple-element.46.refs_0_, f32[1024,256]{1,0:T(8,128)S(1)} %shard_map.90.refs_3_.refs_1_, bf16[1024,256]{1,0:T(8,128)(2,1)S(1)} %collective-permute-done.4.refs_2_, ...), custom_call_target="tpu_custom_call" | custom-call | flops 8000000000 | tf_op jit(solution)/shard_map/pallas_call | solution.py:74
  18.0 1.4 %collective-permute-done.6.refs_1_ = bf16[128,256]{1,0:T(8,128)(2,1)S(1)} collective-permute-done((bf16[128,256]{1,0:T(8,128)(2,1)S(1)}, bf16[128,256]{1,0:T(8,128)(2,1)S(1)}, u32[]{:S(2)}, u32[]{:S(2)}) %collective-permute-start.6) | collective-permute-done | bytes 65568 | tf_op jit(solution)/shard_map/ppermute | solution.py:332
  19.4 2.1 %collective-permute-start.8 = (bf16[128,256]{1,0:T(8,128)(2,1)S(1)}, bf16[128,256]{1,0:T(8,128)(2,1)S(1)}, u32[]{:S(2)}, u32[]{:S(2)}) collective-permute-start(bf16[128,256]{1,0:T(8,128)(2,1)S(1)} %shard_map.93.refs_3_.refs_0_), channel_id=1, source_target_pairs={{0,4},{1,17},{2,6},{3,19},{4,0},{5,21},{6,2},{7,23},{8,12},{9,25},... | collective-permute-start | bytes 196616 | tf_op jit(solution)/shard_map/ppermute | solution.py:332
  21.5 0.7 %collective-permute-start.5 = (bf16[256,1024]{1,0:T(8,128)(2,1)S(1)}, bf16[256,1024]{1,0:T(8,128)(2,1)S(1)}, u32[]{:S(2)}, u32[]{:S(2)}) collective-permute-start(bf16[256,1024]{1,0:T(8,128)(2,1)S(1)} %bitcast.11), channel_id=1, source_target_pairs={{0,1},{1,0},{2,3},{3,2},{4,5},{5,4},{6,7},{7,6},{8,9},{9,8},{10,11... | collective-permute-start | bytes 1572872 | tf_op jit(solution)/shard_map/ppermute | solution.py:315
  22.2 1.5 %shard_map.94 = (f32[256,1024]{1,0:T(8,128)S(1)}, bf16[1,256,1024]{2,1,0:T(8,128)(2,1)S(1)}) custom-call(bf16[1024,2048]{1,0:T(8,128)(2,1)S(1)} %get-tuple-element.40.refs_0_, bf16[128,2048]{1,0:T(8,128)(2,1)S(1)} %get-tuple-element.44.refs_1_, bf16[256,1024]{1,0:T(8,128)(2,1)S(1)} %get-tuple-element.54.refs_2_.refs_1_, ...), custom_call_target="tpu_custom_call" | custom-call | flops 8000000000 | tf_op jit(solution)/shard_map/pallas_call | solution.py:74
  23.7 0.1 collective-permute-start.10
  23.7 0.0 collective-permute-done.5.refs_4_
  23.8 0.0 copy-start
  23.8 0.0 copy-start.1
  23.8 1.6 %shard_map.95 = (f32[256,1024]{1,0:T(8,128)S(1)}, f32[256,1024]{1,0:T(8,128)S(1)}, bf16[1,256,1024]{2,1,0:T(8,128)(2,1)S(1)}) custom-call(bf16[1024,2048]{1,0:T(8,128)(2,1)S(1)} %get-tuple-element.40.refs_0_, bf16[128,2048]{1,0:T(8,128)(2,1)S(1)} %get-tuple-element.44.refs_1_, f32[8,128]{1,0:T(8,128)S(1)} %get-tuple-element.45.refs_2_, ...), custom_call_target="tpu_custom_call" | custom-call | flops 8000000000 | tf_op jit(solution)/shard_map/pallas_call | solution.py:74
  25.4 0.0 collective-permute-done.8.refs_1_
  25.4 1.6 %collective-permute-start.11 = (bf16[128,256]{1,0:T(8,128)(2,1)S(1)}, bf16[128,256]{1,0:T(8,128)(2,1)S(1)}, u32[]{:S(2)}, u32[]{:S(2)}) collective-permute-start(bf16[128,256]{1,0:T(8,128)(2,1)S(1)} %shard_map.96.refs_4_.refs_0_), channel_id=1, source_target_pairs={{0,8},{1,3},{2,10},{3,1},{4,12},{5,7},{6,14},{7,5},{8,0},{9,11},{1... | collective-permute-start | bytes 196616 | tf_op jit(solution)/shard_map/ppermute | solution.py:332
  27.0 0.1 collective-permute-start.7
  27.1 0.0 copy-done
  27.1 0.0 copy-done.1
  27.1 0.8 %shard_map.97 = (f32[1024,256]{1,0:T(8,128)S(1)}, bf16[1024,256]{1,0:T(8,128)(2,1)S(1)}, f32[128,256]{1,0:T(8,128)S(1)}) custom-call(f32[256,1024]{1,0:T(8,128)S(1)} %get-tuple-element.58.refs_2_.refs_0_, bf16[256,1024]{1,0:T(8,128)(2,1)S(1)} %get-tuple-element.54.refs_2_.refs_1_, f32[256,128]{1,0:T(8,128)S(1)} %copy-done, bf16[256,256]{1,0:T(8,128)(2,1)S(1)} %copy-done.1, ...), custom_call_target="tpu_custom_call" | custom-call | flops 8000000000 | tf_op jit(solution)/shard_map/pallas_call | solution.py:74
  27.9 1.0 %collective-permute-done.7.refs_3_ = bf16[256,1024]{1,0:T(8,128)(2,1)S(1)} collective-permute-done((bf16[256,1024]{1,0:T(8,128)(2,1)S(1)}, bf16[256,1024]{1,0:T(8,128)(2,1)S(1)}, u32[]{:S(2)}, u32[]{:S(2)}) %collective-permute-start.7) | collective-permute-done | bytes 524320 | tf_op jit(solution)/shard_map/ppermute | solution.py:315
  28.9 0.9 %shard_map.98 = (f32[256,1024]{1,0:T(8,128)S(1)}, bf16[1,256,1024]{2,1,0:T(8,128)(2,1)S(1)}) custom-call(bf16[1024,2048]{1,0:T(8,128)(2,1)S(1)} %get-tuple-element.35.refs_0_, f32[256,1024]{1,0:T(8,128)S(1)} %get-tuple-element.39.refs_1_, f32[256,1024]{1,0:T(8,128)S(1)} %get-tuple-element.56.refs_2_, bf16[256,1024]{1,0:T(8,128)(2,1)S(1)} %collective-permute-done.7.refs_3_, ...), custom_call_target="tpu_custom_call" | custom-call | flops 8000000000 | tf_op jit(solution)/shard_map/pallas_call | solution.py:74
  29.8 0.0 collective-permute-done.11.refs_1_
  29.9 2.5 %collective-permute-start.13 = (bf16[128,256]{1,0:T(8,128)(2,1)S(1)}, bf16[128,256]{1,0:T(8,128)(2,1)S(1)}, u32[]{:S(2)}, u32[]{:S(2)}) collective-permute-start(bf16[128,256]{1,0:T(8,128)(2,1)S(1)} %shard_map.99.refs_4_.refs_1_), channel_id=1, source_target_pairs={{0,16},{1,5},{2,18},{3,7},{4,20},{5,1},{6,22},{7,3},{8,24},{9,13},... | collective-permute-start | bytes 196616 | tf_op jit(solution)/shard_map/ppermute | solution.py:332
  32.3 0.0 collective-permute-start.9
  32.3 0.0 collective-permute-done.10.refs_3_
  32.3 1.1 %shard_map.100 = (f32[256,1024]{1,0:T(8,128)S(1)}, bf16[1,256,1024]{2,1,0:T(8,128)(2,1)S(1)}) custom-call(bf16[1024,2048]{1,0:T(8,128)(2,1)S(1)} %get-tuple-element.35.refs_0_, bf16[256,1024]{1,0:T(8,128)(2,1)S(1)} %get-tuple-element.62.refs_1_, f32[256,1024]{1,0:T(8,128)S(1)} %get-tuple-element.55.refs_5_.refs_2_, ...), custom_call_target="tpu_custom_call" | custom-call | flops 8000000000 | tf_op jit(solution)/shard_map/pallas_call | solution.py:74
  33.5 1.2 %collective-permute-start.12 = (bf16[256,1024]{1,0:T(8,128)(2,1)S(1)}, bf16[256,1024]{1,0:T(8,128)(2,1)S(1)}, u32[]{:S(2)}, u32[]{:S(2)}) collective-permute-start(bf16[256,1024]{1,0:T(8,128)(2,1)S(1)} %bitcast.12), channel_id=1, source_target_pairs={{0,1},{1,0},{2,3},{3,2},{4,5},{5,4},{6,7},{7,6},{8,9},{9,8},{10,11... | collective-permute-start | bytes 1572872 | tf_op jit(solution)/shard_map/ppermute | solution.py:315
  34.7 0.0 collective-permute-done.9.refs_1_
  34.7 0.3 shard_map.101.refs_3_.refs_0_
  35.0 1.2 %collective-permute-done.12.refs_2_ = bf16[256,1024]{1,0:T(8,128)(2,1)S(1)} collective-permute-done((bf16[256,1024]{1,0:T(8,128)(2,1)S(1)}, bf16[256,1024]{1,0:T(8,128)(2,1)S(1)}, u32[]{:S(2)}, u32[]{:S(2)}) %collective-permute-start.12) | collective-permute-done | bytes 524320 | tf_op jit(solution)/shard_map/ppermute | solution.py:315
  36.2 0.6 %shard_map.102.refs_3_.refs_2_ = bf16[1024,256]{1,0:T(8,128)(2,1)S(1)} custom-call(f32[256,1024]{1,0:T(8,128)S(1)} %get-tuple-element.64.refs_2_.refs_0_, bf16[256,256]{1,0:T(8,128)(2,1)S(1)} %copy-done.1, bf16[256,1024]{1,0:T(8,128)(2,1)S(1)} %collective-permute-done.12.refs_2_, f32[1024,256]{1,0:T(8,128)S(1)} %shard_map.101.refs_3_.refs_0_), custom_call_target="tpu_custom_call" | custom-call | flops 8000000000 | tf_op jit(solution)/shard_map/pallas_call | solution.py:74
  36.9 0.0 collective-permute-done.13.refs_2_
  36.9 0.4 %collective-permute-start.14 = (bf16[128,256]{1,0:T(8,128)(2,1)S(1)}, bf16[128,256]{1,0:T(8,128)(2,1)S(1)}, u32[]{:S(2)}, u32[]{:S(2)}) collective-permute-start(bf16[128,256]{1,0:T(8,128)(2,1)S(1)} %shard_map.103.refs_1_.refs_4_), channel_id=1, source_target_pairs={{0,1},{1,0},{2,3},{3,2},{4,5},{5,4},{6,7},{7,6},{8,9},{9,8},{10,11... | collective-permute-start | bytes 196616 | tf_op jit(solution)/shard_map/ppermute | solution.py:315
  37.4 1.1 %shard_map.104.refs_6_ = f32[256,128]{1,0:T(8,128)} custom-call(bf16[256,256]{1,0:T(8,128)(2,1)S(1)} %copy-done.1, bf16[128,256]{1,0:T(8,128)(2,1)S(1)} %shard_map.103.refs_1_.refs_4_), custom_call_target="tpu_custom_call" | custom-call | flops 8000000000 | tf_op jit(solution)/shard_map/pallas_call | solution.py:74
  38.4 0.0 collective-permute-done.14.refs_5_
  38.4 1.3 %shard_map.105 = bf16[2,1024,256]{2,1,0:T(8,128)(2,1)} custom-call(f32[1024,256]{1,0:T(8,128)S(1)} %shard_map.101.refs_3_.refs_0_, f32[1024,256]{1,0:T(8,128)S(1)} %get-tuple-element.65.refs_1_, bf16[1024,256]{1,0:T(8,128)(2,1)S(1)} %shard_map.102.refs_3_.refs_2_, bf16[1024,256]{1,0:T(8,128)(2,1)S(1)} %get-tuple-element.67.refs_3_, ...), custom_call_target="tpu_custom_call" | custom-call | flops 8000000000 | tf_op jit(solution)/shard_map/pallas_call | solution.py:74
  (5 shorter events, 0.1 us)
Async XLA Ops:
  0.6 4.4 %collective-permute-start = (bf16[2,1024,256]{2,1,0:T(8,128)(2,1)}, bf16[2,1024,256]{2,1,0:T(8,128)(2,1)S(1)}, u32[]{:S(2)}, u32[]{:S(2)}) collective-permute-start(bf16[2,1024,256]{2,1,0:T(8,128)(2,1)} %refs_3_.4), channel_id=1, source_target_pairs={{0,1},{1,0},{2,3},{3,2},{4,5},{5,4},{6,7},{7,6},{8,9},{9,8},{10,11... | collective-permute-start | bytes 3145736 | tf_op jit(solution)/shard_map/ppermute | solution.py:315
  4.0 4.4 %collective-permute-start.2 = (bf16[256,1024]{1,0:T(8,128)(2,1)S(1)}, bf16[256,1024]{1,0:T(8,128)(2,1)S(1)}, u32[]{:S(2)}, u32[]{:S(2)}) collective-permute-start(bf16[256,1024]{1,0:T(8,128)(2,1)S(1)} %bitcast.9), channel_id=1, source_target_pairs={{0,1},{1,0},{2,3},{3,2},{4,5},{5,4},{6,7},{7,6},{8,9},{9,8},{10,11... | collective-permute-start | bytes 1572872 | tf_op jit(solution)/shard_map/ppermute | solution.py:315
  6.8 2.0 %collective-permute-start.1 = (bf16[1024,256]{1,0:T(8,128)(2,1)S(1)}, bf16[1024,256]{1,0:T(8,128)(2,1)S(1)}, u32[]{:S(2)}, u32[]{:S(2)}) collective-permute-start(bf16[1024,256]{1,0:T(8,128)(2,1)S(1)} %get-tuple-element.41.refs_2_), channel_id=1, source_target_pairs={{0,1},{1,0},{2,3},{3,2},{4,5},{5,4},{6,7},{7,6},{8,9},{9,8},{10,11... | collective-permute-start | bytes 1572872 | tf_op jit(solution)/shard_map/ppermute | solution.py:315
  12.6 1.3 %collective-permute-start.3 = (bf16[128,256]{1,0:T(8,128)(2,1)S(1)}, bf16[128,256]{1,0:T(8,128)(2,1)S(1)}, u32[]{:S(2)}, u32[]{:S(2)}) collective-permute-start(bf16[128,256]{1,0:T(8,128)(2,1)S(1)} %bitcast.13), channel_id=1, source_target_pairs={{0,1},{1,0},{2,3},{3,2},{4,5},{5,4},{6,7},{7,6},{8,9},{9,8},{10,11... | collective-permute-start | bytes 196616 | tf_op jit(solution)/shard_map/ppermute | solution.py:315
  13.9 3.2 %collective-permute-start.4 = (bf16[1024,256]{1,0:T(8,128)(2,1)S(1)}, bf16[1024,256]{1,0:T(8,128)(2,1)S(1)}, u32[]{:S(2)}, u32[]{:S(2)}) collective-permute-start(bf16[1024,256]{1,0:T(8,128)(2,1)S(1)} %get-tuple-element.50), channel_id=1, source_target_pairs={{0,1},{1,0},{2,3},{3,2},{4,5},{5,4},{6,7},{7,6},{8,9},{9,8},{10,11... | collective-permute-start | bytes 1572872 | tf_op jit(solution)/shard_map/ppermute | solution.py:315
  14.2 5.2 %collective-permute-start.6 = (bf16[128,256]{1,0:T(8,128)(2,1)S(1)}, bf16[128,256]{1,0:T(8,128)(2,1)S(1)}, u32[]{:S(2)}, u32[]{:S(2)}) collective-permute-start(bf16[128,256]{1,0:T(8,128)(2,1)S(1)} %get-tuple-element.51.refs_3_.refs_0_), channel_id=1, source_target_pairs={{0,2},{1,9},{2,0},{3,11},{4,6},{5,13},{6,4},{7,15},{8,10},{9,1},{1... | collective-permute-start | bytes 196616 | tf_op jit(solution)/shard_map/ppermute | solution.py:332
  19.4 6.0 %collective-permute-start.8 = (bf16[128,256]{1,0:T(8,128)(2,1)S(1)}, bf16[128,256]{1,0:T(8,128)(2,1)S(1)}, u32[]{:S(2)}, u32[]{:S(2)}) collective-permute-start(bf16[128,256]{1,0:T(8,128)(2,1)S(1)} %shard_map.93.refs_3_.refs_0_), channel_id=1, source_target_pairs={{0,4},{1,17},{2,6},{3,19},{4,0},{5,21},{6,2},{7,23},{8,12},{9,25},... | collective-permute-start | bytes 196616 | tf_op jit(solution)/shard_map/ppermute | solution.py:332
  21.5 2.3 %collective-permute-start.5 = (bf16[256,1024]{1,0:T(8,128)(2,1)S(1)}, bf16[256,1024]{1,0:T(8,128)(2,1)S(1)}, u32[]{:S(2)}, u32[]{:S(2)}) collective-permute-start(bf16[256,1024]{1,0:T(8,128)(2,1)S(1)} %bitcast.11), channel_id=1, source_target_pairs={{0,1},{1,0},{2,3},{3,2},{4,5},{5,4},{6,7},{7,6},{8,9},{9,8},{10,11... | collective-permute-start | bytes 1572872 | tf_op jit(solution)/shard_map/ppermute | solution.py:315
  23.7 8.7 %collective-permute-start.10 = (bf16[256,1024]{1,0:T(8,128)(2,1)S(1)}, bf16[256,1024]{1,0:T(8,128)(2,1)S(1)}, u32[]{:S(2)}, u32[]{:S(2)}) collective-permute-start(bf16[256,1024]{1,0:T(8,128)(2,1)S(1)} %bitcast.7), channel_id=1, source_target_pairs={{0,1},{1,0},{2,3},{3,2},{4,5},{5,4},{6,7},{7,6},{8,9},{9,8},{10,11... | collective-permute-start | bytes 1572872 | tf_op jit(solution)/shard_map/ppermute | solution.py:315
  23.8 3.4 %copy-start = (f32[256,128]{1,0:T(8,128)S(1)}, f32[256,128]{1,0:T(8,128)}, u32[]{:S(2)}) copy-start(f32[256,128]{1,0:T(8,128)} %refs_2_.5) | copy-start | bytes 393220
  23.8 3.4 %copy-start.1 = (bf16[256,256]{1,0:T(8,128)(2,1)S(1)}, bf16[256,256]{1,0:T(8,128)(2,1)}, u32[]{:S(2)}) copy-start(bf16[256,256]{1,0:T(8,128)(2,1)} %refs_0_.5) | copy-start | bytes 393220
  25.4 4.4 %collective-permute-start.11 = (bf16[128,256]{1,0:T(8,128)(2,1)S(1)}, bf16[128,256]{1,0:T(8,128)(2,1)S(1)}, u32[]{:S(2)}, u32[]{:S(2)}) collective-permute-start(bf16[128,256]{1,0:T(8,128)(2,1)S(1)} %shard_map.96.refs_4_.refs_0_), channel_id=1, source_target_pairs={{0,8},{1,3},{2,10},{3,1},{4,12},{5,7},{6,14},{7,5},{8,0},{9,11},{1... | collective-permute-start | bytes 196616 | tf_op jit(solution)/shard_map/ppermute | solution.py:332
  27.0 1.9 %collective-permute-start.7 = (bf16[256,1024]{1,0:T(8,128)(2,1)S(1)}, bf16[256,1024]{1,0:T(8,128)(2,1)S(1)}, u32[]{:S(2)}, u32[]{:S(2)}) collective-permute-start(bf16[256,1024]{1,0:T(8,128)(2,1)S(1)} %bitcast.10), channel_id=1, source_target_pairs={{0,1},{1,0},{2,3},{3,2},{4,5},{5,4},{6,7},{7,6},{8,9},{9,8},{10,11... | collective-permute-start | bytes 1572872 | tf_op jit(solution)/shard_map/ppermute | solution.py:315
  29.9 7.0 %collective-permute-start.13 = (bf16[128,256]{1,0:T(8,128)(2,1)S(1)}, bf16[128,256]{1,0:T(8,128)(2,1)S(1)}, u32[]{:S(2)}, u32[]{:S(2)}) collective-permute-start(bf16[128,256]{1,0:T(8,128)(2,1)S(1)} %shard_map.99.refs_4_.refs_1_), channel_id=1, source_target_pairs={{0,16},{1,5},{2,18},{3,7},{4,20},{5,1},{6,22},{7,3},{8,24},{9,13},... | collective-permute-start | bytes 196616 | tf_op jit(solution)/shard_map/ppermute | solution.py:332
  32.3 2.4 %collective-permute-start.9 = (bf16[256,1024]{1,0:T(8,128)(2,1)S(1)}, bf16[256,1024]{1,0:T(8,128)(2,1)S(1)}, u32[]{:S(2)}, u32[]{:S(2)}) collective-permute-start(bf16[256,1024]{1,0:T(8,128)(2,1)S(1)} %bitcast.8), channel_id=1, source_target_pairs={{0,1},{1,0},{2,3},{3,2},{4,5},{5,4},{6,7},{7,6},{8,9},{9,8},{10,11... | collective-permute-start | bytes 1572872 | tf_op jit(solution)/shard_map/ppermute | solution.py:315
  33.5 2.8 %collective-permute-start.12 = (bf16[256,1024]{1,0:T(8,128)(2,1)S(1)}, bf16[256,1024]{1,0:T(8,128)(2,1)S(1)}, u32[]{:S(2)}, u32[]{:S(2)}) collective-permute-start(bf16[256,1024]{1,0:T(8,128)(2,1)S(1)} %bitcast.12), channel_id=1, source_target_pairs={{0,1},{1,0},{2,3},{3,2},{4,5},{5,4},{6,7},{7,6},{8,9},{9,8},{10,11... | collective-permute-start | bytes 1572872 | tf_op jit(solution)/shard_map/ppermute | solution.py:315
  36.9 1.5 %collective-permute-start.14 = (bf16[128,256]{1,0:T(8,128)(2,1)S(1)}, bf16[128,256]{1,0:T(8,128)(2,1)S(1)}, u32[]{:S(2)}, u32[]{:S(2)}) collective-permute-start(bf16[128,256]{1,0:T(8,128)(2,1)S(1)} %shard_map.103.refs_1_.refs_4_), channel_id=1, source_target_pairs={{0,1},{1,0},{2,3},{3,2},{4,5},{5,4},{6,7},{7,6},{8,9},{9,8},{10,11... | collective-permute-start | bytes 196616 | tf_op jit(solution)/shard_map/ppermute | solution.py:315

commit v8 on v7

--- a/solution.py
+++ b/solution.py
@@ -102,14 +102,10 @@
             at = j * tile
             own_ref[:, at : at + tile] = dot(left[:, at:], factor[at:, block(0, at, tile)])
 
-    def full_rows(left, factor, tail, own_ref, other_ref):
-        for step in (*peers, 0):
-            product = dot(left[:, :head], factor[:head, block(step)])
-            product = product + dot(left[:, head:], tail[:, block(step)])
-            if step:
-                other_ref[step - 1] = product.astype(BF)
-            else:
-                own_ref[...] = product
+    def full_rows(left, factor, own_ref, other_ref):
+        for step in peers:
+            other_ref[step - 1] = dot(left[...], factor[:, block(step)]).astype(BF)
+        own_ref[...] = dot(left[...], factor[:, block(0)])
 
     def lower_own(factor, right, out_ref, wait=None):
         for i in range(tiles):
@@ -185,9 +181,11 @@
             copies[-1].start(priority=i % 2)
         return copies
 
-    def first_value_kernel(d0, n0, coupling, *refs):
-        got, (out, bar, k1, sems) = refs[: n_space - 1], refs[n_space - 1 :]
+    def first_value_kernel(d0, n0, coupling, noise, *refs):
+        got, (out, bar, k1, n1, sems) = refs[: n_space - 1], refs[n_space - 1 :]
         copies = k1_copies(coupling, k1, 0, 3, sems)
+        copies.append(pltpu.make_async_copy(noise.at[1], n1, sems.at[3]))
+        copies[-1].start()
         lower_own(d0, n0, out)
         lower_rest(d0, [piece.at[0] for piece in got], out)
         bar[...] = out[...].astype(BF)
@@ -200,34 +198,37 @@
         for copy in copies:
             copy.wait()
 
-    def target_kernel(k1, coupling, bar, noise, arrow, own, *refs):
+    def target_kernel(k1, coupling, bar, n1, arrow, own, *refs):
         got, refs = refs[: n_space - 1], refs[n_space - 1 :]
         got_own, refs = refs[: n_space - 1], refs[n_space - 1 :]
-        tail, target, part_own, part_other, response, e0, n1, whole, sems = refs
-        noise_copy = pltpu.make_async_copy(noise.at[1], n1, sems.at[1])
-        arrow_copy = pltpu.make_async_copy(arrow.at[0], e0, sems.at[2])
-        noise_copy.start()
+        target, part_own, part_other, response, e0, tail, whole, sems = refs
+        arrow_copy = pltpu.make_async_copy(arrow.at[0], e0, sems.at[1])
         (tail_copy,) = k1_copies(coupling, tail, 7, 1, sems)
         arrow_copy.start()
 
-        def pull(factor, part, before):
-            pulled = dot(factor[:, block(0)], bar[...])
-            for step in peers:
-                pulled = pulled + dot(factor[:, block(step)], got[step - 1][...])
-            before.wait()
-            target[part] = (n1[part].astype(F32) - pulled).astype(BF)
+        def pull(at, size):
+            factor = tail if at == head else k1.at[at : at + size]
+            pulled = jnp.zeros((size, columns), F32)
+            for step, piece in enumerate([bar, *got]):
+                pulled = pulled + dot(factor[:, block(step)], piece[...])
+            target[at : at + size] = (n1[at : at + size].astype(F32) - pulled).astype(BF)
 
         response[...] = total_of(own, got_own).astype(BF)
-        pull(k1.at[:head], pl.ds(0, head), noise_copy)
+        for at in range(0, head, tile):
+            pull(at, min(tile, head - at))
+        arrow_copy.wait()
+        whole[...] = dot(e0[...], bar[...])
         tail_copy.wait()
-        pull(tail, pl.ds(head, eighth), arrow_copy)
-        whole[...] = (dot(e0[...], bar[...]) + dot(response[...], target[...])).T
+        pull(head, eighth)
+        whole[...] = (whole[...] + dot(response[...], target[...])).T
         part_own[...] = whole[part_rows(0)]
         for step in peers:
             part_other[step - 1] = whole[part_rows(step)].astype(BF)
 
-    def last_own_kernel(d1, target, value):
+    def last_own_kernel(d1, target, coupling, _, value, k1, sems):
+        (tail_copy,) = k1_copies(coupling, k1, 7, 1, sems)
         lower_own(d1, target, value)
+        tail_copy.wait()
 
     def core_sum_kernel(part, _, *refs):
         got, (out, _) = refs[:-2], refs[-2:]
@@ -245,19 +246,19 @@
         lower_rest(d1, got, value)
         lower_rows(value[...].T.astype(BF), d1, own, other)
 
-    def response_kernel(k1, tail, response, own, other):
-        full_rows(response, k1, tail, own, other)
-
-    def pass_kernel(k1, tail, mask, solved, *refs):
+    def response_kernel(k1, response, own, other):
+        full_rows(response, k1, own, other)
+
+    def pass_kernel(k1, mask, solved, *refs):
         got, (base, own, other) = refs[: n_space - 1], refs[n_space - 1 :]
         value = jnp.where(mask[:1, :1] > 0, total_of(solved, got), 0.0)
         base[...] = value
-        full_rows(value.astype(BF), k1, tail, own, other)
-
-    def first_response_kernel(d0, e0, pushed, *refs):
+        full_rows(value.astype(BF), k1, own, other)
+
+    def first_response_kernel(d0, e0, tip, pushed, *refs):
         got, (own, other) = refs[: n_space - 1], refs[n_space - 1 :]
         left = (e0[...].astype(F32) - total_of(pushed, got)).astype(BF)
-        lower_rows(left, d0, own, other)
+        lower_rows(through_tip(tip[...], left).astype(BF), d0, own, other)
 
     def first_solve_kernel(d0, value_rows, passed, *refs):
         got, (own, other) = refs[: n_space - 1], refs[n_space - 1 :]
@@ -266,16 +267,16 @@
 
     def through_tip(tip, right):
         inner = dot(tip, right).astype(BF)
-        return dot(tip.astype(F32).T.astype(BF), inner).T.astype(BF)
+        return dot(tip.astype(F32).T.astype(BF), inner)
 
     def turn_last_kernel(base, response, noise_fixed, tip, last_base, last_resp, noise_rows):
         noise_rows[...] = noise_fixed[...].T
         last_base[...] = base[...].T
-        last_resp[...] = through_tip(tip[...], response[...])
-
-    def turn_response_kernel(first, tip, *refs):
+        last_resp[...] = through_tip(tip[...], response[...]).T.astype(BF)
+
+    def turn_response_kernel(first, *refs):
         got, out = refs[:-1], refs[-1]
-        out[...] = through_tip(tip[...], total_of(first, got).astype(BF))
+        out[...] = total_of(first, got).T.astype(BF)
 
     def turn_first_kernel(solved, *refs):
         got, out = refs[:-1], refs[-1]
@@ -363,13 +364,13 @@
             ],
         )
         got_response = send_down(other)
-        value, bar, k1 = call(
+        value, bar, k1, n1 = call(
             first_value_kernel,
-            [node_f32, node_bf, in_vmem],
-            [d0, n0, coupling, *got_noise],
-            8,
-            {2: pltpu.HBM},
-            [dma((3,))],
+            [node_f32, node_bf, in_vmem, node_bf],
+            [d0, n0, coupling, noise, *got_noise],
+            8,
+            {2: pltpu.HBM, 3: pltpu.HBM},
+            [dma((4,))],
         )
         got_bar = send_up(bar)
         value_rows, k1 = call(
@@ -381,27 +382,34 @@
             [dma((4,))],
             aliases={2: 1},
         )
-        tail, target, part_own, part_other, response, e0 = call(
+        target, part_own, part_other, response, e0 = call(
             target_kernel,
             [
-                pltpu.VMEM((eighth, nodes), BF),
                 node_bf,
                 shape_of((width, fixed_rows), F32),
                 shape_of((n_space - 1, width, fixed_rows), BF),
                 fixed_bf,
                 fixed_bf,
             ],
-            [k1, coupling, bar, noise, arrow, own, *got_bar, *got_response],
-            8,
-            {1: pltpu.HBM, 3: pltpu.HBM, 4: pltpu.HBM},
+            [k1, coupling, bar, n1, arrow, own, *got_bar, *got_response],
+            8,
+            {1: pltpu.HBM, 4: pltpu.HBM},
             [
-                pltpu.VMEM((rows, columns), BF),
+                pltpu.VMEM((eighth, nodes), BF),
                 pltpu.VMEM((columns, fixed_rows), F32),
-                dma((3,)),
+                dma((2,)),
             ],
         )
         got_parts = send_down(part_other)
-        (value,) = call(last_own_kernel, [node_f32], [d1, target], 8)
+        value, k1 = call(
+            last_own_kernel,
+            [node_f32, in_vmem],
+            [d1, target, coupling, k1],
+            8,
+            {2: pltpu.HBM, 3: pl.ANY, ("out", 1): pl.ANY},
+            [dma((1,))],
+            aliases={3: 1},
+        )
         sent, target = call(
             core_sum_kernel,
             [part_bf, node_bf],
@@ -436,13 +444,13 @@
         got_solved = send_down(other)
         advance(solved)
         pushed, other = call(
-            response_kernel, [fixed_f32, fixed_others], [k1, tail, response], 8, after=sent
+            response_kernel, [fixed_f32, fixed_others], [k1, response], 5, after=sent
         )
         got_pushed = send_down(other)
         base, passed, other = call(
             pass_kernel,
             [flat_f32, flat_f32, flat_others],
-            [k1, tail, mask, solved, *got_solved],
+            [k1, mask, solved, *got_solved],
             8,
             after=pushed,
         )
@@ -452,7 +460,7 @@
             turn_last_kernel,
             [node_f32, by_node, shape_of((width, fixed_rows), F32)],
             [base, response, noise_fixed, tip_inverse],
-            8,
+            5,
             after=sent,
         )
         solved, other = call(
@@ -467,14 +475,14 @@
         first, other = call(
             first_response_kernel,
             [fixed_f32, fixed_others],
-            [d0, e0, pushed, *got_pushed],
-            8,
+            [d0, e0, tip_inverse, pushed, *got_pushed],
+            5,
             after=sent,
         )
         got_first = send_down(other)
         (first_base,) = call(turn_first_kernel, [node_f32], [solved, *got_solved], 8, after=first)
         (first_resp,) = call(
-            turn_response_kernel, [by_node], [first, tip_inverse, *got_first], 8, after=first_base
+            turn_response_kernel, [by_node], [first, *got_first], 8, after=first_base
         )
         while step < steps:
             advance()

time: 40.1 us -> 37.2 us (0.928)
  waiting for transfers between devices: 4.51 us -> 2.13 us
  Pallas kernels: 20.5 us -> 19.2 us
  starting transfers between devices: 13.9 us -> 14.7 us
    pallas_call x20, Pallas kernels: 20.5 us -> 19.2 us  [call(): pl.pallas_call(run, in_specs=specs, out_specs=[pl.BlockSpec(memory_space=...]
    ppermute x4, waiting for transfers between devices: 1.41 us -> 0.19 us  [swap_step(): return lax.ppermute(value, ('tm', 'space'), pairs)]
    ppermute x11, waiting for transfers between devices: 3.1 us -> 1.94 us  [swap(): return lax.ppermute(value, 'space', pairs)]
    ppermute x11, starting transfers between devices: 4.73 us -> 5.74 us  [swap(): return lax.ppermute(value, 'space', pairs)]
  transfers between devices with their start and end apart: 15 -> 15, of which waited for: 5 -> 4; matrix products, arithmetic and copies ran while one was open for 0% -> 0% of each run, Pallas kernels for 38% -> 42%
where the time goes in v8:
time: 37.2 us; the launch traced here: 36.9 us
  Pallas kernels  19.2 us (52%)
  starting transfers between devices  14.7 us (40%)
  waiting for transfers between devices  2.13 us (6%)
  between operations  0.83 us (2%)
    pallas_call x20, Pallas kernels, call(): pl.pallas_call(run, in_specs=specs, out_specs=[pl.BlockSpec(memory_space=...  19.2 us
    ppermute x4, starting transfers between devices, swap_step(): return lax.ppermute(value, ('tm', 'space'), pairs)  9 us
    ppermute x11, starting transfers between devices, swap(): return lax.ppermute(value, 'space', pairs)  5.74 us
    ppermute x11, waiting for transfers between devices, swap(): return lax.ppermute(value, 'space', pairs)  1.94 us
  transfers between devices with their start and end apart: 15, of which 4 were waited for; matrix products, arithmetic and copies ran while one was open for 0% of the time, Pallas kernels for 42%

profile of v8, /device:TPU:0, one launch (start us, length us, event | category | flops | bytes accessed | tf_op | source)
XLA Modules:
  0.0 36.9 jit_solution(8420003970206439317)
XLA Ops:
  0.6 0.5 %collective-permute-start = (bf16[2,1024,256]{2,1,0:T(8,128)(2,1)}, bf16[2,1024,256]{2,1,0:T(8,128)(2,1)S(1)}, u32[]{:S(2)}, u32[]{:S(2)}) collective-permute-start(bf16[2,1024,256]{2,1,0:T(8,128)(2,1)} %refs_3_.4), channel_id=1, source_target_pairs={{0,1},{1,0},{2,3},{3,2},{4,5},{5,4},{6,7},{7,6},{8,9},{9,8},{10,11... | collective-permute-start | bytes 3145736 | tf_op jit(solution)/shard_map/ppermute | solution.py:316
  1.1 2.8 %shard_map.86 = (bf16[1024,2048]{1,0:T(8,128)(2,1)S(1)}, bf16[1024,2048]{1,0:T(8,128)(2,1)S(1)}, f32[256,1024]{1,0:T(8,128)S(1)}, bf16[1,256,1024]{2,1,0:T(8,128...) custom-call(bf16[2,1024,2048]{2,1,0:T(8,128)(2,1)} %refs_0_.3, bf16[2,256,1024]{2,1,0:T(8,128)(2,1)} %refs_4_.1, ...), custom_call_target="tpu_custom_call" | custom-call | flops 8000000000 | tf_op jit(solution)/shard_map/pallas_call | solution.py:74
  4.0 1.1 %collective-permute-start.2 = (bf16[256,1024]{1,0:T(8,128)(2,1)S(1)}, bf16[256,1024]{1,0:T(8,128)(2,1)S(1)}, u32[]{:S(2)}, u32[]{:S(2)}) collective-permute-start(bf16[256,1024]{1,0:T(8,128)(2,1)S(1)} %bitcast.10), channel_id=1, source_target_pairs={{0,1},{1,0},{2,3},{3,2},{4,5},{5,4},{6,7},{7,6},{8,9},{9,8},{10,11... | collective-permute-start | bytes 1572872 | tf_op jit(solution)/shard_map/ppermute | solution.py:316
  5.1 0.0 collective-permute-done.refs_4_
  5.1 1.7 %shard_map.87 = (f32[1024,256]{1,0:T(8,128)S(1)}, bf16[1024,256]{1,0:T(8,128)(2,1)S(1)}, bf16[1024,2048]{1,0:T(8,128)(2,1)S(1)}, bf16[1024,256]{1,0:T(8,128)(2,1)S(1)}) custom-call(bf16[1024,2048]{1,0:T(8,128)(2,1)S(1)} %get-tuple-element.37.refs_0_, bf16[1024,256]{1,0:T(8,128)(2,1)S(1)} %get-tuple-element.38.refs_1_, bf16[2,1024,2048]{2,1,0:T(8,128)(2,1)} %refs_2_.7, ...), custom_call_target="tpu_custom_call" | custom-call | flops 8000000000 | tf_op jit(solution)/shard_map/pallas_call | solution.py:74
  6.8 0.1 collective-permute-start.1
  6.9 1.6 %shard_map.88 = (f32[256,1024]{1,0:T(8,128)S(1)}, bf16[1024,2048]{1,0:T(8,128)(2,1)S(1)}) custom-call(bf16[2,1024,2048]{2,1,0:T(8,128)(2,1)} %refs_2_.7, f32[1024,256]{1,0:T(8,128)S(1)} %get-tuple-element.39.refs_1_, bf16[1024,2048]{1,0:T(8,128)(2,1)S(1)} %get-tuple-element.40.refs_2_), custom_call_target="tpu_custom_call", output_to_operand_aliasing={{1}: (2, {})} | custom-call | flops 8000000000 | tf_op jit(solution)/shard_map/pallas_call | solution.py:74
  8.5 0.0 collective-permute-done.2.refs_7_
  8.5 0.3 collective-permute-done.1.refs_6_
  8.8 2.5 %shard_map.89 = (bf16[1024,256]{1,0:T(8,128)(2,1)S(1)}, f32[128,256]{1,0:T(8,128)S(1)}, bf16[1,128,256]{2,1,0:T(8,128)(2,1)S(1)}, bf16[256,1024]{1,0:T(8,128)(2,1)S(1)}, bf16[256,1024]{1,0:T(8,128)(2,1)S(1)}) custom-call(bf16[1024,2048]{1,0:T(8,128)(2,1)S(1)} %get-tuple-element.43.refs_0_.refs_3_, bf16[2,1024,2048]{2,1,0:T(8,128)(2,1)} %refs_2_.7, ...), custom_call_target="tpu_custom_call" | custom-call | flops 8000000000 | tf_op jit(solution)/shard_map/pallas_call | solution.py:74
  11.3 0.3 collective-permute-start.3
  11.5 1.4 %shard_map.90 = (f32[1024,256]{1,0:T(8,128)S(1)}, bf16[1024,2048]{1,0:T(8,128)(2,1)S(1)}) custom-call(bf16[1024,2048]{1,0:T(8,128)(2,1)S(1)} %get-tuple-element.42.refs_0_, bf16[1024,256]{1,0:T(8,128)(2,1)S(1)} %get-tuple-element.48.refs_1_, bf16[2,1024,2048]{2,1,0:T(8,128)(2,1)} %refs_2_.7, ...), custom_call_target="tpu_custom_call", output_to_operand_aliasing={{1}: (3, {})} | custom-call | flops 8000000000 | tf_op jit(solution)/shard_map/pallas_call | solution.py:74
  12.9 0.0 collective-permute-done.3.refs_2_
  12.9 0.4 %collective-permute-start.4 = (bf16[1024,256]{1,0:T(8,128)(2,1)S(1)}, bf16[1024,256]{1,0:T(8,128)(2,1)S(1)}, u32[]{:S(2)}, u32[]{:S(2)}) collective-permute-start(bf16[1024,256]{1,0:T(8,128)(2,1)S(1)} %get-tuple-element.54), channel_id=1, source_target_pairs={{0,1},{1,0},{2,3},{3,2},{4,5},{5,4},{6,7},{7,6},{8,9},{9,8},{10,11... | collective-permute-start | bytes 1572872 | tf_op jit(solution)/shard_map/ppermute | solution.py:316
  13.3 2.9 %collective-permute-start.6 = (bf16[128,256]{1,0:T(8,128)(2,1)S(1)}, bf16[128,256]{1,0:T(8,128)(2,1)S(1)}, u32[]{:S(2)}, u32[]{:S(2)}) collective-permute-start(bf16[128,256]{1,0:T(8,128)(2,1)S(1)} %get-tuple-element.55.refs_3_.refs_0_), channel_id=1, source_target_pairs={{0,2},{1,9},{2,0},{3,11},{4,6},{5,13},{6,4},{7,15},{8,10},{9,1},{1... | collective-permute-start | bytes 196616 | tf_op jit(solution)/shard_map/ppermute | solution.py:333
  16.3 0.0 collective-permute-done.4.refs_2_
  16.3 0.8 %shard_map.92 = (f32[256,1024]{1,0:T(8,128)S(1)}, bf16[1,256,1024]{2,1,0:T(8,128)(2,1)S(1)}) custom-call(bf16[1024,2048]{1,0:T(8,128)(2,1)S(1)} %get-tuple-element.42.refs_0_, f32[1024,256]{1,0:T(8,128)S(1)} %get-tuple-element.51.refs_3_.refs_1_, bf16[1024,256]{1,0:T(8,128)(2,1)S(1)} %collective-permute-done.4.refs_2_, ...), custom_call_target="tpu_custom_call" | custom-call | flops 8000000000 | tf_op jit(solution)/shard_map/pallas_call | solution.py:74
  17.1 1.4 %collective-permute-start.5 = (bf16[256,1024]{1,0:T(8,128)(2,1)S(1)}, bf16[256,1024]{1,0:T(8,128)(2,1)S(1)}, u32[]{:S(2)}, u32[]{:S(2)}) collective-permute-start(bf16[256,1024]{1,0:T(8,128)(2,1)S(1)} %bitcast.11), channel_id=1, source_target_pairs={{0,1},{1,0},{2,3},{3,2},{4,5},{5,4},{6,7},{7,6},{8,9},{9,8},{10,11... | collective-permute-start | bytes 1572872 | tf_op jit(solution)/shard_map/ppermute | solution.py:316
  18.5 0.0 collective-permute-done.6.refs_1_
  18.6 2.1 %collective-permute-start.8 = (bf16[128,256]{1,0:T(8,128)(2,1)S(1)}, bf16[128,256]{1,0:T(8,128)(2,1)S(1)}, u32[]{:S(2)}, u32[]{:S(2)}) collective-permute-start(bf16[128,256]{1,0:T(8,128)(2,1)S(1)} %shard_map.93.refs_2_.refs_0_), channel_id=1, source_target_pairs={{0,4},{1,17},{2,6},{3,19},{4,0},{5,21},{6,2},{7,23},{8,12},{9,25},... | collective-permute-start | bytes 196616 | tf_op jit(solution)/shard_map/ppermute | solution.py:333
  20.6 1.2 %shard_map.94 = (f32[256,1024]{1,0:T(8,128)S(1)}, bf16[1,256,1024]{2,1,0:T(8,128)(2,1)S(1)}) custom-call(bf16[1024,2048]{1,0:T(8,128)(2,1)S(1)} %get-tuple-element.49.refs_0_, bf16[256,1024]{1,0:T(8,128)(2,1)S(1)} %get-tuple-element.58.refs_1_, bf16[128,256]{1,0:T(8,128)(2,1)S(1)} %shard_map.93.refs_2_.refs_0_), custom_call_target="tpu_custom_call" | custom-call | flops 5000000000 | tf_op jit(solution)/shard_map/pallas_call | solution.py:74
  21.9 0.0 collective-permute-done.5.refs_3_
  21.9 0.0 copy-start
  21.9 0.0 copy-start.1
  21.9 1.3 %shard_map.95 = (f32[256,1024]{1,0:T(8,128)S(1)}, f32[256,1024]{1,0:T(8,128)S(1)}, bf16[1,256,1024]{2,1,0:T(8,128)(2,1)S(1)}) custom-call(bf16[1024,2048]{1,0:T(8,128)(2,1)S(1)} %get-tuple-element.49.refs_0_, f32[8,128]{1,0:T(8,128)S(1)} %get-tuple-element.50.refs_1_, f32[256,1024]{1,0:T(8,128)S(1)} %get-tuple-element.56.refs_2_, ...), custom_call_target="tpu_custom_call" | custom-call | flops 8000000000 | tf_op jit(solution)/shard_map/pallas_call | solution.py:74
  23.2 0.8 %collective-permute-start.7 = (bf16[256,1024]{1,0:T(8,128)(2,1)S(1)}, bf16[256,1024]{1,0:T(8,128)(2,1)S(1)}, u32[]{:S(2)}, u32[]{:S(2)}) collective-permute-start(bf16[256,1024]{1,0:T(8,128)(2,1)S(1)} %bitcast.9), channel_id=1, source_target_pairs={{0,1},{1,0},{2,3},{3,2},{4,5},{5,4},{6,7},{7,6},{8,9},{9,8},{10,11... | collective-permute-start | bytes 1572872 | tf_op jit(solution)/shard_map/ppermute | solution.py:316
  24.0 0.1 collective-permute-start.10
  24.1 0.0 collective-permute-done.8.refs_1_
  24.1 1.6 %collective-permute-start.11 = (bf16[128,256]{1,0:T(8,128)(2,1)S(1)}, bf16[128,256]{1,0:T(8,128)(2,1)S(1)}, u32[]{:S(2)}, u32[]{:S(2)}) collective-permute-start(bf16[128,256]{1,0:T(8,128)(2,1)S(1)} %shard_map.96.refs_4_.refs_0_), channel_id=1, source_target_pairs={{0,8},{1,3},{2,10},{3,1},{4,12},{5,7},{6,14},{7,5},{8,0},{9,11},{1... | collective-permute-start | bytes 196616 | tf_op jit(solution)/shard_map/ppermute | solution.py:333
  25.8 0.0 copy-done
  25.8 0.0 copy-done.1
  25.8 0.8 %shard_map.97 = (f32[1024,256]{1,0:T(8,128)S(1)}, bf16[1024,256]{1,0:T(8,128)(2,1)S(1)}, f32[128,256]{1,0:T(8,128)S(1)}) custom-call(f32[256,1024]{1,0:T(8,128)S(1)} %get-tuple-element.62.refs_2_.refs_0_, bf16[256,1024]{1,0:T(8,128)(2,1)S(1)} %get-tuple-element.58.refs_1_, f32[256,128]{1,0:T(8,128)S(1)} %copy-done, bf16[256,256]{1,0:T(8,128)(2,1)S(1)} %copy-done.1, ...), custom_call_target="tpu_custom_call" | custom-call | flops 5000000000 | tf_op jit(solution)/shard_map/pallas_call | solution.py:74
  26.6 0.0 collective-permute-done.7.refs_3_
  26.6 0.9 %shard_map.98 = (f32[256,1024]{1,0:T(8,128)S(1)}, bf16[1,256,1024]{2,1,0:T(8,128)(2,1)S(1)}) custom-call(bf16[1024,2048]{1,0:T(8,128)(2,1)S(1)} %get-tuple-element.37.refs_0_, f32[256,1024]{1,0:T(8,128)S(1)} %get-tuple-element.41.refs_1_, f32[256,1024]{1,0:T(8,128)S(1)} %get-tuple-element.60.refs_2_, bf16[256,1024]{1,0:T(8,128)(2,1)S(1)} %collective-permute-done.7.refs_3_, ...), custom_call_target="tpu_custom_call" | custom-call | flops 8000000000 | tf_op jit(solution)/shard_map/pallas_call | solution.py:74
  27.5 0.8 %collective-permute-start.9 = (bf16[256,1024]{1,0:T(8,128)(2,1)S(1)}, bf16[256,1024]{1,0:T(8,128)(2,1)S(1)}, u32[]{:S(2)}, u32[]{:S(2)}) collective-permute-start(bf16[256,1024]{1,0:T(8,128)(2,1)S(1)} %bitcast.8), channel_id=1, source_target_pairs={{0,1},{1,0},{2,3},{3,2},{4,5},{5,4},{6,7},{7,6},{8,9},{9,8},{10,11... | collective-permute-start | bytes 1572872 | tf_op jit(solution)/shard_map/ppermute | solution.py:316
  28.3 0.2 collective-permute-done.11.refs_1_
  28.5 2.3 %collective-permute-start.13 = (bf16[128,256]{1,0:T(8,128)(2,1)S(1)}, bf16[128,256]{1,0:T(8,128)(2,1)S(1)}, u32[]{:S(2)}, u32[]{:S(2)}) collective-permute-start(bf16[128,256]{1,0:T(8,128)(2,1)S(1)} %shard_map.99.refs_5_.refs_1_), channel_id=1, source_target_pairs={{0,16},{1,5},{2,18},{3,7},{4,20},{5,1},{6,22},{7,3},{8,24},{9,13},... | collective-permute-start | bytes 196616 | tf_op jit(solution)/shard_map/ppermute | solution.py:333
  30.8 0.0 collective-permute-done.10.refs_4_
  30.8 1.2 %shard_map.100 = (f32[256,1024]{1,0:T(8,128)S(1)}, bf16[1,256,1024]{2,1,0:T(8,128)(2,1)S(1)}) custom-call(bf16[1024,2048]{1,0:T(8,128)(2,1)S(1)} %get-tuple-element.37.refs_0_, bf16[256,1024]{1,0:T(8,128)(2,1)S(1)} %get-tuple-element.66.refs_1_, bf16[256,256]{1,0:T(8,128)(2,1)S(1)} %copy-done.1, f32[256,1024]{1,0:T(8,128)S(1)} %get-tuple-element.59.refs_4_.refs_3_, ...), custom_call_target="tpu_custom_call" | custom-call | flops 5000000000 | tf_op jit(solution)/shard_map/pallas_call | solution.py:74
  32.0 0.1 collective-permute-start.12
  32.1 0.0 collective-permute-done.9.refs_1_
  32.1 0.3 shard_map.101.refs_2_.refs_0_
  32.5 1.5 %collective-permute-done.12.refs_1_ = bf16[256,1024]{1,0:T(8,128)(2,1)S(1)} collective-permute-done((bf16[256,1024]{1,0:T(8,128)(2,1)S(1)}, bf16[256,1024]{1,0:T(8,128)(2,1)S(1)}, u32[]{:S(2)}, u32[]{:S(2)}) %collective-permute-start.12) | collective-permute-done | bytes 524320 | tf_op jit(solution)/shard_map/ppermute | solution.py:316
  34.0 0.2 shard_map.102.refs_3_.refs_2_
  34.2 0.0 collective-permute-done.13.refs_2_
  34.3 0.2 collective-permute-start.14
  34.5 1.1 %shard_map.104.refs_6_ = f32[256,128]{1,0:T(8,128)} custom-call(bf16[256,256]{1,0:T(8,128)(2,1)S(1)} %copy-done.1, bf16[128,256]{1,0:T(8,128)(2,1)S(1)} %shard_map.103.refs_1_.refs_4_), custom_call_target="tpu_custom_call" | custom-call | flops 8000000000 | tf_op jit(solution)/shard_map/pallas_call | solution.py:74
  35.5 0.1 collective-permute-done.14.refs_5_
  35.6 1.3 %shard_map.105 = bf16[2,1024,256]{2,1,0:T(8,128)(2,1)} custom-call(f32[1024,256]{1,0:T(8,128)S(1)} %shard_map.101.refs_2_.refs_0_, f32[1024,256]{1,0:T(8,128)S(1)} %get-tuple-element.69.refs_1_, bf16[1024,256]{1,0:T(8,128)(2,1)S(1)} %shard_map.102.refs_3_.refs_2_, bf16[1024,256]{1,0:T(8,128)(2,1)S(1)} %get-tuple-element.71.refs_3_, ...), custom_call_target="tpu_custom_call" | custom-call | flops 8000000000 | tf_op jit(solution)/shard_map/pallas_call | solution.py:74
  (5 shorter events, 0.1 us)
Async XLA Ops:
  0.6 4.4 %collective-permute-start = (bf16[2,1024,256]{2,1,0:T(8,128)(2,1)}, bf16[2,1024,256]{2,1,0:T(8,128)(2,1)S(1)}, u32[]{:S(2)}, u32[]{:S(2)}) collective-permute-start(bf16[2,1024,256]{2,1,0:T(8,128)(2,1)} %refs_3_.4), channel_id=1, source_target_pairs={{0,1},{1,0},{2,3},{3,2},{4,5},{5,4},{6,7},{7,6},{8,9},{9,8},{10,11... | collective-permute-start | bytes 3145736 | tf_op jit(solution)/shard_map/ppermute | solution.py:316
  4.0 4.5 %collective-permute-start.2 = (bf16[256,1024]{1,0:T(8,128)(2,1)S(1)}, bf16[256,1024]{1,0:T(8,128)(2,1)S(1)}, u32[]{:S(2)}, u32[]{:S(2)}) collective-permute-start(bf16[256,1024]{1,0:T(8,128)(2,1)S(1)} %bitcast.10), channel_id=1, source_target_pairs={{0,1},{1,0},{2,3},{3,2},{4,5},{5,4},{6,7},{7,6},{8,9},{9,8},{10,11... | collective-permute-start | bytes 1572872 | tf_op jit(solution)/shard_map/ppermute | solution.py:316
  6.8 2.0 %collective-permute-start.1 = (bf16[1024,256]{1,0:T(8,128)(2,1)S(1)}, bf16[1024,256]{1,0:T(8,128)(2,1)S(1)}, u32[]{:S(2)}, u32[]{:S(2)}) collective-permute-start(bf16[1024,256]{1,0:T(8,128)(2,1)S(1)} %get-tuple-element.44.refs_2_), channel_id=1, source_target_pairs={{0,1},{1,0},{2,3},{3,2},{4,5},{5,4},{6,7},{7,6},{8,9},{9,8},{10,11... | collective-permute-start | bytes 1572872 | tf_op jit(solution)/shard_map/ppermute | solution.py:316
  11.3 1.6 %collective-permute-start.3 = (bf16[128,256]{1,0:T(8,128)(2,1)S(1)}, bf16[128,256]{1,0:T(8,128)(2,1)S(1)}, u32[]{:S(2)}, u32[]{:S(2)}) collective-permute-start(bf16[128,256]{1,0:T(8,128)(2,1)S(1)} %bitcast.13), channel_id=1, source_target_pairs={{0,1},{1,0},{2,3},{3,2},{4,5},{5,4},{6,7},{7,6},{8,9},{9,8},{10,11... | collective-permute-start | bytes 196616 | tf_op jit(solution)/shard_map/ppermute | solution.py:316
  12.9 3.3 %collective-permute-start.4 = (bf16[1024,256]{1,0:T(8,128)(2,1)S(1)}, bf16[1024,256]{1,0:T(8,128)(2,1)S(1)}, u32[]{:S(2)}, u32[]{:S(2)}) collective-permute-start(bf16[1024,256]{1,0:T(8,128)(2,1)S(1)} %get-tuple-element.54), channel_id=1, source_target_pairs={{0,1},{1,0},{2,3},{3,2},{4,5},{5,4},{6,7},{7,6},{8,9},{9,8},{10,11... | collective-permute-start | bytes 1572872 | tf_op jit(solution)/shard_map/ppermute | solution.py:316
  13.3 5.2 %collective-permute-start.6 = (bf16[128,256]{1,0:T(8,128)(2,1)S(1)}, bf16[128,256]{1,0:T(8,128)(2,1)S(1)}, u32[]{:S(2)}, u32[]{:S(2)}) collective-permute-start(bf16[128,256]{1,0:T(8,128)(2,1)S(1)} %get-tuple-element.55.refs_3_.refs_0_), channel_id=1, source_target_pairs={{0,2},{1,9},{2,0},{3,11},{4,6},{5,13},{6,4},{7,15},{8,10},{9,1},{1... | collective-permute-start | bytes 196616 | tf_op jit(solution)/shard_map/ppermute | solution.py:333
  17.1 4.8 %collective-permute-start.5 = (bf16[256,1024]{1,0:T(8,128)(2,1)S(1)}, bf16[256,1024]{1,0:T(8,128)(2,1)S(1)}, u32[]{:S(2)}, u32[]{:S(2)}) collective-permute-start(bf16[256,1024]{1,0:T(8,128)(2,1)S(1)} %bitcast.11), channel_id=1, source_target_pairs={{0,1},{1,0},{2,3},{3,2},{4,5},{5,4},{6,7},{7,6},{8,9},{9,8},{10,11... | collective-permute-start | bytes 1572872 | tf_op jit(solution)/shard_map/ppermute | solution.py:316
  18.6 5.6 %collective-permute-start.8 = (bf16[128,256]{1,0:T(8,128)(2,1)S(1)}, bf16[128,256]{1,0:T(8,128)(2,1)S(1)}, u32[]{:S(2)}, u32[]{:S(2)}) collective-permute-start(bf16[128,256]{1,0:T(8,128)(2,1)S(1)} %shard_map.93.refs_2_.refs_0_), channel_id=1, source_target_pairs={{0,4},{1,17},{2,6},{3,19},{4,0},{5,21},{6,2},{7,23},{8,12},{9,25},... | collective-permute-start | bytes 196616 | tf_op jit(solution)/shard_map/ppermute | solution.py:333
  21.9 3.9 %copy-start = (f32[256,128]{1,0:T(8,128)S(1)}, f32[256,128]{1,0:T(8,128)}, u32[]{:S(2)}) copy-start(f32[256,128]{1,0:T(8,128)} %refs_2_.8) | copy-start | bytes 393220
  21.9 3.9 %copy-start.1 = (bf16[256,256]{1,0:T(8,128)(2,1)S(1)}, bf16[256,256]{1,0:T(8,128)(2,1)}, u32[]{:S(2)}) copy-start(bf16[256,256]{1,0:T(8,128)(2,1)} %refs_0_.5) | copy-start | bytes 393220
  23.2 3.4 %collective-permute-start.7 = (bf16[256,1024]{1,0:T(8,128)(2,1)S(1)}, bf16[256,1024]{1,0:T(8,128)(2,1)S(1)}, u32[]{:S(2)}, u32[]{:S(2)}) collective-permute-start(bf16[256,1024]{1,0:T(8,128)(2,1)S(1)} %bitcast.9), channel_id=1, source_target_pairs={{0,1},{1,0},{2,3},{3,2},{4,5},{5,4},{6,7},{7,6},{8,9},{9,8},{10,11... | collective-permute-start | bytes 1572872 | tf_op jit(solution)/shard_map/ppermute | solution.py:316
  24.0 6.8 %collective-permute-start.10 = (bf16[256,1024]{1,0:T(8,128)(2,1)S(1)}, bf16[256,1024]{1,0:T(8,128)(2,1)S(1)}, u32[]{:S(2)}, u32[]{:S(2)}) collective-permute-start(bf16[256,1024]{1,0:T(8,128)(2,1)S(1)} %bitcast.7), channel_id=1, source_target_pairs={{0,1},{1,0},{2,3},{3,2},{4,5},{5,4},{6,7},{7,6},{8,9},{9,8},{10,11... | collective-permute-start | bytes 1572872 | tf_op jit(solution)/shard_map/ppermute | solution.py:316
  24.1 4.3 %collective-permute-start.11 = (bf16[128,256]{1,0:T(8,128)(2,1)S(1)}, bf16[128,256]{1,0:T(8,128)(2,1)S(1)}, u32[]{:S(2)}, u32[]{:S(2)}) collective-permute-start(bf16[128,256]{1,0:T(8,128)(2,1)S(1)} %shard_map.96.refs_4_.refs_0_), channel_id=1, source_target_pairs={{0,8},{1,3},{2,10},{3,1},{4,12},{5,7},{6,14},{7,5},{8,0},{9,11},{1... | collective-permute-start | bytes 196616 | tf_op jit(solution)/shard_map/ppermute | solution.py:333
  27.5 4.6 %collective-permute-start.9 = (bf16[256,1024]{1,0:T(8,128)(2,1)S(1)}, bf16[256,1024]{1,0:T(8,128)(2,1)S(1)}, u32[]{:S(2)}, u32[]{:S(2)}) collective-permute-start(bf16[256,1024]{1,0:T(8,128)(2,1)S(1)} %bitcast.8), channel_id=1, source_target_pairs={{0,1},{1,0},{2,3},{3,2},{4,5},{5,4},{6,7},{7,6},{8,9},{9,8},{10,11... | collective-permute-start | bytes 1572872 | tf_op jit(solution)/shard_map/ppermute | solution.py:316
  28.5 5.7 %collective-permute-start.13 = (bf16[128,256]{1,0:T(8,128)(2,1)S(1)}, bf16[128,256]{1,0:T(8,128)(2,1)S(1)}, u32[]{:S(2)}, u32[]{:S(2)}) collective-permute-start(bf16[128,256]{1,0:T(8,128)(2,1)S(1)} %shard_map.99.refs_5_.refs_1_), channel_id=1, source_target_pairs={{0,16},{1,5},{2,18},{3,7},{4,20},{5,1},{6,22},{7,3},{8,24},{9,13},... | collective-permute-start | bytes 196616 | tf_op jit(solution)/shard_map/ppermute | solution.py:333
  32.0 2.0 %collective-permute-start.12 = (bf16[256,1024]{1,0:T(8,128)(2,1)S(1)}, bf16[256,1024]{1,0:T(8,128)(2,1)S(1)}, u32[]{:S(2)}, u32[]{:S(2)}) collective-permute-start(bf16[256,1024]{1,0:T(8,128)(2,1)S(1)} %bitcast.12), channel_id=1, source_target_pairs={{0,1},{1,0},{2,3},{3,2},{4,5},{5,4},{6,7},{7,6},{8,9},{9,8},{10,11... | collective-permute-start | bytes 1572872 | tf_op jit(solution)/shard_map/ppermute | solution.py:316
  34.3 1.3 %collective-permute-start.14 = (bf16[128,256]{1,0:T(8,128)(2,1)S(1)}, bf16[128,256]{1,0:T(8,128)(2,1)S(1)}, u32[]{:S(2)}, u32[]{:S(2)}) collective-permute-start(bf16[128,256]{1,0:T(8,128)(2,1)S(1)} %shard_map.103.refs_1_.refs_4_), channel_id=1, source_target_pairs={{0,1},{1,0},{2,3},{3,2},{4,5},{5,4},{6,7},{7,6},{8,9},{9,8},{10,11... | collective-permute-start | bytes 196616 | tf_op jit(solution)/shard_map/ppermute | solution.py:316

commit v9 on v8

--- a/solution.py
+++ b/solution.py
@@ -37,6 +37,7 @@
     nodes = n_space * rows
     tile = 256 if rows % 256 == 0 else rows
     tiles = rows // tile
+    wide = 2 * tile if rows % (2 * tile) == 0 else tile
     eighth = rows // 8
     head = rows - eighth
     width = columns // n_space
@@ -98,9 +99,8 @@
             def _():
                 other_ref[step - 1] = jnp.zeros_like(other_ref[step - 1])
 
-        for j in range(tiles):
-            at = j * tile
-            own_ref[:, at : at + tile] = dot(left[:, at:], factor[at:, block(0, at, tile)])
+        for at in range(0, rows, wide):
+            own_ref[:, at : at + wide] = dot(left[:, at:], factor[at:, block(0, at, wide)])
 
     def full_rows(left, factor, own_ref, other_ref):
         for step in peers:
@@ -158,6 +158,11 @@
         arrow_copy.start()
         for i in range(tiles):
             each(copies1, i, lambda copy: copy.start(priority=i % 2))
+        for factor in (d0, d1):
+            for at in range(0, rows, wide):
+                for inner in range(at + tile, at + wide, tile):
+                    part = (pl.ds(at, inner - at), block(0, inner, tile))
+                    factor[part] = jnp.zeros((inner - at, tile), BF)
         live_copy.wait()
         arrow_copy.wait()
         live = live_scratch[lax.axis_index("tm")] > 1
@@ -172,11 +177,12 @@
             each(copies0, i, lambda copy: copy.wait())
         noise_copy.wait()
 
-    def k1_copies(coupling, k1, first, count, sems):
+    def k1_copies(coupling, k1, first, count, sems, split=2):
         copies = []
-        for i in range(count):
-            part = pl.ds((first + i) * eighth, eighth)
-            target = k1.at[part] if k1.shape[0] == rows else k1
+        size = max(eighth // split, 16)
+        for i in range(count * eighth // size):
+            part = pl.ds(first * eighth + i * size, size)
+            target = k1.at[part] if k1.shape[0] == rows else k1.at[pl.ds(i * size, size)]
             copies.append(pltpu.make_async_copy(coupling.at[1, part], target, sems.at[i]))
             copies[-1].start(priority=i % 2)
         return copies
@@ -184,7 +190,7 @@
     def first_value_kernel(d0, n0, coupling, noise, *refs):
         got, (out, bar, k1, n1, sems) = refs[: n_space - 1], refs[n_space - 1 :]
         copies = k1_copies(coupling, k1, 0, 3, sems)
-        copies.append(pltpu.make_async_copy(noise.at[1], n1, sems.at[3]))
+        copies.append(pltpu.make_async_copy(noise.at[1], n1, sems.at[6]))
         copies[-1].start()
         lower_own(d0, n0, out)
         lower_rest(d0, [piece.at[0] for piece in got], out)
@@ -202,8 +208,8 @@
         got, refs = refs[: n_space - 1], refs[n_space - 1 :]
         got_own, refs = refs[: n_space - 1], refs[n_space - 1 :]
         target, part_own, part_other, response, e0, tail, whole, sems = refs
-        arrow_copy = pltpu.make_async_copy(arrow.at[0], e0, sems.at[1])
-        (tail_copy,) = k1_copies(coupling, tail, 7, 1, sems)
+        arrow_copy = pltpu.make_async_copy(arrow.at[0], e0, sems.at[2])
+        tail_copies = k1_copies(coupling, tail, 7, 1, sems)
         arrow_copy.start()
 
         def pull(at, size):
@@ -218,7 +224,8 @@
             pull(at, min(tile, head - at))
         arrow_copy.wait()
         whole[...] = dot(e0[...], bar[...])
-        tail_copy.wait()
+        for copy in tail_copies:
+            copy.wait()
         pull(head, eighth)
         whole[...] = (whole[...] + dot(response[...], target[...])).T
         part_own[...] = whole[part_rows(0)]
@@ -226,9 +233,10 @@
             part_other[step - 1] = whole[part_rows(step)].astype(BF)
 
     def last_own_kernel(d1, target, coupling, _, value, k1, sems):
-        (tail_copy,) = k1_copies(coupling, k1, 7, 1, sems)
+        copies = k1_copies(coupling, k1, 7, 1, sems, 4)
         lower_own(d1, target, value)
-        tail_copy.wait()
+        for copy in copies:
+            copy.wait()
 
     def core_sum_kernel(part, _, *refs):
         got, (out, _) = refs[:-2], refs[-2:]
@@ -244,7 +252,7 @@
         got, (own, other, value) = refs[: n_space - 1], refs[n_space - 1 :]
         value[...] = first[...]
         lower_rest(d1, got, value)
-        lower_rows(value[...].T.astype(BF), d1, own, other)
+        lower_rows(value[...].astype(BF).T, d1, own, other)
 
     def response_kernel(k1, response, own, other):
         full_rows(response, k1, own, other)
@@ -328,7 +336,9 @@
         pairs = []
         for i in range(n_tm):
             for core in range(n_space):
-                bit = 1 << (step + core * steps // n_space) % steps
+                bit = 1 << step
+                if step < steps - 1:
+                    bit = 1 << (step + core * (steps - 1) // n_space) % (steps - 1)
                 pairs.append((i * n_space + core, (i ^ bit) * n_space + core))
         return lax.ppermute(value, ("tm", "space"), pairs)
 
@@ -370,7 +380,7 @@
             [d0, n0, coupling, noise, *got_noise],
             8,
             {2: pltpu.HBM, 3: pltpu.HBM},
-            [dma((4,))],
+            [dma((7,))],
         )
         got_bar = send_up(bar)
         value_rows, k1 = call(
@@ -379,7 +389,7 @@
             [coupling, value, k1],
             8,
             {0: pltpu.HBM, 2: pl.ANY, ("out", 1): pl.ANY},
-            [dma((4,))],
+            [dma((8,))],
             aliases={2: 1},
         )
         target, part_own, part_other, response, e0 = call(
@@ -397,7 +407,7 @@
             [
                 pltpu.VMEM((eighth, nodes), BF),
                 pltpu.VMEM((columns, fixed_rows), F32),
-                dma((2,)),
+                dma((3,)),
             ],
         )
         got_parts = send_down(part_other)
@@ -407,7 +417,7 @@
             [d1, target, coupling, k1],
             8,
             {2: pltpu.HBM, 3: pl.ANY, ("out", 1): pl.ANY},
-            [dma((1,))],
+            [dma((4,))],
             aliases={3: 1},
         )
         sent, target = call(

time: 37.2 us -> 37.4 us (level)
    ppermute x11, starting transfers between devices: 5.74 us -> 5.06 us  [swap(): return lax.ppermute(value, 'space', pairs)]
where the time goes in v9:
time: 37.4 us; the launch traced here: 37.1 us
  Pallas kernels  19.5 us (52%)
  starting transfers between devices  14.4 us (39%)
  waiting for transfers between devices  2.42 us (6%)
  between operations  0.82 us (2%)
    pallas_call x20, Pallas kernels, call(): pl.pallas_call(run, in_specs=specs, out_specs=[pl.BlockSpec(memory_space=...  19.5 us
    ppermute x4, starting transfers between devices, swap_step(): return lax.ppermute(value, ('tm', 'space'), pairs)  9.3 us
    ppermute x11, starting transfers between devices, swap(): return lax.ppermute(value, 'space', pairs)  5.06 us
    ppermute x11, waiting for transfers between devices, swap(): return lax.ppermute(value, 'space', pairs)  1.92 us
  transfers between devices with their start and end apart: 15, of which 4 were waited for; matrix products, arithmetic and copies ran while one was open for 0% of the time, Pallas kernels for 42%

profile of v9, /device:TPU:0, one launch (start us, length us, event | category | flops | bytes accessed | tf_op | source)
XLA Modules:
  0.0 37.1 jit_solution(4886201891537208224)
XLA Ops:
  0.6 0.5 %collective-permute-start = (bf16[2,1024,256]{2,1,0:T(8,128)(2,1)}, bf16[2,1024,256]{2,1,0:T(8,128)(2,1)S(1)}, u32[]{:S(2)}, u32[]{:S(2)}) collective-permute-start(bf16[2,1024,256]{2,1,0:T(8,128)(2,1)} %refs_3_.4), channel_id=1, source_target_pairs={{0,1},{1,0},{2,3},{3,2},{4,5},{5,4},{6,7},{7,6},{8,9},{9,8},{10,11... | collective-permute-start | bytes 3145736 | tf_op jit(solution)/shard_map/ppermute | solution.py:324
  1.1 2.8 %shard_map.86 = (bf16[1024,2048]{1,0:T(8,128)(2,1)S(1)}, bf16[1024,2048]{1,0:T(8,128)(2,1)S(1)}, f32[256,1024]{1,0:T(8,128)S(1)}, bf16[1,256,1024]{2,1,0:T(8,128...) custom-call(bf16[2,1024,2048]{2,1,0:T(8,128)(2,1)} %refs_0_.3, bf16[2,256,1024]{2,1,0:T(8,128)(2,1)} %refs_4_.1, ...), custom_call_target="tpu_custom_call" | custom-call | flops 8000000000 | tf_op jit(solution)/shard_map/pallas_call | solution.py:75
  4.0 1.1 %collective-permute-start.2 = (bf16[256,1024]{1,0:T(8,128)(2,1)S(1)}, bf16[256,1024]{1,0:T(8,128)(2,1)S(1)}, u32[]{:S(2)}, u32[]{:S(2)}) collective-permute-start(bf16[256,1024]{1,0:T(8,128)(2,1)S(1)} %bitcast.10), channel_id=1, source_target_pairs={{0,1},{1,0},{2,3},{3,2},{4,5},{5,4},{6,7},{7,6},{8,9},{9,8},{10,11... | collective-permute-start | bytes 1572872 | tf_op jit(solution)/shard_map/ppermute | solution.py:324
  5.1 0.0 collective-permute-done.refs_4_
  5.1 1.8 %shard_map.87 = (f32[1024,256]{1,0:T(8,128)S(1)}, bf16[1024,256]{1,0:T(8,128)(2,1)S(1)}, bf16[1024,2048]{1,0:T(8,128)(2,1)S(1)}, bf16[1024,256]{1,0:T(8,128)(2,1)S(1)}) custom-call(bf16[1024,2048]{1,0:T(8,128)(2,1)S(1)} %get-tuple-element.37.refs_0_, bf16[1024,256]{1,0:T(8,128)(2,1)S(1)} %get-tuple-element.38.refs_1_, bf16[2,1024,2048]{2,1,0:T(8,128)(2,1)} %refs_2_.7, ...), custom_call_target="tpu_custom_call" | custom-call | flops 8000000000 | tf_op jit(solution)/shard_map/pallas_call | solution.py:75
  6.9 0.1 collective-permute-start.1
  7.0 1.6 %shard_map.88 = (f32[256,1024]{1,0:T(8,128)S(1)}, bf16[1024,2048]{1,0:T(8,128)(2,1)S(1)}) custom-call(bf16[2,1024,2048]{2,1,0:T(8,128)(2,1)} %refs_2_.7, f32[1024,256]{1,0:T(8,128)S(1)} %get-tuple-element.39.refs_1_, bf16[1024,2048]{1,0:T(8,128)(2,1)S(1)} %get-tuple-element.40.refs_2_), custom_call_target="tpu_custom_call", output_to_operand_aliasing={{1}: (2, {})} | custom-call | flops 8000000000 | tf_op jit(solution)/shard_map/pallas_call | solution.py:75
  8.6 0.0 collective-permute-done.2.refs_7_
  8.6 0.3 collective-permute-done.1.refs_6_
  8.9 2.5 %shard_map.89 = (bf16[1024,256]{1,0:T(8,128)(2,1)S(1)}, f32[128,256]{1,0:T(8,128)S(1)}, bf16[1,128,256]{2,1,0:T(8,128)(2,1)S(1)}, bf16[256,1024]{1,0:T(8,128)(2,1)S(1)}, bf16[256,1024]{1,0:T(8,128)(2,1)S(1)}) custom-call(bf16[1024,2048]{1,0:T(8,128)(2,1)S(1)} %get-tuple-element.43.refs_0_.refs_3_, bf16[2,1024,2048]{2,1,0:T(8,128)(2,1)} %refs_2_.7, ...), custom_call_target="tpu_custom_call" | custom-call | flops 8000000000 | tf_op jit(solution)/shard_map/pallas_call | solution.py:75
  11.4 0.3 collective-permute-start.3
  11.7 1.4 %shard_map.90 = (f32[1024,256]{1,0:T(8,128)S(1)}, bf16[1024,2048]{1,0:T(8,128)(2,1)S(1)}) custom-call(bf16[1024,2048]{1,0:T(8,128)(2,1)S(1)} %get-tuple-element.42.refs_0_, bf16[1024,256]{1,0:T(8,128)(2,1)S(1)} %get-tuple-element.48.refs_1_, bf16[2,1024,2048]{2,1,0:T(8,128)(2,1)} %refs_2_.7, ...), custom_call_target="tpu_custom_call", output_to_operand_aliasing={{1}: (3, {})} | custom-call | flops 8000000000 | tf_op jit(solution)/shard_map/pallas_call | solution.py:75
  13.1 0.0 collective-permute-done.3.refs_2_
  13.1 0.4 collective-permute-start.4
  13.5 2.9 %collective-permute-start.6 = (bf16[128,256]{1,0:T(8,128)(2,1)S(1)}, bf16[128,256]{1,0:T(8,128)(2,1)S(1)}, u32[]{:S(2)}, u32[]{:S(2)}) collective-permute-start(bf16[128,256]{1,0:T(8,128)(2,1)S(1)} %get-tuple-element.55.refs_3_.refs_0_), channel_id=1, source_target_pairs={{0,2},{1,5},{2,0},{3,7},{4,6},{5,1},{6,4},{7,3},{8,10},{9,13},{10,... | collective-permute-start | bytes 196616 | tf_op jit(solution)/shard_map/ppermute | solution.py:343
  16.4 0.0 collective-permute-done.4.refs_2_
  16.4 0.9 %shard_map.92 = (f32[256,1024]{1,0:T(8,128)S(1)}, bf16[1,256,1024]{2,1,0:T(8,128)(2,1)S(1)}) custom-call(bf16[1024,2048]{1,0:T(8,128)(2,1)S(1)} %get-tuple-element.42.refs_0_, f32[1024,256]{1,0:T(8,128)S(1)} %get-tuple-element.51.refs_3_.refs_1_, bf16[1024,256]{1,0:T(8,128)(2,1)S(1)} %collective-permute-done.4.refs_2_, ...), custom_call_target="tpu_custom_call" | custom-call | flops 8000000000 | tf_op jit(solution)/shard_map/pallas_call | solution.py:75
  17.3 1.4 %collective-permute-start.5 = (bf16[256,1024]{1,0:T(8,128)(2,1)S(1)}, bf16[256,1024]{1,0:T(8,128)(2,1)S(1)}, u32[]{:S(2)}, u32[]{:S(2)}) collective-permute-start(bf16[256,1024]{1,0:T(8,128)(2,1)S(1)} %bitcast.11), channel_id=1, source_target_pairs={{0,1},{1,0},{2,3},{3,2},{4,5},{5,4},{6,7},{7,6},{8,9},{9,8},{10,11... | collective-permute-start | bytes 1572872 | tf_op jit(solution)/shard_map/ppermute | solution.py:324
  18.7 0.0 collective-permute-done.6.refs_1_
  18.7 2.1 %collective-permute-start.8 = (bf16[128,256]{1,0:T(8,128)(2,1)S(1)}, bf16[128,256]{1,0:T(8,128)(2,1)S(1)}, u32[]{:S(2)}, u32[]{:S(2)}) collective-permute-start(bf16[128,256]{1,0:T(8,128)(2,1)S(1)} %shard_map.93.refs_2_.refs_0_), channel_id=1, source_target_pairs={{0,4},{1,9},{2,6},{3,11},{4,0},{5,13},{6,2},{7,15},{8,12},{9,1},{1... | collective-permute-start | bytes 196616 | tf_op jit(solution)/shard_map/ppermute | solution.py:343
  20.8 1.2 %shard_map.94 = (f32[256,1024]{1,0:T(8,128)S(1)}, bf16[1,256,1024]{2,1,0:T(8,128)(2,1)S(1)}) custom-call(bf16[1024,2048]{1,0:T(8,128)(2,1)S(1)} %get-tuple-element.49.refs_0_, bf16[256,1024]{1,0:T(8,128)(2,1)S(1)} %get-tuple-element.58.refs_1_, bf16[128,256]{1,0:T(8,128)(2,1)S(1)} %shard_map.93.refs_2_.refs_0_), custom_call_target="tpu_custom_call" | custom-call | flops 5000000000 | tf_op jit(solution)/shard_map/pallas_call | solution.py:75
  22.0 0.0 collective-permute-done.5.refs_3_
  22.0 0.0 copy-start
  22.1 0.0 copy-start.1
  22.1 1.3 %shard_map.95 = (f32[256,1024]{1,0:T(8,128)S(1)}, f32[256,1024]{1,0:T(8,128)S(1)}, bf16[1,256,1024]{2,1,0:T(8,128)(2,1)S(1)}) custom-call(bf16[1024,2048]{1,0:T(8,128)(2,1)S(1)} %get-tuple-element.49.refs_0_, f32[8,128]{1,0:T(8,128)S(1)} %get-tuple-element.50.refs_1_, f32[256,1024]{1,0:T(8,128)S(1)} %get-tuple-element.56.refs_2_, ...), custom_call_target="tpu_custom_call" | custom-call | flops 8000000000 | tf_op jit(solution)/shard_map/pallas_call | solution.py:75
  23.4 0.1 collective-permute-start.7
  23.4 0.5 %collective-permute-start.10 = (bf16[256,1024]{1,0:T(8,128)(2,1)S(1)}, bf16[256,1024]{1,0:T(8,128)(2,1)S(1)}, u32[]{:S(2)}, u32[]{:S(2)}) collective-permute-start(bf16[256,1024]{1,0:T(8,128)(2,1)S(1)} %bitcast.7), channel_id=1, source_target_pairs={{0,1},{1,0},{2,3},{3,2},{4,5},{5,4},{6,7},{7,6},{8,9},{9,8},{10,11... | collective-permute-start | bytes 1572872 | tf_op jit(solution)/shard_map/ppermute | solution.py:324
  23.9 0.0 collective-permute-done.8.refs_1_
  24.0 1.6 %collective-permute-start.11 = (bf16[128,256]{1,0:T(8,128)(2,1)S(1)}, bf16[128,256]{1,0:T(8,128)(2,1)S(1)}, u32[]{:S(2)}, u32[]{:S(2)}) collective-permute-start(bf16[128,256]{1,0:T(8,128)(2,1)S(1)} %shard_map.96.refs_4_.refs_0_), channel_id=1, source_target_pairs={{0,8},{1,3},{2,10},{3,1},{4,12},{5,7},{6,14},{7,5},{8,0},{9,11},{1... | collective-permute-start | bytes 196616 | tf_op jit(solution)/shard_map/ppermute | solution.py:343
  25.6 0.0 copy-done
  25.6 0.0 copy-done.1
  25.6 0.8 %shard_map.97 = (f32[1024,256]{1,0:T(8,128)S(1)}, bf16[1024,256]{1,0:T(8,128)(2,1)S(1)}, f32[128,256]{1,0:T(8,128)S(1)}) custom-call(f32[256,1024]{1,0:T(8,128)S(1)} %get-tuple-element.62.refs_2_.refs_0_, bf16[256,1024]{1,0:T(8,128)(2,1)S(1)} %get-tuple-element.58.refs_1_, f32[256,128]{1,0:T(8,128)S(1)} %copy-done, bf16[256,256]{1,0:T(8,128)(2,1)S(1)} %copy-done.1, ...), custom_call_target="tpu_custom_call" | custom-call | flops 5000000000 | tf_op jit(solution)/shard_map/pallas_call | solution.py:75
  26.4 0.0 collective-permute-done.7.refs_3_
  26.4 0.9 %shard_map.98 = (f32[256,1024]{1,0:T(8,128)S(1)}, bf16[1,256,1024]{2,1,0:T(8,128)(2,1)S(1)}) custom-call(bf16[1024,2048]{1,0:T(8,128)(2,1)S(1)} %get-tuple-element.37.refs_0_, f32[256,1024]{1,0:T(8,128)S(1)} %get-tuple-element.41.refs_1_, f32[256,1024]{1,0:T(8,128)S(1)} %get-tuple-element.60.refs_2_, bf16[256,1024]{1,0:T(8,128)(2,1)S(1)} %collective-permute-done.7.refs_3_, ...), custom_call_target="tpu_custom_call" | custom-call | flops 8000000000 | tf_op jit(solution)/shard_map/pallas_call | solution.py:75
  27.4 0.5 %collective-permute-start.9 = (bf16[256,1024]{1,0:T(8,128)(2,1)S(1)}, bf16[256,1024]{1,0:T(8,128)(2,1)S(1)}, u32[]{:S(2)}, u32[]{:S(2)}) collective-permute-start(bf16[256,1024]{1,0:T(8,128)(2,1)S(1)} %bitcast.8), channel_id=1, source_target_pairs={{0,1},{1,0},{2,3},{3,2},{4,5},{5,4},{6,7},{7,6},{8,9},{9,8},{10,11... | collective-permute-start | bytes 1572872 | tf_op jit(solution)/shard_map/ppermute | solution.py:324
  27.8 0.5 %collective-permute-done.11.refs_1_ = bf16[128,256]{1,0:T(8,128)(2,1)S(1)} collective-permute-done((bf16[128,256]{1,0:T(8,128)(2,1)S(1)}, bf16[128,256]{1,0:T(8,128)(2,1)S(1)}, u32[]{:S(2)}, u32[]{:S(2)}) %collective-permute-start.11) | collective-permute-done | bytes 65568 | tf_op jit(solution)/shard_map/ppermute | solution.py:343
  28.3 2.7 %collective-permute-start.13 = (bf16[128,256]{1,0:T(8,128)(2,1)S(1)}, bf16[128,256]{1,0:T(8,128)(2,1)S(1)}, u32[]{:S(2)}, u32[]{:S(2)}) collective-permute-start(bf16[128,256]{1,0:T(8,128)(2,1)S(1)} %shard_map.99.refs_5_.refs_1_), channel_id=1, source_target_pairs={{0,16},{1,17},{2,18},{3,19},{4,20},{5,21},{6,22},{7,23},{8,24},{9,... | collective-permute-start | bytes 196616 | tf_op jit(solution)/shard_map/ppermute | solution.py:343
  31.0 0.0 collective-permute-done.10.refs_4_
  31.0 1.2 %shard_map.100 = (f32[256,1024]{1,0:T(8,128)S(1)}, bf16[1,256,1024]{2,1,0:T(8,128)(2,1)S(1)}) custom-call(bf16[1024,2048]{1,0:T(8,128)(2,1)S(1)} %get-tuple-element.37.refs_0_, bf16[256,1024]{1,0:T(8,128)(2,1)S(1)} %get-tuple-element.66.refs_1_, bf16[256,256]{1,0:T(8,128)(2,1)S(1)} %copy-done.1, f32[256,1024]{1,0:T(8,128)S(1)} %get-tuple-element.59.refs_4_.refs_3_, ...), custom_call_target="tpu_custom_call" | custom-call | flops 5000000000 | tf_op jit(solution)/shard_map/pallas_call | solution.py:75
  32.2 0.1 collective-permute-start.12
  32.3 0.0 collective-permute-done.9.refs_1_
  32.3 0.3 shard_map.101.refs_2_.refs_0_
  32.7 1.5 %collective-permute-done.12.refs_1_ = bf16[256,1024]{1,0:T(8,128)(2,1)S(1)} collective-permute-done((bf16[256,1024]{1,0:T(8,128)(2,1)S(1)}, bf16[256,1024]{1,0:T(8,128)(2,1)S(1)}, u32[]{:S(2)}, u32[]{:S(2)}) %collective-permute-start.12) | collective-permute-done | bytes 524320 | tf_op jit(solution)/shard_map/ppermute | solution.py:324
  34.2 0.2 shard_map.102.refs_3_.refs_2_
  34.4 0.0 collective-permute-done.13.refs_2_
  34.5 0.2 collective-permute-start.14
  34.7 1.1 %shard_map.104.refs_6_ = f32[256,128]{1,0:T(8,128)} custom-call(bf16[256,256]{1,0:T(8,128)(2,1)S(1)} %copy-done.1, bf16[128,256]{1,0:T(8,128)(2,1)S(1)} %shard_map.103.refs_1_.refs_4_), custom_call_target="tpu_custom_call" | custom-call | flops 8000000000 | tf_op jit(solution)/shard_map/pallas_call | solution.py:75
  35.7 0.1 collective-permute-done.14.refs_5_
  35.8 1.3 %shard_map.105 = bf16[2,1024,256]{2,1,0:T(8,128)(2,1)} custom-call(f32[1024,256]{1,0:T(8,128)S(1)} %shard_map.101.refs_2_.refs_0_, f32[1024,256]{1,0:T(8,128)S(1)} %get-tuple-element.69.refs_1_, bf16[1024,256]{1,0:T(8,128)(2,1)S(1)} %shard_map.102.refs_3_.refs_2_, bf16[1024,256]{1,0:T(8,128)(2,1)S(1)} %get-tuple-element.71.refs_3_, ...), custom_call_target="tpu_custom_call" | custom-call | flops 8000000000 | tf_op jit(solution)/shard_map/pallas_call | solution.py:75
  (5 shorter events, 0.1 us)
Async XLA Ops:
  0.6 4.4 %collective-permute-start = (bf16[2,1024,256]{2,1,0:T(8,128)(2,1)}, bf16[2,1024,256]{2,1,0:T(8,128)(2,1)S(1)}, u32[]{:S(2)}, u32[]{:S(2)}) collective-permute-start(bf16[2,1024,256]{2,1,0:T(8,128)(2,1)} %refs_3_.4), channel_id=1, source_target_pairs={{0,1},{1,0},{2,3},{3,2},{4,5},{5,4},{6,7},{7,6},{8,9},{9,8},{10,11... | collective-permute-start | bytes 3145736 | tf_op jit(solution)/shard_map/ppermute | solution.py:324
  4.0 4.6 %collective-permute-start.2 = (bf16[256,1024]{1,0:T(8,128)(2,1)S(1)}, bf16[256,1024]{1,0:T(8,128)(2,1)S(1)}, u32[]{:S(2)}, u32[]{:S(2)}) collective-permute-start(bf16[256,1024]{1,0:T(8,128)(2,1)S(1)} %bitcast.10), channel_id=1, source_target_pairs={{0,1},{1,0},{2,3},{3,2},{4,5},{5,4},{6,7},{7,6},{8,9},{9,8},{10,11... | collective-permute-start | bytes 1572872 | tf_op jit(solution)/shard_map/ppermute | solution.py:324
  6.9 2.0 %collective-permute-start.1 = (bf16[1024,256]{1,0:T(8,128)(2,1)S(1)}, bf16[1024,256]{1,0:T(8,128)(2,1)S(1)}, u32[]{:S(2)}, u32[]{:S(2)}) collective-permute-start(bf16[1024,256]{1,0:T(8,128)(2,1)S(1)} %get-tuple-element.44.refs_2_), channel_id=1, source_target_pairs={{0,1},{1,0},{2,3},{3,2},{4,5},{5,4},{6,7},{7,6},{8,9},{9,8},{10,11... | collective-permute-start | bytes 1572872 | tf_op jit(solution)/shard_map/ppermute | solution.py:324
  11.4 1.7 %collective-permute-start.3 = (bf16[128,256]{1,0:T(8,128)(2,1)S(1)}, bf16[128,256]{1,0:T(8,128)(2,1)S(1)}, u32[]{:S(2)}, u32[]{:S(2)}) collective-permute-start(bf16[128,256]{1,0:T(8,128)(2,1)S(1)} %bitcast.13), channel_id=1, source_target_pairs={{0,1},{1,0},{2,3},{3,2},{4,5},{5,4},{6,7},{7,6},{8,9},{9,8},{10,11... | collective-permute-start | bytes 196616 | tf_op jit(solution)/shard_map/ppermute | solution.py:324
  13.1 3.3 %collective-permute-start.4 = (bf16[1024,256]{1,0:T(8,128)(2,1)S(1)}, bf16[1024,256]{1,0:T(8,128)(2,1)S(1)}, u32[]{:S(2)}, u32[]{:S(2)}) collective-permute-start(bf16[1024,256]{1,0:T(8,128)(2,1)S(1)} %get-tuple-element.54), channel_id=1, source_target_pairs={{0,1},{1,0},{2,3},{3,2},{4,5},{5,4},{6,7},{7,6},{8,9},{9,8},{10,11... | collective-permute-start | bytes 1572872 | tf_op jit(solution)/shard_map/ppermute | solution.py:324
  13.5 5.2 %collective-permute-start.6 = (bf16[128,256]{1,0:T(8,128)(2,1)S(1)}, bf16[128,256]{1,0:T(8,128)(2,1)S(1)}, u32[]{:S(2)}, u32[]{:S(2)}) collective-permute-start(bf16[128,256]{1,0:T(8,128)(2,1)S(1)} %get-tuple-element.55.refs_3_.refs_0_), channel_id=1, source_target_pairs={{0,2},{1,5},{2,0},{3,7},{4,6},{5,1},{6,4},{7,3},{8,10},{9,13},{10,... | collective-permute-start | bytes 196616 | tf_op jit(solution)/shard_map/ppermute | solution.py:343
  17.3 4.8 %collective-permute-start.5 = (bf16[256,1024]{1,0:T(8,128)(2,1)S(1)}, bf16[256,1024]{1,0:T(8,128)(2,1)S(1)}, u32[]{:S(2)}, u32[]{:S(2)}) collective-permute-start(bf16[256,1024]{1,0:T(8,128)(2,1)S(1)} %bitcast.11), channel_id=1, source_target_pairs={{0,1},{1,0},{2,3},{3,2},{4,5},{5,4},{6,7},{7,6},{8,9},{9,8},{10,11... | collective-permute-start | bytes 1572872 | tf_op jit(solution)/shard_map/ppermute | solution.py:324
  18.7 5.2 %collective-permute-start.8 = (bf16[128,256]{1,0:T(8,128)(2,1)S(1)}, bf16[128,256]{1,0:T(8,128)(2,1)S(1)}, u32[]{:S(2)}, u32[]{:S(2)}) collective-permute-start(bf16[128,256]{1,0:T(8,128)(2,1)S(1)} %shard_map.93.refs_2_.refs_0_), channel_id=1, source_target_pairs={{0,4},{1,9},{2,6},{3,11},{4,0},{5,13},{6,2},{7,15},{8,12},{9,1},{1... | collective-permute-start | bytes 196616 | tf_op jit(solution)/shard_map/ppermute | solution.py:343
  22.0 3.6 %copy-start = (f32[256,128]{1,0:T(8,128)S(1)}, f32[256,128]{1,0:T(8,128)}, u32[]{:S(2)}) copy-start(f32[256,128]{1,0:T(8,128)} %refs_2_.8) | copy-start | bytes 393220
  22.1 3.6 %copy-start.1 = (bf16[256,256]{1,0:T(8,128)(2,1)S(1)}, bf16[256,256]{1,0:T(8,128)(2,1)}, u32[]{:S(2)}) copy-start(bf16[256,256]{1,0:T(8,128)(2,1)} %refs_0_.5) | copy-start | bytes 393220
  23.4 3.0 %collective-permute-start.7 = (bf16[256,1024]{1,0:T(8,128)(2,1)S(1)}, bf16[256,1024]{1,0:T(8,128)(2,1)S(1)}, u32[]{:S(2)}, u32[]{:S(2)}) collective-permute-start(bf16[256,1024]{1,0:T(8,128)(2,1)S(1)} %bitcast.9), channel_id=1, source_target_pairs={{0,1},{1,0},{2,3},{3,2},{4,5},{5,4},{6,7},{7,6},{8,9},{9,8},{10,11... | collective-permute-start | bytes 1572872 | tf_op jit(solution)/shard_map/ppermute | solution.py:324
  23.4 7.5 %collective-permute-start.10 = (bf16[256,1024]{1,0:T(8,128)(2,1)S(1)}, bf16[256,1024]{1,0:T(8,128)(2,1)S(1)}, u32[]{:S(2)}, u32[]{:S(2)}) collective-permute-start(bf16[256,1024]{1,0:T(8,128)(2,1)S(1)} %bitcast.7), channel_id=1, source_target_pairs={{0,1},{1,0},{2,3},{3,2},{4,5},{5,4},{6,7},{7,6},{8,9},{9,8},{10,11... | collective-permute-start | bytes 1572872 | tf_op jit(solution)/shard_map/ppermute | solution.py:324
  24.0 4.3 %collective-permute-start.11 = (bf16[128,256]{1,0:T(8,128)(2,1)S(1)}, bf16[128,256]{1,0:T(8,128)(2,1)S(1)}, u32[]{:S(2)}, u32[]{:S(2)}) collective-permute-start(bf16[128,256]{1,0:T(8,128)(2,1)S(1)} %shard_map.96.refs_4_.refs_0_), channel_id=1, source_target_pairs={{0,8},{1,3},{2,10},{3,1},{4,12},{5,7},{6,14},{7,5},{8,0},{9,11},{1... | collective-permute-start | bytes 196616 | tf_op jit(solution)/shard_map/ppermute | solution.py:343
  27.4 5.0 %collective-permute-start.9 = (bf16[256,1024]{1,0:T(8,128)(2,1)S(1)}, bf16[256,1024]{1,0:T(8,128)(2,1)S(1)}, u32[]{:S(2)}, u32[]{:S(2)}) collective-permute-start(bf16[256,1024]{1,0:T(8,128)(2,1)S(1)} %bitcast.8), channel_id=1, source_target_pairs={{0,1},{1,0},{2,3},{3,2},{4,5},{5,4},{6,7},{7,6},{8,9},{9,8},{10,11... | collective-permute-start | bytes 1572872 | tf_op jit(solution)/shard_map/ppermute | solution.py:324
  28.3 6.1 %collective-permute-start.13 = (bf16[128,256]{1,0:T(8,128)(2,1)S(1)}, bf16[128,256]{1,0:T(8,128)(2,1)S(1)}, u32[]{:S(2)}, u32[]{:S(2)}) collective-permute-start(bf16[128,256]{1,0:T(8,128)(2,1)S(1)} %shard_map.99.refs_5_.refs_1_), channel_id=1, source_target_pairs={{0,16},{1,17},{2,18},{3,19},{4,20},{5,21},{6,22},{7,23},{8,24},{9,... | collective-permute-start | bytes 196616 | tf_op jit(solution)/shard_map/ppermute | solution.py:343
  32.2 2.0 %collective-permute-start.12 = (bf16[256,1024]{1,0:T(8,128)(2,1)S(1)}, bf16[256,1024]{1,0:T(8,128)(2,1)S(1)}, u32[]{:S(2)}, u32[]{:S(2)}) collective-permute-start(bf16[256,1024]{1,0:T(8,128)(2,1)S(1)} %bitcast.12), channel_id=1, source_target_pairs={{0,1},{1,0},{2,3},{3,2},{4,5},{5,4},{6,7},{7,6},{8,9},{9,8},{10,11... | collective-permute-start | bytes 1572872 | tf_op jit(solution)/shard_map/ppermute | solution.py:324
  34.5 1.3 %collective-permute-start.14 = (bf16[128,256]{1,0:T(8,128)(2,1)S(1)}, bf16[128,256]{1,0:T(8,128)(2,1)S(1)}, u32[]{:S(2)}, u32[]{:S(2)}) collective-permute-start(bf16[128,256]{1,0:T(8,128)(2,1)S(1)} %shard_map.103.refs_1_.refs_4_), channel_id=1, source_target_pairs={{0,1},{1,0},{2,3},{3,2},{4,5},{5,4},{6,7},{7,6},{8,9},{9,8},{10,11... | collective-permute-start | bytes 196616 | tf_op jit(solution)/shard_map/ppermute | solution.py:324

commit v10 on v8

--- a/solution.py
+++ b/solution.py
@@ -37,8 +37,8 @@
     nodes = n_space * rows
     tile = 256 if rows % 256 == 0 else rows
     tiles = rows // tile
-    eighth = rows // 8
-    head = rows - eighth
+    quarter = rows // 4
+    head = rows - quarter
     width = columns // n_space
     peers = range(1, n_space)
 
@@ -174,17 +174,18 @@
 
     def k1_copies(coupling, k1, first, count, sems):
         copies = []
-        for i in range(count):
-            part = pl.ds((first + i) * eighth, eighth)
-            target = k1.at[part] if k1.shape[0] == rows else k1
+        size = quarter // 2
+        for i in range(2 * count):
+            part = pl.ds(first * quarter + i * size, size)
+            target = k1.at[part] if k1.shape[0] == rows else k1.at[pl.ds(i * size, size)]
             copies.append(pltpu.make_async_copy(coupling.at[1, part], target, sems.at[i]))
             copies[-1].start(priority=i % 2)
         return copies
 
     def first_value_kernel(d0, n0, coupling, noise, *refs):
         got, (out, bar, k1, n1, sems) = refs[: n_space - 1], refs[n_space - 1 :]
-        copies = k1_copies(coupling, k1, 0, 3, sems)
-        copies.append(pltpu.make_async_copy(noise.at[1], n1, sems.at[3]))
+        copies = k1_copies(coupling, k1, 0, 1, sems)
+        copies.append(pltpu.make_async_copy(noise.at[1], n1, sems.at[2]))
         copies[-1].start()
         lower_own(d0, n0, out)
         lower_rest(d0, [piece.at[0] for piece in got], out)
@@ -193,7 +194,7 @@
             copy.wait()
 
     def load_kernel(coupling, value, _, value_rows, k1, sems):
-        copies = k1_copies(coupling, k1, 3, 4, sems)
+        copies = k1_copies(coupling, k1, 1, 2, sems)
         value_rows[...] = value[...].T
         for copy in copies:
             copy.wait()
@@ -202,8 +203,8 @@
         got, refs = refs[: n_space - 1], refs[n_space - 1 :]
         got_own, refs = refs[: n_space - 1], refs[n_space - 1 :]
         target, part_own, part_other, response, e0, tail, whole, sems = refs
-        arrow_copy = pltpu.make_async_copy(arrow.at[0], e0, sems.at[1])
-        (tail_copy,) = k1_copies(coupling, tail, 7, 1, sems)
+        arrow_copy = pltpu.make_async_copy(arrow.at[0], e0, sems.at[2])
+        tail_copies = k1_copies(coupling, tail, 3, 1, sems)
         arrow_copy.start()
 
         def pull(at, size):
@@ -218,17 +219,16 @@
             pull(at, min(tile, head - at))
         arrow_copy.wait()
         whole[...] = dot(e0[...], bar[...])
-        tail_copy.wait()
-        pull(head, eighth)
+        for copy in tail_copies:
+            copy.wait()
+        pull(head, quarter)
         whole[...] = (whole[...] + dot(response[...], target[...])).T
         part_own[...] = whole[part_rows(0)]
         for step in peers:
             part_other[step - 1] = whole[part_rows(step)].astype(BF)
 
-    def last_own_kernel(d1, target, coupling, _, value, k1, sems):
-        (tail_copy,) = k1_copies(coupling, k1, 7, 1, sems)
+    def last_own_kernel(d1, target, value):
         lower_own(d1, target, value)
-        tail_copy.wait()
 
     def core_sum_kernel(part, _, *refs):
         got, (out, _) = refs[:-2], refs[-2:]
@@ -240,11 +240,14 @@
     def fold_kernel(sent, got, out):
         out[...] = (sent[...].astype(F32) + got[...].astype(F32)).astype(BF)
 
-    def last_solve_kernel(d1, first, *refs):
-        got, (own, other, value) = refs[: n_space - 1], refs[n_space - 1 :]
+    def last_solve_kernel(d1, first, coupling, _, *refs):
+        got, (own, other, k1, value, sems) = refs[: n_space - 1], refs[n_space - 1 :]
+        copies = k1_copies(coupling, k1, 3, 1, sems)
         value[...] = first[...]
         lower_rest(d1, got, value)
-        lower_rows(value[...].T.astype(BF), d1, own, other)
+        lower_rows(value[...].astype(BF).T, d1, own, other)
+        for copy in copies:
+            copy.wait()
 
     def response_kernel(k1, response, own, other):
         full_rows(response, k1, own, other)
@@ -370,7 +373,7 @@
             [d0, n0, coupling, noise, *got_noise],
             8,
             {2: pltpu.HBM, 3: pltpu.HBM},
-            [dma((4,))],
+            [dma((3,))],
         )
         got_bar = send_up(bar)
         value_rows, k1 = call(
@@ -395,21 +398,13 @@
             8,
             {1: pltpu.HBM, 4: pltpu.HBM},
             [
-                pltpu.VMEM((eighth, nodes), BF),
+                pltpu.VMEM((quarter, nodes), BF),
                 pltpu.VMEM((columns, fixed_rows), F32),
-                dma((2,)),
+                dma((3,)),
             ],
         )
         got_parts = send_down(part_other)
-        value, k1 = call(
-            last_own_kernel,
-            [node_f32, in_vmem],
-            [d1, target, coupling, k1],
-            8,
-            {2: pltpu.HBM, 3: pl.ANY, ("out", 1): pl.ANY},
-            [dma((1,))],
-            aliases={3: 1},
-        )
+        (value,) = call(last_own_kernel, [node_f32], [d1, target], 8)
         sent, target = call(
             core_sum_kernel,
             [part_bf, node_bf],
@@ -433,12 +428,14 @@
             step += 1
 
         advance()
-        solved, other = call(
+        solved, other, k1 = call(
             last_solve_kernel,
-            [flat_f32, flat_others],
-            [d1, value, *got_target],
-            8,
-            scratch=[pltpu.VMEM((rows, columns), F32)],
+            [flat_f32, flat_others, in_vmem],
+            [d1, value, coupling, k1, *got_target],
+            8,
+            {2: pltpu.HBM, 3: pl.ANY, ("out", 2): pl.ANY},
+            [pltpu.VMEM((rows, columns), F32), dma((2,))],
+            aliases={3: 2},
             after=sent,
         )
         got_solved = send_down(other)
@@ -456,6 +453,23 @@
         )
         got_passed = send_down(other)
         advance(base)
+        first, other = call(
+            first_response_kernel,
+            [fixed_f32, fixed_others],
+            [d0, e0, tip_inverse, pushed, *got_pushed],
+            5,
+            after=sent,
+        )
+        got_first = send_down(other)
+        solved, other = call(
+            first_solve_kernel,
+            [flat_f32, flat_others],
+            [d0, value_rows, passed, *got_passed],
+            8,
+            after=first,
+        )
+        got_solved = send_down(other)
+        advance(solved)
         last_base, last_resp, noise_rows = call(
             turn_last_kernel,
             [node_f32, by_node, shape_of((width, fixed_rows), F32)],
@@ -463,30 +477,13 @@
             5,
             after=sent,
         )
-        solved, other = call(
-            first_solve_kernel,
-            [flat_f32, flat_others],
-            [d0, value_rows, passed, *got_passed],
-            8,
-            after=noise_rows,
-        )
-        got_solved = send_down(other)
-        advance(solved)
-        first, other = call(
-            first_response_kernel,
-            [fixed_f32, fixed_others],
-            [d0, e0, tip_inverse, pushed, *got_pushed],
-            5,
-            after=sent,
-        )
-        got_first = send_down(other)
-        (first_base,) = call(turn_first_kernel, [node_f32], [solved, *got_solved], 8, after=first)
-        (first_resp,) = call(
-            turn_response_kernel, [by_node], [first, *got_first], 8, after=first_base
+        (first_resp,) = call(turn_response_kernel, [by_node], [first, *got_first], 8, after=noise_rows)
+        (first_base,) = call(
+            turn_first_kernel, [node_f32], [solved, *got_solved], 8, after=first_resp
         )
         while step < steps:
             advance()
-        (mixed,) = call(mixed_kernel, [part_bf], [noise_rows, sent, *got], 0.2, after=first_resp)
+        (mixed,) = call(mixed_kernel, [part_bf], [noise_rows, sent, *got], 0.2, after=first_base)
         got_mixed = send_up(mixed)
         (fixed_out,) = call(
             fixed_kernel, [shape_of((fixed_rows, width), F32)], [tip_inverse, mixed], 8

time: 37.2 us -> 38.5 us (1.035)
  waiting for transfers between devices: 2.13 us -> 2.86 us
  Pallas kernels: 19.2 us -> 19.9 us
    ppermute x4, waiting for transfers between devices: 0.19 us -> 1.78 us  [swap_step(): return lax.ppermute(value, ('tm', 'space'), pairs)]
    ppermute x11, waiting for transfers between devices: 1.94 us -> 1.07 us  [swap(): return lax.ppermute(value, 'space', pairs)]
    pallas_call x20, Pallas kernels: 19.2 us -> 19.9 us  [call(): pl.pallas_call(run, in_specs=specs, out_specs=[pl.BlockSpec(memory_space=...]
    ppermute x4, starting transfers between devices: 9 us -> 8.58 us  [swap_step(): return lax.ppermute(value, ('tm', 'space'), pairs)]
  transfers between devices with their start and end apart: 15 -> 15, of which waited for: 4 -> 4; matrix products, arithmetic and copies ran while one was open for 0% -> 0% of each run, Pallas kernels for 42% -> 39%
where the time goes in v10:
time: 38.5 us; the launch traced here: 38.3 us
  Pallas kernels  19.9 us (52%)
  starting transfers between devices  14.6 us (38%)
  waiting for transfers between devices  2.86 us (7%)
  between operations  0.95 us (2%)
    pallas_call x20, Pallas kernels, call(): pl.pallas_call(run, in_specs=specs, out_specs=[pl.BlockSpec(memory_space=...  19.9 us
    ppermute x4, starting transfers between devices, swap_step(): return lax.ppermute(value, ('tm', 'space'), pairs)  8.58 us
    ppermute x11, starting transfers between devices, swap(): return lax.ppermute(value, 'space', pairs)  6.01 us
    ppermute x4, waiting for transfers between devices, swap_step(): return lax.ppermute(value, ('tm', 'space'), pairs)  1.78 us
    ppermute x11, waiting for transfers between devices, swap(): return lax.ppermute(value, 'space', pairs)  1.07 us
  transfers between devices with their start and end apart: 15, of which 4 were waited for; matrix products, arithmetic and copies ran while one was open for 0% of the time, Pallas kernels for 39%

profile of v10, /device:TPU:0, one launch (start us, length us, event | category | flops | bytes accessed | tf_op | source)
XLA Modules:
  0.0 38.3 jit_solution(8115660019300742759)
XLA Ops:
  0.6 0.5 %collective-permute-start = (bf16[2,1024,256]{2,1,0:T(8,128)(2,1)}, bf16[2,1024,256]{2,1,0:T(8,128)(2,1)S(1)}, u32[]{:S(2)}, u32[]{:S(2)}) collective-permute-start(bf16[2,1024,256]{2,1,0:T(8,128)(2,1)} %refs_3_.4), channel_id=1, source_target_pairs={{0,1},{1,0},{2,3},{3,2},{4,5},{5,4},{6,7},{7,6},{8,9},{9,8},{10,11... | collective-permute-start | bytes 3145736 | tf_op jit(solution)/shard_map/ppermute | solution.py:319
  1.1 2.8 %shard_map.86 = (bf16[1024,2048]{1,0:T(8,128)(2,1)S(1)}, bf16[1024,2048]{1,0:T(8,128)(2,1)S(1)}, f32[256,1024]{1,0:T(8,128)S(1)}, bf16[1,256,1024]{2,1,0:T(8,128...) custom-call(bf16[2,1024,2048]{2,1,0:T(8,128)(2,1)} %refs_0_.3, bf16[2,256,1024]{2,1,0:T(8,128)(2,1)} %refs_4_.1, ...), custom_call_target="tpu_custom_call" | custom-call | flops 8000000000 | tf_op jit(solution)/shard_map/pallas_call | solution.py:74
  4.0 1.1 %collective-permute-start.2 = (bf16[256,1024]{1,0:T(8,128)(2,1)S(1)}, bf16[256,1024]{1,0:T(8,128)(2,1)S(1)}, u32[]{:S(2)}, u32[]{:S(2)}) collective-permute-start(bf16[256,1024]{1,0:T(8,128)(2,1)S(1)} %bitcast.11), channel_id=1, source_target_pairs={{0,1},{1,0},{2,3},{3,2},{4,5},{5,4},{6,7},{7,6},{8,9},{9,8},{10,11... | collective-permute-start | bytes 1572872 | tf_op jit(solution)/shard_map/ppermute | solution.py:319
  5.1 0.0 collective-permute-done.refs_4_
  5.1 1.6 %shard_map.87 = (f32[1024,256]{1,0:T(8,128)S(1)}, bf16[1024,256]{1,0:T(8,128)(2,1)S(1)}, bf16[1024,2048]{1,0:T(8,128)(2,1)S(1)}, bf16[1024,256]{1,0:T(8,128)(2,1)S(1)}) custom-call(bf16[1024,2048]{1,0:T(8,128)(2,1)S(1)} %get-tuple-element.36.refs_0_, bf16[1024,256]{1,0:T(8,128)(2,1)S(1)} %get-tuple-element.37.refs_1_, bf16[2,1024,2048]{2,1,0:T(8,128)(2,1)} %refs_2_.7, ...), custom_call_target="tpu_custom_call" | custom-call | flops 8000000000 | tf_op jit(solution)/shard_map/pallas_call | solution.py:74
  6.6 0.1 collective-permute-start.1
  6.7 1.6 %shard_map.88 = (f32[256,1024]{1,0:T(8,128)S(1)}, bf16[1024,2048]{1,0:T(8,128)(2,1)S(1)}) custom-call(bf16[2,1024,2048]{2,1,0:T(8,128)(2,1)} %refs_2_.7, f32[1024,256]{1,0:T(8,128)S(1)} %get-tuple-element.38.refs_1_, bf16[1024,2048]{1,0:T(8,128)(2,1)S(1)} %get-tuple-element.39.refs_2_), custom_call_target="tpu_custom_call", output_to_operand_aliasing={{1}: (2, {})} | custom-call | flops 8000000000 | tf_op jit(solution)/shard_map/pallas_call | solution.py:74
  8.3 0.0 collective-permute-done.2.refs_7_
  8.3 0.3 collective-permute-done.1.refs_6_
  8.6 3.6 %shard_map.89 = (bf16[1024,256]{1,0:T(8,128)(2,1)S(1)}, f32[128,256]{1,0:T(8,128)S(1)}, bf16[1,128,256]{2,1,0:T(8,128)(2,1)S(1)}, bf16[256,1024]{1,0:T(8,128)(2,1)S(1)}, bf16[256,1024]{1,0:T(8,128)(2,1)S(1)}) custom-call(bf16[1024,2048]{1,0:T(8,128)(2,1)S(1)} %get-tuple-element.42.refs_0_.refs_3_, bf16[2,1024,2048]{2,1,0:T(8,128)(2,1)} %refs_2_.7, ...), custom_call_target="tpu_custom_call" | custom-call | flops 8000000000 | tf_op jit(solution)/shard_map/pallas_call | solution.py:74
  12.2 0.3 collective-permute-start.3
  12.5 0.5 %shard_map.90.refs_3_.refs_1_ = f32[1024,256]{1,0:T(8,128)S(1)} custom-call(bf16[1024,2048]{1,0:T(8,128)(2,1)S(1)} %get-tuple-element.41.refs_0_, bf16[1024,256]{1,0:T(8,128)(2,1)S(1)} %get-tuple-element.47.refs_1_), custom_call_target="tpu_custom_call" | custom-call | flops 8000000000 | tf_op jit(solution)/shard_map/pallas_call | solution.py:74
  13.0 0.6 %collective-permute-done.3.refs_2_ = bf16[128,256]{1,0:T(8,128)(2,1)S(1)} collective-permute-done((bf16[128,256]{1,0:T(8,128)(2,1)S(1)}, bf16[128,256]{1,0:T(8,128)(2,1)S(1)}, u32[]{:S(2)}, u32[]{:S(2)}) %collective-permute-start.3) | collective-permute-done | bytes 65568 | tf_op jit(solution)/shard_map/ppermute | solution.py:319
  13.5 0.3 collective-permute-start.4
  13.8 2.9 %collective-permute-start.6 = (bf16[128,256]{1,0:T(8,128)(2,1)S(1)}, bf16[128,256]{1,0:T(8,128)(2,1)S(1)}, u32[]{:S(2)}, u32[]{:S(2)}) collective-permute-start(bf16[128,256]{1,0:T(8,128)(2,1)S(1)} %get-tuple-element.51.refs_5_.refs_0_), channel_id=1, source_target_pairs={{0,2},{1,9},{2,0},{3,11},{4,6},{5,13},{6,4},{7,15},{8,10},{9,1},{1... | collective-permute-start | bytes 196616 | tf_op jit(solution)/shard_map/ppermute | solution.py:336
  16.7 0.0 collective-permute-done.4.refs_4_
  16.7 1.2 %shard_map.92 = (f32[256,1024]{1,0:T(8,128)S(1)}, bf16[1,256,1024]{2,1,0:T(8,128)(2,1)S(1)}, bf16[1024,2048]{1,0:T(8,128)(2,1)S(1)}) custom-call(bf16[1024,2048]{1,0:T(8,128)(2,1)S(1)} %get-tuple-element.41.refs_0_, f32[1024,256]{1,0:T(8,128)S(1)} %shard_map.90.refs_3_.refs_1_, bf16[2,1024,2048]{2,1,0:T(8,128)(2,1)} %refs_2_.7, ...), custom_call_target="tpu_custom_call", output_to_operand_aliasing={{2}: (3, {})} | custom-call | flops 8000000000 | tf_op jit(solution)/shard_map/pallas_call | solution.py:74
  18.0 1.2 %collective-permute-start.5 = (bf16[256,1024]{1,0:T(8,128)(2,1)S(1)}, bf16[256,1024]{1,0:T(8,128)(2,1)S(1)}, u32[]{:S(2)}, u32[]{:S(2)}) collective-permute-start(bf16[256,1024]{1,0:T(8,128)(2,1)S(1)} %bitcast.12), channel_id=1, source_target_pairs={{0,1},{1,0},{2,3},{3,2},{4,5},{5,4},{6,7},{7,6},{8,9},{9,8},{10,11... | collective-permute-start | bytes 1572872 | tf_op jit(solution)/shard_map/ppermute | solution.py:319
  19.2 0.0 collective-permute-done.6.refs_1_
  19.2 1.9 %collective-permute-start.9 = (bf16[128,256]{1,0:T(8,128)(2,1)S(1)}, bf16[128,256]{1,0:T(8,128)(2,1)S(1)}, u32[]{:S(2)}, u32[]{:S(2)}) collective-permute-start(bf16[128,256]{1,0:T(8,128)(2,1)S(1)} %shard_map.93.refs_2_.refs_0_), channel_id=1, source_target_pairs={{0,4},{1,17},{2,6},{3,19},{4,0},{5,21},{6,2},{7,23},{8,12},{9,25},... | collective-permute-start | bytes 196616 | tf_op jit(solution)/shard_map/ppermute | solution.py:336
  21.1 1.2 %shard_map.94 = (f32[256,1024]{1,0:T(8,128)S(1)}, bf16[1,256,1024]{2,1,0:T(8,128)(2,1)S(1)}) custom-call(bf16[1024,2048]{1,0:T(8,128)(2,1)S(1)} %get-tuple-element.52.refs_0_, bf16[256,1024]{1,0:T(8,128)(2,1)S(1)} %get-tuple-element.56.refs_1_, bf16[128,256]{1,0:T(8,128)(2,1)S(1)} %shard_map.93.refs_2_.refs_0_), custom_call_target="tpu_custom_call" | custom-call | flops 5000000000 | tf_op jit(solution)/shard_map/pallas_call | solution.py:74
  22.4 0.8 %collective-permute-start.8 = (bf16[256,1024]{1,0:T(8,128)(2,1)S(1)}, bf16[256,1024]{1,0:T(8,128)(2,1)S(1)}, u32[]{:S(2)}, u32[]{:S(2)}) collective-permute-start(bf16[256,1024]{1,0:T(8,128)(2,1)S(1)} %bitcast.9), channel_id=1, source_target_pairs={{0,1},{1,0},{2,3},{3,2},{4,5},{5,4},{6,7},{7,6},{8,9},{9,8},{10,11... | collective-permute-start | bytes 1572872 | tf_op jit(solution)/shard_map/ppermute | solution.py:319
  23.2 0.0 collective-permute-done.5.refs_3_
  23.2 0.0 copy-start.1
  23.2 1.3 %shard_map.95 = (f32[256,1024]{1,0:T(8,128)S(1)}, f32[256,1024]{1,0:T(8,128)S(1)}, bf16[1,256,1024]{2,1,0:T(8,128)(2,1)S(1)}) custom-call(bf16[1024,2048]{1,0:T(8,128)(2,1)S(1)} %get-tuple-element.52.refs_0_, f32[8,128]{1,0:T(8,128)S(1)} %get-tuple-element.53.refs_1_, f32[256,1024]{1,0:T(8,128)S(1)} %get-tuple-element.54.refs_2_, ...), custom_call_target="tpu_custom_call" | custom-call | flops 8000000000 | tf_op jit(solution)/shard_map/pallas_call | solution.py:74
  24.5 0.1 collective-permute-start.7
  24.6 0.0 collective-permute-done.9.refs_1_
  24.6 1.6 %collective-permute-start.12 = (bf16[128,256]{1,0:T(8,128)(2,1)S(1)}, bf16[128,256]{1,0:T(8,128)(2,1)S(1)}, u32[]{:S(2)}, u32[]{:S(2)}) collective-permute-start(bf16[128,256]{1,0:T(8,128)(2,1)S(1)} %shard_map.96.refs_5_.refs_0_), channel_id=1, source_target_pairs={{0,8},{1,3},{2,10},{3,1},{4,12},{5,7},{6,14},{7,5},{8,0},{9,11},{1... | collective-permute-start | bytes 196616 | tf_op jit(solution)/shard_map/ppermute | solution.py:336
  26.3 0.0 collective-permute-done.8.refs_4_
  26.3 0.0 copy-done.1
  26.3 1.2 %shard_map.97 = (f32[256,1024]{1,0:T(8,128)S(1)}, bf16[1,256,1024]{2,1,0:T(8,128)(2,1)S(1)}) custom-call(bf16[1024,2048]{1,0:T(8,128)(2,1)S(1)} %get-tuple-element.36.refs_0_, bf16[256,1024]{1,0:T(8,128)(2,1)S(1)} %get-tuple-element.60.refs_1_, bf16[256,256]{1,0:T(8,128)(2,1)S(1)} %copy-done.1, f32[256,1024]{1,0:T(8,128)S(1)} %get-tuple-element.57.refs_4_.refs_3_, ...), custom_call_target="tpu_custom_call" | custom-call | flops 5000000000 | tf_op jit(solution)/shard_map/pallas_call | solution.py:74
  27.5 0.8 %collective-permute-start.11 = (bf16[256,1024]{1,0:T(8,128)(2,1)S(1)}, bf16[256,1024]{1,0:T(8,128)(2,1)S(1)}, u32[]{:S(2)}, u32[]{:S(2)}) collective-permute-start(bf16[256,1024]{1,0:T(8,128)(2,1)S(1)} %bitcast.7), channel_id=1, source_target_pairs={{0,1},{1,0},{2,3},{3,2},{4,5},{5,4},{6,7},{7,6},{8,9},{9,8},{10,11... | collective-permute-start | bytes 1572872 | tf_op jit(solution)/shard_map/ppermute | solution.py:319
  28.4 0.0 collective-permute-done.7.refs_3_
  28.4 0.0 copy-start
  28.4 1.1 %shard_map.98 = (f32[256,1024]{1,0:T(8,128)S(1)}, bf16[1,256,1024]{2,1,0:T(8,128)(2,1)S(1)}) custom-call(bf16[1024,2048]{1,0:T(8,128)(2,1)S(1)} %get-tuple-element.36.refs_0_, f32[256,1024]{1,0:T(8,128)S(1)} %get-tuple-element.40.refs_1_, f32[256,1024]{1,0:T(8,128)S(1)} %get-tuple-element.58.refs_2_, bf16[256,1024]{1,0:T(8,128)(2,1)S(1)} %collective-permute-done.7.refs_3_, ...), custom_call_target="tpu_custom_call" | custom-call | flops 8000000000 | tf_op jit(solution)/shard_map/pallas_call | solution.py:74
  29.4 0.8 %collective-permute-start.10 = (bf16[256,1024]{1,0:T(8,128)(2,1)S(1)}, bf16[256,1024]{1,0:T(8,128)(2,1)S(1)}, u32[]{:S(2)}, u32[]{:S(2)}) collective-permute-start(bf16[256,1024]{1,0:T(8,128)(2,1)S(1)} %bitcast.10), channel_id=1, source_target_pairs={{0,1},{1,0},{2,3},{3,2},{4,5},{5,4},{6,7},{7,6},{8,9},{9,8},{10,11... | collective-permute-start | bytes 1572872 | tf_op jit(solution)/shard_map/ppermute | solution.py:319
  30.2 0.0 collective-permute-done.12.refs_1_
  30.2 2.1 %collective-permute-start.13 = (bf16[128,256]{1,0:T(8,128)(2,1)S(1)}, bf16[128,256]{1,0:T(8,128)(2,1)S(1)}, u32[]{:S(2)}, u32[]{:S(2)}) collective-permute-start(bf16[128,256]{1,0:T(8,128)(2,1)S(1)} %shard_map.99.refs_4_.refs_1_), channel_id=1, source_target_pairs={{0,16},{1,5},{2,18},{3,7},{4,20},{5,1},{6,22},{7,3},{8,24},{9,13},... | collective-permute-start | bytes 196616 | tf_op jit(solution)/shard_map/ppermute | solution.py:336
  32.3 0.0 copy-done
  32.3 0.8 %shard_map.100 = (f32[1024,256]{1,0:T(8,128)S(1)}, bf16[1024,256]{1,0:T(8,128)(2,1)S(1)}, f32[128,256]{1,0:T(8,128)S(1)}) custom-call(f32[256,1024]{1,0:T(8,128)S(1)} %get-tuple-element.62.refs_2_.refs_0_, bf16[256,1024]{1,0:T(8,128)(2,1)S(1)} %get-tuple-element.56.refs_1_, f32[256,128]{1,0:T(8,128)S(1)} %copy-done, bf16[256,256]{1,0:T(8,128)(2,1)S(1)} %copy-done.1, ...), custom_call_target="tpu_custom_call" | custom-call | flops 5000000000 | tf_op jit(solution)/shard_map/pallas_call | solution.py:74
  33.1 0.0 collective-permute-done.11.refs_1_
  33.1 0.2 shard_map.101.refs_2_
  33.3 0.0 collective-permute-done.10.refs_1_
  33.3 0.3 shard_map.102.refs_3_.refs_0_
  33.7 1.8 %collective-permute-done.13.refs_2_ = bf16[128,256]{1,0:T(8,128)(2,1)S(1)} collective-permute-done((bf16[128,256]{1,0:T(8,128)(2,1)S(1)}, bf16[128,256]{1,0:T(8,128)(2,1)S(1)}, u32[]{:S(2)}, u32[]{:S(2)}) %collective-permute-start.13) | collective-permute-done | bytes 65568 | tf_op jit(solution)/shard_map/ppermute | solution.py:336
  35.5 0.1 collective-permute-start.14
  35.6 1.1 %shard_map.104.refs_6_ = f32[256,128]{1,0:T(8,128)} custom-call(bf16[256,256]{1,0:T(8,128)(2,1)S(1)} %copy-done.1, bf16[128,256]{1,0:T(8,128)(2,1)S(1)} %shard_map.103.refs_1_.refs_4_), custom_call_target="tpu_custom_call" | custom-call | flops 8000000000 | tf_op jit(solution)/shard_map/pallas_call | solution.py:74
  36.6 0.2 collective-permute-done.14.refs_5_
  36.8 1.3 %shard_map.105 = bf16[2,1024,256]{2,1,0:T(8,128)(2,1)} custom-call(f32[1024,256]{1,0:T(8,128)S(1)} %shard_map.102.refs_3_.refs_0_, f32[1024,256]{1,0:T(8,128)S(1)} %get-tuple-element.68.refs_1_, bf16[1024,256]{1,0:T(8,128)(2,1)S(1)} %shard_map.101.refs_2_, bf16[1024,256]{1,0:T(8,128)(2,1)S(1)} %get-tuple-element.69.refs_3_, ...), custom_call_target="tpu_custom_call" | custom-call | flops 8000000000 | tf_op jit(solution)/shard_map/pallas_call | solution.py:74
  (5 shorter events, 0.1 us)
Async XLA Ops:
  0.6 4.4 %collective-permute-start = (bf16[2,1024,256]{2,1,0:T(8,128)(2,1)}, bf16[2,1024,256]{2,1,0:T(8,128)(2,1)S(1)}, u32[]{:S(2)}, u32[]{:S(2)}) collective-permute-start(bf16[2,1024,256]{2,1,0:T(8,128)(2,1)} %refs_3_.4), channel_id=1, source_target_pairs={{0,1},{1,0},{2,3},{3,2},{4,5},{5,4},{6,7},{7,6},{8,9},{9,8},{10,11... | collective-permute-start | bytes 3145736 | tf_op jit(solution)/shard_map/ppermute | solution.py:319
  4.0 4.3 %collective-permute-start.2 = (bf16[256,1024]{1,0:T(8,128)(2,1)S(1)}, bf16[256,1024]{1,0:T(8,128)(2,1)S(1)}, u32[]{:S(2)}, u32[]{:S(2)}) collective-permute-start(bf16[256,1024]{1,0:T(8,128)(2,1)S(1)} %bitcast.11), channel_id=1, source_target_pairs={{0,1},{1,0},{2,3},{3,2},{4,5},{5,4},{6,7},{7,6},{8,9},{9,8},{10,11... | collective-permute-start | bytes 1572872 | tf_op jit(solution)/shard_map/ppermute | solution.py:319
  6.6 2.0 %collective-permute-start.1 = (bf16[1024,256]{1,0:T(8,128)(2,1)S(1)}, bf16[1024,256]{1,0:T(8,128)(2,1)S(1)}, u32[]{:S(2)}, u32[]{:S(2)}) collective-permute-start(bf16[1024,256]{1,0:T(8,128)(2,1)S(1)} %get-tuple-element.43.refs_2_), channel_id=1, source_target_pairs={{0,1},{1,0},{2,3},{3,2},{4,5},{5,4},{6,7},{7,6},{8,9},{9,8},{10,11... | collective-permute-start | bytes 1572872 | tf_op jit(solution)/shard_map/ppermute | solution.py:319
  12.2 1.3 %collective-permute-start.3 = (bf16[128,256]{1,0:T(8,128)(2,1)S(1)}, bf16[128,256]{1,0:T(8,128)(2,1)S(1)}, u32[]{:S(2)}, u32[]{:S(2)}) collective-permute-start(bf16[128,256]{1,0:T(8,128)(2,1)S(1)} %bitcast.13), channel_id=1, source_target_pairs={{0,1},{1,0},{2,3},{3,2},{4,5},{5,4},{6,7},{7,6},{8,9},{9,8},{10,11... | collective-permute-start | bytes 196616 | tf_op jit(solution)/shard_map/ppermute | solution.py:319
  13.5 3.2 %collective-permute-start.4 = (bf16[1024,256]{1,0:T(8,128)(2,1)S(1)}, bf16[1024,256]{1,0:T(8,128)(2,1)S(1)}, u32[]{:S(2)}, u32[]{:S(2)}) collective-permute-start(bf16[1024,256]{1,0:T(8,128)(2,1)S(1)} %get-tuple-element.50), channel_id=1, source_target_pairs={{0,1},{1,0},{2,3},{3,2},{4,5},{5,4},{6,7},{7,6},{8,9},{9,8},{10,11... | collective-permute-start | bytes 1572872 | tf_op jit(solution)/shard_map/ppermute | solution.py:319
  13.8 5.4 %collective-permute-start.6 = (bf16[128,256]{1,0:T(8,128)(2,1)S(1)}, bf16[128,256]{1,0:T(8,128)(2,1)S(1)}, u32[]{:S(2)}, u32[]{:S(2)}) collective-permute-start(bf16[128,256]{1,0:T(8,128)(2,1)S(1)} %get-tuple-element.51.refs_5_.refs_0_), channel_id=1, source_target_pairs={{0,2},{1,9},{2,0},{3,11},{4,6},{5,13},{6,4},{7,15},{8,10},{9,1},{1... | collective-permute-start | bytes 196616 | tf_op jit(solution)/shard_map/ppermute | solution.py:336
  18.0 5.2 %collective-permute-start.5 = (bf16[256,1024]{1,0:T(8,128)(2,1)S(1)}, bf16[256,1024]{1,0:T(8,128)(2,1)S(1)}, u32[]{:S(2)}, u32[]{:S(2)}) collective-permute-start(bf16[256,1024]{1,0:T(8,128)(2,1)S(1)} %bitcast.12), channel_id=1, source_target_pairs={{0,1},{1,0},{2,3},{3,2},{4,5},{5,4},{6,7},{7,6},{8,9},{9,8},{10,11... | collective-permute-start | bytes 1572872 | tf_op jit(solution)/shard_map/ppermute | solution.py:319
  19.2 5.4 %collective-permute-start.9 = (bf16[128,256]{1,0:T(8,128)(2,1)S(1)}, bf16[128,256]{1,0:T(8,128)(2,1)S(1)}, u32[]{:S(2)}, u32[]{:S(2)}) collective-permute-start(bf16[128,256]{1,0:T(8,128)(2,1)S(1)} %shard_map.93.refs_2_.refs_0_), channel_id=1, source_target_pairs={{0,4},{1,17},{2,6},{3,19},{4,0},{5,21},{6,2},{7,23},{8,12},{9,25},... | collective-permute-start | bytes 196616 | tf_op jit(solution)/shard_map/ppermute | solution.py:336
  22.4 3.9 %collective-permute-start.8 = (bf16[256,1024]{1,0:T(8,128)(2,1)S(1)}, bf16[256,1024]{1,0:T(8,128)(2,1)S(1)}, u32[]{:S(2)}, u32[]{:S(2)}) collective-permute-start(bf16[256,1024]{1,0:T(8,128)(2,1)S(1)} %bitcast.9), channel_id=1, source_target_pairs={{0,1},{1,0},{2,3},{3,2},{4,5},{5,4},{6,7},{7,6},{8,9},{9,8},{10,11... | collective-permute-start | bytes 1572872 | tf_op jit(solution)/shard_map/ppermute | solution.py:319
  23.2 3.1 %copy-start.1 = (bf16[256,256]{1,0:T(8,128)(2,1)S(1)}, bf16[256,256]{1,0:T(8,128)(2,1)}, u32[]{:S(2)}) copy-start(bf16[256,256]{1,0:T(8,128)(2,1)} %refs_0_.5) | copy-start | bytes 393220
  24.5 3.8 %collective-permute-start.7 = (bf16[256,1024]{1,0:T(8,128)(2,1)S(1)}, bf16[256,1024]{1,0:T(8,128)(2,1)S(1)}, u32[]{:S(2)}, u32[]{:S(2)}) collective-permute-start(bf16[256,1024]{1,0:T(8,128)(2,1)S(1)} %bitcast.8), channel_id=1, source_target_pairs={{0,1},{1,0},{2,3},{3,2},{4,5},{5,4},{6,7},{7,6},{8,9},{9,8},{10,11... | collective-permute-start | bytes 1572872 | tf_op jit(solution)/shard_map/ppermute | solution.py:319
  24.6 5.6 %collective-permute-start.12 = (bf16[128,256]{1,0:T(8,128)(2,1)S(1)}, bf16[128,256]{1,0:T(8,128)(2,1)S(1)}, u32[]{:S(2)}, u32[]{:S(2)}) collective-permute-start(bf16[128,256]{1,0:T(8,128)(2,1)S(1)} %shard_map.96.refs_5_.refs_0_), channel_id=1, source_target_pairs={{0,8},{1,3},{2,10},{3,1},{4,12},{5,7},{6,14},{7,5},{8,0},{9,11},{1... | collective-permute-start | bytes 196616 | tf_op jit(solution)/shard_map/ppermute | solution.py:336
  27.5 5.6 %collective-permute-start.11 = (bf16[256,1024]{1,0:T(8,128)(2,1)S(1)}, bf16[256,1024]{1,0:T(8,128)(2,1)S(1)}, u32[]{:S(2)}, u32[]{:S(2)}) collective-permute-start(bf16[256,1024]{1,0:T(8,128)(2,1)S(1)} %bitcast.7), channel_id=1, source_target_pairs={{0,1},{1,0},{2,3},{3,2},{4,5},{5,4},{6,7},{7,6},{8,9},{9,8},{10,11... | collective-permute-start | bytes 1572872 | tf_op jit(solution)/shard_map/ppermute | solution.py:319
  28.4 3.9 %copy-start = (f32[256,128]{1,0:T(8,128)S(1)}, f32[256,128]{1,0:T(8,128)}, u32[]{:S(2)}) copy-start(f32[256,128]{1,0:T(8,128)} %refs_2_.9) | copy-start | bytes 393220
  29.4 3.9 %collective-permute-start.10 = (bf16[256,1024]{1,0:T(8,128)(2,1)S(1)}, bf16[256,1024]{1,0:T(8,128)(2,1)S(1)}, u32[]{:S(2)}, u32[]{:S(2)}) collective-permute-start(bf16[256,1024]{1,0:T(8,128)(2,1)S(1)} %bitcast.10), channel_id=1, source_target_pairs={{0,1},{1,0},{2,3},{3,2},{4,5},{5,4},{6,7},{7,6},{8,9},{9,8},{10,11... | collective-permute-start | bytes 1572872 | tf_op jit(solution)/shard_map/ppermute | solution.py:319
  30.2 5.2 %collective-permute-start.13 = (bf16[128,256]{1,0:T(8,128)(2,1)S(1)}, bf16[128,256]{1,0:T(8,128)(2,1)S(1)}, u32[]{:S(2)}, u32[]{:S(2)}) collective-permute-start(bf16[128,256]{1,0:T(8,128)(2,1)S(1)} %shard_map.99.refs_4_.refs_1_), channel_id=1, source_target_pairs={{0,16},{1,5},{2,18},{3,7},{4,20},{5,1},{6,22},{7,3},{8,24},{9,13},... | collective-permute-start | bytes 196616 | tf_op jit(solution)/shard_map/ppermute | solution.py:336
  35.5 1.3 %collective-permute-start.14 = (bf16[128,256]{1,0:T(8,128)(2,1)S(1)}, bf16[128,256]{1,0:T(8,128)(2,1)S(1)}, u32[]{:S(2)}, u32[]{:S(2)}) collective-permute-start(bf16[128,256]{1,0:T(8,128)(2,1)S(1)} %shard_map.103.refs_1_.refs_4_), channel_id=1, source_target_pairs={{0,1},{1,0},{2,3},{3,2},{4,5},{5,4},{6,7},{7,6},{8,9},{9,8},{10,11... | collective-permute-start | bytes 196616 | tf_op jit(solution)/shard_map/ppermute | solution.py:319

commit v11 on v8

--- a/solution.py
+++ b/solution.py
@@ -37,8 +37,7 @@
     nodes = n_space * rows
     tile = 256 if rows % 256 == 0 else rows
     tiles = rows // tile
-    eighth = rows // 8
-    head = rows - eighth
+    quarter = rows // 4
     width = columns // n_space
     peers = range(1, n_space)
 
@@ -174,17 +173,17 @@
 
     def k1_copies(coupling, k1, first, count, sems):
         copies = []
-        for i in range(count):
-            part = pl.ds((first + i) * eighth, eighth)
-            target = k1.at[part] if k1.shape[0] == rows else k1
-            copies.append(pltpu.make_async_copy(coupling.at[1, part], target, sems.at[i]))
+        size = quarter // 2
+        for i in range(2 * count):
+            part = pl.ds(first * quarter + i * size, size)
+            copies.append(pltpu.make_async_copy(coupling.at[1, part], k1.at[part], sems.at[i]))
             copies[-1].start(priority=i % 2)
         return copies
 
     def first_value_kernel(d0, n0, coupling, noise, *refs):
         got, (out, bar, k1, n1, sems) = refs[: n_space - 1], refs[n_space - 1 :]
-        copies = k1_copies(coupling, k1, 0, 3, sems)
-        copies.append(pltpu.make_async_copy(noise.at[1], n1, sems.at[3]))
+        copies = k1_copies(coupling, k1, 0, 1, sems)
+        copies.append(pltpu.make_async_copy(noise.at[1], n1, sems.at[2]))
         copies[-1].start()
         lower_own(d0, n0, out)
         lower_rest(d0, [piece.at[0] for piece in got], out)
@@ -192,43 +191,31 @@
         for copy in copies:
             copy.wait()
 
-    def load_kernel(coupling, value, _, value_rows, k1, sems):
-        copies = k1_copies(coupling, k1, 3, 4, sems)
+    def load_kernel(coupling, arrow, value, _, value_rows, e0, k1, sems):
+        copies = k1_copies(coupling, k1, 1, 3, sems)
+        copies.append(pltpu.make_async_copy(arrow.at[0], e0, sems.at[6]))
+        copies[-1].start()
         value_rows[...] = value[...].T
         for copy in copies:
             copy.wait()
 
-    def target_kernel(k1, coupling, bar, n1, arrow, own, *refs):
+    def target_kernel(k1, bar, n1, e0, own, *refs):
         got, refs = refs[: n_space - 1], refs[n_space - 1 :]
         got_own, refs = refs[: n_space - 1], refs[n_space - 1 :]
-        target, part_own, part_other, response, e0, tail, whole, sems = refs
-        arrow_copy = pltpu.make_async_copy(arrow.at[0], e0, sems.at[1])
-        (tail_copy,) = k1_copies(coupling, tail, 7, 1, sems)
-        arrow_copy.start()
-
-        def pull(at, size):
-            factor = tail if at == head else k1.at[at : at + size]
-            pulled = jnp.zeros((size, columns), F32)
+        target, part_own, part_other, response, whole = refs
+        response[...] = total_of(own, got_own).astype(BF)
+        for at in range(0, rows, tile):
+            pulled = jnp.zeros((tile, columns), F32)
             for step, piece in enumerate([bar, *got]):
-                pulled = pulled + dot(factor[:, block(step)], piece[...])
-            target[at : at + size] = (n1[at : at + size].astype(F32) - pulled).astype(BF)
-
-        response[...] = total_of(own, got_own).astype(BF)
-        for at in range(0, head, tile):
-            pull(at, min(tile, head - at))
-        arrow_copy.wait()
-        whole[...] = dot(e0[...], bar[...])
-        tail_copy.wait()
-        pull(head, eighth)
-        whole[...] = (whole[...] + dot(response[...], target[...])).T
+                pulled = pulled + dot(k1[at : at + tile, block(step)], piece[...])
+            target[at : at + tile] = (n1[at : at + tile].astype(F32) - pulled).astype(BF)
+        whole[...] = (dot(e0[...], bar[...]) + dot(response[...], target[...])).T
         part_own[...] = whole[part_rows(0)]
         for step in peers:
             part_other[step - 1] = whole[part_rows(step)].astype(BF)
 
-    def last_own_kernel(d1, target, coupling, _, value, k1, sems):
-        (tail_copy,) = k1_copies(coupling, k1, 7, 1, sems)
+    def last_own_kernel(d1, target, value):
         lower_own(d1, target, value)
-        tail_copy.wait()
 
     def core_sum_kernel(part, _, *refs):
         got, (out, _) = refs[:-2], refs[-2:]
@@ -244,7 +231,7 @@
         got, (own, other, value) = refs[: n_space - 1], refs[n_space - 1 :]
         value[...] = first[...]
         lower_rest(d1, got, value)
-        lower_rows(value[...].T.astype(BF), d1, own, other)
+        lower_rows(value[...].astype(BF).T, d1, own, other)
 
     def response_kernel(k1, response, own, other):
         full_rows(response, k1, own, other)
@@ -269,10 +256,12 @@
         inner = dot(tip, right).astype(BF)
         return dot(tip.astype(F32).T.astype(BF), inner)
 
-    def turn_last_kernel(base, response, noise_fixed, tip, last_base, last_resp, noise_rows):
+    def turn_tip_kernel(response, noise_fixed, tip, last_resp, noise_rows):
         noise_rows[...] = noise_fixed[...].T
-        last_base[...] = base[...].T
         last_resp[...] = through_tip(tip[...], response[...]).T.astype(BF)
+
+    def turn_last_kernel(base, out):
+        out[...] = base[...].T
 
     def turn_response_kernel(first, *refs):
         got, out = refs[:-1], refs[-1]
@@ -328,7 +317,9 @@
         pairs = []
         for i in range(n_tm):
             for core in range(n_space):
-                bit = 1 << (step + core * steps // n_space) % steps
+                bit = 1 << step
+                if step < steps - 1:
+                    bit = 1 << (step + core * (steps - 1) // n_space) % (steps - 1)
                 pairs.append((i * n_space + core, (i ^ bit) * n_space + core))
         return lax.ppermute(value, ("tm", "space"), pairs)
 
@@ -370,46 +361,32 @@
             [d0, n0, coupling, noise, *got_noise],
             8,
             {2: pltpu.HBM, 3: pltpu.HBM},
-            [dma((4,))],
+            [dma((3,))],
         )
         got_bar = send_up(bar)
-        value_rows, k1 = call(
+        value_rows, e0, k1 = call(
             load_kernel,
-            [flat_f32, in_vmem],
-            [coupling, value, k1],
-            8,
-            {0: pltpu.HBM, 2: pl.ANY, ("out", 1): pl.ANY},
-            [dma((4,))],
-            aliases={2: 1},
-        )
-        target, part_own, part_other, response, e0 = call(
+            [flat_f32, fixed_bf, in_vmem],
+            [coupling, arrow, value, k1],
+            8,
+            {0: pltpu.HBM, 1: pltpu.HBM, 3: pl.ANY, ("out", 2): pl.ANY},
+            [dma((7,))],
+            aliases={3: 2},
+        )
+        target, part_own, part_other, response = call(
             target_kernel,
             [
                 node_bf,
                 shape_of((width, fixed_rows), F32),
                 shape_of((n_space - 1, width, fixed_rows), BF),
                 fixed_bf,
-                fixed_bf,
             ],
-            [k1, coupling, bar, n1, arrow, own, *got_bar, *got_response],
-            8,
-            {1: pltpu.HBM, 4: pltpu.HBM},
-            [
-                pltpu.VMEM((eighth, nodes), BF),
-                pltpu.VMEM((columns, fixed_rows), F32),
-                dma((2,)),
-            ],
+            [k1, bar, n1, e0, own, *got_bar, *got_response],
+            8,
+            scratch=[pltpu.VMEM((columns, fixed_rows), F32)],
         )
         got_parts = send_down(part_other)
-        value, k1 = call(
-            last_own_kernel,
-            [node_f32, in_vmem],
-            [d1, target, coupling, k1],
-            8,
-            {2: pltpu.HBM, 3: pl.ANY, ("out", 1): pl.ANY},
-            [dma((1,))],
-            aliases={3: 1},
-        )
+        (value,) = call(last_own_kernel, [node_f32], [d1, target], 8)
         sent, target = call(
             core_sum_kernel,
             [part_bf, node_bf],
@@ -443,32 +420,32 @@
         )
         got_solved = send_down(other)
         advance(solved)
-        pushed, other = call(
-            response_kernel, [fixed_f32, fixed_others], [k1, response], 5, after=sent
-        )
-        got_pushed = send_down(other)
+        last_resp, noise_rows = call(
+            turn_tip_kernel,
+            [by_node, shape_of((width, fixed_rows), F32)],
+            [response, noise_fixed, tip_inverse],
+            5,
+            after=sent,
+        )
         base, passed, other = call(
             pass_kernel,
             [flat_f32, flat_f32, flat_others],
             [k1, mask, solved, *got_solved],
             8,
-            after=pushed,
+            after=noise_rows,
         )
         got_passed = send_down(other)
         advance(base)
-        last_base, last_resp, noise_rows = call(
-            turn_last_kernel,
-            [node_f32, by_node, shape_of((width, fixed_rows), F32)],
-            [base, response, noise_fixed, tip_inverse],
-            5,
-            after=sent,
-        )
+        pushed, other = call(
+            response_kernel, [fixed_f32, fixed_others], [k1, response], 5, after=sent
+        )
+        got_pushed = send_down(other)
         solved, other = call(
             first_solve_kernel,
             [flat_f32, flat_others],
             [d0, value_rows, passed, *got_passed],
             8,
-            after=noise_rows,
+            after=pushed,
         )
         got_solved = send_down(other)
         advance(solved)
@@ -480,10 +457,9 @@
             after=sent,
         )
         got_first = send_down(other)
-        (first_base,) = call(turn_first_kernel, [node_f32], [solved, *got_solved], 8, after=first)
-        (first_resp,) = call(
-            turn_response_kernel, [by_node], [first, *got_first], 8, after=first_base
-        )
+        (first_base,) = call(turn_first_kernel, [node_f32], [solved, *got_solved], 1, after=first)
+        (last_base,) = call(turn_last_kernel, [node_f32], [base], 8, after=first_base)
+        (first_resp,) = call(turn_response_kernel, [by_node], [first, *got_first], 1, after=last_base)
         while step < steps:
             advance()
         (mixed,) = call(mixed_kernel, [part_bf], [noise_rows, sent, *got], 0.2, after=first_resp)

time: 37.2 us -> 37.2 us (level)
  starting transfers between devices: 14.7 us -> 16 us
  Pallas kernels: 19.2 us -> 18.4 us
    ppermute x4, starting transfers between devices: 9 us -> 9.86 us  [swap_step(): return lax.ppermute(value, ('tm', 'space'), pairs)]
    pallas_call x20 -> x21, Pallas kernels: 19.2 us -> 18.4 us  [call(): pl.pallas_call(run, in_specs=specs, out_specs=[pl.BlockSpec(memory_space=...]
    ppermute x11, waiting for transfers between devices: 1.94 us -> 1.28 us  [swap(): return lax.ppermute(value, 'space', pairs)]
    ppermute x11, starting transfers between devices: 5.74 us -> 6.15 us  [swap(): return lax.ppermute(value, 'space', pairs)]
  transfers between devices with their start and end apart: 15 -> 15, of which waited for: 4 -> 5; matrix products, arithmetic and copies ran while one was open for 0% -> 0% of each run, Pallas kernels for 42% -> 40%
where the time goes in v11:
time: 37.2 us; the launch traced here: 37 us
  Pallas kernels  18.4 us (49%)
  starting transfers between devices  16 us (43%)
  waiting for transfers between devices  1.77 us (5%)
  between operations  0.8 us (2%)
    pallas_call x21, Pallas kernels, call(): pl.pallas_call(run, in_specs=specs, out_specs=[pl.BlockSpec(memory_space=...  18.4 us
    ppermute x4, starting transfers between devices, swap_step(): return lax.ppermute(value, ('tm', 'space'), pairs)  9.86 us
    ppermute x11, starting transfers between devices, swap(): return lax.ppermute(value, 'space', pairs)  6.15 us
    ppermute x11, waiting for transfers between devices, swap(): return lax.ppermute(value, 'space', pairs)  1.28 us
  transfers between devices with their start and end apart: 15, of which 5 were waited for; matrix products, arithmetic and copies ran while one was open for 0% of the time, Pallas kernels for 40%

profile of v11, /device:TPU:0, one launch (start us, length us, event | category | flops | bytes accessed | tf_op | source)
XLA Modules:
  0.0 37.0 jit_solution(12472269071311330013)
XLA Ops:
  0.6 0.5 %collective-permute-start = (bf16[2,1024,256]{2,1,0:T(8,128)(2,1)}, bf16[2,1024,256]{2,1,0:T(8,128)(2,1)S(1)}, u32[]{:S(2)}, u32[]{:S(2)}) collective-permute-start(bf16[2,1024,256]{2,1,0:T(8,128)(2,1)} %refs_3_.3), channel_id=1, source_target_pairs={{0,1},{1,0},{2,3},{3,2},{4,5},{5,4},{6,7},{7,6},{8,9},{9,8},{10,11... | collective-permute-start | bytes 3145736 | tf_op jit(solution)/shard_map/ppermute | solution.py:305
  1.1 2.8 %shard_map.86 = (bf16[1024,2048]{1,0:T(8,128)(2,1)S(1)}, bf16[1024,2048]{1,0:T(8,128)(2,1)S(1)}, f32[256,1024]{1,0:T(8,128)S(1)}, bf16[1,256,1024]{2,1,0:T(8,128...) custom-call(bf16[2,1024,2048]{2,1,0:T(8,128)(2,1)} %refs_0_.3, bf16[2,256,1024]{2,1,0:T(8,128)(2,1)} %refs_1_.4, ...), custom_call_target="tpu_custom_call" | custom-call | flops 8000000000 | tf_op jit(solution)/shard_map/pallas_call | solution.py:73
  4.0 1.1 %collective-permute-start.2 = (bf16[256,1024]{1,0:T(8,128)(2,1)S(1)}, bf16[256,1024]{1,0:T(8,128)(2,1)S(1)}, u32[]{:S(2)}, u32[]{:S(2)}) collective-permute-start(bf16[256,1024]{1,0:T(8,128)(2,1)S(1)} %bitcast.9), channel_id=1, source_target_pairs={{0,1},{1,0},{2,3},{3,2},{4,5},{5,4},{6,7},{7,6},{8,9},{9,8},{10,11... | collective-permute-start | bytes 1572872 | tf_op jit(solution)/shard_map/ppermute | solution.py:305
  5.1 0.0 collective-permute-done.refs_4_
  5.1 1.6 %shard_map.87 = (f32[1024,256]{1,0:T(8,128)S(1)}, bf16[1024,256]{1,0:T(8,128)(2,1)S(1)}, bf16[1024,2048]{1,0:T(8,128)(2,1)S(1)}, bf16[1024,256]{1,0:T(8,128)(2,1)S(1)}) custom-call(bf16[1024,2048]{1,0:T(8,128)(2,1)S(1)} %get-tuple-element.34.refs_0_, bf16[1024,256]{1,0:T(8,128)(2,1)S(1)} %get-tuple-element.35.refs_1_, bf16[2,1024,2048]{2,1,0:T(8,128)(2,1)} %refs_0_.4, ...), custom_call_target="tpu_custom_call" | custom-call | flops 8000000000 | tf_op jit(solution)/shard_map/pallas_call | solution.py:73
  6.6 0.1 collective-permute-start.1
  6.7 2.0 %shard_map.88 = (f32[256,1024]{1,0:T(8,128)S(1)}, bf16[256,1024]{1,0:T(8,128)(2,1)S(1)}, bf16[1024,2048]{1,0:T(8,128)(2,1)S(1)}) custom-call(bf16[2,1024,2048]{2,1,0:T(8,128)(2,1)} %refs_0_.4, bf16[2,256,1024]{2,1,0:T(8,128)(2,1)} %refs_1_.4, f32[1024,256]{1,0:T(8,128)S(1)} %get-tuple-element.36.refs_2_, ...), custom_call_target="tpu_custom_call", output_to_operand_aliasing={{2}: (3, {})} | custom-call | flops 8000000000 | tf_op jit(solution)/shard_map/pallas_call | solution.py:73
  8.8 0.0 collective-permute-done.2.refs_6_
  8.8 0.0 collective-permute-done.1.refs_5_
  8.8 2.1 %shard_map.89 = (bf16[1024,256]{1,0:T(8,128)(2,1)S(1)}, f32[128,256]{1,0:T(8,128)S(1)}, bf16[1,128,256]{2,1,0:T(8,128)(2,1)S(1)}, bf16[256,1024]{1,0:T(8,128)(2,1)S(1)}) custom-call(bf16[1024,2048]{1,0:T(8,128)(2,1)S(1)} %get-tuple-element.39.refs_0_, bf16[1024,256]{1,0:T(8,128)(2,1)S(1)} %get-tuple-element.42.refs_1_, ...), custom_call_target="tpu_custom_call" | custom-call | flops 8000000000 | tf_op jit(solution)/shard_map/pallas_call | solution.py:73
  10.9 0.6 %collective-permute-start.3 = (bf16[128,256]{1,0:T(8,128)(2,1)S(1)}, bf16[128,256]{1,0:T(8,128)(2,1)S(1)}, u32[]{:S(2)}, u32[]{:S(2)}) collective-permute-start(bf16[128,256]{1,0:T(8,128)(2,1)S(1)} %bitcast.13), channel_id=1, source_target_pairs={{0,1},{1,0},{2,3},{3,2},{4,5},{5,4},{6,7},{7,6},{8,9},{9,8},{10,11... | collective-permute-start | bytes 196616 | tf_op jit(solution)/shard_map/ppermute | solution.py:305
  11.5 0.5 %shard_map.90.refs_3_.refs_1_ = f32[1024,256]{1,0:T(8,128)S(1)} custom-call(bf16[1024,2048]{1,0:T(8,128)(2,1)S(1)} %get-tuple-element.41.refs_0_, bf16[1024,256]{1,0:T(8,128)(2,1)S(1)} %get-tuple-element.47.refs_1_), custom_call_target="tpu_custom_call" | custom-call | flops 8000000000 | tf_op jit(solution)/shard_map/pallas_call | solution.py:73
  12.0 0.4 %collective-permute-done.3.refs_2_ = bf16[128,256]{1,0:T(8,128)(2,1)S(1)} collective-permute-done((bf16[128,256]{1,0:T(8,128)(2,1)S(1)}, bf16[128,256]{1,0:T(8,128)(2,1)S(1)}, u32[]{:S(2)}, u32[]{:S(2)}) %collective-permute-start.3) | collective-permute-done | bytes 65568 | tf_op jit(solution)/shard_map/ppermute | solution.py:305
  12.4 0.4 %collective-permute-start.4 = (bf16[1024,256]{1,0:T(8,128)(2,1)S(1)}, bf16[1024,256]{1,0:T(8,128)(2,1)S(1)}, u32[]{:S(2)}, u32[]{:S(2)}) collective-permute-start(bf16[1024,256]{1,0:T(8,128)(2,1)S(1)} %get-tuple-element.50), channel_id=1, source_target_pairs={{0,1},{1,0},{2,3},{3,2},{4,5},{5,4},{6,7},{7,6},{8,9},{9,8},{10,11... | collective-permute-start | bytes 1572872 | tf_op jit(solution)/shard_map/ppermute | solution.py:305
  12.8 0.0 copy-start
  12.8 0.0 copy-start.1
  12.8 2.9 %collective-permute-start.6 = (bf16[128,256]{1,0:T(8,128)(2,1)S(1)}, bf16[128,256]{1,0:T(8,128)(2,1)S(1)}, u32[]{:S(2)}, u32[]{:S(2)}) collective-permute-start(bf16[128,256]{1,0:T(8,128)(2,1)S(1)} %get-tuple-element.51.refs_3_.refs_0_), channel_id=1, source_target_pairs={{0,2},{1,5},{2,0},{3,7},{4,6},{5,1},{6,4},{7,3},{8,10},{9,13},{10,... | collective-permute-start | bytes 196616 | tf_op jit(solution)/shard_map/ppermute | solution.py:324
  15.7 0.0 collective-permute-done.4.refs_2_
  15.7 0.8 %shard_map.92 = (f32[256,1024]{1,0:T(8,128)S(1)}, bf16[1,256,1024]{2,1,0:T(8,128)(2,1)S(1)}) custom-call(bf16[1024,2048]{1,0:T(8,128)(2,1)S(1)} %get-tuple-element.41.refs_0_, f32[1024,256]{1,0:T(8,128)S(1)} %shard_map.90.refs_3_.refs_1_, bf16[1024,256]{1,0:T(8,128)(2,1)S(1)} %collective-permute-done.4.refs_2_, ...), custom_call_target="tpu_custom_call" | custom-call | flops 8000000000 | tf_op jit(solution)/shard_map/pallas_call | solution.py:73
  16.6 1.4 %collective-permute-start.5 = (bf16[256,1024]{1,0:T(8,128)(2,1)S(1)}, bf16[256,1024]{1,0:T(8,128)(2,1)S(1)}, u32[]{:S(2)}, u32[]{:S(2)}) collective-permute-start(bf16[256,1024]{1,0:T(8,128)(2,1)S(1)} %bitcast.11), channel_id=1, source_target_pairs={{0,1},{1,0},{2,3},{3,2},{4,5},{5,4},{6,7},{7,6},{8,9},{9,8},{10,11... | collective-permute-start | bytes 1572872 | tf_op jit(solution)/shard_map/ppermute | solution.py:305
  17.9 0.1 collective-permute-done.6.refs_1_
  18.0 2.1 %collective-permute-start.8 = (bf16[128,256]{1,0:T(8,128)(2,1)S(1)}, bf16[128,256]{1,0:T(8,128)(2,1)S(1)}, u32[]{:S(2)}, u32[]{:S(2)}) collective-permute-start(bf16[128,256]{1,0:T(8,128)(2,1)S(1)} %shard_map.93.refs_3_.refs_0_), channel_id=1, source_target_pairs={{0,4},{1,9},{2,6},{3,11},{4,0},{5,13},{6,2},{7,15},{8,12},{9,1},{1... | collective-permute-start | bytes 196616 | tf_op jit(solution)/shard_map/ppermute | solution.py:324
  20.1 0.0 copy-done
  20.1 0.0 copy-done.1
  20.1 0.6 %shard_map.94 = (bf16[1024,256]{1,0:T(8,128)(2,1)S(1)}, f32[128,256]{1,0:T(8,128)S(1)}) custom-call(bf16[256,1024]{1,0:T(8,128)(2,1)S(1)} %get-tuple-element.54.refs_0_.refs_1_, f32[256,128]{1,0:T(8,128)S(1)} %copy-done, bf16[256,256]{1,0:T(8,128)(2,1)S(1)} %copy-done.1, bf16[128,256]{1,0:T(8,128)(2,1)S(1)} %shard_map.93.refs_3_.refs_0_), custom_call_target="tpu_custom_call" | custom-call | flops 5000000000 | tf_op jit(solution)/shard_map/pallas_call | solution.py:73
  20.7 0.0 collective-permute-done.5.refs_3_
  20.7 1.3 %shard_map.95 = (f32[256,1024]{1,0:T(8,128)S(1)}, f32[256,1024]{1,0:T(8,128)S(1)}, bf16[1,256,1024]{2,1,0:T(8,128)(2,1)S(1)}) custom-call(bf16[1024,2048]{1,0:T(8,128)(2,1)S(1)} %get-tuple-element.39.refs_0_, f32[8,128]{1,0:T(8,128)S(1)} %get-tuple-element.40.refs_1_, f32[256,1024]{1,0:T(8,128)S(1)} %get-tuple-element.52.refs_2_, ...), custom_call_target="tpu_custom_call" | custom-call | flops 8000000000 | tf_op jit(solution)/shard_map/pallas_call | solution.py:73
  22.1 0.1 collective-permute-start.7
  22.1 0.2 collective-permute-done.8.refs_1_
  22.4 2.1 %collective-permute-start.11 = (bf16[128,256]{1,0:T(8,128)(2,1)S(1)}, bf16[128,256]{1,0:T(8,128)(2,1)S(1)}, u32[]{:S(2)}, u32[]{:S(2)}) collective-permute-start(bf16[128,256]{1,0:T(8,128)(2,1)S(1)} %shard_map.96.refs_2_.refs_0_), channel_id=1, source_target_pairs={{0,8},{1,3},{2,10},{3,1},{4,12},{5,7},{6,14},{7,5},{8,0},{9,11},{1... | collective-permute-start | bytes 196616 | tf_op jit(solution)/shard_map/ppermute | solution.py:324
  24.5 1.2 %shard_map.97 = (f32[256,1024]{1,0:T(8,128)S(1)}, bf16[1,256,1024]{2,1,0:T(8,128)(2,1)S(1)}) custom-call(bf16[1024,2048]{1,0:T(8,128)(2,1)S(1)} %get-tuple-element.39.refs_0_, bf16[256,1024]{1,0:T(8,128)(2,1)S(1)} %get-tuple-element.54.refs_0_.refs_1_, bf16[128,256]{1,0:T(8,128)(2,1)S(1)} %shard_map.96.refs_2_.refs_0_), custom_call_target="tpu_custom_call" | custom-call | flops 5000000000 | tf_op jit(solution)/shard_map/pallas_call | solution.py:73
  25.8 0.1 collective-permute-start.10
  25.9 0.0 collective-permute-done.7.refs_3_
  25.9 0.9 %shard_map.98 = (f32[256,1024]{1,0:T(8,128)S(1)}, bf16[1,256,1024]{2,1,0:T(8,128)(2,1)S(1)}) custom-call(bf16[1024,2048]{1,0:T(8,128)(2,1)S(1)} %get-tuple-element.34.refs_0_, f32[256,1024]{1,0:T(8,128)S(1)} %get-tuple-element.38.refs_1_, f32[256,1024]{1,0:T(8,128)S(1)} %get-tuple-element.56.refs_2_, bf16[256,1024]{1,0:T(8,128)(2,1)S(1)} %collective-permute-done.7.refs_3_, ...), custom_call_target="tpu_custom_call" | custom-call | flops 8000000000 | tf_op jit(solution)/shard_map/pallas_call | solution.py:73
  26.8 1.2 %collective-permute-start.9 = (bf16[256,1024]{1,0:T(8,128)(2,1)S(1)}, bf16[256,1024]{1,0:T(8,128)(2,1)S(1)}, u32[]{:S(2)}, u32[]{:S(2)}) collective-permute-start(bf16[256,1024]{1,0:T(8,128)(2,1)S(1)} %bitcast.8), channel_id=1, source_target_pairs={{0,1},{1,0},{2,3},{3,2},{4,5},{5,4},{6,7},{7,6},{8,9},{9,8},{10,11... | collective-permute-start | bytes 1572872 | tf_op jit(solution)/shard_map/ppermute | solution.py:305
  28.0 0.0 collective-permute-done.11.refs_1_
  28.0 2.7 %collective-permute-start.13 = (bf16[128,256]{1,0:T(8,128)(2,1)S(1)}, bf16[128,256]{1,0:T(8,128)(2,1)S(1)}, u32[]{:S(2)}, u32[]{:S(2)}) collective-permute-start(bf16[128,256]{1,0:T(8,128)(2,1)S(1)} %shard_map.99.refs_5_.refs_1_), channel_id=1, source_target_pairs={{0,16},{1,17},{2,18},{3,19},{4,20},{5,21},{6,22},{7,23},{8,24},{9,... | collective-permute-start | bytes 196616 | tf_op jit(solution)/shard_map/ppermute | solution.py:324
  30.7 0.0 collective-permute-done.10.refs_4_
  30.7 1.2 %shard_map.100 = (f32[256,1024]{1,0:T(8,128)S(1)}, bf16[1,256,1024]{2,1,0:T(8,128)(2,1)S(1)}) custom-call(bf16[1024,2048]{1,0:T(8,128)(2,1)S(1)} %get-tuple-element.34.refs_0_, bf16[256,1024]{1,0:T(8,128)(2,1)S(1)} %get-tuple-element.44.refs_3_.refs_1_, bf16[256,256]{1,0:T(8,128)(2,1)S(1)} %copy-done.1, f32[256,1024]{1,0:T(8,128)S(1)} %get-tuple-element.59.refs_4_.refs_3_, ...), custom_call_target="tpu_custom_call" | custom-call | flops 5000000000 | tf_op jit(solution)/shard_map/pallas_call | solution.py:73
  31.9 0.5 %collective-permute-start.12 = (bf16[256,1024]{1,0:T(8,128)(2,1)S(1)}, bf16[256,1024]{1,0:T(8,128)(2,1)S(1)}, u32[]{:S(2)}, u32[]{:S(2)}) collective-permute-start(bf16[256,1024]{1,0:T(8,128)(2,1)S(1)} %bitcast.12), channel_id=1, source_target_pairs={{0,1},{1,0},{2,3},{3,2},{4,5},{5,4},{6,7},{7,6},{8,9},{9,8},{10,11... | collective-permute-start | bytes 1572872 | tf_op jit(solution)/shard_map/ppermute | solution.py:305
  32.4 0.0 collective-permute-done.9.refs_1_
  32.4 0.3 shard_map.101.refs_1_.refs_0_
  32.7 0.3 shard_map.102.refs_2_.refs_1_
  33.0 0.9 %collective-permute-done.12.refs_1_ = bf16[256,1024]{1,0:T(8,128)(2,1)S(1)} collective-permute-done((bf16[256,1024]{1,0:T(8,128)(2,1)S(1)}, bf16[256,1024]{1,0:T(8,128)(2,1)S(1)}, u32[]{:S(2)}, u32[]{:S(2)}) %collective-permute-start.12) | collective-permute-done | bytes 524320 | tf_op jit(solution)/shard_map/ppermute | solution.py:305
  33.9 0.2 shard_map.103.refs_3_.refs_2_
  34.1 0.2 collective-permute-done.13.refs_2_
  34.4 0.3 collective-permute-start.14
  34.6 1.1 %shard_map.105.refs_6_ = f32[256,128]{1,0:T(8,128)} custom-call(bf16[256,256]{1,0:T(8,128)(2,1)S(1)} %copy-done.1, bf16[128,256]{1,0:T(8,128)(2,1)S(1)} %shard_map.104.refs_1_.refs_4_), custom_call_target="tpu_custom_call" | custom-call | flops 8000000000 | tf_op jit(solution)/shard_map/pallas_call | solution.py:73
  35.7 0.0 collective-permute-done.14.refs_5_
  35.7 1.3 %shard_map.106 = bf16[2,1024,256]{2,1,0:T(8,128)(2,1)} custom-call(f32[1024,256]{1,0:T(8,128)S(1)} %shard_map.101.refs_1_.refs_0_, f32[1024,256]{1,0:T(8,128)S(1)} %shard_map.102.refs_2_.refs_1_, bf16[1024,256]{1,0:T(8,128)(2,1)S(1)} %shard_map.103.refs_3_.refs_2_, bf16[1024,256]{1,0:T(8,128)(2,1)S(1)} %get-tuple-element.65.refs_3_, ...), custom_call_target="tpu_custom_call" | custom-call | flops 8000000000 | tf_op jit(solution)/shard_map/pallas_call | solution.py:73
  (5 shorter events, 0.1 us)
Async XLA Ops:
  0.6 4.4 %collective-permute-start = (bf16[2,1024,256]{2,1,0:T(8,128)(2,1)}, bf16[2,1024,256]{2,1,0:T(8,128)(2,1)S(1)}, u32[]{:S(2)}, u32[]{:S(2)}) collective-permute-start(bf16[2,1024,256]{2,1,0:T(8,128)(2,1)} %refs_3_.3), channel_id=1, source_target_pairs={{0,1},{1,0},{2,3},{3,2},{4,5},{5,4},{6,7},{7,6},{8,9},{9,8},{10,11... | collective-permute-start | bytes 3145736 | tf_op jit(solution)/shard_map/ppermute | solution.py:305
  4.0 4.8 %collective-permute-start.2 = (bf16[256,1024]{1,0:T(8,128)(2,1)S(1)}, bf16[256,1024]{1,0:T(8,128)(2,1)S(1)}, u32[]{:S(2)}, u32[]{:S(2)}) collective-permute-start(bf16[256,1024]{1,0:T(8,128)(2,1)S(1)} %bitcast.9), channel_id=1, source_target_pairs={{0,1},{1,0},{2,3},{3,2},{4,5},{5,4},{6,7},{7,6},{8,9},{9,8},{10,11... | collective-permute-start | bytes 1572872 | tf_op jit(solution)/shard_map/ppermute | solution.py:305
  6.6 2.2 %collective-permute-start.1 = (bf16[1024,256]{1,0:T(8,128)(2,1)S(1)}, bf16[1024,256]{1,0:T(8,128)(2,1)S(1)}, u32[]{:S(2)}, u32[]{:S(2)}) collective-permute-start(bf16[1024,256]{1,0:T(8,128)(2,1)S(1)} %get-tuple-element.42.refs_1_), channel_id=1, source_target_pairs={{0,1},{1,0},{2,3},{3,2},{4,5},{5,4},{6,7},{7,6},{8,9},{9,8},{10,11... | collective-permute-start | bytes 1572872 | tf_op jit(solution)/shard_map/ppermute | solution.py:305
  10.9 1.5 %collective-permute-start.3 = (bf16[128,256]{1,0:T(8,128)(2,1)S(1)}, bf16[128,256]{1,0:T(8,128)(2,1)S(1)}, u32[]{:S(2)}, u32[]{:S(2)}) collective-permute-start(bf16[128,256]{1,0:T(8,128)(2,1)S(1)} %bitcast.13), channel_id=1, source_target_pairs={{0,1},{1,0},{2,3},{3,2},{4,5},{5,4},{6,7},{7,6},{8,9},{9,8},{10,11... | collective-permute-start | bytes 196616 | tf_op jit(solution)/shard_map/ppermute | solution.py:305
  12.4 3.4 %collective-permute-start.4 = (bf16[1024,256]{1,0:T(8,128)(2,1)S(1)}, bf16[1024,256]{1,0:T(8,128)(2,1)S(1)}, u32[]{:S(2)}, u32[]{:S(2)}) collective-permute-start(bf16[1024,256]{1,0:T(8,128)(2,1)S(1)} %get-tuple-element.50), channel_id=1, source_target_pairs={{0,1},{1,0},{2,3},{3,2},{4,5},{5,4},{6,7},{7,6},{8,9},{9,8},{10,11... | collective-permute-start | bytes 1572872 | tf_op jit(solution)/shard_map/ppermute | solution.py:305
  12.8 7.3 %copy-start = (f32[256,128]{1,0:T(8,128)S(1)}, f32[256,128]{1,0:T(8,128)}, u32[]{:S(2)}) copy-start(f32[256,128]{1,0:T(8,128)} %refs_1_.5) | copy-start | bytes 393220
  12.8 7.3 %copy-start.1 = (bf16[256,256]{1,0:T(8,128)(2,1)S(1)}, bf16[256,256]{1,0:T(8,128)(2,1)}, u32[]{:S(2)}) copy-start(bf16[256,256]{1,0:T(8,128)(2,1)} %refs_0_.5) | copy-start | bytes 393220
  12.8 5.2 %collective-permute-start.6 = (bf16[128,256]{1,0:T(8,128)(2,1)S(1)}, bf16[128,256]{1,0:T(8,128)(2,1)S(1)}, u32[]{:S(2)}, u32[]{:S(2)}) collective-permute-start(bf16[128,256]{1,0:T(8,128)(2,1)S(1)} %get-tuple-element.51.refs_3_.refs_0_), channel_id=1, source_target_pairs={{0,2},{1,5},{2,0},{3,7},{4,6},{5,1},{6,4},{7,3},{8,10},{9,13},{10,... | collective-permute-start | bytes 196616 | tf_op jit(solution)/shard_map/ppermute | solution.py:324
  16.6 4.2 %collective-permute-start.5 = (bf16[256,1024]{1,0:T(8,128)(2,1)S(1)}, bf16[256,1024]{1,0:T(8,128)(2,1)S(1)}, u32[]{:S(2)}, u32[]{:S(2)}) collective-permute-start(bf16[256,1024]{1,0:T(8,128)(2,1)S(1)} %bitcast.11), channel_id=1, source_target_pairs={{0,1},{1,0},{2,3},{3,2},{4,5},{5,4},{6,7},{7,6},{8,9},{9,8},{10,11... | collective-permute-start | bytes 1572872 | tf_op jit(solution)/shard_map/ppermute | solution.py:305
  18.0 4.4 %collective-permute-start.8 = (bf16[128,256]{1,0:T(8,128)(2,1)S(1)}, bf16[128,256]{1,0:T(8,128)(2,1)S(1)}, u32[]{:S(2)}, u32[]{:S(2)}) collective-permute-start(bf16[128,256]{1,0:T(8,128)(2,1)S(1)} %shard_map.93.refs_3_.refs_0_), channel_id=1, source_target_pairs={{0,4},{1,9},{2,6},{3,11},{4,0},{5,13},{6,2},{7,15},{8,12},{9,1},{1... | collective-permute-start | bytes 196616 | tf_op jit(solution)/shard_map/ppermute | solution.py:324
  22.1 3.8 %collective-permute-start.7 = (bf16[256,1024]{1,0:T(8,128)(2,1)S(1)}, bf16[256,1024]{1,0:T(8,128)(2,1)S(1)}, u32[]{:S(2)}, u32[]{:S(2)}) collective-permute-start(bf16[256,1024]{1,0:T(8,128)(2,1)S(1)} %bitcast.10), channel_id=1, source_target_pairs={{0,1},{1,0},{2,3},{3,2},{4,5},{5,4},{6,7},{7,6},{8,9},{9,8},{10,11... | collective-permute-start | bytes 1572872 | tf_op jit(solution)/shard_map/ppermute | solution.py:305
  22.4 5.6 %collective-permute-start.11 = (bf16[128,256]{1,0:T(8,128)(2,1)S(1)}, bf16[128,256]{1,0:T(8,128)(2,1)S(1)}, u32[]{:S(2)}, u32[]{:S(2)}) collective-permute-start(bf16[128,256]{1,0:T(8,128)(2,1)S(1)} %shard_map.96.refs_2_.refs_0_), channel_id=1, source_target_pairs={{0,8},{1,3},{2,10},{3,1},{4,12},{5,7},{6,14},{7,5},{8,0},{9,11},{1... | collective-permute-start | bytes 196616 | tf_op jit(solution)/shard_map/ppermute | solution.py:324
  25.8 4.9 %collective-permute-start.10 = (bf16[256,1024]{1,0:T(8,128)(2,1)S(1)}, bf16[256,1024]{1,0:T(8,128)(2,1)S(1)}, u32[]{:S(2)}, u32[]{:S(2)}) collective-permute-start(bf16[256,1024]{1,0:T(8,128)(2,1)S(1)} %bitcast.7), channel_id=1, source_target_pairs={{0,1},{1,0},{2,3},{3,2},{4,5},{5,4},{6,7},{7,6},{8,9},{9,8},{10,11... | collective-permute-start | bytes 1572872 | tf_op jit(solution)/shard_map/ppermute | solution.py:305
  26.8 5.6 %collective-permute-start.9 = (bf16[256,1024]{1,0:T(8,128)(2,1)S(1)}, bf16[256,1024]{1,0:T(8,128)(2,1)S(1)}, u32[]{:S(2)}, u32[]{:S(2)}) collective-permute-start(bf16[256,1024]{1,0:T(8,128)(2,1)S(1)} %bitcast.8), channel_id=1, source_target_pairs={{0,1},{1,0},{2,3},{3,2},{4,5},{5,4},{6,7},{7,6},{8,9},{9,8},{10,11... | collective-permute-start | bytes 1572872 | tf_op jit(solution)/shard_map/ppermute | solution.py:305
  28.0 6.3 %collective-permute-start.13 = (bf16[128,256]{1,0:T(8,128)(2,1)S(1)}, bf16[128,256]{1,0:T(8,128)(2,1)S(1)}, u32[]{:S(2)}, u32[]{:S(2)}) collective-permute-start(bf16[128,256]{1,0:T(8,128)(2,1)S(1)} %shard_map.99.refs_5_.refs_1_), channel_id=1, source_target_pairs={{0,16},{1,17},{2,18},{3,19},{4,20},{5,21},{6,22},{7,23},{8,24},{9,... | collective-permute-start | bytes 196616 | tf_op jit(solution)/shard_map/ppermute | solution.py:324
  31.9 2.0 %collective-permute-start.12 = (bf16[256,1024]{1,0:T(8,128)(2,1)S(1)}, bf16[256,1024]{1,0:T(8,128)(2,1)S(1)}, u32[]{:S(2)}, u32[]{:S(2)}) collective-permute-start(bf16[256,1024]{1,0:T(8,128)(2,1)S(1)} %bitcast.12), channel_id=1, source_target_pairs={{0,1},{1,0},{2,3},{3,2},{4,5},{5,4},{6,7},{7,6},{8,9},{9,8},{10,11... | collective-permute-start | bytes 1572872 | tf_op jit(solution)/shard_map/ppermute | solution.py:305
  34.4 1.3 %collective-permute-start.14 = (bf16[128,256]{1,0:T(8,128)(2,1)S(1)}, bf16[128,256]{1,0:T(8,128)(2,1)S(1)}, u32[]{:S(2)}, u32[]{:S(2)}) collective-permute-start(bf16[128,256]{1,0:T(8,128)(2,1)S(1)} %shard_map.104.refs_1_.refs_4_), channel_id=1, source_target_pairs={{0,1},{1,0},{2,3},{3,2},{4,5},{5,4},{6,7},{7,6},{8,9},{9,8},{10,11... | collective-permute-start | bytes 196616 | tf_op jit(solution)/shard_map/ppermute | solution.py:305

commit v12 on v11

--- a/solution.py
+++ b/solution.py
@@ -233,43 +233,37 @@
         lower_rest(d1, got, value)
         lower_rows(value[...].astype(BF).T, d1, own, other)
 
-    def response_kernel(k1, response, own, other):
-        full_rows(response, k1, own, other)
-
-    def pass_kernel(k1, mask, solved, *refs):
-        got, (base, own, other) = refs[: n_space - 1], refs[n_space - 1 :]
+    def pass_kernel(k1, mask, response, solved, *refs):
+        got, (base, own, other, left) = refs[: n_space - 1], refs[n_space - 1 :]
         value = jnp.where(mask[:1, :1] > 0, total_of(solved, got), 0.0)
         base[...] = value
-        full_rows(value.astype(BF), k1, own, other)
-
-    def first_response_kernel(d0, e0, tip, pushed, *refs):
-        got, (own, other) = refs[: n_space - 1], refs[n_space - 1 :]
-        left = (e0[...].astype(F32) - total_of(pushed, got)).astype(BF)
-        lower_rows(through_tip(tip[...], left).astype(BF), d0, own, other)
-
-    def first_solve_kernel(d0, value_rows, passed, *refs):
-        got, (own, other) = refs[: n_space - 1], refs[n_space - 1 :]
-        left = (value_rows[...] - total_of(passed, got)).astype(BF)
+        left[:columns] = value.astype(BF)
+        left[columns:] = response[...]
+        full_rows(left, k1, own, other)
+
+    def first_solve_kernel(d0, value_rows, e0, tip, passed, *refs):
+        got, (own, other, left) = refs[: n_space - 1], refs[n_space - 1 :]
+        total = total_of(passed, got)
+        left[:columns] = (value_rows[...] - total[:columns]).astype(BF)
+        pushed = (e0[...].astype(F32) - total[columns:]).astype(BF)
+        left[columns:] = through_tip(tip[...], pushed).astype(BF)
         lower_rows(left, d0, own, other)
 
     def through_tip(tip, right):
         inner = dot(tip, right).astype(BF)
         return dot(tip.astype(F32).T.astype(BF), inner)
 
-    def turn_tip_kernel(response, noise_fixed, tip, last_resp, noise_rows):
-        noise_rows[...] = noise_fixed[...].T
+    def turn_tip_kernel(response, tip, last_resp):
         last_resp[...] = through_tip(tip[...], response[...]).T.astype(BF)
 
-    def turn_last_kernel(base, out):
-        out[...] = base[...].T
-
-    def turn_response_kernel(first, *refs):
-        got, out = refs[:-1], refs[-1]
-        out[...] = total_of(first, got).T.astype(BF)
+    def turn_kernel(value, out):
+        out[...] = value[...].T
 
     def turn_first_kernel(solved, *refs):
-        got, out = refs[:-1], refs[-1]
-        out[...] = total_of(solved, got).T
+        got, (base, response) = refs[: n_space - 1], refs[n_space - 1 :]
+        total = total_of(solved, got)
+        base[...] = total[:columns].T
+        response[...] = total[columns:].T.astype(BF)
 
     def mixed_kernel(noise_rows, *refs):
         terms, out = refs[:-1], refs[-1]
@@ -317,9 +311,7 @@
         pairs = []
         for i in range(n_tm):
             for core in range(n_space):
-                bit = 1 << step
-                if step < steps - 1:
-                    bit = 1 << (step + core * (steps - 1) // n_space) % (steps - 1)
+                bit = 1 << (step + core * steps // n_space) % steps
                 pairs.append((i * n_space + core, (i ^ bit) * n_space + core))
         return lax.ppermute(value, ("tm", "space"), pairs)
 
@@ -327,6 +319,9 @@
     flat_f32 = shape_of((columns, rows), F32)
     flat_others = shape_of((n_space - 1, columns, rows), BF)
     fixed_f32 = shape_of((fixed_rows, rows), F32)
+    both_f32 = shape_of((columns + fixed_rows, rows), F32)
+    both_others = shape_of((n_space - 1, columns + fixed_rows, rows), BF)
+    both_left = pltpu.VMEM((columns + fixed_rows, rows), BF)
     fixed_bf = shape_of((fixed_rows, rows), BF)
     fixed_others = shape_of((n_space - 1, fixed_rows, rows), BF)
     part_bf = shape_of((width, fixed_rows), BF)
@@ -420,46 +415,40 @@
         )
         got_solved = send_down(other)
         advance(solved)
-        last_resp, noise_rows = call(
-            turn_tip_kernel,
-            [by_node, shape_of((width, fixed_rows), F32)],
-            [response, noise_fixed, tip_inverse],
-            5,
-            after=sent,
+        (last_resp,) = call(
+            turn_tip_kernel, [by_node], [response, tip_inverse], 5, after=sent
         )
         base, passed, other = call(
             pass_kernel,
-            [flat_f32, flat_f32, flat_others],
-            [k1, mask, solved, *got_solved],
-            8,
-            after=noise_rows,
+            [flat_f32, both_f32, both_others],
+            [k1, mask, response, solved, *got_solved],
+            10,
+            scratch=[both_left],
+            after=last_resp,
         )
         got_passed = send_down(other)
         advance(base)
-        pushed, other = call(
-            response_kernel, [fixed_f32, fixed_others], [k1, response], 5, after=sent
-        )
-        got_pushed = send_down(other)
+        (last_base,) = call(turn_kernel, [node_f32], [base], 11, after=sent)
         solved, other = call(
             first_solve_kernel,
-            [flat_f32, flat_others],
-            [d0, value_rows, passed, *got_passed],
-            8,
-            after=pushed,
+            [both_f32, both_others],
+            [d0, value_rows, e0, tip_inverse, passed, *got_passed],
+            10,
+            scratch=[both_left],
+            after=last_base,
         )
         got_solved = send_down(other)
         advance(solved)
-        first, other = call(
-            first_response_kernel,
-            [fixed_f32, fixed_others],
-            [d0, e0, tip_inverse, pushed, *got_pushed],
-            5,
+        (noise_rows,) = call(
+            turn_kernel,
+            [shape_of((width, fixed_rows), F32)],
+            [noise_fixed],
+            11,
             after=sent,
         )
-        got_first = send_down(other)
-        (first_base,) = call(turn_first_kernel, [node_f32], [solved, *got_solved], 1, after=first)
-        (last_base,) = call(turn_last_kernel, [node_f32], [base], 8, after=first_base)
-        (first_resp,) = call(turn_response_kernel, [by_node], [first, *got_first], 1, after=last_base)
+        first_base, first_resp = call(
+            turn_first_kernel, [node_f32, by_node], [solved, *got_solved], 1, after=noise_rows
+        )
         while step < steps:
             advance()
         (mixed,) = call(mixed_kernel, [part_bf], [noise_rows, sent, *got], 0.2, after=first_resp)

time: 37.2 us -> 37.9 us (1.019)
  waiting for transfers between devices: 1.77 us -> 3.46 us
  starting transfers between devices: 16 us -> 15.3 us
    ppermute x4, waiting for transfers between devices: 0.49 us -> 2.5 us  [swap_step(): return lax.ppermute(value, ('tm', 'space'), pairs)]
    ppermute x4, starting transfers between devices: 9.86 us -> 8.78 us  [swap_step(): return lax.ppermute(value, ('tm', 'space'), pairs)]
    ppermute x11 -> x9, starting transfers between devices: 6.15 us -> 6.55 us  [swap(): return lax.ppermute(value, 'space', pairs)]
    ppermute x11 -> x9, waiting for transfers between devices: 1.28 us -> 0.96 us  [swap(): return lax.ppermute(value, 'space', pairs)]
    pallas_call x21 -> x19, Pallas kernels: 18.4 us -> 18.1 us  [call(): pl.pallas_call(run, in_specs=specs, out_specs=[pl.BlockSpec(memory_space=...]
  transfers between devices with their start and end apart: 15 -> 13, of which waited for: 5 -> 5; matrix products, arithmetic and copies ran while one was open for 0% -> 0% of each run, Pallas kernels for 40% -> 39%
where the time goes in v12:
time: 37.9 us; the launch traced here: 37.7 us
  Pallas kernels  18.1 us (48%)
  starting transfers between devices  15.3 us (40%)
  waiting for transfers between devices  3.46 us (9%)
  between operations  0.78 us (2%)
    pallas_call x19, Pallas kernels, call(): pl.pallas_call(run, in_specs=specs, out_specs=[pl.BlockSpec(memory_space=...  18.1 us
    ppermute x4, starting transfers between devices, swap_step(): return lax.ppermute(value, ('tm', 'space'), pairs)  8.78 us
    ppermute x9, starting transfers between devices, swap(): return lax.ppermute(value, 'space', pairs)  6.55 us
    ppermute x4, waiting for transfers between devices, swap_step(): return lax.ppermute(value, ('tm', 'space'), pairs)  2.5 us
    ppermute x9, waiting for transfers between devices, swap(): return lax.ppermute(value, 'space', pairs)  0.96 us
  transfers between devices with their start and end apart: 13, of which 5 were waited for; matrix products, arithmetic and copies ran while one was open for 0% of the time, Pallas kernels for 39%

profile of v12, /device:TPU:0, one launch (start us, length us, event | category | flops | bytes accessed | tf_op | source)
XLA Modules:
  0.0 37.7 jit_solution(6769326118655977334)
XLA Ops:
  0.6 0.5 %collective-permute-start = (bf16[2,1024,256]{2,1,0:T(8,128)(2,1)}, bf16[2,1024,256]{2,1,0:T(8,128)(2,1)S(1)}, u32[]{:S(2)}, u32[]{:S(2)}) collective-permute-start(bf16[2,1024,256]{2,1,0:T(8,128)(2,1)} %refs_3_.4), channel_id=1, source_target_pairs={{0,1},{1,0},{2,3},{3,2},{4,5},{5,4},{6,7},{7,6},{8,9},{9,8},{10,11... | collective-permute-start | bytes 3145736 | tf_op jit(solution)/shard_map/ppermute | solution.py:299
  1.1 2.8 %shard_map.86 = (bf16[1024,2048]{1,0:T(8,128)(2,1)S(1)}, bf16[1024,2048]{1,0:T(8,128)(2,1)S(1)}, f32[256,1024]{1,0:T(8,128)S(1)}, bf16[1,256,1024]{2,1,0:T(8,128...) custom-call(bf16[2,1024,2048]{2,1,0:T(8,128)(2,1)} %refs_0_.4, bf16[2,256,1024]{2,1,0:T(8,128)(2,1)} %refs_1_.4, ...), custom_call_target="tpu_custom_call" | custom-call | flops 8000000000 | tf_op jit(solution)/shard_map/pallas_call | solution.py:73
  4.0 1.1 %collective-permute-start.2 = (bf16[256,1024]{1,0:T(8,128)(2,1)S(1)}, bf16[256,1024]{1,0:T(8,128)(2,1)S(1)}, u32[]{:S(2)}, u32[]{:S(2)}) collective-permute-start(bf16[256,1024]{1,0:T(8,128)(2,1)S(1)} %bitcast.7), channel_id=1, source_target_pairs={{0,1},{1,0},{2,3},{3,2},{4,5},{5,4},{6,7},{7,6},{8,9},{9,8},{10,11... | collective-permute-start | bytes 1572872 | tf_op jit(solution)/shard_map/ppermute | solution.py:299
  5.1 0.0 collective-permute-done.refs_4_
  5.1 1.6 %shard_map.87 = (f32[1024,256]{1,0:T(8,128)S(1)}, bf16[1024,256]{1,0:T(8,128)(2,1)S(1)}, bf16[1024,2048]{1,0:T(8,128)(2,1)S(1)}, bf16[1024,256]{1,0:T(8,128)(2,1)S(1)}) custom-call(bf16[1024,2048]{1,0:T(8,128)(2,1)S(1)} %get-tuple-element.30.refs_0_, bf16[1024,256]{1,0:T(8,128)(2,1)S(1)} %get-tuple-element.31.refs_1_, bf16[2,1024,2048]{2,1,0:T(8,128)(2,1)} %refs_0_.5, ...), custom_call_target="tpu_custom_call" | custom-call | flops 8000000000 | tf_op jit(solution)/shard_map/pallas_call | solution.py:73
  6.7 0.1 collective-permute-start.1
  6.7 2.0 %shard_map.88 = (f32[256,1024]{1,0:T(8,128)S(1)}, bf16[256,1024]{1,0:T(8,128)(2,1)S(1)}, bf16[1024,2048]{1,0:T(8,128)(2,1)S(1)}) custom-call(bf16[2,1024,2048]{2,1,0:T(8,128)(2,1)} %refs_0_.5, bf16[2,256,1024]{2,1,0:T(8,128)(2,1)} %refs_1_.4, f32[1024,256]{1,0:T(8,128)S(1)} %get-tuple-element.32.refs_2_, ...), custom_call_target="tpu_custom_call", output_to_operand_aliasing={{2}: (3, {})} | custom-call | flops 8000000000 | tf_op jit(solution)/shard_map/pallas_call | solution.py:73
  8.8 0.0 collective-permute-done.2.refs_6_
  8.8 0.0 collective-permute-done.1.refs_5_
  8.8 2.1 %shard_map.89 = (bf16[1024,256]{1,0:T(8,128)(2,1)S(1)}, f32[128,256]{1,0:T(8,128)S(1)}, bf16[1,128,256]{2,1,0:T(8,128)(2,1)S(1)}, bf16[256,1024]{1,0:T(8,128)(2,1)S(1)}) custom-call(bf16[1024,2048]{1,0:T(8,128)(2,1)S(1)} %get-tuple-element.36.refs_0_, bf16[1024,256]{1,0:T(8,128)(2,1)S(1)} %get-tuple-element.38.refs_1_, ...), custom_call_target="tpu_custom_call" | custom-call | flops 8000000000 | tf_op jit(solution)/shard_map/pallas_call | solution.py:73
  10.9 0.6 %collective-permute-start.3 = (bf16[128,256]{1,0:T(8,128)(2,1)S(1)}, bf16[128,256]{1,0:T(8,128)(2,1)S(1)}, u32[]{:S(2)}, u32[]{:S(2)}) collective-permute-start(bf16[128,256]{1,0:T(8,128)(2,1)S(1)} %bitcast.9), channel_id=1, source_target_pairs={{0,1},{1,0},{2,3},{3,2},{4,5},{5,4},{6,7},{7,6},{8,9},{9,8},{10,11... | collective-permute-start | bytes 196616 | tf_op jit(solution)/shard_map/ppermute | solution.py:299
  11.5 0.5 %shard_map.90.refs_3_.refs_1_ = f32[1024,256]{1,0:T(8,128)S(1)} custom-call(bf16[1024,2048]{1,0:T(8,128)(2,1)S(1)} %get-tuple-element.43.refs_0_, bf16[1024,256]{1,0:T(8,128)(2,1)S(1)} %get-tuple-element.44.refs_1_), custom_call_target="tpu_custom_call" | custom-call | flops 8000000000 | tf_op jit(solution)/shard_map/pallas_call | solution.py:73
  12.0 0.4 %collective-permute-done.3.refs_2_ = bf16[128,256]{1,0:T(8,128)(2,1)S(1)} collective-permute-done((bf16[128,256]{1,0:T(8,128)(2,1)S(1)}, bf16[128,256]{1,0:T(8,128)(2,1)S(1)}, u32[]{:S(2)}, u32[]{:S(2)}) %collective-permute-start.3) | collective-permute-done | bytes 65568 | tf_op jit(solution)/shard_map/ppermute | solution.py:299
  12.4 0.4 %collective-permute-start.4 = (bf16[1024,256]{1,0:T(8,128)(2,1)S(1)}, bf16[1024,256]{1,0:T(8,128)(2,1)S(1)}, u32[]{:S(2)}, u32[]{:S(2)}) collective-permute-start(bf16[1024,256]{1,0:T(8,128)(2,1)S(1)} %get-tuple-element.47), channel_id=1, source_target_pairs={{0,1},{1,0},{2,3},{3,2},{4,5},{5,4},{6,7},{7,6},{8,9},{9,8},{10,11... | collective-permute-start | bytes 1572872 | tf_op jit(solution)/shard_map/ppermute | solution.py:299
  12.8 0.0 copy-start.1
  12.8 2.9 %collective-permute-start.6 = (bf16[128,256]{1,0:T(8,128)(2,1)S(1)}, bf16[128,256]{1,0:T(8,128)(2,1)S(1)}, u32[]{:S(2)}, u32[]{:S(2)}) collective-permute-start(bf16[128,256]{1,0:T(8,128)(2,1)S(1)} %get-tuple-element.48.refs_3_.refs_0_), channel_id=1, source_target_pairs={{0,2},{1,9},{2,0},{3,11},{4,6},{5,13},{6,4},{7,15},{8,10},{9,1},{1... | collective-permute-start | bytes 196616 | tf_op jit(solution)/shard_map/ppermute | solution.py:316
  15.8 0.0 collective-permute-done.4.refs_2_
  15.8 0.8 %shard_map.92 = (f32[256,1024]{1,0:T(8,128)S(1)}, bf16[1,256,1024]{2,1,0:T(8,128)(2,1)S(1)}) custom-call(bf16[1024,2048]{1,0:T(8,128)(2,1)S(1)} %get-tuple-element.43.refs_0_, f32[1024,256]{1,0:T(8,128)S(1)} %shard_map.90.refs_3_.refs_1_, bf16[1024,256]{1,0:T(8,128)(2,1)S(1)} %collective-permute-done.4.refs_2_, ...), custom_call_target="tpu_custom_call" | custom-call | flops 8000000000 | tf_op jit(solution)/shard_map/pallas_call | solution.py:73
  16.6 1.4 %collective-permute-start.5 = (bf16[256,1024]{1,0:T(8,128)(2,1)S(1)}, bf16[256,1024]{1,0:T(8,128)(2,1)S(1)}, u32[]{:S(2)}, u32[]{:S(2)}) collective-permute-start(bf16[256,1024]{1,0:T(8,128)(2,1)S(1)} %bitcast.8), channel_id=1, source_target_pairs={{0,1},{1,0},{2,3},{3,2},{4,5},{5,4},{6,7},{7,6},{8,9},{9,8},{10,11... | collective-permute-start | bytes 1572872 | tf_op jit(solution)/shard_map/ppermute | solution.py:299
  18.0 0.0 collective-permute-done.6.refs_1_
  18.0 2.1 %collective-permute-start.8 = (bf16[128,256]{1,0:T(8,128)(2,1)S(1)}, bf16[128,256]{1,0:T(8,128)(2,1)S(1)}, u32[]{:S(2)}, u32[]{:S(2)}) collective-permute-start(bf16[128,256]{1,0:T(8,128)(2,1)S(1)} %shard_map.93.refs_2_.refs_0_), channel_id=1, source_target_pairs={{0,4},{1,17},{2,6},{3,19},{4,0},{5,21},{6,2},{7,23},{8,12},{9,25},... | collective-permute-start | bytes 196616 | tf_op jit(solution)/shard_map/ppermute | solution.py:316
  20.1 0.0 copy-done.1
  20.2 0.6 %shard_map.94.refs_5_.refs_3_ = bf16[1024,256]{1,0:T(8,128)(2,1)S(1)} custom-call(bf16[256,1024]{1,0:T(8,128)(2,1)S(1)} %get-tuple-element.42.refs_0_.refs_2_, bf16[256,256]{1,0:T(8,128)(2,1)S(1)} %copy-done.1, bf16[128,256]{1,0:T(8,128)(2,1)S(1)} %shard_map.93.refs_2_.refs_0_), custom_call_target="tpu_custom_call" | custom-call | flops 5000000000 | tf_op jit(solution)/shard_map/pallas_call | solution.py:73
  20.7 0.0 collective-permute-done.5.refs_4_
  20.8 2.4 %shard_map.95 = (f32[256,1024]{1,0:T(8,128)S(1)}, f32[512,1024]{1,0:T(8,128)S(1)}, bf16[1,512,1024]{2,1,0:T(8,128)(2,1)S(1)}) custom-call(bf16[1024,2048]{1,0:T(8,128)(2,1)S(1)} %get-tuple-element.36.refs_0_, f32[8,128]{1,0:T(8,128)S(1)} %get-tuple-element.37.refs_1_, bf16[256,1024]{1,0:T(8,128)(2,1)S(1)} %get-tuple-element.42.refs_0_.refs_2_, ...), custom_call_target="tpu_custom_call" | custom-call | flops 10000000000 | tf_op jit(solution)/shard_map/pallas_call | solution.py:73
  23.2 0.8 %collective-permute-start.7 = (bf16[512,1024]{1,0:T(8,128)(2,1)S(1)}, bf16[512,1024]{1,0:T(8,128)(2,1)S(1)}, u32[]{:S(2)}, u32[]{:S(2)}) collective-permute-start(bf16[512,1024]{1,0:T(8,128)(2,1)S(1)} %bitcast.5), channel_id=1, source_target_pairs={{0,1},{1,0},{2,3},{3,2},{4,5},{5,4},{6,7},{7,6},{8,9},{9,8},{10,11... | collective-permute-start | bytes 3145736 | tf_op jit(solution)/shard_map/ppermute | solution.py:299
  23.9 0.0 collective-permute-done.8.refs_1_
  24.0 1.6 %collective-permute-start.10 = (bf16[128,256]{1,0:T(8,128)(2,1)S(1)}, bf16[128,256]{1,0:T(8,128)(2,1)S(1)}, u32[]{:S(2)}, u32[]{:S(2)}) collective-permute-start(bf16[128,256]{1,0:T(8,128)(2,1)S(1)} %shard_map.96.refs_1_.refs_0_), channel_id=1, source_target_pairs={{0,8},{1,3},{2,10},{3,1},{4,12},{5,7},{6,14},{7,5},{8,0},{9,11},{1... | collective-permute-start | bytes 196616 | tf_op jit(solution)/shard_map/ppermute | solution.py:316
  25.6 0.3 shard_map.97.refs_6_.refs_1_
  25.9 0.3 collective-permute-done.7.refs_5_
  26.2 0.0 copy-start
  26.2 1.9 %shard_map.98 = (f32[512,1024]{1,0:T(8,128)S(1)}, bf16[1,512,1024]{2,1,0:T(8,128)(2,1)S(1)}) custom-call(bf16[1024,2048]{1,0:T(8,128)(2,1)S(1)} %get-tuple-element.30.refs_0_, f32[256,1024]{1,0:T(8,128)S(1)} %get-tuple-element.34.refs_1_, bf16[256,1024]{1,0:T(8,128)(2,1)S(1)} %get-tuple-element.35.refs_3_.refs_2_, bf16[256,256]{1,0:T(8,128)(2,1)S(1)} %copy-done.1, ...), custom_call_target="tpu_custom_call" | custom-call | flops 10000000000 | tf_op jit(solution)/shard_map/pallas_call | solution.py:73
  28.1 1.6 %collective-permute-start.9 = (bf16[512,1024]{1,0:T(8,128)(2,1)S(1)}, bf16[512,1024]{1,0:T(8,128)(2,1)S(1)}, u32[]{:S(2)}, u32[]{:S(2)}) collective-permute-start(bf16[512,1024]{1,0:T(8,128)(2,1)S(1)} %bitcast.6), channel_id=1, source_target_pairs={{0,1},{1,0},{2,3},{3,2},{4,5},{5,4},{6,7},{7,6},{8,9},{9,8},{10,11... | collective-permute-start | bytes 3145736 | tf_op jit(solution)/shard_map/ppermute | solution.py:299
  29.8 0.0 collective-permute-done.10.refs_1_
  29.8 2.1 %collective-permute-start.11 = (bf16[128,256]{1,0:T(8,128)(2,1)S(1)}, bf16[128,256]{1,0:T(8,128)(2,1)S(1)}, u32[]{:S(2)}, u32[]{:S(2)}) collective-permute-start(bf16[128,256]{1,0:T(8,128)(2,1)S(1)} %shard_map.99.refs_1_), channel_id=1, source_target_pairs={{0,16},{1,5},{2,18},{3,7},{4,20},{5,1},{6,22},{7,3},{8,24},{9,13},... | collective-permute-start | bytes 196616 | tf_op jit(solution)/shard_map/ppermute | solution.py:316
  31.9 0.0 copy-done
  31.9 0.1 shard_map.100.refs_2_.refs_0_
  32.0 0.1 collective-permute-done.9.refs_1_
  32.0 0.5 %shard_map.101 = (f32[1024,256]{1,0:T(8,128)S(1)}, bf16[1024,256]{1,0:T(8,128)(2,1)S(1)}) custom-call(f32[512,1024]{1,0:T(8,128)S(1)} %get-tuple-element.54.refs_2_.refs_0_, bf16[512,1024]{1,0:T(8,128)(2,1)S(1)} %collective-permute-done.9.refs_1_, f32[128,256]{1,0:T(8,128)S(1)} %shard_map.100.refs_2_.refs_0_), custom_call_target="tpu_custom_call" | custom-call | flops 1000000000 | tf_op jit(solution)/shard_map/pallas_call | solution.py:73
  32.5 2.5 %collective-permute-done.11.refs_2_ = bf16[128,256]{1,0:T(8,128)(2,1)S(1)} collective-permute-done((bf16[128,256]{1,0:T(8,128)(2,1)S(1)}, bf16[128,256]{1,0:T(8,128)(2,1)S(1)}, u32[]{:S(2)}, u32[]{:S(2)}) %collective-permute-start.11) | collective-permute-done | bytes 65568 | tf_op jit(solution)/shard_map/ppermute | solution.py:316
  35.0 0.1 collective-permute-start.12
  35.1 1.1 %shard_map.103.refs_6_ = f32[256,128]{1,0:T(8,128)} custom-call(bf16[256,256]{1,0:T(8,128)(2,1)S(1)} %copy-done.1, bf16[128,256]{1,0:T(8,128)(2,1)S(1)} %shard_map.102.refs_1_.refs_4_), custom_call_target="tpu_custom_call" | custom-call | flops 8000000000 | tf_op jit(solution)/shard_map/pallas_call | solution.py:73
  36.2 0.2 collective-permute-done.12.refs_5_
  36.4 1.3 %shard_map.104 = bf16[2,1024,256]{2,1,0:T(8,128)(2,1)} custom-call(f32[1024,256]{1,0:T(8,128)S(1)} %get-tuple-element.56.refs_0_, f32[1024,256]{1,0:T(8,128)S(1)} %shard_map.97.refs_6_.refs_1_, bf16[1024,256]{1,0:T(8,128)(2,1)S(1)} %get-tuple-element.57.refs_3_.refs_2_, bf16[1024,256]{1,0:T(8,128)(2,1)S(1)} %shard_map.94.refs_5_.refs_3_, ...), custom_call_target="tpu_custom_call" | custom-call | flops 8000000000 | tf_op jit(solution)/shard_map/pallas_call | solution.py:73
  (5 shorter events, 0.1 us)
Async XLA Ops:
  0.6 4.4 %collective-permute-start = (bf16[2,1024,256]{2,1,0:T(8,128)(2,1)}, bf16[2,1024,256]{2,1,0:T(8,128)(2,1)S(1)}, u32[]{:S(2)}, u32[]{:S(2)}) collective-permute-start(bf16[2,1024,256]{2,1,0:T(8,128)(2,1)} %refs_3_.4), channel_id=1, source_target_pairs={{0,1},{1,0},{2,3},{3,2},{4,5},{5,4},{6,7},{7,6},{8,9},{9,8},{10,11... | collective-permute-start | bytes 3145736 | tf_op jit(solution)/shard_map/ppermute | solution.py:299
  4.0 4.8 %collective-permute-start.2 = (bf16[256,1024]{1,0:T(8,128)(2,1)S(1)}, bf16[256,1024]{1,0:T(8,128)(2,1)S(1)}, u32[]{:S(2)}, u32[]{:S(2)}) collective-permute-start(bf16[256,1024]{1,0:T(8,128)(2,1)S(1)} %bitcast.7), channel_id=1, source_target_pairs={{0,1},{1,0},{2,3},{3,2},{4,5},{5,4},{6,7},{7,6},{8,9},{9,8},{10,11... | collective-permute-start | bytes 1572872 | tf_op jit(solution)/shard_map/ppermute | solution.py:299
  6.7 2.2 %collective-permute-start.1 = (bf16[1024,256]{1,0:T(8,128)(2,1)S(1)}, bf16[1024,256]{1,0:T(8,128)(2,1)S(1)}, u32[]{:S(2)}, u32[]{:S(2)}) collective-permute-start(bf16[1024,256]{1,0:T(8,128)(2,1)S(1)} %get-tuple-element.38.refs_1_), channel_id=1, source_target_pairs={{0,1},{1,0},{2,3},{3,2},{4,5},{5,4},{6,7},{7,6},{8,9},{9,8},{10,11... | collective-permute-start | bytes 1572872 | tf_op jit(solution)/shard_map/ppermute | solution.py:299
  10.9 1.5 %collective-permute-start.3 = (bf16[128,256]{1,0:T(8,128)(2,1)S(1)}, bf16[128,256]{1,0:T(8,128)(2,1)S(1)}, u32[]{:S(2)}, u32[]{:S(2)}) collective-permute-start(bf16[128,256]{1,0:T(8,128)(2,1)S(1)} %bitcast.9), channel_id=1, source_target_pairs={{0,1},{1,0},{2,3},{3,2},{4,5},{5,4},{6,7},{7,6},{8,9},{9,8},{10,11... | collective-permute-start | bytes 196616 | tf_op jit(solution)/shard_map/ppermute | solution.py:299
  12.4 3.4 %collective-permute-start.4 = (bf16[1024,256]{1,0:T(8,128)(2,1)S(1)}, bf16[1024,256]{1,0:T(8,128)(2,1)S(1)}, u32[]{:S(2)}, u32[]{:S(2)}) collective-permute-start(bf16[1024,256]{1,0:T(8,128)(2,1)S(1)} %get-tuple-element.47), channel_id=1, source_target_pairs={{0,1},{1,0},{2,3},{3,2},{4,5},{5,4},{6,7},{7,6},{8,9},{9,8},{10,11... | collective-permute-start | bytes 1572872 | tf_op jit(solution)/shard_map/ppermute | solution.py:299
  12.8 7.3 %copy-start.1 = (bf16[256,256]{1,0:T(8,128)(2,1)S(1)}, bf16[256,256]{1,0:T(8,128)(2,1)}, u32[]{:S(2)}) copy-start(bf16[256,256]{1,0:T(8,128)(2,1)} %refs_0_.7) | copy-start | bytes 393220
  12.8 5.2 %collective-permute-start.6 = (bf16[128,256]{1,0:T(8,128)(2,1)S(1)}, bf16[128,256]{1,0:T(8,128)(2,1)S(1)}, u32[]{:S(2)}, u32[]{:S(2)}) collective-permute-start(bf16[128,256]{1,0:T(8,128)(2,1)S(1)} %get-tuple-element.48.refs_3_.refs_0_), channel_id=1, source_target_pairs={{0,2},{1,9},{2,0},{3,11},{4,6},{5,13},{6,4},{7,15},{8,10},{9,1},{1... | collective-permute-start | bytes 196616 | tf_op jit(solution)/shard_map/ppermute | solution.py:316
  16.6 4.2 %collective-permute-start.5 = (bf16[256,1024]{1,0:T(8,128)(2,1)S(1)}, bf16[256,1024]{1,0:T(8,128)(2,1)S(1)}, u32[]{:S(2)}, u32[]{:S(2)}) collective-permute-start(bf16[256,1024]{1,0:T(8,128)(2,1)S(1)} %bitcast.8), channel_id=1, source_target_pairs={{0,1},{1,0},{2,3},{3,2},{4,5},{5,4},{6,7},{7,6},{8,9},{9,8},{10,11... | collective-permute-start | bytes 1572872 | tf_op jit(solution)/shard_map/ppermute | solution.py:299
  18.0 5.9 %collective-permute-start.8 = (bf16[128,256]{1,0:T(8,128)(2,1)S(1)}, bf16[128,256]{1,0:T(8,128)(2,1)S(1)}, u32[]{:S(2)}, u32[]{:S(2)}) collective-permute-start(bf16[128,256]{1,0:T(8,128)(2,1)S(1)} %shard_map.93.refs_2_.refs_0_), channel_id=1, source_target_pairs={{0,4},{1,17},{2,6},{3,19},{4,0},{5,21},{6,2},{7,23},{8,12},{9,25},... | collective-permute-start | bytes 196616 | tf_op jit(solution)/shard_map/ppermute | solution.py:316
  23.2 3.1 %collective-permute-start.7 = (bf16[512,1024]{1,0:T(8,128)(2,1)S(1)}, bf16[512,1024]{1,0:T(8,128)(2,1)S(1)}, u32[]{:S(2)}, u32[]{:S(2)}) collective-permute-start(bf16[512,1024]{1,0:T(8,128)(2,1)S(1)} %bitcast.5), channel_id=1, source_target_pairs={{0,1},{1,0},{2,3},{3,2},{4,5},{5,4},{6,7},{7,6},{8,9},{9,8},{10,11... | collective-permute-start | bytes 3145736 | tf_op jit(solution)/shard_map/ppermute | solution.py:299
  24.0 5.8 %collective-permute-start.10 = (bf16[128,256]{1,0:T(8,128)(2,1)S(1)}, bf16[128,256]{1,0:T(8,128)(2,1)S(1)}, u32[]{:S(2)}, u32[]{:S(2)}) collective-permute-start(bf16[128,256]{1,0:T(8,128)(2,1)S(1)} %shard_map.96.refs_1_.refs_0_), channel_id=1, source_target_pairs={{0,8},{1,3},{2,10},{3,1},{4,12},{5,7},{6,14},{7,5},{8,0},{9,11},{1... | collective-permute-start | bytes 196616 | tf_op jit(solution)/shard_map/ppermute | solution.py:316
  26.2 5.6 %copy-start = (f32[256,128]{1,0:T(8,128)S(1)}, f32[256,128]{1,0:T(8,128)}, u32[]{:S(2)}) copy-start(f32[256,128]{1,0:T(8,128)} %refs_0_.6) | copy-start | bytes 393220
  28.1 3.9 %collective-permute-start.9 = (bf16[512,1024]{1,0:T(8,128)(2,1)S(1)}, bf16[512,1024]{1,0:T(8,128)(2,1)S(1)}, u32[]{:S(2)}, u32[]{:S(2)}) collective-permute-start(bf16[512,1024]{1,0:T(8,128)(2,1)S(1)} %bitcast.6), channel_id=1, source_target_pairs={{0,1},{1,0},{2,3},{3,2},{4,5},{5,4},{6,7},{7,6},{8,9},{9,8},{10,11... | collective-permute-start | bytes 3145736 | tf_op jit(solution)/shard_map/ppermute | solution.py:299
  29.8 5.2 %collective-permute-start.11 = (bf16[128,256]{1,0:T(8,128)(2,1)S(1)}, bf16[128,256]{1,0:T(8,128)(2,1)S(1)}, u32[]{:S(2)}, u32[]{:S(2)}) collective-permute-start(bf16[128,256]{1,0:T(8,128)(2,1)S(1)} %shard_map.99.refs_1_), channel_id=1, source_target_pairs={{0,16},{1,5},{2,18},{3,7},{4,20},{5,1},{6,22},{7,3},{8,24},{9,13},... | collective-permute-start | bytes 196616 | tf_op jit(solution)/shard_map/ppermute | solution.py:316
  35.0 1.3 %collective-permute-start.12 = (bf16[128,256]{1,0:T(8,128)(2,1)S(1)}, bf16[128,256]{1,0:T(8,128)(2,1)S(1)}, u32[]{:S(2)}, u32[]{:S(2)}) collective-permute-start(bf16[128,256]{1,0:T(8,128)(2,1)S(1)} %shard_map.102.refs_1_.refs_4_), channel_id=1, source_target_pairs={{0,1},{1,0},{2,3},{3,2},{4,5},{5,4},{6,7},{7,6},{8,9},{9,8},{10,11... | collective-permute-start | bytes 196616 | tf_op jit(solution)/shard_map/ppermute | solution.py:299

commit v13 on v11

--- a/solution.py
+++ b/solution.py
@@ -86,7 +86,7 @@
             compiler_params=pltpu.CompilerParams(vmem_limit_bytes=16 * MIB),
         )(*args)
 
-    def lower_rows(left, factor, own_ref, other_ref):
+    def lower_others(left, factor, other_ref):
         for step in peers:
 
             @pl.when(at_core() >= step)
@@ -97,9 +97,14 @@
             def _():
                 other_ref[step - 1] = jnp.zeros_like(other_ref[step - 1])
 
+    def lower_block(left, factor, own_ref):
         for j in range(tiles):
             at = j * tile
             own_ref[:, at : at + tile] = dot(left[:, at:], factor[at:, block(0, at, tile)])
+
+    def lower_rows(left, factor, own_ref, other_ref):
+        lower_others(left, factor, other_ref)
+        lower_block(left, factor, own_ref)
 
     def full_rows(left, factor, own_ref, other_ref):
         for step in peers:
@@ -243,9 +248,13 @@
         full_rows(value.astype(BF), k1, own, other)
 
     def first_response_kernel(d0, e0, tip, pushed, *refs):
-        got, (own, other) = refs[: n_space - 1], refs[n_space - 1 :]
-        left = (e0[...].astype(F32) - total_of(pushed, got)).astype(BF)
-        lower_rows(through_tip(tip[...], left).astype(BF), d0, own, other)
+        got, (left, other) = refs[: n_space - 1], refs[n_space - 1 :]
+        inner = (e0[...].astype(F32) - total_of(pushed, got)).astype(BF)
+        left[...] = through_tip(tip[...], inner).astype(BF)
+        lower_others(left, d0, other)
+
+    def own_response_kernel(d0, left, own):
+        lower_block(left, d0, own)
 
     def first_solve_kernel(d0, value_rows, passed, *refs):
         got, (own, other) = refs[: n_space - 1], refs[n_space - 1 :]
@@ -256,12 +265,10 @@
         inner = dot(tip, right).astype(BF)
         return dot(tip.astype(F32).T.astype(BF), inner)
 
-    def turn_tip_kernel(response, noise_fixed, tip, last_resp, noise_rows):
+    def turn_last_kernel(base, response, noise_fixed, tip, last_base, last_resp, noise_rows):
         noise_rows[...] = noise_fixed[...].T
+        last_base[...] = base[...].T
         last_resp[...] = through_tip(tip[...], response[...]).T.astype(BF)
-
-    def turn_last_kernel(base, out):
-        out[...] = base[...].T
 
     def turn_response_kernel(first, *refs):
         got, out = refs[:-1], refs[-1]
@@ -317,9 +324,7 @@
         pairs = []
         for i in range(n_tm):
             for core in range(n_space):
-                bit = 1 << step
-                if step < steps - 1:
-                    bit = 1 << (step + core * (steps - 1) // n_space) % (steps - 1)
+                bit = 1 << (step + core * steps // n_space) % steps
                 pairs.append((i * n_space + core, (i ^ bit) * n_space + core))
         return lax.ppermute(value, ("tm", "space"), pairs)
 
@@ -420,46 +425,46 @@
         )
         got_solved = send_down(other)
         advance(solved)
-        last_resp, noise_rows = call(
-            turn_tip_kernel,
-            [by_node, shape_of((width, fixed_rows), F32)],
-            [response, noise_fixed, tip_inverse],
-            5,
-            after=sent,
-        )
+        pushed, other = call(
+            response_kernel, [fixed_f32, fixed_others], [k1, response], 5, after=sent
+        )
+        got_pushed = send_down(other)
         base, passed, other = call(
             pass_kernel,
             [flat_f32, flat_f32, flat_others],
             [k1, mask, solved, *got_solved],
             8,
-            after=noise_rows,
+            after=pushed,
         )
         got_passed = send_down(other)
         advance(base)
-        pushed, other = call(
-            response_kernel, [fixed_f32, fixed_others], [k1, response], 5, after=sent
-        )
-        got_pushed = send_down(other)
+        last_base, last_resp, noise_rows = call(
+            turn_last_kernel,
+            [node_f32, by_node, shape_of((width, fixed_rows), F32)],
+            [base, response, noise_fixed, tip_inverse],
+            5,
+            after=sent,
+        )
         solved, other = call(
             first_solve_kernel,
             [flat_f32, flat_others],
             [d0, value_rows, passed, *got_passed],
             8,
-            after=pushed,
+            after=noise_rows,
         )
         got_solved = send_down(other)
         advance(solved)
-        first, other = call(
+        left, other = call(
             first_response_kernel,
-            [fixed_f32, fixed_others],
+            [fixed_bf, fixed_others],
             [d0, e0, tip_inverse, pushed, *got_pushed],
             5,
             after=sent,
         )
         got_first = send_down(other)
-        (first_base,) = call(turn_first_kernel, [node_f32], [solved, *got_solved], 1, after=first)
-        (last_base,) = call(turn_last_kernel, [node_f32], [base], 8, after=first_base)
-        (first_resp,) = call(turn_response_kernel, [by_node], [first, *got_first], 1, after=last_base)
+        (first_base,) = call(turn_first_kernel, [node_f32], [solved, *got_solved], 1, after=left)
+        (first,) = call(own_response_kernel, [fixed_f32], [d0, left], 8, after=first_base)
+        (first_resp,) = call(turn_response_kernel, [by_node], [first, *got_first], 1, after=first)
         while step < steps:
             advance()
         (mixed,) = call(mixed_kernel, [part_bf], [noise_rows, sent, *got], 0.2, after=first_resp)

time: 37.2 us -> 36.1 us (0.970)
  starting transfers between devices: 16 us -> 15.1 us
    ppermute x4, starting transfers between devices: 9.86 us -> 9.05 us  [swap_step(): return lax.ppermute(value, ('tm', 'space'), pairs)]
  transfers between devices with their start and end apart: 15 -> 15, of which waited for: 5 -> 4; matrix products, arithmetic and copies ran while one was open for 0% -> 0% of each run, Pallas kernels for 40% -> 41%
where the time goes in v13:
time: 36.1 us; the launch traced here: 35.9 us
  Pallas kernels  18.3 us (51%)
  starting transfers between devices  15.1 us (42%)
  waiting for transfers between devices  1.67 us (5%)
  between operations  0.83 us (2%)
    pallas_call x21, Pallas kernels, call(): pl.pallas_call(run, in_specs=specs, out_specs=[pl.BlockSpec(memory_space=...  18.3 us
    ppermute x4, starting transfers between devices, swap_step(): return lax.ppermute(value, ('tm', 'space'), pairs)  9.05 us
    ppermute x11, starting transfers between devices, swap(): return lax.ppermute(value, 'space', pairs)  6.04 us
    ppermute x11, waiting for transfers between devices, swap(): return lax.ppermute(value, 'space', pairs)  1.47 us
  transfers between devices with their start and end apart: 15, of which 4 were waited for; matrix products, arithmetic and copies ran while one was open for 0% of the time, Pallas kernels for 41%

profile of v13, /device:TPU:0, one launch (start us, length us, event | category | flops | bytes accessed | tf_op | source)
XLA Modules:
  0.0 35.9 jit_solution(10383869037327625385)
XLA Ops:
  0.6 0.5 %collective-permute-start = (bf16[2,1024,256]{2,1,0:T(8,128)(2,1)}, bf16[2,1024,256]{2,1,0:T(8,128)(2,1)S(1)}, u32[]{:S(2)}, u32[]{:S(2)}) collective-permute-start(bf16[2,1024,256]{2,1,0:T(8,128)(2,1)} %refs_3_.4), channel_id=1, source_target_pairs={{0,1},{1,0},{2,3},{3,2},{4,5},{5,4},{6,7},{7,6},{8,9},{9,8},{10,11... | collective-permute-start | bytes 3145736 | tf_op jit(solution)/shard_map/ppermute | solution.py:312
  1.1 2.8 %shard_map.86 = (bf16[1024,2048]{1,0:T(8,128)(2,1)S(1)}, bf16[1024,2048]{1,0:T(8,128)(2,1)S(1)}, f32[256,1024]{1,0:T(8,128)S(1)}, bf16[1,256,1024]{2,1,0:T(8,128...) custom-call(bf16[2,1024,2048]{2,1,0:T(8,128)(2,1)} %refs_0_.3, bf16[2,256,1024]{2,1,0:T(8,128)(2,1)} %refs_1_.3, ...), custom_call_target="tpu_custom_call" | custom-call | flops 8000000000 | tf_op jit(solution)/shard_map/pallas_call | solution.py:73
  4.0 1.1 %collective-permute-start.2 = (bf16[256,1024]{1,0:T(8,128)(2,1)S(1)}, bf16[256,1024]{1,0:T(8,128)(2,1)S(1)}, u32[]{:S(2)}, u32[]{:S(2)}) collective-permute-start(bf16[256,1024]{1,0:T(8,128)(2,1)S(1)} %bitcast.10), channel_id=1, source_target_pairs={{0,1},{1,0},{2,3},{3,2},{4,5},{5,4},{6,7},{7,6},{8,9},{9,8},{10,11... | collective-permute-start | bytes 1572872 | tf_op jit(solution)/shard_map/ppermute | solution.py:312
  5.1 0.0 collective-permute-done.refs_4_
  5.1 1.6 %shard_map.87 = (f32[1024,256]{1,0:T(8,128)S(1)}, bf16[1024,256]{1,0:T(8,128)(2,1)S(1)}, bf16[1024,2048]{1,0:T(8,128)(2,1)S(1)}, bf16[1024,256]{1,0:T(8,128)(2,1)S(1)}) custom-call(bf16[1024,2048]{1,0:T(8,128)(2,1)S(1)} %get-tuple-element.35.refs_0_, bf16[1024,256]{1,0:T(8,128)(2,1)S(1)} %get-tuple-element.36.refs_1_, bf16[2,1024,2048]{2,1,0:T(8,128)(2,1)} %refs_0_.4, ...), custom_call_target="tpu_custom_call" | custom-call | flops 8000000000 | tf_op jit(solution)/shard_map/pallas_call | solution.py:73
  6.6 0.1 collective-permute-start.1
  6.7 2.0 %shard_map.88 = (f32[256,1024]{1,0:T(8,128)S(1)}, bf16[256,1024]{1,0:T(8,128)(2,1)S(1)}, bf16[1024,2048]{1,0:T(8,128)(2,1)S(1)}) custom-call(bf16[2,1024,2048]{2,1,0:T(8,128)(2,1)} %refs_0_.4, bf16[2,256,1024]{2,1,0:T(8,128)(2,1)} %refs_1_.3, f32[1024,256]{1,0:T(8,128)S(1)} %get-tuple-element.37.refs_2_, ...), custom_call_target="tpu_custom_call", output_to_operand_aliasing={{2}: (3, {})} | custom-call | flops 8000000000 | tf_op jit(solution)/shard_map/pallas_call | solution.py:73
  8.8 0.0 collective-permute-done.2.refs_6_
  8.8 0.0 collective-permute-done.1.refs_5_
  8.8 2.1 %shard_map.89 = (bf16[1024,256]{1,0:T(8,128)(2,1)S(1)}, f32[128,256]{1,0:T(8,128)S(1)}, bf16[1,128,256]{2,1,0:T(8,128)(2,1)S(1)}, bf16[256,1024]{1,0:T(8,128)(2,1)S(1)}) custom-call(bf16[1024,2048]{1,0:T(8,128)(2,1)S(1)} %get-tuple-element.40.refs_0_, bf16[1024,256]{1,0:T(8,128)(2,1)S(1)} %get-tuple-element.43.refs_1_, ...), custom_call_target="tpu_custom_call" | custom-call | flops 8000000000 | tf_op jit(solution)/shard_map/pallas_call | solution.py:73
  10.9 0.6 %collective-permute-start.3 = (bf16[128,256]{1,0:T(8,128)(2,1)S(1)}, bf16[128,256]{1,0:T(8,128)(2,1)S(1)}, u32[]{:S(2)}, u32[]{:S(2)}) collective-permute-start(bf16[128,256]{1,0:T(8,128)(2,1)S(1)} %bitcast.13), channel_id=1, source_target_pairs={{0,1},{1,0},{2,3},{3,2},{4,5},{5,4},{6,7},{7,6},{8,9},{9,8},{10,11... | collective-permute-start | bytes 196616 | tf_op jit(solution)/shard_map/ppermute | solution.py:312
  11.5 0.5 %shard_map.90.refs_3_.refs_1_ = f32[1024,256]{1,0:T(8,128)S(1)} custom-call(bf16[1024,2048]{1,0:T(8,128)(2,1)S(1)} %get-tuple-element.42.refs_0_, bf16[1024,256]{1,0:T(8,128)(2,1)S(1)} %get-tuple-element.48.refs_1_), custom_call_target="tpu_custom_call" | custom-call | flops 8000000000 | tf_op jit(solution)/shard_map/pallas_call | solution.py:73
  12.0 0.4 %collective-permute-done.3.refs_2_ = bf16[128,256]{1,0:T(8,128)(2,1)S(1)} collective-permute-done((bf16[128,256]{1,0:T(8,128)(2,1)S(1)}, bf16[128,256]{1,0:T(8,128)(2,1)S(1)}, u32[]{:S(2)}, u32[]{:S(2)}) %collective-permute-start.3) | collective-permute-done | bytes 65568 | tf_op jit(solution)/shard_map/ppermute | solution.py:312
  12.4 0.4 %collective-permute-start.4 = (bf16[1024,256]{1,0:T(8,128)(2,1)S(1)}, bf16[1024,256]{1,0:T(8,128)(2,1)S(1)}, u32[]{:S(2)}, u32[]{:S(2)}) collective-permute-start(bf16[1024,256]{1,0:T(8,128)(2,1)S(1)} %get-tuple-element.51), channel_id=1, source_target_pairs={{0,1},{1,0},{2,3},{3,2},{4,5},{5,4},{6,7},{7,6},{8,9},{9,8},{10,11... | collective-permute-start | bytes 1572872 | tf_op jit(solution)/shard_map/ppermute | solution.py:312
  12.8 2.9 %collective-permute-start.6 = (bf16[128,256]{1,0:T(8,128)(2,1)S(1)}, bf16[128,256]{1,0:T(8,128)(2,1)S(1)}, u32[]{:S(2)}, u32[]{:S(2)}) collective-permute-start(bf16[128,256]{1,0:T(8,128)(2,1)S(1)} %get-tuple-element.52.refs_3_.refs_0_), channel_id=1, source_target_pairs={{0,2},{1,9},{2,0},{3,11},{4,6},{5,13},{6,4},{7,15},{8,10},{9,1},{1... | collective-permute-start | bytes 196616 | tf_op jit(solution)/shard_map/ppermute | solution.py:329
  15.7 0.0 collective-permute-done.4.refs_2_
  15.7 0.8 %shard_map.92 = (f32[256,1024]{1,0:T(8,128)S(1)}, bf16[1,256,1024]{2,1,0:T(8,128)(2,1)S(1)}) custom-call(bf16[1024,2048]{1,0:T(8,128)(2,1)S(1)} %get-tuple-element.42.refs_0_, f32[1024,256]{1,0:T(8,128)S(1)} %shard_map.90.refs_3_.refs_1_, bf16[1024,256]{1,0:T(8,128)(2,1)S(1)} %collective-permute-done.4.refs_2_, ...), custom_call_target="tpu_custom_call" | custom-call | flops 8000000000 | tf_op jit(solution)/shard_map/pallas_call | solution.py:73
  16.6 1.4 %collective-permute-start.5 = (bf16[256,1024]{1,0:T(8,128)(2,1)S(1)}, bf16[256,1024]{1,0:T(8,128)(2,1)S(1)}, u32[]{:S(2)}, u32[]{:S(2)}) collective-permute-start(bf16[256,1024]{1,0:T(8,128)(2,1)S(1)} %bitcast.11), channel_id=1, source_target_pairs={{0,1},{1,0},{2,3},{3,2},{4,5},{5,4},{6,7},{7,6},{8,9},{9,8},{10,11... | collective-permute-start | bytes 1572872 | tf_op jit(solution)/shard_map/ppermute | solution.py:312
  18.0 0.0 collective-permute-done.6.refs_1_
  18.0 2.1 %collective-permute-start.8 = (bf16[128,256]{1,0:T(8,128)(2,1)S(1)}, bf16[128,256]{1,0:T(8,128)(2,1)S(1)}, u32[]{:S(2)}, u32[]{:S(2)}) collective-permute-start(bf16[128,256]{1,0:T(8,128)(2,1)S(1)} %shard_map.93.refs_2_.refs_0_), channel_id=1, source_target_pairs={{0,4},{1,17},{2,6},{3,19},{4,0},{5,21},{6,2},{7,23},{8,12},{9,25},... | collective-permute-start | bytes 196616 | tf_op jit(solution)/shard_map/ppermute | solution.py:329
  20.1 1.2 %shard_map.94 = (f32[256,1024]{1,0:T(8,128)S(1)}, bf16[1,256,1024]{2,1,0:T(8,128)(2,1)S(1)}) custom-call(bf16[1024,2048]{1,0:T(8,128)(2,1)S(1)} %get-tuple-element.40.refs_0_, bf16[256,1024]{1,0:T(8,128)(2,1)S(1)} %get-tuple-element.55.refs_1_, bf16[128,256]{1,0:T(8,128)(2,1)S(1)} %shard_map.93.refs_2_.refs_0_), custom_call_target="tpu_custom_call" | custom-call | flops 5000000000 | tf_op jit(solution)/shard_map/pallas_call | solution.py:73
  21.4 0.0 collective-permute-done.5.refs_3_
  21.4 0.0 copy-start
  21.4 0.0 copy-start.1
  21.4 1.3 %shard_map.95 = (f32[256,1024]{1,0:T(8,128)S(1)}, f32[256,1024]{1,0:T(8,128)S(1)}, bf16[1,256,1024]{2,1,0:T(8,128)(2,1)S(1)}) custom-call(bf16[1024,2048]{1,0:T(8,128)(2,1)S(1)} %get-tuple-element.40.refs_0_, f32[8,128]{1,0:T(8,128)S(1)} %get-tuple-element.41.refs_1_, f32[256,1024]{1,0:T(8,128)S(1)} %get-tuple-element.53.refs_2_, ...), custom_call_target="tpu_custom_call" | custom-call | flops 8000000000 | tf_op jit(solution)/shard_map/pallas_call | solution.py:73
  22.7 0.8 %collective-permute-start.7 = (bf16[256,1024]{1,0:T(8,128)(2,1)S(1)}, bf16[256,1024]{1,0:T(8,128)(2,1)S(1)}, u32[]{:S(2)}, u32[]{:S(2)}) collective-permute-start(bf16[256,1024]{1,0:T(8,128)(2,1)S(1)} %bitcast.9), channel_id=1, source_target_pairs={{0,1},{1,0},{2,3},{3,2},{4,5},{5,4},{6,7},{7,6},{8,9},{9,8},{10,11... | collective-permute-start | bytes 1572872 | tf_op jit(solution)/shard_map/ppermute | solution.py:312
  23.5 0.1 collective-permute-start.10
  23.6 0.0 collective-permute-done.8.refs_1_
  23.6 1.6 %collective-permute-start.11 = (bf16[128,256]{1,0:T(8,128)(2,1)S(1)}, bf16[128,256]{1,0:T(8,128)(2,1)S(1)}, u32[]{:S(2)}, u32[]{:S(2)}) collective-permute-start(bf16[128,256]{1,0:T(8,128)(2,1)S(1)} %shard_map.96.refs_4_.refs_0_), channel_id=1, source_target_pairs={{0,8},{1,3},{2,10},{3,1},{4,12},{5,7},{6,14},{7,5},{8,0},{9,11},{1... | collective-permute-start | bytes 196616 | tf_op jit(solution)/shard_map/ppermute | solution.py:329
  25.3 0.0 copy-done
  25.3 0.0 copy-done.1
  25.3 0.8 %shard_map.97 = (f32[1024,256]{1,0:T(8,128)S(1)}, bf16[1024,256]{1,0:T(8,128)(2,1)S(1)}, f32[128,256]{1,0:T(8,128)S(1)}) custom-call(f32[256,1024]{1,0:T(8,128)S(1)} %get-tuple-element.59.refs_2_.refs_0_, bf16[256,1024]{1,0:T(8,128)(2,1)S(1)} %get-tuple-element.55.refs_1_, f32[256,128]{1,0:T(8,128)S(1)} %copy-done, bf16[256,256]{1,0:T(8,128)(2,1)S(1)} %copy-done.1, ...), custom_call_target="tpu_custom_call" | custom-call | flops 5000000000 | tf_op jit(solution)/shard_map/pallas_call | solution.py:73
  26.1 0.0 collective-permute-done.7.refs_3_
  26.1 0.9 %shard_map.98 = (f32[256,1024]{1,0:T(8,128)S(1)}, bf16[1,256,1024]{2,1,0:T(8,128)(2,1)S(1)}) custom-call(bf16[1024,2048]{1,0:T(8,128)(2,1)S(1)} %get-tuple-element.35.refs_0_, f32[256,1024]{1,0:T(8,128)S(1)} %get-tuple-element.39.refs_1_, f32[256,1024]{1,0:T(8,128)S(1)} %get-tuple-element.57.refs_2_, bf16[256,1024]{1,0:T(8,128)(2,1)S(1)} %collective-permute-done.7.refs_3_, ...), custom_call_target="tpu_custom_call" | custom-call | flops 8000000000 | tf_op jit(solution)/shard_map/pallas_call | solution.py:73
  27.0 0.8 %collective-permute-start.9 = (bf16[256,1024]{1,0:T(8,128)(2,1)S(1)}, bf16[256,1024]{1,0:T(8,128)(2,1)S(1)}, u32[]{:S(2)}, u32[]{:S(2)}) collective-permute-start(bf16[256,1024]{1,0:T(8,128)(2,1)S(1)} %bitcast.8), channel_id=1, source_target_pairs={{0,1},{1,0},{2,3},{3,2},{4,5},{5,4},{6,7},{7,6},{8,9},{9,8},{10,11... | collective-permute-start | bytes 1572872 | tf_op jit(solution)/shard_map/ppermute | solution.py:312
  27.8 0.2 collective-permute-done.11.refs_1_
  28.0 2.4 %collective-permute-start.13 = (bf16[128,256]{1,0:T(8,128)(2,1)S(1)}, bf16[128,256]{1,0:T(8,128)(2,1)S(1)}, u32[]{:S(2)}, u32[]{:S(2)}) collective-permute-start(bf16[128,256]{1,0:T(8,128)(2,1)S(1)} %shard_map.99.refs_5_.refs_1_), channel_id=1, source_target_pairs={{0,16},{1,5},{2,18},{3,7},{4,20},{5,1},{6,22},{7,3},{8,24},{9,13},... | collective-permute-start | bytes 196616 | tf_op jit(solution)/shard_map/ppermute | solution.py:329
  30.4 0.0 collective-permute-done.10.refs_4_
  30.4 0.7 %shard_map.100 = (bf16[256,1024]{1,0:T(8,128)(2,1)S(1)}, bf16[1,256,1024]{2,1,0:T(8,128)(2,1)S(1)}) custom-call(bf16[1024,2048]{1,0:T(8,128)(2,1)S(1)} %get-tuple-element.35.refs_0_, bf16[256,1024]{1,0:T(8,128)(2,1)S(1)} %get-tuple-element.45.refs_3_.refs_1_, bf16[256,256]{1,0:T(8,128)(2,1)S(1)} %copy-done.1, ...), custom_call_target="tpu_custom_call" | custom-call | flops 5000000000 | tf_op jit(solution)/shard_map/pallas_call | solution.py:73
  31.0 0.1 collective-permute-start.12
  31.1 0.0 collective-permute-done.9.refs_1_
  31.1 0.3 shard_map.101.refs_2_.refs_0_
  31.5 0.5 %shard_map.102.refs_0_.refs_2_ = f32[256,1024]{1,0:T(8,128)S(1)} custom-call(bf16[1024,2048]{1,0:T(8,128)(2,1)S(1)} %get-tuple-element.35.refs_0_, bf16[256,1024]{1,0:T(8,128)(2,1)S(1)} %get-tuple-element.64.refs_2_.refs_1_, f32[1024,256]{1,0:T(8,128)S(1)} %shard_map.101.refs_2_.refs_0_), custom_call_target="tpu_custom_call" | custom-call | flops 8000000000 | tf_op jit(solution)/shard_map/pallas_call | solution.py:73
  32.0 1.0 %collective-permute-done.12.refs_1_ = bf16[256,1024]{1,0:T(8,128)(2,1)S(1)} collective-permute-done((bf16[256,1024]{1,0:T(8,128)(2,1)S(1)}, bf16[256,1024]{1,0:T(8,128)(2,1)S(1)}, u32[]{:S(2)}, u32[]{:S(2)}) %collective-permute-start.12) | collective-permute-done | bytes 524320 | tf_op jit(solution)/shard_map/ppermute | solution.py:312
  33.0 0.2 shard_map.103.refs_3_.refs_2_
  33.2 0.0 collective-permute-done.13.refs_2_
  33.3 0.2 collective-permute-start.14
  33.5 1.1 %shard_map.105.refs_6_ = f32[256,128]{1,0:T(8,128)} custom-call(bf16[256,256]{1,0:T(8,128)(2,1)S(1)} %copy-done.1, bf16[128,256]{1,0:T(8,128)(2,1)S(1)} %shard_map.104.refs_1_.refs_4_), custom_call_target="tpu_custom_call" | custom-call | flops 8000000000 | tf_op jit(solution)/shard_map/pallas_call | solution.py:73
  34.5 0.1 collective-permute-done.14.refs_5_
  34.6 1.3 %shard_map.106 = bf16[2,1024,256]{2,1,0:T(8,128)(2,1)} custom-call(f32[1024,256]{1,0:T(8,128)S(1)} %shard_map.101.refs_2_.refs_0_, f32[1024,256]{1,0:T(8,128)S(1)} %get-tuple-element.65.refs_1_, bf16[1024,256]{1,0:T(8,128)(2,1)S(1)} %shard_map.103.refs_3_.refs_2_, bf16[1024,256]{1,0:T(8,128)(2,1)S(1)} %get-tuple-element.67.refs_3_, ...), custom_call_target="tpu_custom_call" | custom-call | flops 8000000000 | tf_op jit(solution)/shard_map/pallas_call | solution.py:73
  (5 shorter events, 0.1 us)
Async XLA Ops:
  0.6 4.4 %collective-permute-start = (bf16[2,1024,256]{2,1,0:T(8,128)(2,1)}, bf16[2,1024,256]{2,1,0:T(8,128)(2,1)S(1)}, u32[]{:S(2)}, u32[]{:S(2)}) collective-permute-start(bf16[2,1024,256]{2,1,0:T(8,128)(2,1)} %refs_3_.4), channel_id=1, source_target_pairs={{0,1},{1,0},{2,3},{3,2},{4,5},{5,4},{6,7},{7,6},{8,9},{9,8},{10,11... | collective-permute-start | bytes 3145736 | tf_op jit(solution)/shard_map/ppermute | solution.py:312
  4.0 4.8 %collective-permute-start.2 = (bf16[256,1024]{1,0:T(8,128)(2,1)S(1)}, bf16[256,1024]{1,0:T(8,128)(2,1)S(1)}, u32[]{:S(2)}, u32[]{:S(2)}) collective-permute-start(bf16[256,1024]{1,0:T(8,128)(2,1)S(1)} %bitcast.10), channel_id=1, source_target_pairs={{0,1},{1,0},{2,3},{3,2},{4,5},{5,4},{6,7},{7,6},{8,9},{9,8},{10,11... | collective-permute-start | bytes 1572872 | tf_op jit(solution)/shard_map/ppermute | solution.py:312
  6.6 2.2 %collective-permute-start.1 = (bf16[1024,256]{1,0:T(8,128)(2,1)S(1)}, bf16[1024,256]{1,0:T(8,128)(2,1)S(1)}, u32[]{:S(2)}, u32[]{:S(2)}) collective-permute-start(bf16[1024,256]{1,0:T(8,128)(2,1)S(1)} %get-tuple-element.43.refs_1_), channel_id=1, source_target_pairs={{0,1},{1,0},{2,3},{3,2},{4,5},{5,4},{6,7},{7,6},{8,9},{9,8},{10,11... | collective-permute-start | bytes 1572872 | tf_op jit(solution)/shard_map/ppermute | solution.py:312
  10.9 1.5 %collective-permute-start.3 = (bf16[128,256]{1,0:T(8,128)(2,1)S(1)}, bf16[128,256]{1,0:T(8,128)(2,1)S(1)}, u32[]{:S(2)}, u32[]{:S(2)}) collective-permute-start(bf16[128,256]{1,0:T(8,128)(2,1)S(1)} %bitcast.13), channel_id=1, source_target_pairs={{0,1},{1,0},{2,3},{3,2},{4,5},{5,4},{6,7},{7,6},{8,9},{9,8},{10,11... | collective-permute-start | bytes 196616 | tf_op jit(solution)/shard_map/ppermute | solution.py:312
  12.4 3.4 %collective-permute-start.4 = (bf16[1024,256]{1,0:T(8,128)(2,1)S(1)}, bf16[1024,256]{1,0:T(8,128)(2,1)S(1)}, u32[]{:S(2)}, u32[]{:S(2)}) collective-permute-start(bf16[1024,256]{1,0:T(8,128)(2,1)S(1)} %get-tuple-element.51), channel_id=1, source_target_pairs={{0,1},{1,0},{2,3},{3,2},{4,5},{5,4},{6,7},{7,6},{8,9},{9,8},{10,11... | collective-permute-start | bytes 1572872 | tf_op jit(solution)/shard_map/ppermute | solution.py:312
  12.8 5.2 %collective-permute-start.6 = (bf16[128,256]{1,0:T(8,128)(2,1)S(1)}, bf16[128,256]{1,0:T(8,128)(2,1)S(1)}, u32[]{:S(2)}, u32[]{:S(2)}) collective-permute-start(bf16[128,256]{1,0:T(8,128)(2,1)S(1)} %get-tuple-element.52.refs_3_.refs_0_), channel_id=1, source_target_pairs={{0,2},{1,9},{2,0},{3,11},{4,6},{5,13},{6,4},{7,15},{8,10},{9,1},{1... | collective-permute-start | bytes 196616 | tf_op jit(solution)/shard_map/ppermute | solution.py:329
  16.6 4.8 %collective-permute-start.5 = (bf16[256,1024]{1,0:T(8,128)(2,1)S(1)}, bf16[256,1024]{1,0:T(8,128)(2,1)S(1)}, u32[]{:S(2)}, u32[]{:S(2)}) collective-permute-start(bf16[256,1024]{1,0:T(8,128)(2,1)S(1)} %bitcast.11), channel_id=1, source_target_pairs={{0,1},{1,0},{2,3},{3,2},{4,5},{5,4},{6,7},{7,6},{8,9},{9,8},{10,11... | collective-permute-start | bytes 1572872 | tf_op jit(solution)/shard_map/ppermute | solution.py:312
  18.0 5.6 %collective-permute-start.8 = (bf16[128,256]{1,0:T(8,128)(2,1)S(1)}, bf16[128,256]{1,0:T(8,128)(2,1)S(1)}, u32[]{:S(2)}, u32[]{:S(2)}) collective-permute-start(bf16[128,256]{1,0:T(8,128)(2,1)S(1)} %shard_map.93.refs_2_.refs_0_), channel_id=1, source_target_pairs={{0,4},{1,17},{2,6},{3,19},{4,0},{5,21},{6,2},{7,23},{8,12},{9,25},... | collective-permute-start | bytes 196616 | tf_op jit(solution)/shard_map/ppermute | solution.py:329
  21.4 3.9 %copy-start = (f32[256,128]{1,0:T(8,128)S(1)}, f32[256,128]{1,0:T(8,128)}, u32[]{:S(2)}) copy-start(f32[256,128]{1,0:T(8,128)} %refs_2_.6) | copy-start | bytes 393220
  21.4 3.9 %copy-start.1 = (bf16[256,256]{1,0:T(8,128)(2,1)S(1)}, bf16[256,256]{1,0:T(8,128)(2,1)}, u32[]{:S(2)}) copy-start(bf16[256,256]{1,0:T(8,128)(2,1)} %refs_0_.5) | copy-start | bytes 393220
  22.7 3.3 %collective-permute-start.7 = (bf16[256,1024]{1,0:T(8,128)(2,1)S(1)}, bf16[256,1024]{1,0:T(8,128)(2,1)S(1)}, u32[]{:S(2)}, u32[]{:S(2)}) collective-permute-start(bf16[256,1024]{1,0:T(8,128)(2,1)S(1)} %bitcast.9), channel_id=1, source_target_pairs={{0,1},{1,0},{2,3},{3,2},{4,5},{5,4},{6,7},{7,6},{8,9},{9,8},{10,11... | collective-permute-start | bytes 1572872 | tf_op jit(solution)/shard_map/ppermute | solution.py:312
  23.5 6.8 %collective-permute-start.10 = (bf16[256,1024]{1,0:T(8,128)(2,1)S(1)}, bf16[256,1024]{1,0:T(8,128)(2,1)S(1)}, u32[]{:S(2)}, u32[]{:S(2)}) collective-permute-start(bf16[256,1024]{1,0:T(8,128)(2,1)S(1)} %bitcast.7), channel_id=1, source_target_pairs={{0,1},{1,0},{2,3},{3,2},{4,5},{5,4},{6,7},{7,6},{8,9},{9,8},{10,11... | collective-permute-start | bytes 1572872 | tf_op jit(solution)/shard_map/ppermute | solution.py:312
  23.6 4.3 %collective-permute-start.11 = (bf16[128,256]{1,0:T(8,128)(2,1)S(1)}, bf16[128,256]{1,0:T(8,128)(2,1)S(1)}, u32[]{:S(2)}, u32[]{:S(2)}) collective-permute-start(bf16[128,256]{1,0:T(8,128)(2,1)S(1)} %shard_map.96.refs_4_.refs_0_), channel_id=1, source_target_pairs={{0,8},{1,3},{2,10},{3,1},{4,12},{5,7},{6,14},{7,5},{8,0},{9,11},{1... | collective-permute-start | bytes 196616 | tf_op jit(solution)/shard_map/ppermute | solution.py:329
  27.0 4.1 %collective-permute-start.9 = (bf16[256,1024]{1,0:T(8,128)(2,1)S(1)}, bf16[256,1024]{1,0:T(8,128)(2,1)S(1)}, u32[]{:S(2)}, u32[]{:S(2)}) collective-permute-start(bf16[256,1024]{1,0:T(8,128)(2,1)S(1)} %bitcast.8), channel_id=1, source_target_pairs={{0,1},{1,0},{2,3},{3,2},{4,5},{5,4},{6,7},{7,6},{8,9},{9,8},{10,11... | collective-permute-start | bytes 1572872 | tf_op jit(solution)/shard_map/ppermute | solution.py:312
  28.0 5.2 %collective-permute-start.13 = (bf16[128,256]{1,0:T(8,128)(2,1)S(1)}, bf16[128,256]{1,0:T(8,128)(2,1)S(1)}, u32[]{:S(2)}, u32[]{:S(2)}) collective-permute-start(bf16[128,256]{1,0:T(8,128)(2,1)S(1)} %shard_map.99.refs_5_.refs_1_), channel_id=1, source_target_pairs={{0,16},{1,5},{2,18},{3,7},{4,20},{5,1},{6,22},{7,3},{8,24},{9,13},... | collective-permute-start | bytes 196616 | tf_op jit(solution)/shard_map/ppermute | solution.py:329
  31.0 2.0 %collective-permute-start.12 = (bf16[256,1024]{1,0:T(8,128)(2,1)S(1)}, bf16[256,1024]{1,0:T(8,128)(2,1)S(1)}, u32[]{:S(2)}, u32[]{:S(2)}) collective-permute-start(bf16[256,1024]{1,0:T(8,128)(2,1)S(1)} %bitcast.12), channel_id=1, source_target_pairs={{0,1},{1,0},{2,3},{3,2},{4,5},{5,4},{6,7},{7,6},{8,9},{9,8},{10,11... | collective-permute-start | bytes 1572872 | tf_op jit(solution)/shard_map/ppermute | solution.py:312
  33.3 1.3 %collective-permute-start.14 = (bf16[128,256]{1,0:T(8,128)(2,1)S(1)}, bf16[128,256]{1,0:T(8,128)(2,1)S(1)}, u32[]{:S(2)}, u32[]{:S(2)}) collective-permute-start(bf16[128,256]{1,0:T(8,128)(2,1)S(1)} %shard_map.104.refs_1_.refs_4_), channel_id=1, source_target_pairs={{0,1},{1,0},{2,3},{3,2},{4,5},{5,4},{6,7},{7,6},{8,9},{9,8},{10,11... | collective-permute-start | bytes 196616 | tf_op jit(solution)/shard_map/ppermute | solution.py:312

commit v14 on v13

--- a/solution.py
+++ b/solution.py
@@ -222,8 +222,8 @@
     def last_own_kernel(d1, target, value):
         lower_own(d1, target, value)
 
-    def core_sum_kernel(part, _, *refs):
-        got, (out, _) = refs[:-2], refs[-2:]
+    def core_sum_kernel(part, *refs):
+        got, out = refs[:-1], refs[-1]
         total = part[...]
         for piece in got:
             total = total + piece[...].astype(F32)
@@ -390,18 +390,10 @@
             8,
             scratch=[pltpu.VMEM((columns, fixed_rows), F32)],
         )
+        got_target = send_up(target)
         got_parts = send_down(part_other)
         (value,) = call(last_own_kernel, [node_f32], [d1, target], 8)
-        sent, target = call(
-            core_sum_kernel,
-            [part_bf, node_bf],
-            [part_own, target, *got_parts],
-            0.2,
-            {1: pl.ANY, ("out", 1): pl.ANY},
-            aliases={1: 1},
-            after=value,
-        )
-        got_target = send_up(target)
+        (sent,) = call(core_sum_kernel, [part_bf], [part_own, *got_parts], 0.2, after=value)
         step = 0
         got = []
 

time: 36.1 us -> 35.8 us (level)
    ppermute x11, starting transfers between devices: 6.04 us -> 5.65 us  [swap(): return lax.ppermute(value, 'space', pairs)]
  transfers between devices with their start and end apart: 15 -> 15, of which waited for: 4 -> 4; matrix products, arithmetic and copies ran while one was open for 0% -> 0% of each run, Pallas kernels for 41% -> 42%
where the time goes in v14:
time: 35.8 us; the launch traced here: 35.6 us
  Pallas kernels  18.3 us (51%)
  starting transfers between devices  14.8 us (41%)
  waiting for transfers between devices  1.59 us (4%)
  between operations  0.83 us (2%)
    pallas_call x21, Pallas kernels, call(): pl.pallas_call(run, in_specs=specs, out_specs=[pl.BlockSpec(memory_space=...  18.3 us
    ppermute x4, starting transfers between devices, swap_step(): return lax.ppermute(value, ('tm', 'space'), pairs)  9.16 us
    ppermute x11, starting transfers between devices, swap(): return lax.ppermute(value, 'space', pairs)  5.65 us
    ppermute x11, waiting for transfers between devices, swap(): return lax.ppermute(value, 'space', pairs)  1.39 us
  transfers between devices with their start and end apart: 15, of which 4 were waited for; matrix products, arithmetic and copies ran while one was open for 0% of the time, Pallas kernels for 42%

profile of v14, /device:TPU:0, one launch (start us, length us, event | category | flops | bytes accessed | tf_op | source)
XLA Modules:
  0.0 35.6 jit_solution(15917697941031012003)
XLA Ops:
  0.6 0.5 %collective-permute-start = (bf16[2,1024,256]{2,1,0:T(8,128)(2,1)}, bf16[2,1024,256]{2,1,0:T(8,128)(2,1)S(1)}, u32[]{:S(2)}, u32[]{:S(2)}) collective-permute-start(bf16[2,1024,256]{2,1,0:T(8,128)(2,1)} %refs_3_.4), channel_id=1, source_target_pairs={{0,1},{1,0},{2,3},{3,2},{4,5},{5,4},{6,7},{7,6},{8,9},{9,8},{10,11... | collective-permute-start | bytes 3145736 | tf_op jit(solution)/shard_map/ppermute | solution.py:312
  1.1 2.8 %shard_map.86 = (bf16[1024,2048]{1,0:T(8,128)(2,1)S(1)}, bf16[1024,2048]{1,0:T(8,128)(2,1)S(1)}, f32[256,1024]{1,0:T(8,128)S(1)}, bf16[1,256,1024]{2,1,0:T(8,128...) custom-call(bf16[2,1024,2048]{2,1,0:T(8,128)(2,1)} %refs_0_.3, bf16[2,256,1024]{2,1,0:T(8,128)(2,1)} %refs_1_.3, ...), custom_call_target="tpu_custom_call" | custom-call | flops 8000000000 | tf_op jit(solution)/shard_map/pallas_call | solution.py:73
  4.0 1.1 %collective-permute-start.2 = (bf16[256,1024]{1,0:T(8,128)(2,1)S(1)}, bf16[256,1024]{1,0:T(8,128)(2,1)S(1)}, u32[]{:S(2)}, u32[]{:S(2)}) collective-permute-start(bf16[256,1024]{1,0:T(8,128)(2,1)S(1)} %bitcast.10), channel_id=1, source_target_pairs={{0,1},{1,0},{2,3},{3,2},{4,5},{5,4},{6,7},{7,6},{8,9},{9,8},{10,11... | collective-permute-start | bytes 1572872 | tf_op jit(solution)/shard_map/ppermute | solution.py:312
  5.1 0.0 collective-permute-done.refs_4_
  5.1 1.6 %shard_map.87 = (f32[1024,256]{1,0:T(8,128)S(1)}, bf16[1024,256]{1,0:T(8,128)(2,1)S(1)}, bf16[1024,2048]{1,0:T(8,128)(2,1)S(1)}, bf16[1024,256]{1,0:T(8,128)(2,1)S(1)}) custom-call(bf16[1024,2048]{1,0:T(8,128)(2,1)S(1)} %get-tuple-element.33.refs_0_, bf16[1024,256]{1,0:T(8,128)(2,1)S(1)} %get-tuple-element.34.refs_1_, bf16[2,1024,2048]{2,1,0:T(8,128)(2,1)} %refs_0_.4, ...), custom_call_target="tpu_custom_call" | custom-call | flops 8000000000 | tf_op jit(solution)/shard_map/pallas_call | solution.py:73
  6.7 0.1 collective-permute-start.1
  6.7 2.0 %shard_map.88 = (f32[256,1024]{1,0:T(8,128)S(1)}, bf16[256,1024]{1,0:T(8,128)(2,1)S(1)}, bf16[1024,2048]{1,0:T(8,128)(2,1)S(1)}) custom-call(bf16[2,1024,2048]{2,1,0:T(8,128)(2,1)} %refs_0_.4, bf16[2,256,1024]{2,1,0:T(8,128)(2,1)} %refs_1_.3, f32[1024,256]{1,0:T(8,128)S(1)} %get-tuple-element.35.refs_2_, ...), custom_call_target="tpu_custom_call", output_to_operand_aliasing={{2}: (3, {})} | custom-call | flops 8000000000 | tf_op jit(solution)/shard_map/pallas_call | solution.py:73
  8.8 0.0 collective-permute-done.2.refs_6_
  8.8 0.0 collective-permute-done.1.refs_5_
  8.8 2.1 %shard_map.89 = (bf16[1024,256]{1,0:T(8,128)(2,1)S(1)}, f32[128,256]{1,0:T(8,128)S(1)}, bf16[1,128,256]{2,1,0:T(8,128)(2,1)S(1)}, bf16[256,1024]{1,0:T(8,128)(2,1)S(1)}) custom-call(bf16[1024,2048]{1,0:T(8,128)(2,1)S(1)} %get-tuple-element.38.refs_0_, bf16[1024,256]{1,0:T(8,128)(2,1)S(1)} %get-tuple-element.41.refs_1_, ...), custom_call_target="tpu_custom_call" | custom-call | flops 8000000000 | tf_op jit(solution)/shard_map/pallas_call | solution.py:73
  10.9 0.6 %collective-permute-start.4 = (bf16[128,256]{1,0:T(8,128)(2,1)S(1)}, bf16[128,256]{1,0:T(8,128)(2,1)S(1)}, u32[]{:S(2)}, u32[]{:S(2)}) collective-permute-start(bf16[128,256]{1,0:T(8,128)(2,1)S(1)} %bitcast.13), channel_id=1, source_target_pairs={{0,1},{1,0},{2,3},{3,2},{4,5},{5,4},{6,7},{7,6},{8,9},{9,8},{10,11... | collective-permute-start | bytes 196616 | tf_op jit(solution)/shard_map/ppermute | solution.py:312
  11.5 0.1 collective-permute-start.3
  11.6 0.5 %shard_map.90.refs_2_.refs_1_ = f32[1024,256]{1,0:T(8,128)S(1)} custom-call(bf16[1024,2048]{1,0:T(8,128)(2,1)S(1)} %get-tuple-element.40.refs_0_, bf16[1024,256]{1,0:T(8,128)(2,1)S(1)} %get-tuple-element.46.refs_1_), custom_call_target="tpu_custom_call" | custom-call | flops 8000000000 | tf_op jit(solution)/shard_map/pallas_call | solution.py:73
  12.1 0.3 collective-permute-done.4.refs_1_
  12.4 3.0 %collective-permute-start.6 = (bf16[128,256]{1,0:T(8,128)(2,1)S(1)}, bf16[128,256]{1,0:T(8,128)(2,1)S(1)}, u32[]{:S(2)}, u32[]{:S(2)}) collective-permute-start(bf16[128,256]{1,0:T(8,128)(2,1)S(1)} %shard_map.91.refs_3_.refs_0_), channel_id=1, source_target_pairs={{0,2},{1,9},{2,0},{3,11},{4,6},{5,13},{6,4},{7,15},{8,10},{9,1},{1... | collective-permute-start | bytes 196616 | tf_op jit(solution)/shard_map/ppermute | solution.py:329
  15.4 0.0 collective-permute-done.3.refs_2_
  15.4 0.8 %shard_map.92 = (f32[256,1024]{1,0:T(8,128)S(1)}, bf16[1,256,1024]{2,1,0:T(8,128)(2,1)S(1)}) custom-call(bf16[1024,2048]{1,0:T(8,128)(2,1)S(1)} %get-tuple-element.40.refs_0_, f32[1024,256]{1,0:T(8,128)S(1)} %shard_map.90.refs_2_.refs_1_, bf16[1024,256]{1,0:T(8,128)(2,1)S(1)} %collective-permute-done.3.refs_2_, bf16[128,256]{1,0:T(8,128)(2,1)S(1)} %shard_map.91.refs_3_.refs_0_), custom_call_target="tpu_custom_call" | custom-call | flops 8000000000 | tf_op jit(solution)/shard_map/pallas_call | solution.py:73
  16.2 1.6 %collective-permute-start.5 = (bf16[256,1024]{1,0:T(8,128)(2,1)S(1)}, bf16[256,1024]{1,0:T(8,128)(2,1)S(1)}, u32[]{:S(2)}, u32[]{:S(2)}) collective-permute-start(bf16[256,1024]{1,0:T(8,128)(2,1)S(1)} %bitcast.11), channel_id=1, source_target_pairs={{0,1},{1,0},{2,3},{3,2},{4,5},{5,4},{6,7},{7,6},{8,9},{9,8},{10,11... | collective-permute-start | bytes 1572872 | tf_op jit(solution)/shard_map/ppermute | solution.py:312
  17.8 0.0 collective-permute-done.6.refs_1_
  17.9 1.9 %collective-permute-start.8 = (bf16[128,256]{1,0:T(8,128)(2,1)S(1)}, bf16[128,256]{1,0:T(8,128)(2,1)S(1)}, u32[]{:S(2)}, u32[]{:S(2)}) collective-permute-start(bf16[128,256]{1,0:T(8,128)(2,1)S(1)} %shard_map.93.refs_2_.refs_0_), channel_id=1, source_target_pairs={{0,4},{1,17},{2,6},{3,19},{4,0},{5,21},{6,2},{7,23},{8,12},{9,25},... | collective-permute-start | bytes 196616 | tf_op jit(solution)/shard_map/ppermute | solution.py:329
  19.8 1.2 %shard_map.94 = (f32[256,1024]{1,0:T(8,128)S(1)}, bf16[1,256,1024]{2,1,0:T(8,128)(2,1)S(1)}) custom-call(bf16[1024,2048]{1,0:T(8,128)(2,1)S(1)} %get-tuple-element.38.refs_0_, bf16[256,1024]{1,0:T(8,128)(2,1)S(1)} %get-tuple-element.51.refs_1_, bf16[128,256]{1,0:T(8,128)(2,1)S(1)} %shard_map.93.refs_2_.refs_0_), custom_call_target="tpu_custom_call" | custom-call | flops 5000000000 | tf_op jit(solution)/shard_map/pallas_call | solution.py:73
  21.0 0.0 collective-permute-done.5.refs_3_
  21.1 0.0 copy-start
  21.1 0.0 copy-start.1
  21.1 1.3 %shard_map.95 = (f32[256,1024]{1,0:T(8,128)S(1)}, f32[256,1024]{1,0:T(8,128)S(1)}, bf16[1,256,1024]{2,1,0:T(8,128)(2,1)S(1)}) custom-call(bf16[1024,2048]{1,0:T(8,128)(2,1)S(1)} %get-tuple-element.38.refs_0_, f32[8,128]{1,0:T(8,128)S(1)} %get-tuple-element.39.refs_1_, f32[256,1024]{1,0:T(8,128)S(1)} %get-tuple-element.49.refs_2_, ...), custom_call_target="tpu_custom_call" | custom-call | flops 8000000000 | tf_op jit(solution)/shard_map/pallas_call | solution.py:73
  22.4 0.5 %collective-permute-start.7 = (bf16[256,1024]{1,0:T(8,128)(2,1)S(1)}, bf16[256,1024]{1,0:T(8,128)(2,1)S(1)}, u32[]{:S(2)}, u32[]{:S(2)}) collective-permute-start(bf16[256,1024]{1,0:T(8,128)(2,1)S(1)} %bitcast.9), channel_id=1, source_target_pairs={{0,1},{1,0},{2,3},{3,2},{4,5},{5,4},{6,7},{7,6},{8,9},{9,8},{10,11... | collective-permute-start | bytes 1572872 | tf_op jit(solution)/shard_map/ppermute | solution.py:312
  22.9 0.1 collective-permute-start.10
  23.0 0.0 collective-permute-done.8.refs_1_
  23.0 1.6 %collective-permute-start.11 = (bf16[128,256]{1,0:T(8,128)(2,1)S(1)}, bf16[128,256]{1,0:T(8,128)(2,1)S(1)}, u32[]{:S(2)}, u32[]{:S(2)}) collective-permute-start(bf16[128,256]{1,0:T(8,128)(2,1)S(1)} %shard_map.96.refs_4_.refs_0_), channel_id=1, source_target_pairs={{0,8},{1,3},{2,10},{3,1},{4,12},{5,7},{6,14},{7,5},{8,0},{9,11},{1... | collective-permute-start | bytes 196616 | tf_op jit(solution)/shard_map/ppermute | solution.py:329
  24.7 0.0 copy-done
  24.7 0.0 copy-done.1
  24.7 0.8 %shard_map.97 = (f32[1024,256]{1,0:T(8,128)S(1)}, bf16[1024,256]{1,0:T(8,128)(2,1)S(1)}, f32[128,256]{1,0:T(8,128)S(1)}) custom-call(f32[256,1024]{1,0:T(8,128)S(1)} %get-tuple-element.55.refs_2_.refs_0_, bf16[256,1024]{1,0:T(8,128)(2,1)S(1)} %get-tuple-element.51.refs_1_, f32[256,128]{1,0:T(8,128)S(1)} %copy-done, bf16[256,256]{1,0:T(8,128)(2,1)S(1)} %copy-done.1, ...), custom_call_target="tpu_custom_call" | custom-call | flops 5000000000 | tf_op jit(solution)/shard_map/pallas_call | solution.py:73
  25.4 0.0 collective-permute-done.7.refs_3_
  25.5 0.9 %shard_map.98 = (f32[256,1024]{1,0:T(8,128)S(1)}, bf16[1,256,1024]{2,1,0:T(8,128)(2,1)S(1)}) custom-call(bf16[1024,2048]{1,0:T(8,128)(2,1)S(1)} %get-tuple-element.33.refs_0_, f32[256,1024]{1,0:T(8,128)S(1)} %get-tuple-element.37.refs_1_, f32[256,1024]{1,0:T(8,128)S(1)} %get-tuple-element.53.refs_2_, bf16[256,1024]{1,0:T(8,128)(2,1)S(1)} %collective-permute-done.7.refs_3_, ...), custom_call_target="tpu_custom_call" | custom-call | flops 8000000000 | tf_op jit(solution)/shard_map/pallas_call | solution.py:73
  26.3 0.8 %collective-permute-start.9 = (bf16[256,1024]{1,0:T(8,128)(2,1)S(1)}, bf16[256,1024]{1,0:T(8,128)(2,1)S(1)}, u32[]{:S(2)}, u32[]{:S(2)}) collective-permute-start(bf16[256,1024]{1,0:T(8,128)(2,1)S(1)} %bitcast.8), channel_id=1, source_target_pairs={{0,1},{1,0},{2,3},{3,2},{4,5},{5,4},{6,7},{7,6},{8,9},{9,8},{10,11... | collective-permute-start | bytes 1572872 | tf_op jit(solution)/shard_map/ppermute | solution.py:312
  27.2 0.2 collective-permute-done.11.refs_1_
  27.4 2.6 %collective-permute-start.13 = (bf16[128,256]{1,0:T(8,128)(2,1)S(1)}, bf16[128,256]{1,0:T(8,128)(2,1)S(1)}, u32[]{:S(2)}, u32[]{:S(2)}) collective-permute-start(bf16[128,256]{1,0:T(8,128)(2,1)S(1)} %shard_map.99.refs_5_.refs_1_), channel_id=1, source_target_pairs={{0,16},{1,5},{2,18},{3,7},{4,20},{5,1},{6,22},{7,3},{8,24},{9,13},... | collective-permute-start | bytes 196616 | tf_op jit(solution)/shard_map/ppermute | solution.py:329
  30.0 0.0 collective-permute-done.10.refs_4_
  30.0 0.7 %shard_map.100 = (bf16[256,1024]{1,0:T(8,128)(2,1)S(1)}, bf16[1,256,1024]{2,1,0:T(8,128)(2,1)S(1)}) custom-call(bf16[1024,2048]{1,0:T(8,128)(2,1)S(1)} %get-tuple-element.33.refs_0_, bf16[256,1024]{1,0:T(8,128)(2,1)S(1)} %get-tuple-element.43.refs_3_.refs_1_, bf16[256,256]{1,0:T(8,128)(2,1)S(1)} %copy-done.1, ...), custom_call_target="tpu_custom_call" | custom-call | flops 5000000000 | tf_op jit(solution)/shard_map/pallas_call | solution.py:73
  30.7 0.1 collective-permute-start.12
  30.8 0.0 collective-permute-done.9.refs_1_
  30.8 0.3 shard_map.101.refs_2_.refs_0_
  31.1 0.5 %shard_map.102.refs_0_.refs_2_ = f32[256,1024]{1,0:T(8,128)S(1)} custom-call(bf16[1024,2048]{1,0:T(8,128)(2,1)S(1)} %get-tuple-element.33.refs_0_, bf16[256,1024]{1,0:T(8,128)(2,1)S(1)} %get-tuple-element.60.refs_2_.refs_1_, f32[1024,256]{1,0:T(8,128)S(1)} %shard_map.101.refs_2_.refs_0_), custom_call_target="tpu_custom_call" | custom-call | flops 8000000000 | tf_op jit(solution)/shard_map/pallas_call | solution.py:73
  31.7 1.0 %collective-permute-done.12.refs_1_ = bf16[256,1024]{1,0:T(8,128)(2,1)S(1)} collective-permute-done((bf16[256,1024]{1,0:T(8,128)(2,1)S(1)}, bf16[256,1024]{1,0:T(8,128)(2,1)S(1)}, u32[]{:S(2)}, u32[]{:S(2)}) %collective-permute-start.12) | collective-permute-done | bytes 524320 | tf_op jit(solution)/shard_map/ppermute | solution.py:312
  32.7 0.2 shard_map.103.refs_3_.refs_2_
  32.9 0.0 collective-permute-done.13.refs_2_
  32.9 0.2 collective-permute-start.14
  33.1 1.1 %shard_map.105.refs_6_ = f32[256,128]{1,0:T(8,128)} custom-call(bf16[256,256]{1,0:T(8,128)(2,1)S(1)} %copy-done.1, bf16[128,256]{1,0:T(8,128)(2,1)S(1)} %shard_map.104.refs_1_.refs_4_), custom_call_target="tpu_custom_call" | custom-call | flops 8000000000 | tf_op jit(solution)/shard_map/pallas_call | solution.py:73
  34.2 0.1 collective-permute-done.14.refs_5_
  34.3 1.3 %shard_map.106 = bf16[2,1024,256]{2,1,0:T(8,128)(2,1)} custom-call(f32[1024,256]{1,0:T(8,128)S(1)} %shard_map.101.refs_2_.refs_0_, f32[1024,256]{1,0:T(8,128)S(1)} %get-tuple-element.61.refs_1_, bf16[1024,256]{1,0:T(8,128)(2,1)S(1)} %shard_map.103.refs_3_.refs_2_, bf16[1024,256]{1,0:T(8,128)(2,1)S(1)} %get-tuple-element.63.refs_3_, ...), custom_call_target="tpu_custom_call" | custom-call | flops 8000000000 | tf_op jit(solution)/shard_map/pallas_call | solution.py:73
  (5 shorter events, 0.1 us)
Async XLA Ops:
  0.6 4.4 %collective-permute-start = (bf16[2,1024,256]{2,1,0:T(8,128)(2,1)}, bf16[2,1024,256]{2,1,0:T(8,128)(2,1)S(1)}, u32[]{:S(2)}, u32[]{:S(2)}) collective-permute-start(bf16[2,1024,256]{2,1,0:T(8,128)(2,1)} %refs_3_.4), channel_id=1, source_target_pairs={{0,1},{1,0},{2,3},{3,2},{4,5},{5,4},{6,7},{7,6},{8,9},{9,8},{10,11... | collective-permute-start | bytes 3145736 | tf_op jit(solution)/shard_map/ppermute | solution.py:312
  4.0 4.8 %collective-permute-start.2 = (bf16[256,1024]{1,0:T(8,128)(2,1)S(1)}, bf16[256,1024]{1,0:T(8,128)(2,1)S(1)}, u32[]{:S(2)}, u32[]{:S(2)}) collective-permute-start(bf16[256,1024]{1,0:T(8,128)(2,1)S(1)} %bitcast.10), channel_id=1, source_target_pairs={{0,1},{1,0},{2,3},{3,2},{4,5},{5,4},{6,7},{7,6},{8,9},{9,8},{10,11... | collective-permute-start | bytes 1572872 | tf_op jit(solution)/shard_map/ppermute | solution.py:312
  6.7 2.2 %collective-permute-start.1 = (bf16[1024,256]{1,0:T(8,128)(2,1)S(1)}, bf16[1024,256]{1,0:T(8,128)(2,1)S(1)}, u32[]{:S(2)}, u32[]{:S(2)}) collective-permute-start(bf16[1024,256]{1,0:T(8,128)(2,1)S(1)} %get-tuple-element.41.refs_1_), channel_id=1, source_target_pairs={{0,1},{1,0},{2,3},{3,2},{4,5},{5,4},{6,7},{7,6},{8,9},{9,8},{10,11... | collective-permute-start | bytes 1572872 | tf_op jit(solution)/shard_map/ppermute | solution.py:312
  10.9 1.5 %collective-permute-start.4 = (bf16[128,256]{1,0:T(8,128)(2,1)S(1)}, bf16[128,256]{1,0:T(8,128)(2,1)S(1)}, u32[]{:S(2)}, u32[]{:S(2)}) collective-permute-start(bf16[128,256]{1,0:T(8,128)(2,1)S(1)} %bitcast.13), channel_id=1, source_target_pairs={{0,1},{1,0},{2,3},{3,2},{4,5},{5,4},{6,7},{7,6},{8,9},{9,8},{10,11... | collective-permute-start | bytes 196616 | tf_op jit(solution)/shard_map/ppermute | solution.py:312
  11.5 3.9 %collective-permute-start.3 = (bf16[1024,256]{1,0:T(8,128)(2,1)S(1)}, bf16[1024,256]{1,0:T(8,128)(2,1)S(1)}, u32[]{:S(2)}, u32[]{:S(2)}) collective-permute-start(bf16[1024,256]{1,0:T(8,128)(2,1)S(1)} %get-tuple-element.46.refs_1_), channel_id=1, source_target_pairs={{0,1},{1,0},{2,3},{3,2},{4,5},{5,4},{6,7},{7,6},{8,9},{9,8},{10,11... | collective-permute-start | bytes 1572872 | tf_op jit(solution)/shard_map/ppermute | solution.py:312
  12.4 5.4 %collective-permute-start.6 = (bf16[128,256]{1,0:T(8,128)(2,1)S(1)}, bf16[128,256]{1,0:T(8,128)(2,1)S(1)}, u32[]{:S(2)}, u32[]{:S(2)}) collective-permute-start(bf16[128,256]{1,0:T(8,128)(2,1)S(1)} %shard_map.91.refs_3_.refs_0_), channel_id=1, source_target_pairs={{0,2},{1,9},{2,0},{3,11},{4,6},{5,13},{6,4},{7,15},{8,10},{9,1},{1... | collective-permute-start | bytes 196616 | tf_op jit(solution)/shard_map/ppermute | solution.py:329
  16.2 4.8 %collective-permute-start.5 = (bf16[256,1024]{1,0:T(8,128)(2,1)S(1)}, bf16[256,1024]{1,0:T(8,128)(2,1)S(1)}, u32[]{:S(2)}, u32[]{:S(2)}) collective-permute-start(bf16[256,1024]{1,0:T(8,128)(2,1)S(1)} %bitcast.11), channel_id=1, source_target_pairs={{0,1},{1,0},{2,3},{3,2},{4,5},{5,4},{6,7},{7,6},{8,9},{9,8},{10,11... | collective-permute-start | bytes 1572872 | tf_op jit(solution)/shard_map/ppermute | solution.py:312
  17.9 5.2 %collective-permute-start.8 = (bf16[128,256]{1,0:T(8,128)(2,1)S(1)}, bf16[128,256]{1,0:T(8,128)(2,1)S(1)}, u32[]{:S(2)}, u32[]{:S(2)}) collective-permute-start(bf16[128,256]{1,0:T(8,128)(2,1)S(1)} %shard_map.93.refs_2_.refs_0_), channel_id=1, source_target_pairs={{0,4},{1,17},{2,6},{3,19},{4,0},{5,21},{6,2},{7,23},{8,12},{9,25},... | collective-permute-start | bytes 196616 | tf_op jit(solution)/shard_map/ppermute | solution.py:329
  21.1 3.6 %copy-start = (f32[256,128]{1,0:T(8,128)S(1)}, f32[256,128]{1,0:T(8,128)}, u32[]{:S(2)}) copy-start(f32[256,128]{1,0:T(8,128)} %refs_2_.6) | copy-start | bytes 393220
  21.1 3.6 %copy-start.1 = (bf16[256,256]{1,0:T(8,128)(2,1)S(1)}, bf16[256,256]{1,0:T(8,128)(2,1)}, u32[]{:S(2)}) copy-start(bf16[256,256]{1,0:T(8,128)(2,1)} %refs_0_.5) | copy-start | bytes 393220
  22.4 3.0 %collective-permute-start.7 = (bf16[256,1024]{1,0:T(8,128)(2,1)S(1)}, bf16[256,1024]{1,0:T(8,128)(2,1)S(1)}, u32[]{:S(2)}, u32[]{:S(2)}) collective-permute-start(bf16[256,1024]{1,0:T(8,128)(2,1)S(1)} %bitcast.9), channel_id=1, source_target_pairs={{0,1},{1,0},{2,3},{3,2},{4,5},{5,4},{6,7},{7,6},{8,9},{9,8},{10,11... | collective-permute-start | bytes 1572872 | tf_op jit(solution)/shard_map/ppermute | solution.py:312
  22.9 7.1 %collective-permute-start.10 = (bf16[256,1024]{1,0:T(8,128)(2,1)S(1)}, bf16[256,1024]{1,0:T(8,128)(2,1)S(1)}, u32[]{:S(2)}, u32[]{:S(2)}) collective-permute-start(bf16[256,1024]{1,0:T(8,128)(2,1)S(1)} %bitcast.7), channel_id=1, source_target_pairs={{0,1},{1,0},{2,3},{3,2},{4,5},{5,4},{6,7},{7,6},{8,9},{9,8},{10,11... | collective-permute-start | bytes 1572872 | tf_op jit(solution)/shard_map/ppermute | solution.py:312
  23.0 4.3 %collective-permute-start.11 = (bf16[128,256]{1,0:T(8,128)(2,1)S(1)}, bf16[128,256]{1,0:T(8,128)(2,1)S(1)}, u32[]{:S(2)}, u32[]{:S(2)}) collective-permute-start(bf16[128,256]{1,0:T(8,128)(2,1)S(1)} %shard_map.96.refs_4_.refs_0_), channel_id=1, source_target_pairs={{0,8},{1,3},{2,10},{3,1},{4,12},{5,7},{6,14},{7,5},{8,0},{9,11},{1... | collective-permute-start | bytes 196616 | tf_op jit(solution)/shard_map/ppermute | solution.py:329
  26.3 4.4 %collective-permute-start.9 = (bf16[256,1024]{1,0:T(8,128)(2,1)S(1)}, bf16[256,1024]{1,0:T(8,128)(2,1)S(1)}, u32[]{:S(2)}, u32[]{:S(2)}) collective-permute-start(bf16[256,1024]{1,0:T(8,128)(2,1)S(1)} %bitcast.8), channel_id=1, source_target_pairs={{0,1},{1,0},{2,3},{3,2},{4,5},{5,4},{6,7},{7,6},{8,9},{9,8},{10,11... | collective-permute-start | bytes 1572872 | tf_op jit(solution)/shard_map/ppermute | solution.py:312
  27.4 5.5 %collective-permute-start.13 = (bf16[128,256]{1,0:T(8,128)(2,1)S(1)}, bf16[128,256]{1,0:T(8,128)(2,1)S(1)}, u32[]{:S(2)}, u32[]{:S(2)}) collective-permute-start(bf16[128,256]{1,0:T(8,128)(2,1)S(1)} %shard_map.99.refs_5_.refs_1_), channel_id=1, source_target_pairs={{0,16},{1,5},{2,18},{3,7},{4,20},{5,1},{6,22},{7,3},{8,24},{9,13},... | collective-permute-start | bytes 196616 | tf_op jit(solution)/shard_map/ppermute | solution.py:329
  30.7 2.0 %collective-permute-start.12 = (bf16[256,1024]{1,0:T(8,128)(2,1)S(1)}, bf16[256,1024]{1,0:T(8,128)(2,1)S(1)}, u32[]{:S(2)}, u32[]{:S(2)}) collective-permute-start(bf16[256,1024]{1,0:T(8,128)(2,1)S(1)} %bitcast.12), channel_id=1, source_target_pairs={{0,1},{1,0},{2,3},{3,2},{4,5},{5,4},{6,7},{7,6},{8,9},{9,8},{10,11... | collective-permute-start | bytes 1572872 | tf_op jit(solution)/shard_map/ppermute | solution.py:312
  32.9 1.3 %collective-permute-start.14 = (bf16[128,256]{1,0:T(8,128)(2,1)S(1)}, bf16[128,256]{1,0:T(8,128)(2,1)S(1)}, u32[]{:S(2)}, u32[]{:S(2)}) collective-permute-start(bf16[128,256]{1,0:T(8,128)(2,1)S(1)} %shard_map.104.refs_1_.refs_4_), channel_id=1, source_target_pairs={{0,1},{1,0},{2,3},{3,2},{4,5},{5,4},{6,7},{7,6},{8,9},{9,8},{10,11... | collective-permute-start | bytes 196616 | tf_op jit(solution)/shard_map/ppermute | solution.py:312

commit v15 on v14

--- a/solution.py
+++ b/solution.py
@@ -324,7 +324,9 @@
         pairs = []
         for i in range(n_tm):
             for core in range(n_space):
-                bit = 1 << (step + core * steps // n_space) % steps
+                bit = 1 << step
+                if step < steps - 1:
+                    bit = 1 << (step + core * (steps - 1) // n_space) % (steps - 1)
                 pairs.append((i * n_space + core, (i ^ bit) * n_space + core))
         return lax.ppermute(value, ("tm", "space"), pairs)
 

time: 35.8 us -> 35.8 us (level)
  starting transfers between devices: 14.8 us -> 14.4 us
  waiting for transfers between devices: 1.59 us -> 1.95 us
    ppermute x11, starting transfers between devices: 5.65 us -> 5.17 us  [swap(): return lax.ppermute(value, 'space', pairs)]
    ppermute x4, waiting for transfers between devices: 0.2 us -> 0.56 us  [swap_step(): return lax.ppermute(value, ('tm', 'space'), pairs)]
where the time goes in v15:
time: 35.8 us; the launch traced here: 35.6 us
  Pallas kernels  18.3 us (51%)
  starting transfers between devices  14.4 us (40%)
  waiting for transfers between devices  1.95 us (5%)
  between operations  0.84 us (2%)
    pallas_call x21, Pallas kernels, call(): pl.pallas_call(run, in_specs=specs, out_specs=[pl.BlockSpec(memory_space=...  18.3 us
    ppermute x4, starting transfers between devices, swap_step(): return lax.ppermute(value, ('tm', 'space'), pairs)  9.28 us
    ppermute x11, starting transfers between devices, swap(): return lax.ppermute(value, 'space', pairs)  5.17 us
    ppermute x11, waiting for transfers between devices, swap(): return lax.ppermute(value, 'space', pairs)  1.39 us
  transfers between devices with their start and end apart: 15, of which 4 were waited for; matrix products, arithmetic and copies ran while one was open for 0% of the time, Pallas kernels for 42%

profile of v15, /device:TPU:0, one launch (start us, length us, event | category | flops | bytes accessed | tf_op | source)
XLA Modules:
  0.0 35.6 jit_solution(13467391180621394660)
XLA Ops:
  0.6 0.5 %collective-permute-start = (bf16[2,1024,256]{2,1,0:T(8,128)(2,1)}, bf16[2,1024,256]{2,1,0:T(8,128)(2,1)S(1)}, u32[]{:S(2)}, u32[]{:S(2)}) collective-permute-start(bf16[2,1024,256]{2,1,0:T(8,128)(2,1)} %refs_3_.4), channel_id=1, source_target_pairs={{0,1},{1,0},{2,3},{3,2},{4,5},{5,4},{6,7},{7,6},{8,9},{9,8},{10,11... | collective-permute-start | bytes 3145736 | tf_op jit(solution)/shard_map/ppermute | solution.py:312
  1.1 2.8 %shard_map.86 = (bf16[1024,2048]{1,0:T(8,128)(2,1)S(1)}, bf16[1024,2048]{1,0:T(8,128)(2,1)S(1)}, f32[256,1024]{1,0:T(8,128)S(1)}, bf16[1,256,1024]{2,1,0:T(8,128...) custom-call(bf16[2,1024,2048]{2,1,0:T(8,128)(2,1)} %refs_0_.3, bf16[2,256,1024]{2,1,0:T(8,128)(2,1)} %refs_1_.3, ...), custom_call_target="tpu_custom_call" | custom-call | flops 8000000000 | tf_op jit(solution)/shard_map/pallas_call | solution.py:73
  4.0 1.1 %collective-permute-start.2 = (bf16[256,1024]{1,0:T(8,128)(2,1)S(1)}, bf16[256,1024]{1,0:T(8,128)(2,1)S(1)}, u32[]{:S(2)}, u32[]{:S(2)}) collective-permute-start(bf16[256,1024]{1,0:T(8,128)(2,1)S(1)} %bitcast.10), channel_id=1, source_target_pairs={{0,1},{1,0},{2,3},{3,2},{4,5},{5,4},{6,7},{7,6},{8,9},{9,8},{10,11... | collective-permute-start | bytes 1572872 | tf_op jit(solution)/shard_map/ppermute | solution.py:312
  5.1 0.0 collective-permute-done.refs_4_
  5.1 1.6 %shard_map.87 = (f32[1024,256]{1,0:T(8,128)S(1)}, bf16[1024,256]{1,0:T(8,128)(2,1)S(1)}, bf16[1024,2048]{1,0:T(8,128)(2,1)S(1)}, bf16[1024,256]{1,0:T(8,128)(2,1)S(1)}) custom-call(bf16[1024,2048]{1,0:T(8,128)(2,1)S(1)} %get-tuple-element.33.refs_0_, bf16[1024,256]{1,0:T(8,128)(2,1)S(1)} %get-tuple-element.34.refs_1_, bf16[2,1024,2048]{2,1,0:T(8,128)(2,1)} %refs_0_.4, ...), custom_call_target="tpu_custom_call" | custom-call | flops 8000000000 | tf_op jit(solution)/shard_map/pallas_call | solution.py:73
  6.7 0.1 collective-permute-start.1
  6.7 2.0 %shard_map.88 = (f32[256,1024]{1,0:T(8,128)S(1)}, bf16[256,1024]{1,0:T(8,128)(2,1)S(1)}, bf16[1024,2048]{1,0:T(8,128)(2,1)S(1)}) custom-call(bf16[2,1024,2048]{2,1,0:T(8,128)(2,1)} %refs_0_.4, bf16[2,256,1024]{2,1,0:T(8,128)(2,1)} %refs_1_.3, f32[1024,256]{1,0:T(8,128)S(1)} %get-tuple-element.35.refs_2_, ...), custom_call_target="tpu_custom_call", output_to_operand_aliasing={{2}: (3, {})} | custom-call | flops 8000000000 | tf_op jit(solution)/shard_map/pallas_call | solution.py:73
  8.8 0.0 collective-permute-done.2.refs_6_
  8.8 0.0 collective-permute-done.1.refs_5_
  8.8 2.1 %shard_map.89 = (bf16[1024,256]{1,0:T(8,128)(2,1)S(1)}, f32[128,256]{1,0:T(8,128)S(1)}, bf16[1,128,256]{2,1,0:T(8,128)(2,1)S(1)}, bf16[256,1024]{1,0:T(8,128)(2,1)S(1)}) custom-call(bf16[1024,2048]{1,0:T(8,128)(2,1)S(1)} %get-tuple-element.38.refs_0_, bf16[1024,256]{1,0:T(8,128)(2,1)S(1)} %get-tuple-element.41.refs_1_, ...), custom_call_target="tpu_custom_call" | custom-call | flops 8000000000 | tf_op jit(solution)/shard_map/pallas_call | solution.py:73
  10.9 0.6 %collective-permute-start.4 = (bf16[128,256]{1,0:T(8,128)(2,1)S(1)}, bf16[128,256]{1,0:T(8,128)(2,1)S(1)}, u32[]{:S(2)}, u32[]{:S(2)}) collective-permute-start(bf16[128,256]{1,0:T(8,128)(2,1)S(1)} %bitcast.13), channel_id=1, source_target_pairs={{0,1},{1,0},{2,3},{3,2},{4,5},{5,4},{6,7},{7,6},{8,9},{9,8},{10,11... | collective-permute-start | bytes 196616 | tf_op jit(solution)/shard_map/ppermute | solution.py:312
  11.5 0.1 collective-permute-start.3
  11.6 0.5 %shard_map.90.refs_2_.refs_1_ = f32[1024,256]{1,0:T(8,128)S(1)} custom-call(bf16[1024,2048]{1,0:T(8,128)(2,1)S(1)} %get-tuple-element.40.refs_0_, bf16[1024,256]{1,0:T(8,128)(2,1)S(1)} %get-tuple-element.46.refs_1_), custom_call_target="tpu_custom_call" | custom-call | flops 8000000000 | tf_op jit(solution)/shard_map/pallas_call | solution.py:73
  12.1 0.3 collective-permute-done.4.refs_1_
  12.4 3.0 %collective-permute-start.6 = (bf16[128,256]{1,0:T(8,128)(2,1)S(1)}, bf16[128,256]{1,0:T(8,128)(2,1)S(1)}, u32[]{:S(2)}, u32[]{:S(2)}) collective-permute-start(bf16[128,256]{1,0:T(8,128)(2,1)S(1)} %shard_map.91.refs_3_.refs_0_), channel_id=1, source_target_pairs={{0,2},{1,5},{2,0},{3,7},{4,6},{5,1},{6,4},{7,3},{8,10},{9,13},{10,... | collective-permute-start | bytes 196616 | tf_op jit(solution)/shard_map/ppermute | solution.py:331
  15.4 0.0 collective-permute-done.3.refs_2_
  15.4 0.8 %shard_map.92 = (f32[256,1024]{1,0:T(8,128)S(1)}, bf16[1,256,1024]{2,1,0:T(8,128)(2,1)S(1)}) custom-call(bf16[1024,2048]{1,0:T(8,128)(2,1)S(1)} %get-tuple-element.40.refs_0_, f32[1024,256]{1,0:T(8,128)S(1)} %shard_map.90.refs_2_.refs_1_, bf16[1024,256]{1,0:T(8,128)(2,1)S(1)} %collective-permute-done.3.refs_2_, bf16[128,256]{1,0:T(8,128)(2,1)S(1)} %shard_map.91.refs_3_.refs_0_), custom_call_target="tpu_custom_call" | custom-call | flops 8000000000 | tf_op jit(solution)/shard_map/pallas_call | solution.py:73
  16.2 1.6 %collective-permute-start.5 = (bf16[256,1024]{1,0:T(8,128)(2,1)S(1)}, bf16[256,1024]{1,0:T(8,128)(2,1)S(1)}, u32[]{:S(2)}, u32[]{:S(2)}) collective-permute-start(bf16[256,1024]{1,0:T(8,128)(2,1)S(1)} %bitcast.11), channel_id=1, source_target_pairs={{0,1},{1,0},{2,3},{3,2},{4,5},{5,4},{6,7},{7,6},{8,9},{9,8},{10,11... | collective-permute-start | bytes 1572872 | tf_op jit(solution)/shard_map/ppermute | solution.py:312
  17.8 0.0 collective-permute-done.6.refs_1_
  17.8 2.0 %collective-permute-start.8 = (bf16[128,256]{1,0:T(8,128)(2,1)S(1)}, bf16[128,256]{1,0:T(8,128)(2,1)S(1)}, u32[]{:S(2)}, u32[]{:S(2)}) collective-permute-start(bf16[128,256]{1,0:T(8,128)(2,1)S(1)} %shard_map.93.refs_2_.refs_0_), channel_id=1, source_target_pairs={{0,4},{1,9},{2,6},{3,11},{4,0},{5,13},{6,2},{7,15},{8,12},{9,1},{1... | collective-permute-start | bytes 196616 | tf_op jit(solution)/shard_map/ppermute | solution.py:331
  19.8 1.2 %shard_map.94 = (f32[256,1024]{1,0:T(8,128)S(1)}, bf16[1,256,1024]{2,1,0:T(8,128)(2,1)S(1)}) custom-call(bf16[1024,2048]{1,0:T(8,128)(2,1)S(1)} %get-tuple-element.38.refs_0_, bf16[256,1024]{1,0:T(8,128)(2,1)S(1)} %get-tuple-element.51.refs_1_, bf16[128,256]{1,0:T(8,128)(2,1)S(1)} %shard_map.93.refs_2_.refs_0_), custom_call_target="tpu_custom_call" | custom-call | flops 5000000000 | tf_op jit(solution)/shard_map/pallas_call | solution.py:73
  21.0 0.0 collective-permute-done.5.refs_3_
  21.1 0.0 copy-start
  21.1 0.0 copy-start.1
  21.1 1.3 %shard_map.95 = (f32[256,1024]{1,0:T(8,128)S(1)}, f32[256,1024]{1,0:T(8,128)S(1)}, bf16[1,256,1024]{2,1,0:T(8,128)(2,1)S(1)}) custom-call(bf16[1024,2048]{1,0:T(8,128)(2,1)S(1)} %get-tuple-element.38.refs_0_, f32[8,128]{1,0:T(8,128)S(1)} %get-tuple-element.39.refs_1_, f32[256,1024]{1,0:T(8,128)S(1)} %get-tuple-element.49.refs_2_, ...), custom_call_target="tpu_custom_call" | custom-call | flops 8000000000 | tf_op jit(solution)/shard_map/pallas_call | solution.py:73
  22.4 0.1 collective-permute-start.7
  22.5 0.5 %collective-permute-start.10 = (bf16[256,1024]{1,0:T(8,128)(2,1)S(1)}, bf16[256,1024]{1,0:T(8,128)(2,1)S(1)}, u32[]{:S(2)}, u32[]{:S(2)}) collective-permute-start(bf16[256,1024]{1,0:T(8,128)(2,1)S(1)} %bitcast.7), channel_id=1, source_target_pairs={{0,1},{1,0},{2,3},{3,2},{4,5},{5,4},{6,7},{7,6},{8,9},{9,8},{10,11... | collective-permute-start | bytes 1572872 | tf_op jit(solution)/shard_map/ppermute | solution.py:312
  23.0 0.0 collective-permute-done.8.refs_1_
  23.0 1.6 %collective-permute-start.11 = (bf16[128,256]{1,0:T(8,128)(2,1)S(1)}, bf16[128,256]{1,0:T(8,128)(2,1)S(1)}, u32[]{:S(2)}, u32[]{:S(2)}) collective-permute-start(bf16[128,256]{1,0:T(8,128)(2,1)S(1)} %shard_map.96.refs_4_.refs_0_), channel_id=1, source_target_pairs={{0,8},{1,3},{2,10},{3,1},{4,12},{5,7},{6,14},{7,5},{8,0},{9,11},{1... | collective-permute-start | bytes 196616 | tf_op jit(solution)/shard_map/ppermute | solution.py:331
  24.7 0.0 copy-done
  24.7 0.0 copy-done.1
  24.7 0.8 %shard_map.97 = (f32[1024,256]{1,0:T(8,128)S(1)}, bf16[1024,256]{1,0:T(8,128)(2,1)S(1)}, f32[128,256]{1,0:T(8,128)S(1)}) custom-call(f32[256,1024]{1,0:T(8,128)S(1)} %get-tuple-element.55.refs_2_.refs_0_, bf16[256,1024]{1,0:T(8,128)(2,1)S(1)} %get-tuple-element.51.refs_1_, f32[256,128]{1,0:T(8,128)S(1)} %copy-done, bf16[256,256]{1,0:T(8,128)(2,1)S(1)} %copy-done.1, ...), custom_call_target="tpu_custom_call" | custom-call | flops 5000000000 | tf_op jit(solution)/shard_map/pallas_call | solution.py:73
  25.4 0.0 collective-permute-done.7.refs_3_
  25.5 0.9 %shard_map.98 = (f32[256,1024]{1,0:T(8,128)S(1)}, bf16[1,256,1024]{2,1,0:T(8,128)(2,1)S(1)}) custom-call(bf16[1024,2048]{1,0:T(8,128)(2,1)S(1)} %get-tuple-element.33.refs_0_, f32[256,1024]{1,0:T(8,128)S(1)} %get-tuple-element.37.refs_1_, f32[256,1024]{1,0:T(8,128)S(1)} %get-tuple-element.53.refs_2_, bf16[256,1024]{1,0:T(8,128)(2,1)S(1)} %collective-permute-done.7.refs_3_, ...), custom_call_target="tpu_custom_call" | custom-call | flops 8000000000 | tf_op jit(solution)/shard_map/pallas_call | solution.py:73
  26.3 0.4 %collective-permute-start.9 = (bf16[256,1024]{1,0:T(8,128)(2,1)S(1)}, bf16[256,1024]{1,0:T(8,128)(2,1)S(1)}, u32[]{:S(2)}, u32[]{:S(2)}) collective-permute-start(bf16[256,1024]{1,0:T(8,128)(2,1)S(1)} %bitcast.8), channel_id=1, source_target_pairs={{0,1},{1,0},{2,3},{3,2},{4,5},{5,4},{6,7},{7,6},{8,9},{9,8},{10,11... | collective-permute-start | bytes 1572872 | tf_op jit(solution)/shard_map/ppermute | solution.py:312
  26.8 0.6 %collective-permute-done.11.refs_1_ = bf16[128,256]{1,0:T(8,128)(2,1)S(1)} collective-permute-done((bf16[128,256]{1,0:T(8,128)(2,1)S(1)}, bf16[128,256]{1,0:T(8,128)(2,1)S(1)}, u32[]{:S(2)}, u32[]{:S(2)}) %collective-permute-start.11) | collective-permute-done | bytes 65568 | tf_op jit(solution)/shard_map/ppermute | solution.py:331
  27.4 2.6 %collective-permute-start.13 = (bf16[128,256]{1,0:T(8,128)(2,1)S(1)}, bf16[128,256]{1,0:T(8,128)(2,1)S(1)}, u32[]{:S(2)}, u32[]{:S(2)}) collective-permute-start(bf16[128,256]{1,0:T(8,128)(2,1)S(1)} %shard_map.99.refs_5_.refs_1_), channel_id=1, source_target_pairs={{0,16},{1,17},{2,18},{3,19},{4,20},{5,21},{6,22},{7,23},{8,24},{9,... | collective-permute-start | bytes 196616 | tf_op jit(solution)/shard_map/ppermute | solution.py:331
  30.0 0.0 collective-permute-done.10.refs_4_
  30.0 0.7 %shard_map.100 = (bf16[256,1024]{1,0:T(8,128)(2,1)S(1)}, bf16[1,256,1024]{2,1,0:T(8,128)(2,1)S(1)}) custom-call(bf16[1024,2048]{1,0:T(8,128)(2,1)S(1)} %get-tuple-element.33.refs_0_, bf16[256,1024]{1,0:T(8,128)(2,1)S(1)} %get-tuple-element.43.refs_3_.refs_1_, bf16[256,256]{1,0:T(8,128)(2,1)S(1)} %copy-done.1, ...), custom_call_target="tpu_custom_call" | custom-call | flops 5000000000 | tf_op jit(solution)/shard_map/pallas_call | solution.py:73
  30.7 0.1 collective-permute-start.12
  30.8 0.0 collective-permute-done.9.refs_1_
  30.8 0.3 shard_map.101.refs_2_.refs_0_
  31.1 0.5 %shard_map.102.refs_0_.refs_2_ = f32[256,1024]{1,0:T(8,128)S(1)} custom-call(bf16[1024,2048]{1,0:T(8,128)(2,1)S(1)} %get-tuple-element.33.refs_0_, bf16[256,1024]{1,0:T(8,128)(2,1)S(1)} %get-tuple-element.60.refs_2_.refs_1_, f32[1024,256]{1,0:T(8,128)S(1)} %shard_map.101.refs_2_.refs_0_), custom_call_target="tpu_custom_call" | custom-call | flops 8000000000 | tf_op jit(solution)/shard_map/pallas_call | solution.py:73
  31.7 1.0 %collective-permute-done.12.refs_1_ = bf16[256,1024]{1,0:T(8,128)(2,1)S(1)} collective-permute-done((bf16[256,1024]{1,0:T(8,128)(2,1)S(1)}, bf16[256,1024]{1,0:T(8,128)(2,1)S(1)}, u32[]{:S(2)}, u32[]{:S(2)}) %collective-permute-start.12) | collective-permute-done | bytes 524320 | tf_op jit(solution)/shard_map/ppermute | solution.py:312
  32.7 0.2 shard_map.103.refs_3_.refs_2_
  32.9 0.0 collective-permute-done.13.refs_2_
  32.9 0.2 collective-permute-start.14
  33.1 1.1 %shard_map.105.refs_6_ = f32[256,128]{1,0:T(8,128)} custom-call(bf16[256,256]{1,0:T(8,128)(2,1)S(1)} %copy-done.1, bf16[128,256]{1,0:T(8,128)(2,1)S(1)} %shard_map.104.refs_1_.refs_4_), custom_call_target="tpu_custom_call" | custom-call | flops 8000000000 | tf_op jit(solution)/shard_map/pallas_call | solution.py:73
  34.2 0.1 collective-permute-done.14.refs_5_
  34.3 1.3 %shard_map.106 = bf16[2,1024,256]{2,1,0:T(8,128)(2,1)} custom-call(f32[1024,256]{1,0:T(8,128)S(1)} %shard_map.101.refs_2_.refs_0_, f32[1024,256]{1,0:T(8,128)S(1)} %get-tuple-element.61.refs_1_, bf16[1024,256]{1,0:T(8,128)(2,1)S(1)} %shard_map.103.refs_3_.refs_2_, bf16[1024,256]{1,0:T(8,128)(2,1)S(1)} %get-tuple-element.63.refs_3_, ...), custom_call_target="tpu_custom_call" | custom-call | flops 8000000000 | tf_op jit(solution)/shard_map/pallas_call | solution.py:73
  (5 shorter events, 0.1 us)
Async XLA Ops:
  0.6 4.4 %collective-permute-start = (bf16[2,1024,256]{2,1,0:T(8,128)(2,1)}, bf16[2,1024,256]{2,1,0:T(8,128)(2,1)S(1)}, u32[]{:S(2)}, u32[]{:S(2)}) collective-permute-start(bf16[2,1024,256]{2,1,0:T(8,128)(2,1)} %refs_3_.4), channel_id=1, source_target_pairs={{0,1},{1,0},{2,3},{3,2},{4,5},{5,4},{6,7},{7,6},{8,9},{9,8},{10,11... | collective-permute-start | bytes 3145736 | tf_op jit(solution)/shard_map/ppermute | solution.py:312
  4.0 4.8 %collective-permute-start.2 = (bf16[256,1024]{1,0:T(8,128)(2,1)S(1)}, bf16[256,1024]{1,0:T(8,128)(2,1)S(1)}, u32[]{:S(2)}, u32[]{:S(2)}) collective-permute-start(bf16[256,1024]{1,0:T(8,128)(2,1)S(1)} %bitcast.10), channel_id=1, source_target_pairs={{0,1},{1,0},{2,3},{3,2},{4,5},{5,4},{6,7},{7,6},{8,9},{9,8},{10,11... | collective-permute-start | bytes 1572872 | tf_op jit(solution)/shard_map/ppermute | solution.py:312
  6.7 2.2 %collective-permute-start.1 = (bf16[1024,256]{1,0:T(8,128)(2,1)S(1)}, bf16[1024,256]{1,0:T(8,128)(2,1)S(1)}, u32[]{:S(2)}, u32[]{:S(2)}) collective-permute-start(bf16[1024,256]{1,0:T(8,128)(2,1)S(1)} %get-tuple-element.41.refs_1_), channel_id=1, source_target_pairs={{0,1},{1,0},{2,3},{3,2},{4,5},{5,4},{6,7},{7,6},{8,9},{9,8},{10,11... | collective-permute-start | bytes 1572872 | tf_op jit(solution)/shard_map/ppermute | solution.py:312
  10.9 1.5 %collective-permute-start.4 = (bf16[128,256]{1,0:T(8,128)(2,1)S(1)}, bf16[128,256]{1,0:T(8,128)(2,1)S(1)}, u32[]{:S(2)}, u32[]{:S(2)}) collective-permute-start(bf16[128,256]{1,0:T(8,128)(2,1)S(1)} %bitcast.13), channel_id=1, source_target_pairs={{0,1},{1,0},{2,3},{3,2},{4,5},{5,4},{6,7},{7,6},{8,9},{9,8},{10,11... | collective-permute-start | bytes 196616 | tf_op jit(solution)/shard_map/ppermute | solution.py:312
  11.5 3.9 %collective-permute-start.3 = (bf16[1024,256]{1,0:T(8,128)(2,1)S(1)}, bf16[1024,256]{1,0:T(8,128)(2,1)S(1)}, u32[]{:S(2)}, u32[]{:S(2)}) collective-permute-start(bf16[1024,256]{1,0:T(8,128)(2,1)S(1)} %get-tuple-element.46.refs_1_), channel_id=1, source_target_pairs={{0,1},{1,0},{2,3},{3,2},{4,5},{5,4},{6,7},{7,6},{8,9},{9,8},{10,11... | collective-permute-start | bytes 1572872 | tf_op jit(solution)/shard_map/ppermute | solution.py:312
  12.4 5.4 %collective-permute-start.6 = (bf16[128,256]{1,0:T(8,128)(2,1)S(1)}, bf16[128,256]{1,0:T(8,128)(2,1)S(1)}, u32[]{:S(2)}, u32[]{:S(2)}) collective-permute-start(bf16[128,256]{1,0:T(8,128)(2,1)S(1)} %shard_map.91.refs_3_.refs_0_), channel_id=1, source_target_pairs={{0,2},{1,5},{2,0},{3,7},{4,6},{5,1},{6,4},{7,3},{8,10},{9,13},{10,... | collective-permute-start | bytes 196616 | tf_op jit(solution)/shard_map/ppermute | solution.py:331
  16.2 4.8 %collective-permute-start.5 = (bf16[256,1024]{1,0:T(8,128)(2,1)S(1)}, bf16[256,1024]{1,0:T(8,128)(2,1)S(1)}, u32[]{:S(2)}, u32[]{:S(2)}) collective-permute-start(bf16[256,1024]{1,0:T(8,128)(2,1)S(1)} %bitcast.11), channel_id=1, source_target_pairs={{0,1},{1,0},{2,3},{3,2},{4,5},{5,4},{6,7},{7,6},{8,9},{9,8},{10,11... | collective-permute-start | bytes 1572872 | tf_op jit(solution)/shard_map/ppermute | solution.py:312
  17.8 5.2 %collective-permute-start.8 = (bf16[128,256]{1,0:T(8,128)(2,1)S(1)}, bf16[128,256]{1,0:T(8,128)(2,1)S(1)}, u32[]{:S(2)}, u32[]{:S(2)}) collective-permute-start(bf16[128,256]{1,0:T(8,128)(2,1)S(1)} %shard_map.93.refs_2_.refs_0_), channel_id=1, source_target_pairs={{0,4},{1,9},{2,6},{3,11},{4,0},{5,13},{6,2},{7,15},{8,12},{9,1},{1... | collective-permute-start | bytes 196616 | tf_op jit(solution)/shard_map/ppermute | solution.py:331
  21.1 3.6 %copy-start = (f32[256,128]{1,0:T(8,128)S(1)}, f32[256,128]{1,0:T(8,128)}, u32[]{:S(2)}) copy-start(f32[256,128]{1,0:T(8,128)} %refs_2_.6) | copy-start | bytes 393220
  21.1 3.6 %copy-start.1 = (bf16[256,256]{1,0:T(8,128)(2,1)S(1)}, bf16[256,256]{1,0:T(8,128)(2,1)}, u32[]{:S(2)}) copy-start(bf16[256,256]{1,0:T(8,128)(2,1)} %refs_0_.5) | copy-start | bytes 393220
  22.4 3.0 %collective-permute-start.7 = (bf16[256,1024]{1,0:T(8,128)(2,1)S(1)}, bf16[256,1024]{1,0:T(8,128)(2,1)S(1)}, u32[]{:S(2)}, u32[]{:S(2)}) collective-permute-start(bf16[256,1024]{1,0:T(8,128)(2,1)S(1)} %bitcast.9), channel_id=1, source_target_pairs={{0,1},{1,0},{2,3},{3,2},{4,5},{5,4},{6,7},{7,6},{8,9},{9,8},{10,11... | collective-permute-start | bytes 1572872 | tf_op jit(solution)/shard_map/ppermute | solution.py:312
  22.5 7.5 %collective-permute-start.10 = (bf16[256,1024]{1,0:T(8,128)(2,1)S(1)}, bf16[256,1024]{1,0:T(8,128)(2,1)S(1)}, u32[]{:S(2)}, u32[]{:S(2)}) collective-permute-start(bf16[256,1024]{1,0:T(8,128)(2,1)S(1)} %bitcast.7), channel_id=1, source_target_pairs={{0,1},{1,0},{2,3},{3,2},{4,5},{5,4},{6,7},{7,6},{8,9},{9,8},{10,11... | collective-permute-start | bytes 1572872 | tf_op jit(solution)/shard_map/ppermute | solution.py:312
  23.0 4.3 %collective-permute-start.11 = (bf16[128,256]{1,0:T(8,128)(2,1)S(1)}, bf16[128,256]{1,0:T(8,128)(2,1)S(1)}, u32[]{:S(2)}, u32[]{:S(2)}) collective-permute-start(bf16[128,256]{1,0:T(8,128)(2,1)S(1)} %shard_map.96.refs_4_.refs_0_), channel_id=1, source_target_pairs={{0,8},{1,3},{2,10},{3,1},{4,12},{5,7},{6,14},{7,5},{8,0},{9,11},{1... | collective-permute-start | bytes 196616 | tf_op jit(solution)/shard_map/ppermute | solution.py:331
  26.3 4.4 %collective-permute-start.9 = (bf16[256,1024]{1,0:T(8,128)(2,1)S(1)}, bf16[256,1024]{1,0:T(8,128)(2,1)S(1)}, u32[]{:S(2)}, u32[]{:S(2)}) collective-permute-start(bf16[256,1024]{1,0:T(8,128)(2,1)S(1)} %bitcast.8), channel_id=1, source_target_pairs={{0,1},{1,0},{2,3},{3,2},{4,5},{5,4},{6,7},{7,6},{8,9},{9,8},{10,11... | collective-permute-start | bytes 1572872 | tf_op jit(solution)/shard_map/ppermute | solution.py:312
  27.4 5.5 %collective-permute-start.13 = (bf16[128,256]{1,0:T(8,128)(2,1)S(1)}, bf16[128,256]{1,0:T(8,128)(2,1)S(1)}, u32[]{:S(2)}, u32[]{:S(2)}) collective-permute-start(bf16[128,256]{1,0:T(8,128)(2,1)S(1)} %shard_map.99.refs_5_.refs_1_), channel_id=1, source_target_pairs={{0,16},{1,17},{2,18},{3,19},{4,20},{5,21},{6,22},{7,23},{8,24},{9,... | collective-permute-start | bytes 196616 | tf_op jit(solution)/shard_map/ppermute | solution.py:331
  30.7 2.0 %collective-permute-start.12 = (bf16[256,1024]{1,0:T(8,128)(2,1)S(1)}, bf16[256,1024]{1,0:T(8,128)(2,1)S(1)}, u32[]{:S(2)}, u32[]{:S(2)}) collective-permute-start(bf16[256,1024]{1,0:T(8,128)(2,1)S(1)} %bitcast.12), channel_id=1, source_target_pairs={{0,1},{1,0},{2,3},{3,2},{4,5},{5,4},{6,7},{7,6},{8,9},{9,8},{10,11... | collective-permute-start | bytes 1572872 | tf_op jit(solution)/shard_map/ppermute | solution.py:312
  32.9 1.3 %collective-permute-start.14 = (bf16[128,256]{1,0:T(8,128)(2,1)S(1)}, bf16[128,256]{1,0:T(8,128)(2,1)S(1)}, u32[]{:S(2)}, u32[]{:S(2)}) collective-permute-start(bf16[128,256]{1,0:T(8,128)(2,1)S(1)} %shard_map.104.refs_1_.refs_4_), channel_id=1, source_target_pairs={{0,1},{1,0},{2,3},{3,2},{4,5},{5,4},{6,7},{7,6},{8,9},{9,8},{10,11... | collective-permute-start | bytes 196616 | tf_op jit(solution)/shard_map/ppermute | solution.py:312

commit v16 on v15

--- a/solution.py
+++ b/solution.py
@@ -265,10 +265,12 @@
         inner = dot(tip, right).astype(BF)
         return dot(tip.astype(F32).T.astype(BF), inner)
 
-    def turn_last_kernel(base, response, noise_fixed, tip, last_base, last_resp, noise_rows):
+    def turn_tip_kernel(response, noise_fixed, tip, last_resp, noise_rows):
         noise_rows[...] = noise_fixed[...].T
-        last_base[...] = base[...].T
         last_resp[...] = through_tip(tip[...], response[...]).T.astype(BF)
+
+    def turn_last_kernel(base, out):
+        out[...] = base[...].T
 
     def turn_response_kernel(first, *refs):
         got, out = refs[:-1], refs[-1]
@@ -419,32 +421,32 @@
         )
         got_solved = send_down(other)
         advance(solved)
-        pushed, other = call(
-            response_kernel, [fixed_f32, fixed_others], [k1, response], 5, after=sent
-        )
-        got_pushed = send_down(other)
+        last_resp, noise_rows = call(
+            turn_tip_kernel,
+            [by_node, shape_of((width, fixed_rows), F32)],
+            [response, noise_fixed, tip_inverse],
+            5,
+            after=sent,
+        )
         base, passed, other = call(
             pass_kernel,
             [flat_f32, flat_f32, flat_others],
             [k1, mask, solved, *got_solved],
             8,
-            after=pushed,
+            after=noise_rows,
         )
         got_passed = send_down(other)
         advance(base)
-        last_base, last_resp, noise_rows = call(
-            turn_last_kernel,
-            [node_f32, by_node, shape_of((width, fixed_rows), F32)],
-            [base, response, noise_fixed, tip_inverse],
-            5,
-            after=sent,
-        )
+        pushed, other = call(
+            response_kernel, [fixed_f32, fixed_others], [k1, response], 5, after=sent
+        )
+        got_pushed = send_down(other)
         solved, other = call(
             first_solve_kernel,
             [flat_f32, flat_others],
             [d0, value_rows, passed, *got_passed],
             8,
-            after=noise_rows,
+            after=pushed,
         )
         got_solved = send_down(other)
         advance(solved)
@@ -458,7 +460,8 @@
         got_first = send_down(other)
         (first_base,) = call(turn_first_kernel, [node_f32], [solved, *got_solved], 1, after=left)
         (first,) = call(own_response_kernel, [fixed_f32], [d0, left], 8, after=first_base)
-        (first_resp,) = call(turn_response_kernel, [by_node], [first, *got_first], 1, after=first)
+        (last_base,) = call(turn_last_kernel, [node_f32], [base], 1, after=first)
+        (first_resp,) = call(turn_response_kernel, [by_node], [first, *got_first], 1, after=last_base)
         while step < steps:
             advance()
         (mixed,) = call(mixed_kernel, [part_bf], [noise_rows, sent, *got], 0.2, after=first_resp)

time: 35.8 us -> 36.9 us (1.031)
  starting transfers between devices: 14.4 us -> 15.5 us
    ppermute x11, starting transfers between devices: 5.17 us -> 5.81 us  [swap(): return lax.ppermute(value, 'space', pairs)]
    ppermute x11, waiting for transfers between devices: 1.39 us -> 0.84 us  [swap(): return lax.ppermute(value, 'space', pairs)]
    ppermute x4, waiting for transfers between devices: 0.56 us -> 1.08 us  [swap_step(): return lax.ppermute(value, ('tm', 'space'), pairs)]
    ppermute x4, starting transfers between devices: 9.28 us -> 9.67 us  [swap_step(): return lax.ppermute(value, ('tm', 'space'), pairs)]
    pallas_call x21 -> x22, Pallas kernels: 18.3 us -> 18.4 us  [call(): pl.pallas_call(run, in_specs=specs, out_specs=[pl.BlockSpec(memory_space=...]
  transfers between devices with their start and end apart: 15 -> 15, of which waited for: 4 -> 5; matrix products, arithmetic and copies ran while one was open for 0% -> 0% of each run, Pallas kernels for 42% -> 41%
where the time goes in v16:
time: 36.9 us; the launch traced here: 36.7 us
  Pallas kernels  18.4 us (50%)
  starting transfers between devices  15.5 us (42%)
  waiting for transfers between devices  1.92 us (5%)
  between operations  0.84 us (2%)
    pallas_call x22, Pallas kernels, call(): pl.pallas_call(run, in_specs=specs, out_specs=[pl.BlockSpec(memory_space=...  18.4 us
    ppermute x4, starting transfers between devices, swap_step(): return lax.ppermute(value, ('tm', 'space'), pairs)  9.67 us
    ppermute x11, starting transfers between devices, swap(): return lax.ppermute(value, 'space', pairs)  5.81 us
    ppermute x4, waiting for transfers between devices, swap_step(): return lax.ppermute(value, ('tm', 'space'), pairs)  1.08 us
    ppermute x11, waiting for transfers between devices, swap(): return lax.ppermute(value, 'space', pairs)  0.84 us
  transfers between devices with their start and end apart: 15, of which 5 were waited for; matrix products, arithmetic and copies ran while one was open for 0% of the time, Pallas kernels for 41%

profile of v16, /device:TPU:0, one launch (start us, length us, event | category | flops | bytes accessed | tf_op | source)
XLA Modules:
  0.0 36.7 jit_solution(14240819666706915077)
XLA Ops:
  0.6 0.5 %collective-permute-start = (bf16[2,1024,256]{2,1,0:T(8,128)(2,1)}, bf16[2,1024,256]{2,1,0:T(8,128)(2,1)S(1)}, u32[]{:S(2)}, u32[]{:S(2)}) collective-permute-start(bf16[2,1024,256]{2,1,0:T(8,128)(2,1)} %refs_3_.3), channel_id=1, source_target_pairs={{0,1},{1,0},{2,3},{3,2},{4,5},{5,4},{6,7},{7,6},{8,9},{9,8},{10,11... | collective-permute-start | bytes 3145736 | tf_op jit(solution)/shard_map/ppermute | solution.py:314
  1.1 2.8 %shard_map.86 = (bf16[1024,2048]{1,0:T(8,128)(2,1)S(1)}, bf16[1024,2048]{1,0:T(8,128)(2,1)S(1)}, f32[256,1024]{1,0:T(8,128)S(1)}, bf16[1,256,1024]{2,1,0:T(8,128...) custom-call(bf16[2,1024,2048]{2,1,0:T(8,128)(2,1)} %refs_0_.3, bf16[2,256,1024]{2,1,0:T(8,128)(2,1)} %refs_1_.4, ...), custom_call_target="tpu_custom_call" | custom-call | flops 8000000000 | tf_op jit(solution)/shard_map/pallas_call | solution.py:73
  4.0 1.1 %collective-permute-start.2 = (bf16[256,1024]{1,0:T(8,128)(2,1)S(1)}, bf16[256,1024]{1,0:T(8,128)(2,1)S(1)}, u32[]{:S(2)}, u32[]{:S(2)}) collective-permute-start(bf16[256,1024]{1,0:T(8,128)(2,1)S(1)} %bitcast.9), channel_id=1, source_target_pairs={{0,1},{1,0},{2,3},{3,2},{4,5},{5,4},{6,7},{7,6},{8,9},{9,8},{10,11... | collective-permute-start | bytes 1572872 | tf_op jit(solution)/shard_map/ppermute | solution.py:314
  5.1 0.0 collective-permute-done.refs_4_
  5.1 1.6 %shard_map.87 = (f32[1024,256]{1,0:T(8,128)S(1)}, bf16[1024,256]{1,0:T(8,128)(2,1)S(1)}, bf16[1024,2048]{1,0:T(8,128)(2,1)S(1)}, bf16[1024,256]{1,0:T(8,128)(2,1)S(1)}) custom-call(bf16[1024,2048]{1,0:T(8,128)(2,1)S(1)} %get-tuple-element.32.refs_0_, bf16[1024,256]{1,0:T(8,128)(2,1)S(1)} %get-tuple-element.33.refs_1_, bf16[2,1024,2048]{2,1,0:T(8,128)(2,1)} %refs_0_.4, ...), custom_call_target="tpu_custom_call" | custom-call | flops 8000000000 | tf_op jit(solution)/shard_map/pallas_call | solution.py:73
  6.7 0.1 collective-permute-start.1
  6.7 2.0 %shard_map.88 = (f32[256,1024]{1,0:T(8,128)S(1)}, bf16[256,1024]{1,0:T(8,128)(2,1)S(1)}, bf16[1024,2048]{1,0:T(8,128)(2,1)S(1)}) custom-call(bf16[2,1024,2048]{2,1,0:T(8,128)(2,1)} %refs_0_.4, bf16[2,256,1024]{2,1,0:T(8,128)(2,1)} %refs_1_.4, f32[1024,256]{1,0:T(8,128)S(1)} %get-tuple-element.34.refs_2_, ...), custom_call_target="tpu_custom_call", output_to_operand_aliasing={{2}: (3, {})} | custom-call | flops 8000000000 | tf_op jit(solution)/shard_map/pallas_call | solution.py:73
  8.8 0.0 collective-permute-done.2.refs_6_
  8.8 0.0 collective-permute-done.1.refs_5_
  8.8 2.1 %shard_map.89 = (bf16[1024,256]{1,0:T(8,128)(2,1)S(1)}, f32[128,256]{1,0:T(8,128)S(1)}, bf16[1,128,256]{2,1,0:T(8,128)(2,1)S(1)}, bf16[256,1024]{1,0:T(8,128)(2,1)S(1)}) custom-call(bf16[1024,2048]{1,0:T(8,128)(2,1)S(1)} %get-tuple-element.37.refs_0_, bf16[1024,256]{1,0:T(8,128)(2,1)S(1)} %get-tuple-element.40.refs_1_, ...), custom_call_target="tpu_custom_call" | custom-call | flops 8000000000 | tf_op jit(solution)/shard_map/pallas_call | solution.py:73
  10.9 0.6 %collective-permute-start.4 = (bf16[128,256]{1,0:T(8,128)(2,1)S(1)}, bf16[128,256]{1,0:T(8,128)(2,1)S(1)}, u32[]{:S(2)}, u32[]{:S(2)}) collective-permute-start(bf16[128,256]{1,0:T(8,128)(2,1)S(1)} %bitcast.13), channel_id=1, source_target_pairs={{0,1},{1,0},{2,3},{3,2},{4,5},{5,4},{6,7},{7,6},{8,9},{9,8},{10,11... | collective-permute-start | bytes 196616 | tf_op jit(solution)/shard_map/ppermute | solution.py:314
  11.5 0.1 collective-permute-start.3
  11.6 0.5 %shard_map.90.refs_2_.refs_1_ = f32[1024,256]{1,0:T(8,128)S(1)} custom-call(bf16[1024,2048]{1,0:T(8,128)(2,1)S(1)} %get-tuple-element.39.refs_0_, bf16[1024,256]{1,0:T(8,128)(2,1)S(1)} %get-tuple-element.45.refs_1_), custom_call_target="tpu_custom_call" | custom-call | flops 8000000000 | tf_op jit(solution)/shard_map/pallas_call | solution.py:73
  12.1 0.3 collective-permute-done.4.refs_1_
  12.4 0.0 copy-start
  12.4 0.0 copy-start.1
  12.4 3.0 %collective-permute-start.6 = (bf16[128,256]{1,0:T(8,128)(2,1)S(1)}, bf16[128,256]{1,0:T(8,128)(2,1)S(1)}, u32[]{:S(2)}, u32[]{:S(2)}) collective-permute-start(bf16[128,256]{1,0:T(8,128)(2,1)S(1)} %shard_map.91.refs_3_.refs_0_), channel_id=1, source_target_pairs={{0,2},{1,5},{2,0},{3,7},{4,6},{5,1},{6,4},{7,3},{8,10},{9,13},{10,... | collective-permute-start | bytes 196616 | tf_op jit(solution)/shard_map/ppermute | solution.py:333
  15.4 0.0 collective-permute-done.3.refs_2_
  15.4 0.8 %shard_map.92 = (f32[256,1024]{1,0:T(8,128)S(1)}, bf16[1,256,1024]{2,1,0:T(8,128)(2,1)S(1)}) custom-call(bf16[1024,2048]{1,0:T(8,128)(2,1)S(1)} %get-tuple-element.39.refs_0_, f32[1024,256]{1,0:T(8,128)S(1)} %shard_map.90.refs_2_.refs_1_, bf16[1024,256]{1,0:T(8,128)(2,1)S(1)} %collective-permute-done.3.refs_2_, bf16[128,256]{1,0:T(8,128)(2,1)S(1)} %shard_map.91.refs_3_.refs_0_), custom_call_target="tpu_custom_call" | custom-call | flops 8000000000 | tf_op jit(solution)/shard_map/pallas_call | solution.py:73
  16.2 1.6 %collective-permute-start.5 = (bf16[256,1024]{1,0:T(8,128)(2,1)S(1)}, bf16[256,1024]{1,0:T(8,128)(2,1)S(1)}, u32[]{:S(2)}, u32[]{:S(2)}) collective-permute-start(bf16[256,1024]{1,0:T(8,128)(2,1)S(1)} %bitcast.11), channel_id=1, source_target_pairs={{0,1},{1,0},{2,3},{3,2},{4,5},{5,4},{6,7},{7,6},{8,9},{9,8},{10,11... | collective-permute-start | bytes 1572872 | tf_op jit(solution)/shard_map/ppermute | solution.py:314
  17.8 0.0 collective-permute-done.6.refs_1_
  17.8 2.0 %collective-permute-start.8 = (bf16[128,256]{1,0:T(8,128)(2,1)S(1)}, bf16[128,256]{1,0:T(8,128)(2,1)S(1)}, u32[]{:S(2)}, u32[]{:S(2)}) collective-permute-start(bf16[128,256]{1,0:T(8,128)(2,1)S(1)} %shard_map.93.refs_3_.refs_0_), channel_id=1, source_target_pairs={{0,4},{1,9},{2,6},{3,11},{4,0},{5,13},{6,2},{7,15},{8,12},{9,1},{1... | collective-permute-start | bytes 196616 | tf_op jit(solution)/shard_map/ppermute | solution.py:333
  19.8 0.0 copy-done
  19.8 0.0 copy-done.1
  19.8 0.6 %shard_map.94 = (bf16[1024,256]{1,0:T(8,128)(2,1)S(1)}, f32[128,256]{1,0:T(8,128)S(1)}) custom-call(bf16[256,1024]{1,0:T(8,128)(2,1)S(1)} %get-tuple-element.50.refs_0_.refs_1_, f32[256,128]{1,0:T(8,128)S(1)} %copy-done, bf16[256,256]{1,0:T(8,128)(2,1)S(1)} %copy-done.1, bf16[128,256]{1,0:T(8,128)(2,1)S(1)} %shard_map.93.refs_3_.refs_0_), custom_call_target="tpu_custom_call" | custom-call | flops 5000000000 | tf_op jit(solution)/shard_map/pallas_call | solution.py:73
  20.4 0.0 collective-permute-done.5.refs_3_
  20.4 1.3 %shard_map.95 = (f32[256,1024]{1,0:T(8,128)S(1)}, f32[256,1024]{1,0:T(8,128)S(1)}, bf16[1,256,1024]{2,1,0:T(8,128)(2,1)S(1)}) custom-call(bf16[1024,2048]{1,0:T(8,128)(2,1)S(1)} %get-tuple-element.37.refs_0_, f32[8,128]{1,0:T(8,128)S(1)} %get-tuple-element.38.refs_1_, f32[256,1024]{1,0:T(8,128)S(1)} %get-tuple-element.48.refs_2_, ...), custom_call_target="tpu_custom_call" | custom-call | flops 8000000000 | tf_op jit(solution)/shard_map/pallas_call | solution.py:73
  21.7 0.1 collective-permute-start.7
  21.8 0.3 collective-permute-done.8.refs_1_
  22.2 2.0 %collective-permute-start.11 = (bf16[128,256]{1,0:T(8,128)(2,1)S(1)}, bf16[128,256]{1,0:T(8,128)(2,1)S(1)}, u32[]{:S(2)}, u32[]{:S(2)}) collective-permute-start(bf16[128,256]{1,0:T(8,128)(2,1)S(1)} %shard_map.96.refs_2_.refs_0_), channel_id=1, source_target_pairs={{0,8},{1,3},{2,10},{3,1},{4,12},{5,7},{6,14},{7,5},{8,0},{9,11},{1... | collective-permute-start | bytes 196616 | tf_op jit(solution)/shard_map/ppermute | solution.py:333
  24.2 1.2 %shard_map.97 = (f32[256,1024]{1,0:T(8,128)S(1)}, bf16[1,256,1024]{2,1,0:T(8,128)(2,1)S(1)}) custom-call(bf16[1024,2048]{1,0:T(8,128)(2,1)S(1)} %get-tuple-element.37.refs_0_, bf16[256,1024]{1,0:T(8,128)(2,1)S(1)} %get-tuple-element.50.refs_0_.refs_1_, bf16[128,256]{1,0:T(8,128)(2,1)S(1)} %shard_map.96.refs_2_.refs_0_), custom_call_target="tpu_custom_call" | custom-call | flops 5000000000 | tf_op jit(solution)/shard_map/pallas_call | solution.py:73
  25.5 0.1 collective-permute-start.10
  25.6 0.0 collective-permute-done.7.refs_3_
  25.6 0.9 %shard_map.98 = (f32[256,1024]{1,0:T(8,128)S(1)}, bf16[1,256,1024]{2,1,0:T(8,128)(2,1)S(1)}) custom-call(bf16[1024,2048]{1,0:T(8,128)(2,1)S(1)} %get-tuple-element.32.refs_0_, f32[256,1024]{1,0:T(8,128)S(1)} %get-tuple-element.36.refs_1_, f32[256,1024]{1,0:T(8,128)S(1)} %get-tuple-element.52.refs_2_, bf16[256,1024]{1,0:T(8,128)(2,1)S(1)} %collective-permute-done.7.refs_3_, ...), custom_call_target="tpu_custom_call" | custom-call | flops 8000000000 | tf_op jit(solution)/shard_map/pallas_call | solution.py:73
  26.4 1.2 %collective-permute-start.9 = (bf16[256,1024]{1,0:T(8,128)(2,1)S(1)}, bf16[256,1024]{1,0:T(8,128)(2,1)S(1)}, u32[]{:S(2)}, u32[]{:S(2)}) collective-permute-start(bf16[256,1024]{1,0:T(8,128)(2,1)S(1)} %bitcast.8), channel_id=1, source_target_pairs={{0,1},{1,0},{2,3},{3,2},{4,5},{5,4},{6,7},{7,6},{8,9},{9,8},{10,11... | collective-permute-start | bytes 1572872 | tf_op jit(solution)/shard_map/ppermute | solution.py:314
  27.7 0.0 collective-permute-done.11.refs_1_
  27.7 2.7 %collective-permute-start.13 = (bf16[128,256]{1,0:T(8,128)(2,1)S(1)}, bf16[128,256]{1,0:T(8,128)(2,1)S(1)}, u32[]{:S(2)}, u32[]{:S(2)}) collective-permute-start(bf16[128,256]{1,0:T(8,128)(2,1)S(1)} %shard_map.99.refs_5_.refs_1_), channel_id=1, source_target_pairs={{0,16},{1,17},{2,18},{3,19},{4,20},{5,21},{6,22},{7,23},{8,24},{9,... | collective-permute-start | bytes 196616 | tf_op jit(solution)/shard_map/ppermute | solution.py:333
  30.4 0.0 collective-permute-done.10.refs_4_
  30.4 0.7 %shard_map.100 = (bf16[256,1024]{1,0:T(8,128)(2,1)S(1)}, bf16[1,256,1024]{2,1,0:T(8,128)(2,1)S(1)}) custom-call(bf16[1024,2048]{1,0:T(8,128)(2,1)S(1)} %get-tuple-element.32.refs_0_, bf16[256,1024]{1,0:T(8,128)(2,1)S(1)} %get-tuple-element.42.refs_3_.refs_1_, bf16[256,256]{1,0:T(8,128)(2,1)S(1)} %copy-done.1, ...), custom_call_target="tpu_custom_call" | custom-call | flops 5000000000 | tf_op jit(solution)/shard_map/pallas_call | solution.py:73
  31.0 0.5 %collective-permute-start.12 = (bf16[256,1024]{1,0:T(8,128)(2,1)S(1)}, bf16[256,1024]{1,0:T(8,128)(2,1)S(1)}, u32[]{:S(2)}, u32[]{:S(2)}) collective-permute-start(bf16[256,1024]{1,0:T(8,128)(2,1)S(1)} %bitcast.12), channel_id=1, source_target_pairs={{0,1},{1,0},{2,3},{3,2},{4,5},{5,4},{6,7},{7,6},{8,9},{9,8},{10,11... | collective-permute-start | bytes 1572872 | tf_op jit(solution)/shard_map/ppermute | solution.py:314
  31.5 0.0 collective-permute-done.9.refs_1_
  31.5 0.3 shard_map.101.refs_2_.refs_0_
  31.9 0.5 %shard_map.102.refs_1_.refs_0_ = f32[256,1024]{1,0:T(8,128)S(1)} custom-call(bf16[1024,2048]{1,0:T(8,128)(2,1)S(1)} %get-tuple-element.32.refs_0_, bf16[256,1024]{1,0:T(8,128)(2,1)S(1)} %get-tuple-element.59.refs_2_.refs_1_, f32[1024,256]{1,0:T(8,128)S(1)} %shard_map.101.refs_2_.refs_0_), custom_call_target="tpu_custom_call" | custom-call | flops 8000000000 | tf_op jit(solution)/shard_map/pallas_call | solution.py:73
  32.4 0.3 shard_map.103.refs_2_.refs_1_
  32.7 0.3 collective-permute-done.12.refs_1_
  33.1 0.2 shard_map.104.refs_3_.refs_2_
  33.3 0.7 %collective-permute-done.13.refs_2_ = bf16[128,256]{1,0:T(8,128)(2,1)S(1)} collective-permute-done((bf16[128,256]{1,0:T(8,128)(2,1)S(1)}, bf16[128,256]{1,0:T(8,128)(2,1)S(1)}, u32[]{:S(2)}, u32[]{:S(2)}) %collective-permute-start.13) | collective-permute-done | bytes 65568 | tf_op jit(solution)/shard_map/ppermute | solution.py:333
  34.0 0.1 collective-permute-start.14
  34.1 1.1 %shard_map.106.refs_6_ = f32[256,128]{1,0:T(8,128)} custom-call(bf16[256,256]{1,0:T(8,128)(2,1)S(1)} %copy-done.1, bf16[128,256]{1,0:T(8,128)(2,1)S(1)} %shard_map.105.refs_1_.refs_4_), custom_call_target="tpu_custom_call" | custom-call | flops 8000000000 | tf_op jit(solution)/shard_map/pallas_call | solution.py:73
  35.2 0.2 collective-permute-done.14.refs_5_
  35.4 1.3 %shard_map.107 = bf16[2,1024,256]{2,1,0:T(8,128)(2,1)} custom-call(f32[1024,256]{1,0:T(8,128)S(1)} %shard_map.101.refs_2_.refs_0_, f32[1024,256]{1,0:T(8,128)S(1)} %shard_map.103.refs_2_.refs_1_, bf16[1024,256]{1,0:T(8,128)(2,1)S(1)} %shard_map.104.refs_3_.refs_2_, bf16[1024,256]{1,0:T(8,128)(2,1)S(1)} %get-tuple-element.61.refs_3_, ...), custom_call_target="tpu_custom_call" | custom-call | flops 8000000000 | tf_op jit(solution)/shard_map/pallas_call | solution.py:73
  (5 shorter events, 0.1 us)
Async XLA Ops:
  0.6 4.4 %collective-permute-start = (bf16[2,1024,256]{2,1,0:T(8,128)(2,1)}, bf16[2,1024,256]{2,1,0:T(8,128)(2,1)S(1)}, u32[]{:S(2)}, u32[]{:S(2)}) collective-permute-start(bf16[2,1024,256]{2,1,0:T(8,128)(2,1)} %refs_3_.3), channel_id=1, source_target_pairs={{0,1},{1,0},{2,3},{3,2},{4,5},{5,4},{6,7},{7,6},{8,9},{9,8},{10,11... | collective-permute-start | bytes 3145736 | tf_op jit(solution)/shard_map/ppermute | solution.py:314
  4.0 4.8 %collective-permute-start.2 = (bf16[256,1024]{1,0:T(8,128)(2,1)S(1)}, bf16[256,1024]{1,0:T(8,128)(2,1)S(1)}, u32[]{:S(2)}, u32[]{:S(2)}) collective-permute-start(bf16[256,1024]{1,0:T(8,128)(2,1)S(1)} %bitcast.9), channel_id=1, source_target_pairs={{0,1},{1,0},{2,3},{3,2},{4,5},{5,4},{6,7},{7,6},{8,9},{9,8},{10,11... | collective-permute-start | bytes 1572872 | tf_op jit(solution)/shard_map/ppermute | solution.py:314
  6.7 2.2 %collective-permute-start.1 = (bf16[1024,256]{1,0:T(8,128)(2,1)S(1)}, bf16[1024,256]{1,0:T(8,128)(2,1)S(1)}, u32[]{:S(2)}, u32[]{:S(2)}) collective-permute-start(bf16[1024,256]{1,0:T(8,128)(2,1)S(1)} %get-tuple-element.40.refs_1_), channel_id=1, source_target_pairs={{0,1},{1,0},{2,3},{3,2},{4,5},{5,4},{6,7},{7,6},{8,9},{9,8},{10,11... | collective-permute-start | bytes 1572872 | tf_op jit(solution)/shard_map/ppermute | solution.py:314
  10.9 1.5 %collective-permute-start.4 = (bf16[128,256]{1,0:T(8,128)(2,1)S(1)}, bf16[128,256]{1,0:T(8,128)(2,1)S(1)}, u32[]{:S(2)}, u32[]{:S(2)}) collective-permute-start(bf16[128,256]{1,0:T(8,128)(2,1)S(1)} %bitcast.13), channel_id=1, source_target_pairs={{0,1},{1,0},{2,3},{3,2},{4,5},{5,4},{6,7},{7,6},{8,9},{9,8},{10,11... | collective-permute-start | bytes 196616 | tf_op jit(solution)/shard_map/ppermute | solution.py:314
  11.5 3.9 %collective-permute-start.3 = (bf16[1024,256]{1,0:T(8,128)(2,1)S(1)}, bf16[1024,256]{1,0:T(8,128)(2,1)S(1)}, u32[]{:S(2)}, u32[]{:S(2)}) collective-permute-start(bf16[1024,256]{1,0:T(8,128)(2,1)S(1)} %get-tuple-element.45.refs_1_), channel_id=1, source_target_pairs={{0,1},{1,0},{2,3},{3,2},{4,5},{5,4},{6,7},{7,6},{8,9},{9,8},{10,11... | collective-permute-start | bytes 1572872 | tf_op jit(solution)/shard_map/ppermute | solution.py:314
  12.4 7.4 %copy-start = (f32[256,128]{1,0:T(8,128)S(1)}, f32[256,128]{1,0:T(8,128)}, u32[]{:S(2)}) copy-start(f32[256,128]{1,0:T(8,128)} %refs_1_.5) | copy-start | bytes 393220
  12.4 7.4 %copy-start.1 = (bf16[256,256]{1,0:T(8,128)(2,1)S(1)}, bf16[256,256]{1,0:T(8,128)(2,1)}, u32[]{:S(2)}) copy-start(bf16[256,256]{1,0:T(8,128)(2,1)} %refs_0_.5) | copy-start | bytes 393220
  12.4 5.4 %collective-permute-start.6 = (bf16[128,256]{1,0:T(8,128)(2,1)S(1)}, bf16[128,256]{1,0:T(8,128)(2,1)S(1)}, u32[]{:S(2)}, u32[]{:S(2)}) collective-permute-start(bf16[128,256]{1,0:T(8,128)(2,1)S(1)} %shard_map.91.refs_3_.refs_0_), channel_id=1, source_target_pairs={{0,2},{1,5},{2,0},{3,7},{4,6},{5,1},{6,4},{7,3},{8,10},{9,13},{10,... | collective-permute-start | bytes 196616 | tf_op jit(solution)/shard_map/ppermute | solution.py:333
  16.2 4.2 %collective-permute-start.5 = (bf16[256,1024]{1,0:T(8,128)(2,1)S(1)}, bf16[256,1024]{1,0:T(8,128)(2,1)S(1)}, u32[]{:S(2)}, u32[]{:S(2)}) collective-permute-start(bf16[256,1024]{1,0:T(8,128)(2,1)S(1)} %bitcast.11), channel_id=1, source_target_pairs={{0,1},{1,0},{2,3},{3,2},{4,5},{5,4},{6,7},{7,6},{8,9},{9,8},{10,11... | collective-permute-start | bytes 1572872 | tf_op jit(solution)/shard_map/ppermute | solution.py:314
  17.8 4.3 %collective-permute-start.8 = (bf16[128,256]{1,0:T(8,128)(2,1)S(1)}, bf16[128,256]{1,0:T(8,128)(2,1)S(1)}, u32[]{:S(2)}, u32[]{:S(2)}) collective-permute-start(bf16[128,256]{1,0:T(8,128)(2,1)S(1)} %shard_map.93.refs_3_.refs_0_), channel_id=1, source_target_pairs={{0,4},{1,9},{2,6},{3,11},{4,0},{5,13},{6,2},{7,15},{8,12},{9,1},{1... | collective-permute-start | bytes 196616 | tf_op jit(solution)/shard_map/ppermute | solution.py:333
  21.7 3.8 %collective-permute-start.7 = (bf16[256,1024]{1,0:T(8,128)(2,1)S(1)}, bf16[256,1024]{1,0:T(8,128)(2,1)S(1)}, u32[]{:S(2)}, u32[]{:S(2)}) collective-permute-start(bf16[256,1024]{1,0:T(8,128)(2,1)S(1)} %bitcast.10), channel_id=1, source_target_pairs={{0,1},{1,0},{2,3},{3,2},{4,5},{5,4},{6,7},{7,6},{8,9},{9,8},{10,11... | collective-permute-start | bytes 1572872 | tf_op jit(solution)/shard_map/ppermute | solution.py:314
  22.2 5.5 %collective-permute-start.11 = (bf16[128,256]{1,0:T(8,128)(2,1)S(1)}, bf16[128,256]{1,0:T(8,128)(2,1)S(1)}, u32[]{:S(2)}, u32[]{:S(2)}) collective-permute-start(bf16[128,256]{1,0:T(8,128)(2,1)S(1)} %shard_map.96.refs_2_.refs_0_), channel_id=1, source_target_pairs={{0,8},{1,3},{2,10},{3,1},{4,12},{5,7},{6,14},{7,5},{8,0},{9,11},{1... | collective-permute-start | bytes 196616 | tf_op jit(solution)/shard_map/ppermute | solution.py:333
  25.5 4.9 %collective-permute-start.10 = (bf16[256,1024]{1,0:T(8,128)(2,1)S(1)}, bf16[256,1024]{1,0:T(8,128)(2,1)S(1)}, u32[]{:S(2)}, u32[]{:S(2)}) collective-permute-start(bf16[256,1024]{1,0:T(8,128)(2,1)S(1)} %bitcast.7), channel_id=1, source_target_pairs={{0,1},{1,0},{2,3},{3,2},{4,5},{5,4},{6,7},{7,6},{8,9},{9,8},{10,11... | collective-permute-start | bytes 1572872 | tf_op jit(solution)/shard_map/ppermute | solution.py:314
  26.4 5.1 %collective-permute-start.9 = (bf16[256,1024]{1,0:T(8,128)(2,1)S(1)}, bf16[256,1024]{1,0:T(8,128)(2,1)S(1)}, u32[]{:S(2)}, u32[]{:S(2)}) collective-permute-start(bf16[256,1024]{1,0:T(8,128)(2,1)S(1)} %bitcast.8), channel_id=1, source_target_pairs={{0,1},{1,0},{2,3},{3,2},{4,5},{5,4},{6,7},{7,6},{8,9},{9,8},{10,11... | collective-permute-start | bytes 1572872 | tf_op jit(solution)/shard_map/ppermute | solution.py:314
  27.7 6.3 %collective-permute-start.13 = (bf16[128,256]{1,0:T(8,128)(2,1)S(1)}, bf16[128,256]{1,0:T(8,128)(2,1)S(1)}, u32[]{:S(2)}, u32[]{:S(2)}) collective-permute-start(bf16[128,256]{1,0:T(8,128)(2,1)S(1)} %shard_map.99.refs_5_.refs_1_), channel_id=1, source_target_pairs={{0,16},{1,17},{2,18},{3,19},{4,20},{5,21},{6,22},{7,23},{8,24},{9,... | collective-permute-start | bytes 196616 | tf_op jit(solution)/shard_map/ppermute | solution.py:333
  31.0 2.0 %collective-permute-start.12 = (bf16[256,1024]{1,0:T(8,128)(2,1)S(1)}, bf16[256,1024]{1,0:T(8,128)(2,1)S(1)}, u32[]{:S(2)}, u32[]{:S(2)}) collective-permute-start(bf16[256,1024]{1,0:T(8,128)(2,1)S(1)} %bitcast.12), channel_id=1, source_target_pairs={{0,1},{1,0},{2,3},{3,2},{4,5},{5,4},{6,7},{7,6},{8,9},{9,8},{10,11... | collective-permute-start | bytes 1572872 | tf_op jit(solution)/shard_map/ppermute | solution.py:314
  34.0 1.3 %collective-permute-start.14 = (bf16[128,256]{1,0:T(8,128)(2,1)S(1)}, bf16[128,256]{1,0:T(8,128)(2,1)S(1)}, u32[]{:S(2)}, u32[]{:S(2)}) collective-permute-start(bf16[128,256]{1,0:T(8,128)(2,1)S(1)} %shard_map.105.refs_1_.refs_4_), channel_id=1, source_target_pairs={{0,1},{1,0},{2,3},{3,2},{4,5},{5,4},{6,7},{7,6},{8,9},{9,8},{10,11... | collective-permute-start | bytes 196616 | tf_op jit(solution)/shard_map/ppermute | solution.py:314

commit v17 on v14

--- a/solution.py
+++ b/solution.py
@@ -169,7 +169,8 @@
         e1[...] = jnp.where(live, e1[...], jnp.zeros_like(e1[...]))
         for i in range(tiles):
             each(copies1, i, lambda copy: copy.wait())
-            each(copies0, i, lambda copy: copy.start(priority=i % 2))
+            for early in range(2 * i, min(2 * i + 2, tiles)):
+                each(copies0, early, lambda copy: copy.start(priority=1))
         noise_copy.start()
         lower_rows(e1, d1, own, other)
         for i in range(tiles):

time: 35.8 us -> 35.7 us (level)
  no operation moved by 1% of the time
where the time goes in v17:
time: 35.7 us; the launch traced here: 35.5 us
  Pallas kernels  18.3 us (51%)
  starting transfers between devices  14.8 us (41%)
  waiting for transfers between devices  1.58 us (4%)
  between operations  0.83 us (2%)
    pallas_call x21, Pallas kernels, call(): pl.pallas_call(run, in_specs=specs, out_specs=[pl.BlockSpec(memory_space=...  18.3 us
    ppermute x4, starting transfers between devices, swap_step(): return lax.ppermute(value, ('tm', 'space'), pairs)  9.16 us
    ppermute x11, starting transfers between devices, swap(): return lax.ppermute(value, 'space', pairs)  5.62 us
    ppermute x11, waiting for transfers between devices, swap(): return lax.ppermute(value, 'space', pairs)  1.39 us
  transfers between devices with their start and end apart: 15, of which 4 were waited for; matrix products, arithmetic and copies ran while one was open for 0% of the time, Pallas kernels for 42%

profile of v17, /device:TPU:0, one launch (start us, length us, event | category | flops | bytes accessed | tf_op | source)
XLA Modules:
  0.0 35.5 jit_solution(10505200001635613581)
XLA Ops:
  0.6 0.5 %collective-permute-start = (bf16[2,1024,256]{2,1,0:T(8,128)(2,1)}, bf16[2,1024,256]{2,1,0:T(8,128)(2,1)S(1)}, u32[]{:S(2)}, u32[]{:S(2)}) collective-permute-start(bf16[2,1024,256]{2,1,0:T(8,128)(2,1)} %refs_3_.4), channel_id=1, source_target_pairs={{0,1},{1,0},{2,3},{3,2},{4,5},{5,4},{6,7},{7,6},{8,9},{9,8},{10,11... | collective-permute-start | bytes 3145736 | tf_op jit(solution)/shard_map/ppermute | solution.py:313
  1.1 2.8 %shard_map.86 = (bf16[1024,2048]{1,0:T(8,128)(2,1)S(1)}, bf16[1024,2048]{1,0:T(8,128)(2,1)S(1)}, f32[256,1024]{1,0:T(8,128)S(1)}, bf16[1,256,1024]{2,1,0:T(8,128...) custom-call(bf16[2,1024,2048]{2,1,0:T(8,128)(2,1)} %refs_0_.3, bf16[2,256,1024]{2,1,0:T(8,128)(2,1)} %refs_1_.3, ...), custom_call_target="tpu_custom_call" | custom-call | flops 8000000000 | tf_op jit(solution)/shard_map/pallas_call | solution.py:73
  4.0 1.0 %collective-permute-start.2 = (bf16[256,1024]{1,0:T(8,128)(2,1)S(1)}, bf16[256,1024]{1,0:T(8,128)(2,1)S(1)}, u32[]{:S(2)}, u32[]{:S(2)}) collective-permute-start(bf16[256,1024]{1,0:T(8,128)(2,1)S(1)} %bitcast.10), channel_id=1, source_target_pairs={{0,1},{1,0},{2,3},{3,2},{4,5},{5,4},{6,7},{7,6},{8,9},{9,8},{10,11... | collective-permute-start | bytes 1572872 | tf_op jit(solution)/shard_map/ppermute | solution.py:313
  5.0 0.0 collective-permute-done.refs_4_
  5.0 1.6 %shard_map.87 = (f32[1024,256]{1,0:T(8,128)S(1)}, bf16[1024,256]{1,0:T(8,128)(2,1)S(1)}, bf16[1024,2048]{1,0:T(8,128)(2,1)S(1)}, bf16[1024,256]{1,0:T(8,128)(2,1)S(1)}) custom-call(bf16[1024,2048]{1,0:T(8,128)(2,1)S(1)} %get-tuple-element.33.refs_0_, bf16[1024,256]{1,0:T(8,128)(2,1)S(1)} %get-tuple-element.34.refs_1_, bf16[2,1024,2048]{2,1,0:T(8,128)(2,1)} %refs_0_.4, ...), custom_call_target="tpu_custom_call" | custom-call | flops 8000000000 | tf_op jit(solution)/shard_map/pallas_call | solution.py:73
  6.6 0.1 collective-permute-start.1
  6.7 2.0 %shard_map.88 = (f32[256,1024]{1,0:T(8,128)S(1)}, bf16[256,1024]{1,0:T(8,128)(2,1)S(1)}, bf16[1024,2048]{1,0:T(8,128)(2,1)S(1)}) custom-call(bf16[2,1024,2048]{2,1,0:T(8,128)(2,1)} %refs_0_.4, bf16[2,256,1024]{2,1,0:T(8,128)(2,1)} %refs_1_.3, f32[1024,256]{1,0:T(8,128)S(1)} %get-tuple-element.35.refs_2_, ...), custom_call_target="tpu_custom_call", output_to_operand_aliasing={{2}: (3, {})} | custom-call | flops 8000000000 | tf_op jit(solution)/shard_map/pallas_call | solution.py:73
  8.7 0.0 collective-permute-done.2.refs_6_
  8.7 0.0 collective-permute-done.1.refs_5_
  8.8 2.1 %shard_map.89 = (bf16[1024,256]{1,0:T(8,128)(2,1)S(1)}, f32[128,256]{1,0:T(8,128)S(1)}, bf16[1,128,256]{2,1,0:T(8,128)(2,1)S(1)}, bf16[256,1024]{1,0:T(8,128)(2,1)S(1)}) custom-call(bf16[1024,2048]{1,0:T(8,128)(2,1)S(1)} %get-tuple-element.38.refs_0_, bf16[1024,256]{1,0:T(8,128)(2,1)S(1)} %get-tuple-element.41.refs_1_, ...), custom_call_target="tpu_custom_call" | custom-call | flops 8000000000 | tf_op jit(solution)/shard_map/pallas_call | solution.py:73
  10.9 0.6 %collective-permute-start.4 = (bf16[128,256]{1,0:T(8,128)(2,1)S(1)}, bf16[128,256]{1,0:T(8,128)(2,1)S(1)}, u32[]{:S(2)}, u32[]{:S(2)}) collective-permute-start(bf16[128,256]{1,0:T(8,128)(2,1)S(1)} %bitcast.13), channel_id=1, source_target_pairs={{0,1},{1,0},{2,3},{3,2},{4,5},{5,4},{6,7},{7,6},{8,9},{9,8},{10,11... | collective-permute-start | bytes 196616 | tf_op jit(solution)/shard_map/ppermute | solution.py:313
  11.4 0.1 collective-permute-start.3
  11.5 0.5 %shard_map.90.refs_2_.refs_1_ = f32[1024,256]{1,0:T(8,128)S(1)} custom-call(bf16[1024,2048]{1,0:T(8,128)(2,1)S(1)} %get-tuple-element.40.refs_0_, bf16[1024,256]{1,0:T(8,128)(2,1)S(1)} %get-tuple-element.46.refs_1_), custom_call_target="tpu_custom_call" | custom-call | flops 8000000000 | tf_op jit(solution)/shard_map/pallas_call | solution.py:73
  12.0 0.3 collective-permute-done.4.refs_1_
  12.3 3.0 %collective-permute-start.6 = (bf16[128,256]{1,0:T(8,128)(2,1)S(1)}, bf16[128,256]{1,0:T(8,128)(2,1)S(1)}, u32[]{:S(2)}, u32[]{:S(2)}) collective-permute-start(bf16[128,256]{1,0:T(8,128)(2,1)S(1)} %shard_map.91.refs_3_.refs_0_), channel_id=1, source_target_pairs={{0,2},{1,9},{2,0},{3,11},{4,6},{5,13},{6,4},{7,15},{8,10},{9,1},{1... | collective-permute-start | bytes 196616 | tf_op jit(solution)/shard_map/ppermute | solution.py:330
  15.3 0.0 collective-permute-done.3.refs_2_
  15.3 0.8 %shard_map.92 = (f32[256,1024]{1,0:T(8,128)S(1)}, bf16[1,256,1024]{2,1,0:T(8,128)(2,1)S(1)}) custom-call(bf16[1024,2048]{1,0:T(8,128)(2,1)S(1)} %get-tuple-element.40.refs_0_, f32[1024,256]{1,0:T(8,128)S(1)} %shard_map.90.refs_2_.refs_1_, bf16[1024,256]{1,0:T(8,128)(2,1)S(1)} %collective-permute-done.3.refs_2_, bf16[128,256]{1,0:T(8,128)(2,1)S(1)} %shard_map.91.refs_3_.refs_0_), custom_call_target="tpu_custom_call" | custom-call | flops 8000000000 | tf_op jit(solution)/shard_map/pallas_call | solution.py:73
  16.2 1.6 %collective-permute-start.5 = (bf16[256,1024]{1,0:T(8,128)(2,1)S(1)}, bf16[256,1024]{1,0:T(8,128)(2,1)S(1)}, u32[]{:S(2)}, u32[]{:S(2)}) collective-permute-start(bf16[256,1024]{1,0:T(8,128)(2,1)S(1)} %bitcast.11), channel_id=1, source_target_pairs={{0,1},{1,0},{2,3},{3,2},{4,5},{5,4},{6,7},{7,6},{8,9},{9,8},{10,11... | collective-permute-start | bytes 1572872 | tf_op jit(solution)/shard_map/ppermute | solution.py:313
  17.8 0.0 collective-permute-done.6.refs_1_
  17.8 1.9 %collective-permute-start.8 = (bf16[128,256]{1,0:T(8,128)(2,1)S(1)}, bf16[128,256]{1,0:T(8,128)(2,1)S(1)}, u32[]{:S(2)}, u32[]{:S(2)}) collective-permute-start(bf16[128,256]{1,0:T(8,128)(2,1)S(1)} %shard_map.93.refs_2_.refs_0_), channel_id=1, source_target_pairs={{0,4},{1,17},{2,6},{3,19},{4,0},{5,21},{6,2},{7,23},{8,12},{9,25},... | collective-permute-start | bytes 196616 | tf_op jit(solution)/shard_map/ppermute | solution.py:330
  19.7 1.2 %shard_map.94 = (f32[256,1024]{1,0:T(8,128)S(1)}, bf16[1,256,1024]{2,1,0:T(8,128)(2,1)S(1)}) custom-call(bf16[1024,2048]{1,0:T(8,128)(2,1)S(1)} %get-tuple-element.38.refs_0_, bf16[256,1024]{1,0:T(8,128)(2,1)S(1)} %get-tuple-element.51.refs_1_, bf16[128,256]{1,0:T(8,128)(2,1)S(1)} %shard_map.93.refs_2_.refs_0_), custom_call_target="tpu_custom_call" | custom-call | flops 5000000000 | tf_op jit(solution)/shard_map/pallas_call | solution.py:73
  21.0 0.0 collective-permute-done.5.refs_3_
  21.0 0.0 copy-start
  21.0 0.0 copy-start.1
  21.0 1.3 %shard_map.95 = (f32[256,1024]{1,0:T(8,128)S(1)}, f32[256,1024]{1,0:T(8,128)S(1)}, bf16[1,256,1024]{2,1,0:T(8,128)(2,1)S(1)}) custom-call(bf16[1024,2048]{1,0:T(8,128)(2,1)S(1)} %get-tuple-element.38.refs_0_, f32[8,128]{1,0:T(8,128)S(1)} %get-tuple-element.39.refs_1_, f32[256,1024]{1,0:T(8,128)S(1)} %get-tuple-element.49.refs_2_, ...), custom_call_target="tpu_custom_call" | custom-call | flops 8000000000 | tf_op jit(solution)/shard_map/pallas_call | solution.py:73
  22.3 0.5 %collective-permute-start.7 = (bf16[256,1024]{1,0:T(8,128)(2,1)S(1)}, bf16[256,1024]{1,0:T(8,128)(2,1)S(1)}, u32[]{:S(2)}, u32[]{:S(2)}) collective-permute-start(bf16[256,1024]{1,0:T(8,128)(2,1)S(1)} %bitcast.9), channel_id=1, source_target_pairs={{0,1},{1,0},{2,3},{3,2},{4,5},{5,4},{6,7},{7,6},{8,9},{9,8},{10,11... | collective-permute-start | bytes 1572872 | tf_op jit(solution)/shard_map/ppermute | solution.py:313
  22.9 0.1 collective-permute-start.10
  23.0 0.0 collective-permute-done.8.refs_1_
  23.0 1.6 %collective-permute-start.11 = (bf16[128,256]{1,0:T(8,128)(2,1)S(1)}, bf16[128,256]{1,0:T(8,128)(2,1)S(1)}, u32[]{:S(2)}, u32[]{:S(2)}) collective-permute-start(bf16[128,256]{1,0:T(8,128)(2,1)S(1)} %shard_map.96.refs_4_.refs_0_), channel_id=1, source_target_pairs={{0,8},{1,3},{2,10},{3,1},{4,12},{5,7},{6,14},{7,5},{8,0},{9,11},{1... | collective-permute-start | bytes 196616 | tf_op jit(solution)/shard_map/ppermute | solution.py:330
  24.6 0.0 copy-done
  24.6 0.0 copy-done.1
  24.6 0.8 %shard_map.97 = (f32[1024,256]{1,0:T(8,128)S(1)}, bf16[1024,256]{1,0:T(8,128)(2,1)S(1)}, f32[128,256]{1,0:T(8,128)S(1)}) custom-call(f32[256,1024]{1,0:T(8,128)S(1)} %get-tuple-element.55.refs_2_.refs_0_, bf16[256,1024]{1,0:T(8,128)(2,1)S(1)} %get-tuple-element.51.refs_1_, f32[256,128]{1,0:T(8,128)S(1)} %copy-done, bf16[256,256]{1,0:T(8,128)(2,1)S(1)} %copy-done.1, ...), custom_call_target="tpu_custom_call" | custom-call | flops 5000000000 | tf_op jit(solution)/shard_map/pallas_call | solution.py:73
  25.4 0.0 collective-permute-done.7.refs_3_
  25.4 0.9 %shard_map.98 = (f32[256,1024]{1,0:T(8,128)S(1)}, bf16[1,256,1024]{2,1,0:T(8,128)(2,1)S(1)}) custom-call(bf16[1024,2048]{1,0:T(8,128)(2,1)S(1)} %get-tuple-element.33.refs_0_, f32[256,1024]{1,0:T(8,128)S(1)} %get-tuple-element.37.refs_1_, f32[256,1024]{1,0:T(8,128)S(1)} %get-tuple-element.53.refs_2_, bf16[256,1024]{1,0:T(8,128)(2,1)S(1)} %collective-permute-done.7.refs_3_, ...), custom_call_target="tpu_custom_call" | custom-call | flops 8000000000 | tf_op jit(solution)/shard_map/pallas_call | solution.py:73
  26.3 0.8 %collective-permute-start.9 = (bf16[256,1024]{1,0:T(8,128)(2,1)S(1)}, bf16[256,1024]{1,0:T(8,128)(2,1)S(1)}, u32[]{:S(2)}, u32[]{:S(2)}) collective-permute-start(bf16[256,1024]{1,0:T(8,128)(2,1)S(1)} %bitcast.8), channel_id=1, source_target_pairs={{0,1},{1,0},{2,3},{3,2},{4,5},{5,4},{6,7},{7,6},{8,9},{9,8},{10,11... | collective-permute-start | bytes 1572872 | tf_op jit(solution)/shard_map/ppermute | solution.py:313
  27.1 0.2 collective-permute-done.11.refs_1_
  27.3 2.6 %collective-permute-start.13 = (bf16[128,256]{1,0:T(8,128)(2,1)S(1)}, bf16[128,256]{1,0:T(8,128)(2,1)S(1)}, u32[]{:S(2)}, u32[]{:S(2)}) collective-permute-start(bf16[128,256]{1,0:T(8,128)(2,1)S(1)} %shard_map.99.refs_5_.refs_1_), channel_id=1, source_target_pairs={{0,16},{1,5},{2,18},{3,7},{4,20},{5,1},{6,22},{7,3},{8,24},{9,13},... | collective-permute-start | bytes 196616 | tf_op jit(solution)/shard_map/ppermute | solution.py:330
  30.0 0.0 collective-permute-done.10.refs_4_
  30.0 0.7 %shard_map.100 = (bf16[256,1024]{1,0:T(8,128)(2,1)S(1)}, bf16[1,256,1024]{2,1,0:T(8,128)(2,1)S(1)}) custom-call(bf16[1024,2048]{1,0:T(8,128)(2,1)S(1)} %get-tuple-element.33.refs_0_, bf16[256,1024]{1,0:T(8,128)(2,1)S(1)} %get-tuple-element.43.refs_3_.refs_1_, bf16[256,256]{1,0:T(8,128)(2,1)S(1)} %copy-done.1, ...), custom_call_target="tpu_custom_call" | custom-call | flops 5000000000 | tf_op jit(solution)/shard_map/pallas_call | solution.py:73
  30.6 0.1 collective-permute-start.12
  30.7 0.0 collective-permute-done.9.refs_1_
  30.7 0.3 shard_map.101.refs_2_.refs_0_
  31.1 0.5 %shard_map.102.refs_0_.refs_2_ = f32[256,1024]{1,0:T(8,128)S(1)} custom-call(bf16[1024,2048]{1,0:T(8,128)(2,1)S(1)} %get-tuple-element.33.refs_0_, bf16[256,1024]{1,0:T(8,128)(2,1)S(1)} %get-tuple-element.60.refs_2_.refs_1_, f32[1024,256]{1,0:T(8,128)S(1)} %shard_map.101.refs_2_.refs_0_), custom_call_target="tpu_custom_call" | custom-call | flops 8000000000 | tf_op jit(solution)/shard_map/pallas_call | solution.py:73
  31.6 1.0 %collective-permute-done.12.refs_1_ = bf16[256,1024]{1,0:T(8,128)(2,1)S(1)} collective-permute-done((bf16[256,1024]{1,0:T(8,128)(2,1)S(1)}, bf16[256,1024]{1,0:T(8,128)(2,1)S(1)}, u32[]{:S(2)}, u32[]{:S(2)}) %collective-permute-start.12) | collective-permute-done | bytes 524320 | tf_op jit(solution)/shard_map/ppermute | solution.py:313
  32.6 0.2 shard_map.103.refs_3_.refs_2_
  32.8 0.0 collective-permute-done.13.refs_2_
  32.9 0.2 collective-permute-start.14
  33.1 1.1 %shard_map.105.refs_6_ = f32[256,128]{1,0:T(8,128)} custom-call(bf16[256,256]{1,0:T(8,128)(2,1)S(1)} %copy-done.1, bf16[128,256]{1,0:T(8,128)(2,1)S(1)} %shard_map.104.refs_1_.refs_4_), custom_call_target="tpu_custom_call" | custom-call | flops 8000000000 | tf_op jit(solution)/shard_map/pallas_call | solution.py:73
  34.1 0.1 collective-permute-done.14.refs_5_
  34.2 1.3 %shard_map.106 = bf16[2,1024,256]{2,1,0:T(8,128)(2,1)} custom-call(f32[1024,256]{1,0:T(8,128)S(1)} %shard_map.101.refs_2_.refs_0_, f32[1024,256]{1,0:T(8,128)S(1)} %get-tuple-element.61.refs_1_, bf16[1024,256]{1,0:T(8,128)(2,1)S(1)} %shard_map.103.refs_3_.refs_2_, bf16[1024,256]{1,0:T(8,128)(2,1)S(1)} %get-tuple-element.63.refs_3_, ...), custom_call_target="tpu_custom_call" | custom-call | flops 8000000000 | tf_op jit(solution)/shard_map/pallas_call | solution.py:73
  (5 shorter events, 0.1 us)
Async XLA Ops:
  0.6 4.4 %collective-permute-start = (bf16[2,1024,256]{2,1,0:T(8,128)(2,1)}, bf16[2,1024,256]{2,1,0:T(8,128)(2,1)S(1)}, u32[]{:S(2)}, u32[]{:S(2)}) collective-permute-start(bf16[2,1024,256]{2,1,0:T(8,128)(2,1)} %refs_3_.4), channel_id=1, source_target_pairs={{0,1},{1,0},{2,3},{3,2},{4,5},{5,4},{6,7},{7,6},{8,9},{9,8},{10,11... | collective-permute-start | bytes 3145736 | tf_op jit(solution)/shard_map/ppermute | solution.py:313
  4.0 4.8 %collective-permute-start.2 = (bf16[256,1024]{1,0:T(8,128)(2,1)S(1)}, bf16[256,1024]{1,0:T(8,128)(2,1)S(1)}, u32[]{:S(2)}, u32[]{:S(2)}) collective-permute-start(bf16[256,1024]{1,0:T(8,128)(2,1)S(1)} %bitcast.10), channel_id=1, source_target_pairs={{0,1},{1,0},{2,3},{3,2},{4,5},{5,4},{6,7},{7,6},{8,9},{9,8},{10,11... | collective-permute-start | bytes 1572872 | tf_op jit(solution)/shard_map/ppermute | solution.py:313
  6.6 2.2 %collective-permute-start.1 = (bf16[1024,256]{1,0:T(8,128)(2,1)S(1)}, bf16[1024,256]{1,0:T(8,128)(2,1)S(1)}, u32[]{:S(2)}, u32[]{:S(2)}) collective-permute-start(bf16[1024,256]{1,0:T(8,128)(2,1)S(1)} %get-tuple-element.41.refs_1_), channel_id=1, source_target_pairs={{0,1},{1,0},{2,3},{3,2},{4,5},{5,4},{6,7},{7,6},{8,9},{9,8},{10,11... | collective-permute-start | bytes 1572872 | tf_op jit(solution)/shard_map/ppermute | solution.py:313
  10.9 1.5 %collective-permute-start.4 = (bf16[128,256]{1,0:T(8,128)(2,1)S(1)}, bf16[128,256]{1,0:T(8,128)(2,1)S(1)}, u32[]{:S(2)}, u32[]{:S(2)}) collective-permute-start(bf16[128,256]{1,0:T(8,128)(2,1)S(1)} %bitcast.13), channel_id=1, source_target_pairs={{0,1},{1,0},{2,3},{3,2},{4,5},{5,4},{6,7},{7,6},{8,9},{9,8},{10,11... | collective-permute-start | bytes 196616 | tf_op jit(solution)/shard_map/ppermute | solution.py:313
  11.4 3.9 %collective-permute-start.3 = (bf16[1024,256]{1,0:T(8,128)(2,1)S(1)}, bf16[1024,256]{1,0:T(8,128)(2,1)S(1)}, u32[]{:S(2)}, u32[]{:S(2)}) collective-permute-start(bf16[1024,256]{1,0:T(8,128)(2,1)S(1)} %get-tuple-element.46.refs_1_), channel_id=1, source_target_pairs={{0,1},{1,0},{2,3},{3,2},{4,5},{5,4},{6,7},{7,6},{8,9},{9,8},{10,11... | collective-permute-start | bytes 1572872 | tf_op jit(solution)/shard_map/ppermute | solution.py:313
  12.3 5.4 %collective-permute-start.6 = (bf16[128,256]{1,0:T(8,128)(2,1)S(1)}, bf16[128,256]{1,0:T(8,128)(2,1)S(1)}, u32[]{:S(2)}, u32[]{:S(2)}) collective-permute-start(bf16[128,256]{1,0:T(8,128)(2,1)S(1)} %shard_map.91.refs_3_.refs_0_), channel_id=1, source_target_pairs={{0,2},{1,9},{2,0},{3,11},{4,6},{5,13},{6,4},{7,15},{8,10},{9,1},{1... | collective-permute-start | bytes 196616 | tf_op jit(solution)/shard_map/ppermute | solution.py:330
  16.2 4.8 %collective-permute-start.5 = (bf16[256,1024]{1,0:T(8,128)(2,1)S(1)}, bf16[256,1024]{1,0:T(8,128)(2,1)S(1)}, u32[]{:S(2)}, u32[]{:S(2)}) collective-permute-start(bf16[256,1024]{1,0:T(8,128)(2,1)S(1)} %bitcast.11), channel_id=1, source_target_pairs={{0,1},{1,0},{2,3},{3,2},{4,5},{5,4},{6,7},{7,6},{8,9},{9,8},{10,11... | collective-permute-start | bytes 1572872 | tf_op jit(solution)/shard_map/ppermute | solution.py:313
  17.8 5.2 %collective-permute-start.8 = (bf16[128,256]{1,0:T(8,128)(2,1)S(1)}, bf16[128,256]{1,0:T(8,128)(2,1)S(1)}, u32[]{:S(2)}, u32[]{:S(2)}) collective-permute-start(bf16[128,256]{1,0:T(8,128)(2,1)S(1)} %shard_map.93.refs_2_.refs_0_), channel_id=1, source_target_pairs={{0,4},{1,17},{2,6},{3,19},{4,0},{5,21},{6,2},{7,23},{8,12},{9,25},... | collective-permute-start | bytes 196616 | tf_op jit(solution)/shard_map/ppermute | solution.py:330
  21.0 3.6 %copy-start = (f32[256,128]{1,0:T(8,128)S(1)}, f32[256,128]{1,0:T(8,128)}, u32[]{:S(2)}) copy-start(f32[256,128]{1,0:T(8,128)} %refs_2_.6) | copy-start | bytes 393220
  21.0 3.6 %copy-start.1 = (bf16[256,256]{1,0:T(8,128)(2,1)S(1)}, bf16[256,256]{1,0:T(8,128)(2,1)}, u32[]{:S(2)}) copy-start(bf16[256,256]{1,0:T(8,128)(2,1)} %refs_0_.5) | copy-start | bytes 393220
  22.3 3.0 %collective-permute-start.7 = (bf16[256,1024]{1,0:T(8,128)(2,1)S(1)}, bf16[256,1024]{1,0:T(8,128)(2,1)S(1)}, u32[]{:S(2)}, u32[]{:S(2)}) collective-permute-start(bf16[256,1024]{1,0:T(8,128)(2,1)S(1)} %bitcast.9), channel_id=1, source_target_pairs={{0,1},{1,0},{2,3},{3,2},{4,5},{5,4},{6,7},{7,6},{8,9},{9,8},{10,11... | collective-permute-start | bytes 1572872 | tf_op jit(solution)/shard_map/ppermute | solution.py:313
  22.9 7.1 %collective-permute-start.10 = (bf16[256,1024]{1,0:T(8,128)(2,1)S(1)}, bf16[256,1024]{1,0:T(8,128)(2,1)S(1)}, u32[]{:S(2)}, u32[]{:S(2)}) collective-permute-start(bf16[256,1024]{1,0:T(8,128)(2,1)S(1)} %bitcast.7), channel_id=1, source_target_pairs={{0,1},{1,0},{2,3},{3,2},{4,5},{5,4},{6,7},{7,6},{8,9},{9,8},{10,11... | collective-permute-start | bytes 1572872 | tf_op jit(solution)/shard_map/ppermute | solution.py:313
  23.0 4.3 %collective-permute-start.11 = (bf16[128,256]{1,0:T(8,128)(2,1)S(1)}, bf16[128,256]{1,0:T(8,128)(2,1)S(1)}, u32[]{:S(2)}, u32[]{:S(2)}) collective-permute-start(bf16[128,256]{1,0:T(8,128)(2,1)S(1)} %shard_map.96.refs_4_.refs_0_), channel_id=1, source_target_pairs={{0,8},{1,3},{2,10},{3,1},{4,12},{5,7},{6,14},{7,5},{8,0},{9,11},{1... | collective-permute-start | bytes 196616 | tf_op jit(solution)/shard_map/ppermute | solution.py:330
  26.3 4.4 %collective-permute-start.9 = (bf16[256,1024]{1,0:T(8,128)(2,1)S(1)}, bf16[256,1024]{1,0:T(8,128)(2,1)S(1)}, u32[]{:S(2)}, u32[]{:S(2)}) collective-permute-start(bf16[256,1024]{1,0:T(8,128)(2,1)S(1)} %bitcast.8), channel_id=1, source_target_pairs={{0,1},{1,0},{2,3},{3,2},{4,5},{5,4},{6,7},{7,6},{8,9},{9,8},{10,11... | collective-permute-start | bytes 1572872 | tf_op jit(solution)/shard_map/ppermute | solution.py:313
  27.3 5.5 %collective-permute-start.13 = (bf16[128,256]{1,0:T(8,128)(2,1)S(1)}, bf16[128,256]{1,0:T(8,128)(2,1)S(1)}, u32[]{:S(2)}, u32[]{:S(2)}) collective-permute-start(bf16[128,256]{1,0:T(8,128)(2,1)S(1)} %shard_map.99.refs_5_.refs_1_), channel_id=1, source_target_pairs={{0,16},{1,5},{2,18},{3,7},{4,20},{5,1},{6,22},{7,3},{8,24},{9,13},... | collective-permute-start | bytes 196616 | tf_op jit(solution)/shard_map/ppermute | solution.py:330
  30.6 2.0 %collective-permute-start.12 = (bf16[256,1024]{1,0:T(8,128)(2,1)S(1)}, bf16[256,1024]{1,0:T(8,128)(2,1)S(1)}, u32[]{:S(2)}, u32[]{:S(2)}) collective-permute-start(bf16[256,1024]{1,0:T(8,128)(2,1)S(1)} %bitcast.12), channel_id=1, source_target_pairs={{0,1},{1,0},{2,3},{3,2},{4,5},{5,4},{6,7},{7,6},{8,9},{9,8},{10,11... | collective-permute-start | bytes 1572872 | tf_op jit(solution)/shard_map/ppermute | solution.py:313
  32.9 1.3 %collective-permute-start.14 = (bf16[128,256]{1,0:T(8,128)(2,1)S(1)}, bf16[128,256]{1,0:T(8,128)(2,1)S(1)}, u32[]{:S(2)}, u32[]{:S(2)}) collective-permute-start(bf16[128,256]{1,0:T(8,128)(2,1)S(1)} %shard_map.104.refs_1_.refs_4_), channel_id=1, source_target_pairs={{0,1},{1,0},{2,3},{3,2},{4,5},{5,4},{6,7},{7,6},{8,9},{9,8},{10,11... | collective-permute-start | bytes 196616 | tf_op jit(solution)/shard_map/ppermute | solution.py:313

commit v18 on v17

--- a/solution.py
+++ b/solution.py
@@ -169,7 +169,7 @@
         e1[...] = jnp.where(live, e1[...], jnp.zeros_like(e1[...]))
         for i in range(tiles):
             each(copies1, i, lambda copy: copy.wait())
-            for early in range(2 * i, min(2 * i + 2, tiles)):
+            for early in range(tiles if i == 0 else 0):
                 each(copies0, early, lambda copy: copy.start(priority=1))
         noise_copy.start()
         lower_rows(e1, d1, own, other)

time: 35.7 us -> 35.5 us (level)
  no operation moved by 1% of the time
where the time goes in v18:
time: 35.5 us; the launch traced here: 35.3 us
  Pallas kernels  18.2 us (51%)
  starting transfers between devices  14.7 us (41%)
  waiting for transfers between devices  1.59 us (4%)
  between operations  0.83 us (2%)
    pallas_call x21, Pallas kernels, call(): pl.pallas_call(run, in_specs=specs, out_specs=[pl.BlockSpec(memory_space=...  18.2 us
    ppermute x4, starting transfers between devices, swap_step(): return lax.ppermute(value, ('tm', 'space'), pairs)  9.14 us
    ppermute x11, starting transfers between devices, swap(): return lax.ppermute(value, 'space', pairs)  5.54 us
    ppermute x11, waiting for transfers between devices, swap(): return lax.ppermute(value, 'space', pairs)  1.39 us
  transfers between devices with their start and end apart: 15, of which 4 were waited for; matrix products, arithmetic and copies ran while one was open for 0% of the time, Pallas kernels for 42%

profile of v18, /device:TPU:0, one launch (start us, length us, event | category | flops | bytes accessed | tf_op | source)
XLA Modules:
  0.0 35.3 jit_solution(5222807995271483783)
XLA Ops:
  0.6 0.5 %collective-permute-start = (bf16[2,1024,256]{2,1,0:T(8,128)(2,1)}, bf16[2,1024,256]{2,1,0:T(8,128)(2,1)S(1)}, u32[]{:S(2)}, u32[]{:S(2)}) collective-permute-start(bf16[2,1024,256]{2,1,0:T(8,128)(2,1)} %refs_3_.4), channel_id=1, source_target_pairs={{0,1},{1,0},{2,3},{3,2},{4,5},{5,4},{6,7},{7,6},{8,9},{9,8},{10,11... | collective-permute-start | bytes 3145736 | tf_op jit(solution)/shard_map/ppermute | solution.py:313
  1.1 2.7 %shard_map.86 = (bf16[1024,2048]{1,0:T(8,128)(2,1)S(1)}, bf16[1024,2048]{1,0:T(8,128)(2,1)S(1)}, f32[256,1024]{1,0:T(8,128)S(1)}, bf16[1,256,1024]{2,1,0:T(8,128...) custom-call(bf16[2,1024,2048]{2,1,0:T(8,128)(2,1)} %refs_0_.3, bf16[2,256,1024]{2,1,0:T(8,128)(2,1)} %refs_1_.3, ...), custom_call_target="tpu_custom_call" | custom-call | flops 8000000000 | tf_op jit(solution)/shard_map/pallas_call | solution.py:73
  3.8 0.9 %collective-permute-start.2 = (bf16[256,1024]{1,0:T(8,128)(2,1)S(1)}, bf16[256,1024]{1,0:T(8,128)(2,1)S(1)}, u32[]{:S(2)}, u32[]{:S(2)}) collective-permute-start(bf16[256,1024]{1,0:T(8,128)(2,1)S(1)} %bitcast.10), channel_id=1, source_target_pairs={{0,1},{1,0},{2,3},{3,2},{4,5},{5,4},{6,7},{7,6},{8,9},{9,8},{10,11... | collective-permute-start | bytes 1572872 | tf_op jit(solution)/shard_map/ppermute | solution.py:313
  4.8 0.0 collective-permute-done.refs_4_
  4.8 1.6 %shard_map.87 = (f32[1024,256]{1,0:T(8,128)S(1)}, bf16[1024,256]{1,0:T(8,128)(2,1)S(1)}, bf16[1024,2048]{1,0:T(8,128)(2,1)S(1)}, bf16[1024,256]{1,0:T(8,128)(2,1)S(1)}) custom-call(bf16[1024,2048]{1,0:T(8,128)(2,1)S(1)} %get-tuple-element.33.refs_0_, bf16[1024,256]{1,0:T(8,128)(2,1)S(1)} %get-tuple-element.34.refs_1_, bf16[2,1024,2048]{2,1,0:T(8,128)(2,1)} %refs_0_.4, ...), custom_call_target="tpu_custom_call" | custom-call | flops 8000000000 | tf_op jit(solution)/shard_map/pallas_call | solution.py:73
  6.4 0.1 collective-permute-start.1
  6.4 2.0 %shard_map.88 = (f32[256,1024]{1,0:T(8,128)S(1)}, bf16[256,1024]{1,0:T(8,128)(2,1)S(1)}, bf16[1024,2048]{1,0:T(8,128)(2,1)S(1)}) custom-call(bf16[2,1024,2048]{2,1,0:T(8,128)(2,1)} %refs_0_.4, bf16[2,256,1024]{2,1,0:T(8,128)(2,1)} %refs_1_.3, f32[1024,256]{1,0:T(8,128)S(1)} %get-tuple-element.35.refs_2_, ...), custom_call_target="tpu_custom_call", output_to_operand_aliasing={{2}: (3, {})} | custom-call | flops 8000000000 | tf_op jit(solution)/shard_map/pallas_call | solution.py:73
  8.5 0.0 collective-permute-done.2.refs_6_
  8.5 0.0 collective-permute-done.1.refs_5_
  8.5 2.1 %shard_map.89 = (bf16[1024,256]{1,0:T(8,128)(2,1)S(1)}, f32[128,256]{1,0:T(8,128)S(1)}, bf16[1,128,256]{2,1,0:T(8,128)(2,1)S(1)}, bf16[256,1024]{1,0:T(8,128)(2,1)S(1)}) custom-call(bf16[1024,2048]{1,0:T(8,128)(2,1)S(1)} %get-tuple-element.38.refs_0_, bf16[1024,256]{1,0:T(8,128)(2,1)S(1)} %get-tuple-element.41.refs_1_, ...), custom_call_target="tpu_custom_call" | custom-call | flops 8000000000 | tf_op jit(solution)/shard_map/pallas_call | solution.py:73
  10.6 0.6 %collective-permute-start.4 = (bf16[128,256]{1,0:T(8,128)(2,1)S(1)}, bf16[128,256]{1,0:T(8,128)(2,1)S(1)}, u32[]{:S(2)}, u32[]{:S(2)}) collective-permute-start(bf16[128,256]{1,0:T(8,128)(2,1)S(1)} %bitcast.13), channel_id=1, source_target_pairs={{0,1},{1,0},{2,3},{3,2},{4,5},{5,4},{6,7},{7,6},{8,9},{9,8},{10,11... | collective-permute-start | bytes 196616 | tf_op jit(solution)/shard_map/ppermute | solution.py:313
  11.2 0.1 collective-permute-start.3
  11.3 0.5 %shard_map.90.refs_2_.refs_1_ = f32[1024,256]{1,0:T(8,128)S(1)} custom-call(bf16[1024,2048]{1,0:T(8,128)(2,1)S(1)} %get-tuple-element.40.refs_0_, bf16[1024,256]{1,0:T(8,128)(2,1)S(1)} %get-tuple-element.46.refs_1_), custom_call_target="tpu_custom_call" | custom-call | flops 8000000000 | tf_op jit(solution)/shard_map/pallas_call | solution.py:73
  11.8 0.3 collective-permute-done.4.refs_1_
  12.1 3.0 %collective-permute-start.6 = (bf16[128,256]{1,0:T(8,128)(2,1)S(1)}, bf16[128,256]{1,0:T(8,128)(2,1)S(1)}, u32[]{:S(2)}, u32[]{:S(2)}) collective-permute-start(bf16[128,256]{1,0:T(8,128)(2,1)S(1)} %shard_map.91.refs_3_.refs_0_), channel_id=1, source_target_pairs={{0,2},{1,9},{2,0},{3,11},{4,6},{5,13},{6,4},{7,15},{8,10},{9,1},{1... | collective-permute-start | bytes 196616 | tf_op jit(solution)/shard_map/ppermute | solution.py:330
  15.1 0.0 collective-permute-done.3.refs_2_
  15.1 0.8 %shard_map.92 = (f32[256,1024]{1,0:T(8,128)S(1)}, bf16[1,256,1024]{2,1,0:T(8,128)(2,1)S(1)}) custom-call(bf16[1024,2048]{1,0:T(8,128)(2,1)S(1)} %get-tuple-element.40.refs_0_, f32[1024,256]{1,0:T(8,128)S(1)} %shard_map.90.refs_2_.refs_1_, bf16[1024,256]{1,0:T(8,128)(2,1)S(1)} %collective-permute-done.3.refs_2_, bf16[128,256]{1,0:T(8,128)(2,1)S(1)} %shard_map.91.refs_3_.refs_0_), custom_call_target="tpu_custom_call" | custom-call | flops 8000000000 | tf_op jit(solution)/shard_map/pallas_call | solution.py:73
  15.9 1.6 %collective-permute-start.5 = (bf16[256,1024]{1,0:T(8,128)(2,1)S(1)}, bf16[256,1024]{1,0:T(8,128)(2,1)S(1)}, u32[]{:S(2)}, u32[]{:S(2)}) collective-permute-start(bf16[256,1024]{1,0:T(8,128)(2,1)S(1)} %bitcast.11), channel_id=1, source_target_pairs={{0,1},{1,0},{2,3},{3,2},{4,5},{5,4},{6,7},{7,6},{8,9},{9,8},{10,11... | collective-permute-start | bytes 1572872 | tf_op jit(solution)/shard_map/ppermute | solution.py:313
  17.5 0.0 collective-permute-done.6.refs_1_
  17.6 1.9 %collective-permute-start.8 = (bf16[128,256]{1,0:T(8,128)(2,1)S(1)}, bf16[128,256]{1,0:T(8,128)(2,1)S(1)}, u32[]{:S(2)}, u32[]{:S(2)}) collective-permute-start(bf16[128,256]{1,0:T(8,128)(2,1)S(1)} %shard_map.93.refs_2_.refs_0_), channel_id=1, source_target_pairs={{0,4},{1,17},{2,6},{3,19},{4,0},{5,21},{6,2},{7,23},{8,12},{9,25},... | collective-permute-start | bytes 196616 | tf_op jit(solution)/shard_map/ppermute | solution.py:330
  19.5 1.2 %shard_map.94 = (f32[256,1024]{1,0:T(8,128)S(1)}, bf16[1,256,1024]{2,1,0:T(8,128)(2,1)S(1)}) custom-call(bf16[1024,2048]{1,0:T(8,128)(2,1)S(1)} %get-tuple-element.38.refs_0_, bf16[256,1024]{1,0:T(8,128)(2,1)S(1)} %get-tuple-element.51.refs_1_, bf16[128,256]{1,0:T(8,128)(2,1)S(1)} %shard_map.93.refs_2_.refs_0_), custom_call_target="tpu_custom_call" | custom-call | flops 5000000000 | tf_op jit(solution)/shard_map/pallas_call | solution.py:73
  20.7 0.0 collective-permute-done.5.refs_3_
  20.8 0.0 copy-start
  20.8 0.0 copy-start.1
  20.8 1.3 %shard_map.95 = (f32[256,1024]{1,0:T(8,128)S(1)}, f32[256,1024]{1,0:T(8,128)S(1)}, bf16[1,256,1024]{2,1,0:T(8,128)(2,1)S(1)}) custom-call(bf16[1024,2048]{1,0:T(8,128)(2,1)S(1)} %get-tuple-element.38.refs_0_, f32[8,128]{1,0:T(8,128)S(1)} %get-tuple-element.39.refs_1_, f32[256,1024]{1,0:T(8,128)S(1)} %get-tuple-element.49.refs_2_, ...), custom_call_target="tpu_custom_call" | custom-call | flops 8000000000 | tf_op jit(solution)/shard_map/pallas_call | solution.py:73
  22.1 0.5 %collective-permute-start.7 = (bf16[256,1024]{1,0:T(8,128)(2,1)S(1)}, bf16[256,1024]{1,0:T(8,128)(2,1)S(1)}, u32[]{:S(2)}, u32[]{:S(2)}) collective-permute-start(bf16[256,1024]{1,0:T(8,128)(2,1)S(1)} %bitcast.9), channel_id=1, source_target_pairs={{0,1},{1,0},{2,3},{3,2},{4,5},{5,4},{6,7},{7,6},{8,9},{9,8},{10,11... | collective-permute-start | bytes 1572872 | tf_op jit(solution)/shard_map/ppermute | solution.py:313
  22.6 0.1 collective-permute-start.10
  22.7 0.0 collective-permute-done.8.refs_1_
  22.8 1.6 %collective-permute-start.11 = (bf16[128,256]{1,0:T(8,128)(2,1)S(1)}, bf16[128,256]{1,0:T(8,128)(2,1)S(1)}, u32[]{:S(2)}, u32[]{:S(2)}) collective-permute-start(bf16[128,256]{1,0:T(8,128)(2,1)S(1)} %shard_map.96.refs_4_.refs_0_), channel_id=1, source_target_pairs={{0,8},{1,3},{2,10},{3,1},{4,12},{5,7},{6,14},{7,5},{8,0},{9,11},{1... | collective-permute-start | bytes 196616 | tf_op jit(solution)/shard_map/ppermute | solution.py:330
  24.4 0.0 copy-done
  24.4 0.0 copy-done.1
  24.4 0.8 %shard_map.97 = (f32[1024,256]{1,0:T(8,128)S(1)}, bf16[1024,256]{1,0:T(8,128)(2,1)S(1)}, f32[128,256]{1,0:T(8,128)S(1)}) custom-call(f32[256,1024]{1,0:T(8,128)S(1)} %get-tuple-element.55.refs_2_.refs_0_, bf16[256,1024]{1,0:T(8,128)(2,1)S(1)} %get-tuple-element.51.refs_1_, f32[256,128]{1,0:T(8,128)S(1)} %copy-done, bf16[256,256]{1,0:T(8,128)(2,1)S(1)} %copy-done.1, ...), custom_call_target="tpu_custom_call" | custom-call | flops 5000000000 | tf_op jit(solution)/shard_map/pallas_call | solution.py:73
  25.1 0.0 collective-permute-done.7.refs_3_
  25.2 0.9 %shard_map.98 = (f32[256,1024]{1,0:T(8,128)S(1)}, bf16[1,256,1024]{2,1,0:T(8,128)(2,1)S(1)}) custom-call(bf16[1024,2048]{1,0:T(8,128)(2,1)S(1)} %get-tuple-element.33.refs_0_, f32[256,1024]{1,0:T(8,128)S(1)} %get-tuple-element.37.refs_1_, f32[256,1024]{1,0:T(8,128)S(1)} %get-tuple-element.53.refs_2_, bf16[256,1024]{1,0:T(8,128)(2,1)S(1)} %collective-permute-done.7.refs_3_, ...), custom_call_target="tpu_custom_call" | custom-call | flops 8000000000 | tf_op jit(solution)/shard_map/pallas_call | solution.py:73
  26.0 0.9 %collective-permute-start.9 = (bf16[256,1024]{1,0:T(8,128)(2,1)S(1)}, bf16[256,1024]{1,0:T(8,128)(2,1)S(1)}, u32[]{:S(2)}, u32[]{:S(2)}) collective-permute-start(bf16[256,1024]{1,0:T(8,128)(2,1)S(1)} %bitcast.8), channel_id=1, source_target_pairs={{0,1},{1,0},{2,3},{3,2},{4,5},{5,4},{6,7},{7,6},{8,9},{9,8},{10,11... | collective-permute-start | bytes 1572872 | tf_op jit(solution)/shard_map/ppermute | solution.py:313
  26.9 0.2 collective-permute-done.11.refs_1_
  27.1 2.6 %collective-permute-start.13 = (bf16[128,256]{1,0:T(8,128)(2,1)S(1)}, bf16[128,256]{1,0:T(8,128)(2,1)S(1)}, u32[]{:S(2)}, u32[]{:S(2)}) collective-permute-start(bf16[128,256]{1,0:T(8,128)(2,1)S(1)} %shard_map.99.refs_5_.refs_1_), channel_id=1, source_target_pairs={{0,16},{1,5},{2,18},{3,7},{4,20},{5,1},{6,22},{7,3},{8,24},{9,13},... | collective-permute-start | bytes 196616 | tf_op jit(solution)/shard_map/ppermute | solution.py:330
  29.7 0.0 collective-permute-done.10.refs_4_
  29.7 0.7 %shard_map.100 = (bf16[256,1024]{1,0:T(8,128)(2,1)S(1)}, bf16[1,256,1024]{2,1,0:T(8,128)(2,1)S(1)}) custom-call(bf16[1024,2048]{1,0:T(8,128)(2,1)S(1)} %get-tuple-element.33.refs_0_, bf16[256,1024]{1,0:T(8,128)(2,1)S(1)} %get-tuple-element.43.refs_3_.refs_1_, bf16[256,256]{1,0:T(8,128)(2,1)S(1)} %copy-done.1, ...), custom_call_target="tpu_custom_call" | custom-call | flops 5000000000 | tf_op jit(solution)/shard_map/pallas_call | solution.py:73
  30.4 0.1 collective-permute-start.12
  30.5 0.0 collective-permute-done.9.refs_1_
  30.5 0.3 shard_map.101.refs_2_.refs_0_
  30.8 0.5 %shard_map.102.refs_0_.refs_2_ = f32[256,1024]{1,0:T(8,128)S(1)} custom-call(bf16[1024,2048]{1,0:T(8,128)(2,1)S(1)} %get-tuple-element.33.refs_0_, bf16[256,1024]{1,0:T(8,128)(2,1)S(1)} %get-tuple-element.60.refs_2_.refs_1_, f32[1024,256]{1,0:T(8,128)S(1)} %shard_map.101.refs_2_.refs_0_), custom_call_target="tpu_custom_call" | custom-call | flops 8000000000 | tf_op jit(solution)/shard_map/pallas_call | solution.py:73
  31.4 1.0 %collective-permute-done.12.refs_1_ = bf16[256,1024]{1,0:T(8,128)(2,1)S(1)} collective-permute-done((bf16[256,1024]{1,0:T(8,128)(2,1)S(1)}, bf16[256,1024]{1,0:T(8,128)(2,1)S(1)}, u32[]{:S(2)}, u32[]{:S(2)}) %collective-permute-start.12) | collective-permute-done | bytes 524320 | tf_op jit(solution)/shard_map/ppermute | solution.py:313
  32.4 0.2 shard_map.103.refs_3_.refs_2_
  32.6 0.0 collective-permute-done.13.refs_2_
  32.6 0.2 collective-permute-start.14
  32.8 1.1 %shard_map.105.refs_6_ = f32[256,128]{1,0:T(8,128)} custom-call(bf16[256,256]{1,0:T(8,128)(2,1)S(1)} %copy-done.1, bf16[128,256]{1,0:T(8,128)(2,1)S(1)} %shard_map.104.refs_1_.refs_4_), custom_call_target="tpu_custom_call" | custom-call | flops 8000000000 | tf_op jit(solution)/shard_map/pallas_call | solution.py:73
  33.9 0.1 collective-permute-done.14.refs_5_
  34.0 1.3 %shard_map.106 = bf16[2,1024,256]{2,1,0:T(8,128)(2,1)} custom-call(f32[1024,256]{1,0:T(8,128)S(1)} %shard_map.101.refs_2_.refs_0_, f32[1024,256]{1,0:T(8,128)S(1)} %get-tuple-element.61.refs_1_, bf16[1024,256]{1,0:T(8,128)(2,1)S(1)} %shard_map.103.refs_3_.refs_2_, bf16[1024,256]{1,0:T(8,128)(2,1)S(1)} %get-tuple-element.63.refs_3_, ...), custom_call_target="tpu_custom_call" | custom-call | flops 8000000000 | tf_op jit(solution)/shard_map/pallas_call | solution.py:73
  (5 shorter events, 0.1 us)
Async XLA Ops:
  0.6 4.2 %collective-permute-start = (bf16[2,1024,256]{2,1,0:T(8,128)(2,1)}, bf16[2,1024,256]{2,1,0:T(8,128)(2,1)S(1)}, u32[]{:S(2)}, u32[]{:S(2)}) collective-permute-start(bf16[2,1024,256]{2,1,0:T(8,128)(2,1)} %refs_3_.4), channel_id=1, source_target_pairs={{0,1},{1,0},{2,3},{3,2},{4,5},{5,4},{6,7},{7,6},{8,9},{9,8},{10,11... | collective-permute-start | bytes 3145736 | tf_op jit(solution)/shard_map/ppermute | solution.py:313
  3.8 4.7 %collective-permute-start.2 = (bf16[256,1024]{1,0:T(8,128)(2,1)S(1)}, bf16[256,1024]{1,0:T(8,128)(2,1)S(1)}, u32[]{:S(2)}, u32[]{:S(2)}) collective-permute-start(bf16[256,1024]{1,0:T(8,128)(2,1)S(1)} %bitcast.10), channel_id=1, source_target_pairs={{0,1},{1,0},{2,3},{3,2},{4,5},{5,4},{6,7},{7,6},{8,9},{9,8},{10,11... | collective-permute-start | bytes 1572872 | tf_op jit(solution)/shard_map/ppermute | solution.py:313
  6.4 2.2 %collective-permute-start.1 = (bf16[1024,256]{1,0:T(8,128)(2,1)S(1)}, bf16[1024,256]{1,0:T(8,128)(2,1)S(1)}, u32[]{:S(2)}, u32[]{:S(2)}) collective-permute-start(bf16[1024,256]{1,0:T(8,128)(2,1)S(1)} %get-tuple-element.41.refs_1_), channel_id=1, source_target_pairs={{0,1},{1,0},{2,3},{3,2},{4,5},{5,4},{6,7},{7,6},{8,9},{9,8},{10,11... | collective-permute-start | bytes 1572872 | tf_op jit(solution)/shard_map/ppermute | solution.py:313
  10.6 1.5 %collective-permute-start.4 = (bf16[128,256]{1,0:T(8,128)(2,1)S(1)}, bf16[128,256]{1,0:T(8,128)(2,1)S(1)}, u32[]{:S(2)}, u32[]{:S(2)}) collective-permute-start(bf16[128,256]{1,0:T(8,128)(2,1)S(1)} %bitcast.13), channel_id=1, source_target_pairs={{0,1},{1,0},{2,3},{3,2},{4,5},{5,4},{6,7},{7,6},{8,9},{9,8},{10,11... | collective-permute-start | bytes 196616 | tf_op jit(solution)/shard_map/ppermute | solution.py:313
  11.2 3.9 %collective-permute-start.3 = (bf16[1024,256]{1,0:T(8,128)(2,1)S(1)}, bf16[1024,256]{1,0:T(8,128)(2,1)S(1)}, u32[]{:S(2)}, u32[]{:S(2)}) collective-permute-start(bf16[1024,256]{1,0:T(8,128)(2,1)S(1)} %get-tuple-element.46.refs_1_), channel_id=1, source_target_pairs={{0,1},{1,0},{2,3},{3,2},{4,5},{5,4},{6,7},{7,6},{8,9},{9,8},{10,11... | collective-permute-start | bytes 1572872 | tf_op jit(solution)/shard_map/ppermute | solution.py:313
  12.1 5.4 %collective-permute-start.6 = (bf16[128,256]{1,0:T(8,128)(2,1)S(1)}, bf16[128,256]{1,0:T(8,128)(2,1)S(1)}, u32[]{:S(2)}, u32[]{:S(2)}) collective-permute-start(bf16[128,256]{1,0:T(8,128)(2,1)S(1)} %shard_map.91.refs_3_.refs_0_), channel_id=1, source_target_pairs={{0,2},{1,9},{2,0},{3,11},{4,6},{5,13},{6,4},{7,15},{8,10},{9,1},{1... | collective-permute-start | bytes 196616 | tf_op jit(solution)/shard_map/ppermute | solution.py:330
  15.9 4.8 %collective-permute-start.5 = (bf16[256,1024]{1,0:T(8,128)(2,1)S(1)}, bf16[256,1024]{1,0:T(8,128)(2,1)S(1)}, u32[]{:S(2)}, u32[]{:S(2)}) collective-permute-start(bf16[256,1024]{1,0:T(8,128)(2,1)S(1)} %bitcast.11), channel_id=1, source_target_pairs={{0,1},{1,0},{2,3},{3,2},{4,5},{5,4},{6,7},{7,6},{8,9},{9,8},{10,11... | collective-permute-start | bytes 1572872 | tf_op jit(solution)/shard_map/ppermute | solution.py:313
  17.6 5.2 %collective-permute-start.8 = (bf16[128,256]{1,0:T(8,128)(2,1)S(1)}, bf16[128,256]{1,0:T(8,128)(2,1)S(1)}, u32[]{:S(2)}, u32[]{:S(2)}) collective-permute-start(bf16[128,256]{1,0:T(8,128)(2,1)S(1)} %shard_map.93.refs_2_.refs_0_), channel_id=1, source_target_pairs={{0,4},{1,17},{2,6},{3,19},{4,0},{5,21},{6,2},{7,23},{8,12},{9,25},... | collective-permute-start | bytes 196616 | tf_op jit(solution)/shard_map/ppermute | solution.py:330
  20.8 3.6 %copy-start = (f32[256,128]{1,0:T(8,128)S(1)}, f32[256,128]{1,0:T(8,128)}, u32[]{:S(2)}) copy-start(f32[256,128]{1,0:T(8,128)} %refs_2_.6) | copy-start | bytes 393220
  20.8 3.6 %copy-start.1 = (bf16[256,256]{1,0:T(8,128)(2,1)S(1)}, bf16[256,256]{1,0:T(8,128)(2,1)}, u32[]{:S(2)}) copy-start(bf16[256,256]{1,0:T(8,128)(2,1)} %refs_0_.5) | copy-start | bytes 393220
  22.1 3.0 %collective-permute-start.7 = (bf16[256,1024]{1,0:T(8,128)(2,1)S(1)}, bf16[256,1024]{1,0:T(8,128)(2,1)S(1)}, u32[]{:S(2)}, u32[]{:S(2)}) collective-permute-start(bf16[256,1024]{1,0:T(8,128)(2,1)S(1)} %bitcast.9), channel_id=1, source_target_pairs={{0,1},{1,0},{2,3},{3,2},{4,5},{5,4},{6,7},{7,6},{8,9},{9,8},{10,11... | collective-permute-start | bytes 1572872 | tf_op jit(solution)/shard_map/ppermute | solution.py:313
  22.6 7.1 %collective-permute-start.10 = (bf16[256,1024]{1,0:T(8,128)(2,1)S(1)}, bf16[256,1024]{1,0:T(8,128)(2,1)S(1)}, u32[]{:S(2)}, u32[]{:S(2)}) collective-permute-start(bf16[256,1024]{1,0:T(8,128)(2,1)S(1)} %bitcast.7), channel_id=1, source_target_pairs={{0,1},{1,0},{2,3},{3,2},{4,5},{5,4},{6,7},{7,6},{8,9},{9,8},{10,11... | collective-permute-start | bytes 1572872 | tf_op jit(solution)/shard_map/ppermute | solution.py:313
  22.8 4.3 %collective-permute-start.11 = (bf16[128,256]{1,0:T(8,128)(2,1)S(1)}, bf16[128,256]{1,0:T(8,128)(2,1)S(1)}, u32[]{:S(2)}, u32[]{:S(2)}) collective-permute-start(bf16[128,256]{1,0:T(8,128)(2,1)S(1)} %shard_map.96.refs_4_.refs_0_), channel_id=1, source_target_pairs={{0,8},{1,3},{2,10},{3,1},{4,12},{5,7},{6,14},{7,5},{8,0},{9,11},{1... | collective-permute-start | bytes 196616 | tf_op jit(solution)/shard_map/ppermute | solution.py:330
  26.0 4.4 %collective-permute-start.9 = (bf16[256,1024]{1,0:T(8,128)(2,1)S(1)}, bf16[256,1024]{1,0:T(8,128)(2,1)S(1)}, u32[]{:S(2)}, u32[]{:S(2)}) collective-permute-start(bf16[256,1024]{1,0:T(8,128)(2,1)S(1)} %bitcast.8), channel_id=1, source_target_pairs={{0,1},{1,0},{2,3},{3,2},{4,5},{5,4},{6,7},{7,6},{8,9},{9,8},{10,11... | collective-permute-start | bytes 1572872 | tf_op jit(solution)/shard_map/ppermute | solution.py:313
  27.1 5.5 %collective-permute-start.13 = (bf16[128,256]{1,0:T(8,128)(2,1)S(1)}, bf16[128,256]{1,0:T(8,128)(2,1)S(1)}, u32[]{:S(2)}, u32[]{:S(2)}) collective-permute-start(bf16[128,256]{1,0:T(8,128)(2,1)S(1)} %shard_map.99.refs_5_.refs_1_), channel_id=1, source_target_pairs={{0,16},{1,5},{2,18},{3,7},{4,20},{5,1},{6,22},{7,3},{8,24},{9,13},... | collective-permute-start | bytes 196616 | tf_op jit(solution)/shard_map/ppermute | solution.py:330
  30.4 2.0 %collective-permute-start.12 = (bf16[256,1024]{1,0:T(8,128)(2,1)S(1)}, bf16[256,1024]{1,0:T(8,128)(2,1)S(1)}, u32[]{:S(2)}, u32[]{:S(2)}) collective-permute-start(bf16[256,1024]{1,0:T(8,128)(2,1)S(1)} %bitcast.12), channel_id=1, source_target_pairs={{0,1},{1,0},{2,3},{3,2},{4,5},{5,4},{6,7},{7,6},{8,9},{9,8},{10,11... | collective-permute-start | bytes 1572872 | tf_op jit(solution)/shard_map/ppermute | solution.py:313
  32.6 1.3 %collective-permute-start.14 = (bf16[128,256]{1,0:T(8,128)(2,1)S(1)}, bf16[128,256]{1,0:T(8,128)(2,1)S(1)}, u32[]{:S(2)}, u32[]{:S(2)}) collective-permute-start(bf16[128,256]{1,0:T(8,128)(2,1)S(1)} %shard_map.104.refs_1_.refs_4_), channel_id=1, source_target_pairs={{0,1},{1,0},{2,3},{3,2},{4,5},{5,4},{6,7},{7,6},{8,9},{9,8},{10,11... | collective-permute-start | bytes 196616 | tf_op jit(solution)/shard_map/ppermute | solution.py:313
